TPU v7x, 512 devices: a whole 4x8x8 slice. The times are simulated.
512 devices in a mesh: dp: 8 (over z_hi, core), expert: 64 (over x, y, z_lo).
Axes of the slice: x: 4, y: 8, z: 8 (z_hi: 4, z_lo: 2; z = z_hi * 2 + z_lo), core: 2. Of those that a mesh axis runs over, the one named last changes fastest.
Arguments:
- tokens: bfloat16 [2048, 3584], P('expert', 'dp'), may hold values from -6 to 6
- cotangent: bfloat16 [2048, 3584], P('expert', 'dp'), may hold values from -6 to 6
- expert_ids: int32 [2048, 8], P('expert'), may hold values from 0 to 63, all different within a row; in each aligned block of 32 rows (0 to 31, 32 to 63, ...) at most 10 rows name the same one
- route_weight: float32 [2048, 8], P('expert'), may hold values from 0.05 to 0.4
- replaced: int32 [1], replicated, may hold values from 0 to 63
- gate_weight: bfloat16 [64, 3584, 1024], P('expert', 'dp'), may hold values from -0.09375 to 0.09375
- up_weight: bfloat16 [64, 3584, 1024], P('expert', 'dp'), may hold values from -0.09375 to 0.09375
- down_weight: bfloat16 [64, 1024, 3584], P('expert', None, 'dp'), may hold values from -0.1875 to 0.1875
- backup: bfloat16 [3, 3584, 1024], P(None, 'dp', 'expert'), may hold values from -0.09375 to 0.09375
Outputs:
- combined: bfloat16 [2048, 3584], P('expert', 'dp')
- token_grad: bfloat16 [2048, 3584], P('expert', 'dp')
- gate_grad: bfloat16 [64, 3584, 1024], P('expert', 'dp')
- up_grad: bfloat16 [64, 3584, 1024], P('expert', 'dp')
Inputs may be any that keep to these rules, and one draw needn't show every extreme that they name: `expert_ids`: each row names 8 different experts. In each aligned block of 32 rows (the tokens of one expert-parallel rank) no expert is named by more than 10 rows, a bound that some block reaches.
All inputs are finite; a program needn't handle non-finite values.
Results may differ from a plain program's by a relative error of at most 0.029.
Values may be sent and summed in bfloat16 or wider, within the bound.
No kernel may reach another device: no remote copies, remote signals or barrier semaphores. Data moves between devices by JAX's collectives and lax.ppermute only.
A program may use at most 64 MiB of HBM per device.

v0:
```python
import jax
import jax.numpy as jnp
from jax import lax
from jax.sharding import PartitionSpec as P


def activate(gate, up):
    return (gate * jax.nn.sigmoid(gate) * up).astype(jnp.bfloat16)


def derive(gate, up, dh):
    sig = jax.nn.sigmoid(gate)
    d_gate = (dh * up * sig * (1.0 + gate * (1.0 - sig))).astype(jnp.bfloat16)
    d_up = (dh * gate * sig).astype(jnp.bfloat16)
    return (d_gate, d_up)


def body(
    tokens,
    cotangent,
    expert_ids,
    route_weight,
    replaced,
    gate_weight,
    up_weight,
    down_weight,
    backup,
):
    ranks = lax.axis_size("expert")
    local_tok, topk = expert_ids.shape
    capacity = min(local_tok, 5 * local_tok * topk // (2 * ranks))
    restored = lax.all_gather(backup, "expert", axis=2, tiled=True)
    is_target = lax.axis_index("expert") == replaced[0]
    w_gate = jnp.where(is_target, restored[0], gate_weight[0])
    w_up = jnp.where(is_target, restored[1], up_weight[0])
    w_down = jnp.where(is_target, jnp.transpose(restored[2]), down_weight[0])
    experts = jnp.arange(ranks, dtype=jnp.int32)
    chosen = expert_ids[:, :, None] == experts
    member = jnp.sum(chosen.astype(jnp.int32), axis=1)
    share = jnp.sum(jnp.where(chosen, route_weight[:, :, None], jnp.float32(0.0)), axis=1)
    place = jnp.cumsum(member, axis=0) - 1
    hit = (place[:, :, None] == jnp.arange(capacity, dtype=jnp.int32)) & (member[:, :, None] == 1)
    hit = jnp.transpose(hit, (1, 2, 0))
    pick = hit.reshape(ranks * capacity, local_tok).astype(jnp.bfloat16)
    pick_weight = jnp.where(hit, jnp.transpose(share)[:, None, :], jnp.float32(0.0)).reshape(
        ranks * capacity, local_tok
    )
    send_rows = jnp.dot(pick, tokens, preferred_element_type=jnp.float32).astype(jnp.bfloat16)
    send_grad = jnp.dot(
        pick_weight, cotangent.astype(jnp.float32), precision=lax.Precision.HIGHEST
    ).astype(jnp.bfloat16)
    rows, douts = (
        lax.all_to_all(send_rows, "expert", split_axis=0, concat_axis=0, tiled=True),
        lax.all_to_all(send_grad, "expert", split_axis=0, concat_axis=0, tiled=True),
    )
    part_gate = jnp.dot(rows, w_gate, preferred_element_type=jnp.float32)
    part_up = jnp.dot(rows, w_up, preferred_element_type=jnp.float32)
    gate, up = (
        lax.psum(part_gate.astype(jnp.bfloat16), "dp").astype(jnp.float32),
        lax.psum(part_up.astype(jnp.bfloat16), "dp").astype(jnp.float32),
    )
    hidden = activate(gate, up)
    result = jnp.dot(hidden, w_down, preferred_element_type=jnp.float32).astype(jnp.bfloat16)
    back_dims = (((1,), (1,)), ((), ()))
    part_dh = lax.dot_general(douts, w_down, back_dims, preferred_element_type=jnp.float32)
    dh = lax.psum(part_dh.astype(jnp.bfloat16), "dp").astype(jnp.float32)
    d_gate, d_up = derive(gate, up, dh)
    d_rows = (
        lax.dot_general(d_gate, w_gate, back_dims, preferred_element_type=jnp.float32)
        + lax.dot_general(d_up, w_up, back_dims, preferred_element_type=jnp.float32)
    ).astype(jnp.bfloat16)
    row_dims = (((0,), (0,)), ((), ()))
    gate_grad = lax.dot_general(rows, d_gate, row_dims, preferred_element_type=jnp.float32).astype(
        jnp.bfloat16
    )
    up_grad = lax.dot_general(rows, d_up, row_dims, preferred_element_type=jnp.float32).astype(
        jnp.bfloat16
    )
    back_out, back_dx = (
        lax.all_to_all(result, "expert", split_axis=0, concat_axis=0, tiled=True),
        lax.all_to_all(d_rows, "expert", split_axis=0, concat_axis=0, tiled=True),
    )
    combined = lax.dot_general(
        pick_weight, back_out.astype(jnp.float32), row_dims, precision=lax.Precision.HIGHEST
    ).astype(jnp.bfloat16)
    token_grad = lax.dot_general(
        pick, back_dx, row_dims, preferred_element_type=jnp.float32
    ).astype(jnp.bfloat16)
    return (combined, token_grad, gate_grad[None], up_grad[None])


def solution(mesh):
    placed = (
        P("expert", "dp"),
        P("expert", "dp"),
        P("expert", None),
        P("expert", None),
        P(),
        P("expert", "dp", None),
        P("expert", "dp", None),
        P("expert", None, "dp"),
        P(None, "dp", "expert"),
    )
    return jax.shard_map(
        body,
        mesh=mesh,
        in_specs=placed,
        out_specs=(
            P("expert", "dp"),
            P("expert", "dp"),
            P("expert", "dp", None),
            P("expert", "dp", None),
        ),
        check_vma=False,
    )
```

profile of v0, /device:TPU:1, one launch (start us, length us, event | category | flops | bytes accessed | tf_op | source)
XLA Modules:
  0.0 541.0 jit_solution(16811922450240549278)
XLA Ops:
  7.2 0.7 all-gather.2.cloned.1.call-update
  7.9 0.8 copy.50
  8.7 0.1 convert_reduce_fusion
  9.3 0.1 eq.68
  9.4 0.2 compare_and_fusion
  9.6 0.4 convolution_convert_fusion.7
  10.0 0.2 copy.55
  10.3 1.3 all_to_all.28
  11.5 12.9 %all-to-all-start = ((bf16[64,10,448]{2,1,0:T(8,128)(2,1)}), bf16[64,10,448]{2,1,0:T(8,128)(2,1)S(1)}, u32[]{:S(2)}, u32[]{:S(2)}) async-start(bf16[64,10,448]{2,1,0:T(8,128)(2,1)} %all_to_all.28), calls=%async_computation | async-start | bytes 2097152 | tf_op jit(solution)/shard_map/all_to_all | solution.py:53
  24.6 0.1 select_reduce_fusion
  24.9 0.7 convolution_convert_fusion.6
  25.6 0.2 copy.62
  25.8 1.3 all_to_all.33
  27.1 26.5 %all-to-all-done = bf16[64,10,448]{2,1,0:T(8,128)(2,1)S(1)} async-done(((bf16[64,10,448]{2,1,0:T(8,128)(2,1)}), bf16[64,10,448]{2,1,0:T(8,128)(2,1)S(1)}, u32[]{:S(2)}, u32[]{:S(2)}) %all-to-all-start) | async-done | bytes 573472 | tf_op jit(solution)/shard_map/all_to_all | solution.py:53
  53.6 6.9 %all-to-all-start.2 = ((bf16[64,10,448]{2,1,0:T(8,128)(2,1)}), bf16[64,10,448]{2,1,0:T(8,128)(2,1)S(1)}, u32[]{:S(2)}, u32[]{:S(2)}) async-start(bf16[64,10,448]{2,1,0:T(8,128)(2,1)} %all_to_all.33), calls=%async_computation.2 | async-start | bytes 2097152 | tf_op jit(solution)/shard_map/all_to_all | solution.py:54
  60.5 0.2 all-reduce.3.cloned.1.call-start
  61.4 1.4 copy.57
  62.8 2.2 copy.56
  65.0 1.5 copy.58
  66.5 1.2 all_to_all.30
  67.8 22.8 %all-to-all-done.2 = bf16[64,10,448]{2,1,0:T(8,128)(2,1)S(1)} async-done(((bf16[64,10,448]{2,1,0:T(8,128)(2,1)}), bf16[64,10,448]{2,1,0:T(8,128)(2,1)S(1)}, u32[]{:S(2)}, u32[]{:S(2)}) %all-to-all-start.2) | async-done | bytes 573472 | tf_op jit(solution)/shard_map/all_to_all | solution.py:54
  90.6 1.2 all_to_all.35
  91.8 193.1 %all-gather.2.cloned.1.call-done = bf16[3,448,1024]{1,2,0:T(8,128)(2,1)} async-done(((bf16[3,448,16]{1,2,0:T(8,128)(2,1)}), bf16[3,448,1024]{1,2,0:T(8,128)(2,1)}) %all-gather.2.cloned.1.call-update) | async-done | bytes 2752528 | tf_op jit(solution)/shard_map/all_gather | solution.py:32
  284.9 3.9 convolution_convert_fusion.1
  288.8 2.1 convolution_convert_fusion.2
  290.8 2.0 convolution_convert_fusion
  292.8 154.1 %all-reduce.3.cloned.1.call-done = (bf16[640,1024]{1,0:T(8,128)(2,1)}, bf16[640,1024]{1,0:T(8,128)(2,1)}, bf16[640,1024]{1,0:T(8,128)(2,1)}) async-done(((bf16[640,1024]{1,0:T(8,128)(2,1)}, bf16[640,1024]{1,0:T(8,128)(2,1)}, bf16[640,1024]{1,0:T(8,128)(2,1)}), (bf16[640,1024]{1,0:T(8,128)(2,1)}, bf16[640,1024]{1,0:T(8,128)(2,1)}, bf16[640,1024]{1,0:T(8,128)(2,1)})) %all-reduce.3.cloned.1.call-update) | async-done | bytes 3932176 | tf_op jit(solution)/shard_map/psum | solution.py:60
  447.0 3.5 fusion.3
  450.5 1.0 fusion.25
  451.6 0.7 copy-done.1
  452.3 0.4 copy-done.2
  452.7 0.3 copy-done.7
  453.0 2.1 fusion.12
  455.1 1.4 copy.63
  456.5 1.3 all_to_all.36
  457.8 13.4 %all-to-all-start.3 = ((bf16[64,10,448]{2,1,0:T(8,128)(2,1)}), bf16[64,10,448]{2,1,0:T(8,128)(2,1)}, u32[]{:S(2)}, u32[]{:S(2)}) async-start(bf16[64,10,448]{2,1,0:T(8,128)(2,1)} %all_to_all.36), calls=%async_computation.3 | async-start | bytes 2097152 | tf_op jit(solution)/shard_map/all_to_all | solution.py:81
  471.3 0.1 broadcast_select_fusion
  471.4 3.6 convolution_convert_fusion.5
  475.0 1.3 copy.59
  476.3 1.3 all_to_all.31
  477.6 20.7 %all-to-all-done.3 = bf16[64,10,448]{2,1,0:T(8,128)(2,1)} async-done(((bf16[64,10,448]{2,1,0:T(8,128)(2,1)}), bf16[64,10,448]{2,1,0:T(8,128)(2,1)}, u32[]{:S(2)}, u32[]{:S(2)}) %all-to-all-start.3) | async-done | bytes 573472 | tf_op jit(solution)/shard_map/all_to_all | solution.py:81
  498.3 7.3 %all-to-all-start.1 = ((bf16[64,10,448]{2,1,0:T(8,128)(2,1)}), bf16[64,10,448]{2,1,0:T(8,128)(2,1)S(1)}, u32[]{:S(2)}, u32[]{:S(2)}) async-start(bf16[64,10,448]{2,1,0:T(8,128)(2,1)} %all_to_all.31), calls=%async_computation.1 | async-start | bytes 2097152 | tf_op jit(solution)/shard_map/all_to_all | solution.py:80
  505.6 0.1 fusion.21
  505.8 3.5 fusion.10
  509.2 2.1 fusion.11
  511.4 2.7 fusion.15
  514.1 18.3 %all-to-all-done.1 = bf16[64,10,448]{2,1,0:T(8,128)(2,1)S(1)} async-done(((bf16[64,10,448]{2,1,0:T(8,128)(2,1)}), bf16[64,10,448]{2,1,0:T(8,128)(2,1)S(1)}, u32[]{:S(2)}, u32[]{:S(2)}) %all-to-all-start.1) | async-done | bytes 573472 | tf_op jit(solution)/shard_map/all_to_all | solution.py:80
  532.4 1.8 fusion.14
  (49 shorter events, 0.9 us)
Async XLA Ops:
  7.2 2.4 copy-start
  7.2 277.7 %all-gather.2.cloned.1.call-start = ((), (), s32[]{:S(2)}) async-start(), calls=%async_computation.4 | async-start | bytes 3194880 | tf_op jit(solution)/shard_map/all_gather | solution.py:32
  10.0 14.5 %copy-start.15 = (f32[32,8]{0,1:T(8,128)S(1)}, f32[32,8]{0,1:T(8,128)}, u32[]{:S(2)}) copy-start(f32[32,8]{0,1:T(8,128)} %param.12) | copy-start | bytes 3076
  10.3 14.6 %copy-start.14 = (bf16[32,448]{1,0:T(8,128)(2,1)S(1)}, bf16[32,448]{1,0:T(8,128)(2,1)}, u32[]{:S(2)}) copy-start(bf16[32,448]{1,0:T(8,128)(2,1)} %param.10) | copy-start | bytes 86020
  11.5 42.1 %all-to-all-start = ((bf16[64,10,448]{2,1,0:T(8,128)(2,1)}), bf16[64,10,448]{2,1,0:T(8,128)(2,1)S(1)}, u32[]{:S(2)}, u32[]{:S(2)}) async-start(bf16[64,10,448]{2,1,0:T(8,128)(2,1)} %all_to_all.28), calls=%async_computation | async-start | bytes 2097152 | tf_op jit(solution)/shard_map/all_to_all | solution.py:53
  25.6 35.9 %copy-start.10 = (bf16[1,448,1024]{2,1,0:T(8,128)(2,1)S(1)}, bf16[1,448,1024]{2,1,0:T(8,128)(2,1)}, u32[]{:S(2)}) copy-start(bf16[1,448,1024]{2,1,0:T(8,128)(2,1)} %param.15) | copy-start | bytes 2752516
  53.6 37.0 %all-to-all-start.2 = ((bf16[64,10,448]{2,1,0:T(8,128)(2,1)}), bf16[64,10,448]{2,1,0:T(8,128)(2,1)S(1)}, u32[]{:S(2)}, u32[]{:S(2)}) async-start(bf16[64,10,448]{2,1,0:T(8,128)(2,1)} %all_to_all.33), calls=%async_computation.2 | async-start | bytes 2097152 | tf_op jit(solution)/shard_map/all_to_all | solution.py:54
  60.5 386.4 %all-reduce.3.cloned.1.call-start = ((), (), s32[]{:S(2)}) async-start(), calls=%async_computation.5 | async-start | bytes 7864320 | tf_op jit(solution)/shard_map/psum | solution.py:60
  66.5 226.3 %copy-start.6 = (bf16[1,1024,448]{2,1,0:T(8,128)(2,1)}, bf16[1,1024,448]{2,1,0:T(8,128)(2,1)S(1)}, u32[]{:S(2)}) copy-start(bf16[1,1024,448]{2,1,0:T(8,128)(2,1)S(1)} %copy.58) | copy-start | bytes 2752516
  91.8 196.9 %copy-start.8 = (bf16[1,448,1024]{1,2,0:T(8,128)(2,1)S(1)}, bf16[1,448,1024]{1,2,0:T(8,128)(2,1)}, u32[]{:S(2)}) copy-start(bf16[1,448,1024]{1,2,0:T(8,128)(2,1)} %copy.56) | copy-start | bytes 2752516
  91.8 196.9 %copy-start.11 = (bf16[640,448]{1,0:T(8,128)(2,1)S(1)}, bf16[640,448]{1,0:T(8,128)(2,1)}, u32[]{:S(2)}) copy-start(bf16[640,448]{1,0:T(8,128)(2,1)} %all_to_all.30) | copy-start | bytes 1720324
  284.9 3.9 copy-start.16
  288.8 2.1 copy-start.13
  447.0 3.5 copy-start.9
  447.0 3.5 copy-start.17
  450.5 1.1 copy-start.4
  450.5 1.8 copy-start.1
  450.5 2.2 copy-start.2
  450.5 2.5 copy-start.7
  455.1 16.3 %copy-start.5 = (bf16[640,1024]{1,0:T(8,128)(2,1)S(1)}, bf16[640,1024]{1,0:T(8,128)(2,1)}, u32[]{:S(2)}) copy-start(bf16[640,1024]{1,0:T(8,128)(2,1)} %get-tuple-element.4) | copy-start | bytes 3932164
  457.8 40.5 %all-to-all-start.3 = ((bf16[64,10,448]{2,1,0:T(8,128)(2,1)}), bf16[64,10,448]{2,1,0:T(8,128)(2,1)}, u32[]{:S(2)}, u32[]{:S(2)}) async-start(bf16[64,10,448]{2,1,0:T(8,128)(2,1)} %all_to_all.36), calls=%async_computation.3 | async-start | bytes 2097152 | tf_op jit(solution)/shard_map/all_to_all | solution.py:81
  498.3 34.1 %all-to-all-start.1 = ((bf16[64,10,448]{2,1,0:T(8,128)(2,1)}), bf16[64,10,448]{2,1,0:T(8,128)(2,1)S(1)}, u32[]{:S(2)}, u32[]{:S(2)}) async-start(bf16[64,10,448]{2,1,0:T(8,128)(2,1)} %all_to_all.31), calls=%async_computation.1 | async-start | bytes 2097152 | tf_op jit(solution)/shard_map/all_to_all | solution.py:80
  505.7 3.5 copy-start.3
  505.8 3.5 copy-start.12
Sparse Core Ops, SparseCore 0:
  10.1 274.7 all-gather.1
  293.0 153.9 all-reduce.2
where the time goes:
time: 542 us; the launch traced here: 541 us
  waiting for transfers between devices  436 us (80%)
  starting transfers between devices  40.8 us (8%)
  matrix products  25.7 us (5%)
  local copies, waits for them, and re-layouts  19 us (4%)
  between operations  15.1 us (3%)
    all_gather x1, waiting for transfers between devices, body(): restored = lax.all_gather(backup, 'expert', axis=2, tiled=True)  193 us
    psum x1, waiting for transfers between devices, body(): lax.psum(part_up.astype(jnp.bfloat16), 'dp').astype(jnp.float32)  154 us
    all_to_all x1, waiting for transfers between devices, body(): lax.all_to_all(send_rows, 'expert', split_axis=0, concat_axis=0, tiled=True)  26.5 us
    all_to_all x1, waiting for transfers between devices, body(): lax.all_to_all(send_grad, 'expert', split_axis=0, concat_axis=0, tiled=True)  22.8 us
    all_to_all x1, waiting for transfers between devices, body(): lax.all_to_all(d_rows, 'expert', split_axis=0, concat_axis=0, tiled=True)  20.7 us
    all_to_all x1, waiting for transfers between devices, body(): lax.all_to_all(result, 'expert', split_axis=0, concat_axis=0, tiled=True)  18.3 us
    all_to_all x1, starting transfers between devices, body(): lax.all_to_all(d_rows, 'expert', split_axis=0, concat_axis=0, tiled=True)  13.4 us
    all_to_all x1, starting transfers between devices, body(): lax.all_to_all(send_rows, 'expert', split_axis=0, concat_axis=0, tiled=True)  12.9 us
  transfers between devices with their start and end apart: 6, of which 6 were waited for; matrix products, arithmetic and copies ran while one was open for 4% of the time, Pallas kernels for 0%

commit v1 on v0

v1 whole, which is shorter than its diff:
```python
import jax
import jax.numpy as jnp
from jax import lax
from jax.sharding import PartitionSpec as P

BF = jnp.bfloat16
F32 = jnp.float32
GRID = {64: (4, 8, 2), 8: (2, 2, 2)}


def dot(a, b, dims=(((1,), (0,)), ((), ()))):
    return lax.dot_general(a, b, dims, preferred_element_type=F32)


def activate(gate, up):
    return (gate * jax.nn.sigmoid(gate) * up).astype(BF)


def derive(gate, up, dh):
    sig = jax.nn.sigmoid(gate)
    d_gate = (dh * up * sig * (1.0 + gate * (1.0 - sig))).astype(BF)
    d_up = (dh * gate * sig).astype(BF)
    return (d_gate, d_up)


def core_swap(x):
    return lax.ppermute(x, "dp", [(i, i ^ 1) for i in range(8)])


def shift(x, k):
    return lax.ppermute(
        x, "dp", [(2 * h + c, 2 * ((h + k) % 4) + c) for h in range(4) for c in range(2)]
    )


def add(a, b):
    return (a.astype(F32) + b.astype(F32)).astype(BF)


def part_of(x, index, size):
    return lax.dynamic_slice_in_dim(x, index * size, size, 0)


def sum_scatter(x):
    me = lax.axis_index("dp")
    h, c = me // 2, me % 2
    half, chunk = x.shape[0] // 2, x.shape[0] // 8
    mid = chunk // 2
    other = core_swap(part_of(x, 1 - c, half))
    s = add(part_of(x, c, half), other)
    far = part_of(s, (h + 2) % 4, chunk)
    from_left = shift(far[:mid], 1)
    from_right = shift(far[mid:], -1)
    right = part_of(s, (h + 1) % 4, chunk)
    left = part_of(s, (h + 3) % 4, chunk)
    right = jnp.concatenate([add(right[:mid], from_left), right[mid:]], axis=0)
    left = jnp.concatenate([left[:mid], add(left[mid:], from_right)], axis=0)
    a = shift(right, 1)
    b = shift(left, -1)
    return part_of(s, h, chunk).astype(F32) + a.astype(F32) + b.astype(F32)


def gather_rows(v):
    me = lax.axis_index("dp")
    h, c = me // 2, me % 2
    chunk, width = v.shape
    mid = chunk // 2
    left = shift(v, 1)
    right = shift(v, -1)
    far = jnp.concatenate([shift(left[:mid], 1), shift(right[mid:], -1)], axis=0)
    half = jnp.zeros((4 * chunk, width), v.dtype)
    for k, block in ((0, v), (3, left), (1, right), (2, far)):
        half = lax.dynamic_update_slice_in_dim(half, block, ((h + k) % 4) * chunk, 0)
    other = core_swap(half)
    low = jnp.where(c == 0, half, other)
    high = jnp.where(c == 0, other, half)
    return jnp.concatenate([low, high], axis=0)


def body(
    tokens,
    cotangent,
    expert_ids,
    route_weight,
    replaced,
    gate_weight,
    up_weight,
    down_weight,
    backup,
):
    ranks = lax.axis_size("expert")
    nx, ny, nz = GRID[ranks]
    nxz = nx * nz
    along_y = [
        [(x * ny + y) * nz + z for y in range(ny)] for x in range(nx) for z in range(nz)
    ]
    along_xz = [
        [(x * ny + y) * nz + z for x in range(nx) for z in range(nz)] for y in range(ny)
    ]

    def over_y(v):
        return lax.all_to_all(v, "expert", 0, 0, axis_index_groups=along_y, tiled=True)

    def over_xz(v):
        return lax.all_to_all(v, "expert", 0, 0, axis_index_groups=along_xz, tiled=True)

    local_tok, topk = expert_ids.shape
    feat = tokens.shape[1]
    ff = gate_weight.shape[2]
    ffr = ff // ranks
    capacity = min(local_tok, 5 * local_tok * topk // (2 * ranks))
    is_target = lax.axis_index("expert") == replaced[0]

    experts = jnp.arange(ranks, dtype=jnp.int32)
    chosen = expert_ids[:, :, None] == experts
    member = jnp.sum(chosen.astype(jnp.int32), axis=1)
    share = jnp.sum(jnp.where(chosen, route_weight[:, :, None], 0.0), axis=1)
    place = jnp.where(member == 1, jnp.cumsum(member, axis=0) - 1, -1)
    share_hi = lax.reduce_precision(share, 8, 7)
    share_lo = share - share_hi
    meta = jnp.stack([place.astype(F32), share_hi, share_lo], axis=0).astype(BF)
    meta = meta.reshape(3, local_tok, nx, ny, nz)
    meta = jnp.transpose(meta, (3, 1, 0, 2, 4)).reshape(ny, local_tok, 3 * nxz)

    saved = jnp.transpose(backup, (0, 2, 1))
    width = 2 * feat + 128
    top = jnp.concatenate(
        [
            jnp.broadcast_to(jnp.concatenate([tokens, cotangent], axis=1), (ny, local_tok, 2 * feat)),
            jnp.pad(meta, ((0, 0), (0, 0), (0, 128 - 3 * nxz))),
        ],
        axis=2,
    )
    low = jnp.concatenate([saved[2, : ffr // 2], saved[2, ffr // 2 :]], axis=1)
    low = jnp.broadcast_to(jnp.pad(low, ((0, 0), (0, 128))), (ny, ffr // 2, width))
    first = jnp.concatenate([top, low], axis=1)
    first = over_y(first.reshape(-1, width)).reshape(ny, local_tok + ffr // 2, width)
    saved_gu = saved[:2].reshape(2 * ffr, feat)
    saved_gu = over_y(jnp.broadcast_to(saved_gu, (ny, 2 * ffr, feat)).reshape(-1, feat))

    seen = first[:, :local_tok].reshape(ny * local_tok, width)
    saved_d = first[:, local_tok:]
    saved_d = jnp.concatenate([saved_d[:, :, :feat], saved_d[:, :, feat : 2 * feat]], axis=1)
    saved_d = saved_d.reshape(ny * ffr, feat)
    tok_y, cot_y = seen[:, :feat], seen[:, feat : 2 * feat]
    meta_y = jnp.transpose(seen[:, 2 * feat : 2 * feat + 3 * nxz].astype(F32)).reshape(
        3, nxz, 1, ny * local_tok
    )

    rows_out = ny * capacity
    row = jnp.arange(rows_out, dtype=jnp.int32)[:, None]
    col = jnp.arange(ny * local_tok, dtype=jnp.int32)[None, :]
    want = jnp.where(row // capacity == col // local_tok, row % capacity, -2).astype(F32)
    hit = meta_y[0] == want[None]
    pick = hit.astype(BF).reshape(nxz * rows_out, -1)
    pick_hi = jnp.where(hit, meta_y[1], 0.0).astype(BF).reshape(nxz * rows_out, -1)
    pick_lo = jnp.where(hit, meta_y[2], 0.0).astype(BF).reshape(nxz * rows_out, -1)
    send_grad = (dot(pick_hi, cot_y) + dot(pick_lo, cot_y)).astype(BF)
    send_rows = dot(pick, tok_y).astype(BF)

    def exchange(rows, saved_rows):
        n = saved_rows.shape[0]
        both = jnp.concatenate(
            [rows.reshape(nxz, rows_out, feat), jnp.broadcast_to(saved_rows, (nxz, n, feat))],
            axis=1,
        )
        both = over_xz(both.reshape(-1, feat)).reshape(nxz, rows_out + n, feat)
        return both[:, :rows_out].reshape(nxz * rows_out, feat), both[:, rows_out:]

    douts, all_d = exchange(send_grad, saved_d)
    rows, all_gu = exchange(send_rows, saved_gu)

    def in_order(blocks, count):
        blocks = blocks.reshape(nx, nz, ny, count, ffr, feat)
        return jnp.transpose(blocks, (3, 0, 2, 1, 4, 5)).reshape(count, ff, feat)

    restored_d = in_order(all_d, 1)
    restored_gu = in_order(all_gu, 2)
    w_down = jnp.where(is_target, restored_d[0], down_weight[0])
    w_gate = jnp.where(is_target, jnp.transpose(restored_gu[0]), gate_weight[0])
    w_up = jnp.where(is_target, jnp.transpose(restored_gu[1]), up_weight[0])

    back_dims = (((1,), (1,)), ((), ()))
    row_dims = (((0,), (0,)), ((), ()))
    dh = sum_scatter(dot(douts, w_down, back_dims).astype(BF))
    gate_up = sum_scatter(
        jnp.concatenate([dot(rows, w_gate).astype(BF), dot(rows, w_up).astype(BF)], axis=1)
    )
    gate, up = gate_up[:, :ff], gate_up[:, ff:]
    hidden = activate(gate, up)
    d_gate, d_up = derive(gate, up, dh)
    d_both = gather_rows(jnp.concatenate([d_gate, d_up], axis=1))
    d_gate, d_up = d_both[:, :ff], d_both[:, ff:]
    hidden = gather_rows(hidden)

    d_rows = (dot(d_gate, w_gate, back_dims) + dot(d_up, w_up, back_dims)).astype(BF)
    back_dx = over_xz(d_rows)
    sum_dx = dot(pick, back_dx, row_dims).astype(BF)
    token_grad = jnp.sum(
        over_y(sum_dx).reshape(ny, local_tok, feat).astype(F32), axis=0
    ).astype(BF)

    result = dot(hidden, w_down).astype(BF)
    back_out = over_xz(result)
    sum_out = (dot(pick_hi, back_out, row_dims) + dot(pick_lo, back_out, row_dims)).astype(BF)
    combined = jnp.sum(
        over_y(sum_out).reshape(ny, local_tok, feat).astype(F32), axis=0
    ).astype(BF)

    gate_grad = dot(rows, d_gate, row_dims).astype(BF)
    up_grad = dot(rows, d_up, row_dims).astype(BF)
    return (combined, token_grad, gate_grad[None], up_grad[None])


def solution(mesh):
    placed = (
        P("expert", "dp"),
        P("expert", "dp"),
        P("expert", None),
        P("expert", None),
        P(),
        P("expert", "dp", None),
        P("expert", "dp", None),
        P("expert", None, "dp"),
        P(None, "dp", "expert"),
    )
    return jax.shard_map(
        body,
        mesh=mesh,
        in_specs=placed,
        out_specs=(
            P("expert", "dp"),
            P("expert", "dp"),
            P("expert", "dp", None),
            P("expert", "dp", None),
        ),
        check_vma=False,
    )
```

time: 542 us -> 298 us (0.55)
  waiting for transfers between devices: 436 us -> 97.3 us
  starting transfers between devices: 40.8 us -> 125 us
  other arithmetic: 4.21 us -> 23.6 us
  between operations: 15.1 us -> 2.38 us
  local copies, waits for them, and re-layouts: 19 us -> 29.7 us
  matrix products: 25.7 us -> 16.5 us
    all_gather x1 -> x0, waiting for transfers between devices: 193 us -> none  [body(): restored = lax.all_gather(backup, 'expert', axis=2, tiled=True)]
    psum x1 -> x0, waiting for transfers between devices: 154 us -> none  [body(): lax.psum(part_up.astype(jnp.bfloat16), 'dp').astype(jnp.float32)]
    ppermute x0 -> x20, starting transfers between devices: none -> 80.9 us  [the longest x16 61.7 us: shift(): lax.ppermute(x, 'dp', [(2 * h + c, 2 * ((h + k) % 4) + c) for h in range(...]
    ppermute x0 -> x20, waiting for transfers between devices: none -> 22 us  [the longest x16 19.7 us: shift(): lax.ppermute(x, 'dp', [(2 * h + c, 2 * ((h + k) % 4) + c) for h in range(...]
    all_to_all x4 -> x8, waiting for transfers between devices: 88.4 us -> 75.3 us  [the longest x4 38.4 us: over_xz(): lax.all_to_all(v, 'expert', 0, 0, axis_index_groups=along_xz, tiled=True)]
    dot_general x12 -> x14, matrix products: 25.7 us -> 16.5 us  [dot(): return lax.dot_general(a, b, dims, preferred_element_type=F32)]
    another operation x1 -> x4, other arithmetic: 0.05 us -> 8.07 us  [the longest x1 8.03 us: body(): place = jnp.where(member == 1, jnp.cumsum(member, axis=0) - 1, -1)]
    slice x0 -> x20, local copies, waits for them, and re-layouts: none -> 7.86 us  [the longest x2 2.63 us: body(): meta_y[2]]
  transfers between devices with their start and end apart: 6 -> 28, of which waited for: 6 -> 14; matrix products, arithmetic and copies ran while one was open for 4% -> 17% of each run, Pallas kernels for 0% -> 0%
where the time goes in v1:
time: 298 us; the launch traced here: 295 us
  starting transfers between devices  125 us (42%)
  waiting for transfers between devices  97.3 us (33%)
  local copies, waits for them, and re-layouts  29.7 us (10%)
  other arithmetic  23.6 us (8%)
  matrix products  16.5 us (6%)
    ppermute x16, starting transfers between devices, shift(): lax.ppermute(x, 'dp', [(2 * h + c, 2 * ((h + k) % 4) + c) for h in range(...  61.7 us
    all_to_all x4, waiting for transfers between devices, over_xz(): lax.all_to_all(v, 'expert', 0, 0, axis_index_groups=along_xz, tiled=True)  38.4 us
    all_to_all x4, waiting for transfers between devices, over_y(): lax.all_to_all(v, 'expert', 0, 0, axis_index_groups=along_y, tiled=True)  36.8 us
    all_to_all x4, starting transfers between devices, over_xz(): lax.all_to_all(v, 'expert', 0, 0, axis_index_groups=along_xz, tiled=True)  26.5 us
    ppermute x16, waiting for transfers between devices, shift(): lax.ppermute(x, 'dp', [(2 * h + c, 2 * ((h + k) % 4) + c) for h in range(...  19.7 us
    ppermute x4, starting transfers between devices, core_swap(): return lax.ppermute(x, 'dp', [(i, i ^ 1) for i in range(8)])  19.1 us
    all_to_all x4, starting transfers between devices, over_y(): lax.all_to_all(v, 'expert', 0, 0, axis_index_groups=along_y, tiled=True)  17.9 us
    dot_general x14, matrix products, dot(): return lax.dot_general(a, b, dims, preferred_element_type=F32)  16.5 us
  transfers between devices with their start and end apart: 28, of which 14 were waited for; matrix products, arithmetic and copies ran while one was open for 17% of the time, Pallas kernels for 0%

profile of v1, /device:TPU:1, one launch (start us, length us, event | category | flops | bytes accessed | tf_op | source)
XLA Modules:
  0.0 294.7 jit_solution(715599707395319001)
XLA Ops:
  3.2 8.0 %fusion.17 = s32[1,32,4,8,2]{4,3,2,1,0:T(8,128)S(1)} fusion(s32[1,32,4,8,2]{4,3,2,1,0:T(8,128)S(1)} %copy.104), kind=kOutput, calls=%fused_computation.49 | output fusion | flops 69632 | bytes 16384 | tf_op jit(solution)/shard_map/jit(cumsum)/reduce_window_sum | solution.py:118
  12.9 7.7 %all-to-all-start = ((bf16[8,40,1024]{2,1,0:T(8,128)(2,1)}), bf16[8,40,1024]{2,1,0:T(8,128)(2,1)S(1)}, u32[]{:S(2)}, u32[]{:S(2)}) async-start(bf16[8,40,1024]{2,1,0:T(8,128)(2,1)} %fusion.19), calls=%async_computation | async-start | bytes 1310720 | tf_op jit(solution)/shard_map/all_to_all | solution.py:102
  20.6 17.9 %all-to-all-done = bf16[8,40,1024]{2,1,0:T(8,128)(2,1)S(1)} async-done(((bf16[8,40,1024]{2,1,0:T(8,128)(2,1)}), bf16[8,40,1024]{2,1,0:T(8,128)(2,1)S(1)}, u32[]{:S(2)}, u32[]{:S(2)}) %all-to-all-start) | async-done | bytes 655392 | tf_op jit(solution)/shard_map/all_to_all | solution.py:102
  39.4 3.4 %all-to-all-start.1 = ((bf16[8,32,448]{2,1,0:T(8,128)(2,1)}), bf16[8,32,448]{2,1,0:T(8,128)(2,1)S(1)}, u32[]{:S(2)}, u32[]{:S(2)}) async-start(bf16[8,32,448]{2,1,0:T(8,128)(2,1)} %broadcast_in_dim.92), calls=%async_computation.1 | async-start | bytes 524288 | tf_op jit(solution)/shard_map/all_to_all | solution.py:102
  44.2 8.0 %all-to-all-done.1 = bf16[8,32,448]{2,1,0:T(8,128)(2,1)S(1)} async-done(((bf16[8,32,448]{2,1,0:T(8,128)(2,1)}), bf16[8,32,448]{2,1,0:T(8,128)(2,1)S(1)}, u32[]{:S(2)}, u32[]{:S(2)}) %all-to-all-start.1) | async-done | bytes 229408 | tf_op jit(solution)/shard_map/all_to_all | solution.py:102
  52.3 1.9 pad_maximum_fusion
  54.2 11.2 %all-to-all-start.2 = ((bf16[8,336,448]{2,1,0:T(8,128)(2,1)}), bf16[8,336,448]{2,1,0:T(8,128)(2,1)S(1)}, u32[]{:S(2)}, u32[]{:S(2)}) async-start(bf16[8,336,448]{2,1,0:T(8,128)(2,1)} %pad_maximum_fusion), calls=%async_computation.2 | async-start | bytes 5505024 | tf_op jit(solution)/shard_map/all_to_all | solution.py:105
  75.0 23.4 %all-to-all-done.2 = bf16[8,336,448]{2,1,0:T(8,128)(2,1)S(1)} async-done(((bf16[8,336,448]{2,1,0:T(8,128)(2,1)}), bf16[8,336,448]{2,1,0:T(8,128)(2,1)S(1)}, u32[]{:S(2)}, u32[]{:S(2)}) %all-to-all-start.2) | async-done | bytes 2408480 | tf_op jit(solution)/shard_map/all_to_all | solution.py:105
  98.4 4.3 %all-to-all-start.3 = ((bf16[8,208,448]{2,1,0:T(8,128)(2,1)}), bf16[8,208,448]{2,1,0:T(8,128)(2,1)}, u32[]{:S(2)}, u32[]{:S(2)}) async-start(bf16[8,208,448]{2,1,0:T(8,128)(2,1)} %pad_maximum_fusion.1), calls=%async_computation.3 | async-start | bytes 3407872 | tf_op jit(solution)/shard_map/all_to_all | solution.py:105
  102.7 2.2 copy.116
  105.6 2.2 copy.118
  114.0 3.9 %collective-permute-start = (bf16[320,2048]{1,0:T(8,128)(2,1)}, bf16[320,2048]{1,0:T(8,128)(2,1)}, u32[]{:S(2)}, u32[]{:S(2)}) collective-permute-start(bf16[320,2048]{1,0:T(8,128)(2,1)} %fusion.5), channel_id=1, source_target_pairs={{0,64},{64,0},{128,192},{192,128},{256,320},{320,256},{384,448},{4... | collective-permute-start | bytes 3932168 | tf_op jit(solution)/shard_map/ppermute | solution.py:27
  118.6 4.6 %all-to-all-done.3 = bf16[8,208,448]{2,1,0:T(8,128)(2,1)} async-done(((bf16[8,208,448]{2,1,0:T(8,128)(2,1)}), bf16[8,208,448]{2,1,0:T(8,128)(2,1)}, u32[]{:S(2)}, u32[]{:S(2)}) %all-to-all-start.3) | async-done | bytes 1490976 | tf_op jit(solution)/shard_map/all_to_all | solution.py:105
  126.8 5.2 %collective-permute-start.10 = (bf16[320,1024]{1,0:T(8,128)(2,1)S(1)}, bf16[320,1024]{1,0:T(8,128)(2,1)S(1)}, u32[]{:S(2)}, u32[]{:S(2)}) collective-permute-start(bf16[320,1024]{1,0:T(8,128)(2,1)S(1)} %constant_dynamic-slice_fusion.4), channel_id=1, source_target_pairs={{0,64},{64,0},{128,192},{192,128},{256,320},{320,256},{384,448},{4... | collective-permute-start | bytes 1966088 | tf_op jit(solution)/shard_map/ppermute | solution.py:27
  133.9 5.8 %collective-permute-start.1 = (bf16[40,2048]{1,0:T(8,128)(2,1)S(1)}, bf16[40,2048]{1,0:T(8,128)(2,1)S(1)}, u32[]{:S(2)}, u32[]{:S(2)}) collective-permute-start(bf16[40,2048]{1,0:T(8,128)(2,1)S(1)} %get-tuple-element.16), channel_id=1, source_target_pairs={{0,128},{64,192},{128,256},{192,320},{256,384},{320,448},{384,0},{... | collective-permute-start | bytes 491528 | tf_op jit(solution)/shard_map/ppermute | solution.py:31
  139.8 5.9 %collective-permute-start.3 = (bf16[40,2048]{1,0:T(8,128)(2,1)S(1)}, bf16[40,2048]{1,0:T(8,128)(2,1)S(1)}, u32[]{:S(2)}, u32[]{:S(2)}) collective-permute-start(bf16[40,2048]{1,0:T(8,128)(2,1)S(1)} %get-tuple-element.18), channel_id=1, source_target_pairs={{0,384},{64,448},{128,0},{192,64},{256,128},{320,192},{384,256},{4... | collective-permute-start | bytes 491528 | tf_op jit(solution)/shard_map/ppermute | solution.py:31
  145.9 2.2 collective-permute-start.11
  148.1 5.2 %collective-permute-start.13 = (bf16[40,1024]{1,0:T(8,128)(2,1)S(1)}, bf16[40,1024]{1,0:T(8,128)(2,1)S(1)}, u32[]{:S(2)}, u32[]{:S(2)}) collective-permute-start(bf16[40,1024]{1,0:T(8,128)(2,1)S(1)} %get-tuple-element.24), channel_id=1, source_target_pairs={{0,384},{64,448},{128,0},{192,64},{256,128},{320,192},{384,256},{4... | collective-permute-start | bytes 245768 | tf_op jit(solution)/shard_map/ppermute | solution.py:31
  154.0 5.2 %collective-permute-start.4 = (bf16[80,2048]{1,0:T(8,128)(2,1)S(1)}, bf16[80,2048]{1,0:T(8,128)(2,1)S(1)}, u32[]{:S(2)}, u32[]{:S(2)}) collective-permute-start(bf16[80,2048]{1,0:T(8,128)(2,1)S(1)} %pad_maximum_fusion.4), channel_id=1, source_target_pairs={{0,384},{64,448},{128,0},{192,64},{256,128},{320,192},{384,256},{4... | collective-permute-start | bytes 983048 | tf_op jit(solution)/shard_map/ppermute | solution.py:31
  159.2 2.2 collective-permute-start.2
  161.5 5.2 %collective-permute-start.14 = (bf16[80,1024]{1,0:T(8,128)(2,1)S(1)}, bf16[80,1024]{1,0:T(8,128)(2,1)S(1)}, u32[]{:S(2)}, u32[]{:S(2)}) collective-permute-start(bf16[80,1024]{1,0:T(8,128)(2,1)S(1)} %pad_maximum_fusion.9), channel_id=1, source_target_pairs={{0,384},{64,448},{128,0},{192,64},{256,128},{320,192},{384,256},{4... | collective-permute-start | bytes 491528 | tf_op jit(solution)/shard_map/ppermute | solution.py:31
  166.7 2.3 collective-permute-start.12
  169.1 9.1 %collective-permute-done.4 = bf16[80,2048]{1,0:T(8,128)(2,1)S(1)} collective-permute-done((bf16[80,2048]{1,0:T(8,128)(2,1)S(1)}, bf16[80,2048]{1,0:T(8,128)(2,1)S(1)}, u32[]{:S(2)}, u32[]{:S(2)}) %collective-permute-start.4) | collective-permute-done | bytes 327712 | tf_op jit(solution)/shard_map/ppermute | solution.py:31
  178.2 4.7 %collective-permute-done.2 = bf16[80,2048]{1,0:T(8,128)(2,1)S(1)} collective-permute-done((bf16[80,2048]{1,0:T(8,128)(2,1)S(1)}, bf16[80,2048]{1,0:T(8,128)(2,1)S(1)}, u32[]{:S(2)}, u32[]{:S(2)}) %collective-permute-start.2) | collective-permute-done | bytes 327712 | tf_op jit(solution)/shard_map/ppermute | solution.py:31
  184.7 1.9 collective-permute-start.5
  186.6 5.5 %collective-permute-start.6 = (bf16[80,1024]{1,0:T(8,128)(2,1)S(1)}, bf16[80,1024]{1,0:T(8,128)(2,1)S(1)}, u32[]{:S(2)}, u32[]{:S(2)}) collective-permute-start(bf16[80,1024]{1,0:T(8,128)(2,1)S(1)} %get-tuple-element.5), channel_id=1, source_target_pairs={{0,384},{64,448},{128,0},{192,64},{256,128},{320,192},{384,256},{4... | collective-permute-start | bytes 491528 | tf_op jit(solution)/shard_map/ppermute | solution.py:31
  192.5 1.9 collective-permute-start.16
  194.4 4.3 %collective-permute-start.15 = (bf16[80,2048]{1,0:T(8,128)(2,1)S(1)}, bf16[80,2048]{1,0:T(8,128)(2,1)S(1)}, u32[]{:S(2)}, u32[]{:S(2)}) collective-permute-start(bf16[80,2048]{1,0:T(8,128)(2,1)S(1)} %get-tuple-element.28), channel_id=1, source_target_pairs={{0,128},{64,192},{128,256},{192,320},{256,384},{320,448},{384,0},{... | collective-permute-start | bytes 983048 | tf_op jit(solution)/shard_map/ppermute | solution.py:31
  198.7 3.1 %collective-permute-start.8 = (bf16[40,1024]{1,0:T(8,128)(2,1)S(1)}, bf16[40,1024]{1,0:T(8,128)(2,1)S(1)}, u32[]{:S(2)}, u32[]{:S(2)}) collective-permute-start(bf16[40,1024]{1,0:T(8,128)(2,1)S(1)} %slice.175), channel_id=1, source_target_pairs={{0,384},{64,448},{128,0},{192,64},{256,128},{320,192},{384,256},{4... | collective-permute-start | bytes 245768 | tf_op jit(solution)/shard_map/ppermute | solution.py:31
  201.9 3.1 %collective-permute-start.7 = (bf16[40,1024]{1,0:T(8,128)(2,1)S(1)}, bf16[40,1024]{1,0:T(8,128)(2,1)S(1)}, u32[]{:S(2)}, u32[]{:S(2)}) collective-permute-start(bf16[40,1024]{1,0:T(8,128)(2,1)S(1)} %slice.174), channel_id=1, source_target_pairs={{0,128},{64,192},{128,256},{192,320},{256,384},{320,448},{384,0},{... | collective-permute-start | bytes 245768 | tf_op jit(solution)/shard_map/ppermute | solution.py:31
  206.3 5.3 %collective-permute-start.18 = (bf16[40,2048]{1,0:T(8,128)(2,1)S(1)}, bf16[40,2048]{1,0:T(8,128)(2,1)S(1)}, u32[]{:S(2)}, u32[]{:S(2)}) collective-permute-start(bf16[40,2048]{1,0:T(8,128)(2,1)S(1)} %slice.183), channel_id=1, source_target_pairs={{0,384},{64,448},{128,0},{192,64},{256,128},{320,192},{384,256},{4... | collective-permute-start | bytes 491528 | tf_op jit(solution)/shard_map/ppermute | solution.py:31
  211.7 2.7 collective-permute-start.17
  215.2 4.6 %collective-permute-done.17 = bf16[40,2048]{1,0:T(8,128)(2,1)S(1)} collective-permute-done((bf16[40,2048]{1,0:T(8,128)(2,1)S(1)}, bf16[40,2048]{1,0:T(8,128)(2,1)S(1)}, u32[]{:S(2)}, u32[]{:S(2)}) %collective-permute-start.17) | collective-permute-done | bytes 163872 | tf_op jit(solution)/shard_map/ppermute | solution.py:31
  219.9 8.1 %collective-permute-start.19 = (bf16[320,2048]{1,0:T(8,128)(2,1)S(1)}, bf16[320,2048]{1,0:T(8,128)(2,1)}, u32[]{:S(2)}, u32[]{:S(2)}) collective-permute-start(bf16[320,2048]{1,0:T(8,128)(2,1)S(1)} %maximum_dynamic-update-slice_fusion), channel_id=1, source_target_pairs={{0,64},{64,0},{128,192},{192,128},{256,320},{320,256},{384,448},{4... | collective-permute-start | bytes 3932168 | tf_op jit(solution)/shard_map/ppermute | solution.py:27
  228.7 1.9 collective-permute-start.9
  230.8 2.3 collective-permute-done.9
  236.5 6.8 %all-to-all-start.4 = ((bf16[8,80,448]{2,1,0:T(8,128)(2,1)}), bf16[8,80,448]{2,1,0:T(8,128)(2,1)S(1)}, u32[]{:S(2)}, u32[]{:S(2)}) async-start(bf16[8,80,448]{2,1,0:T(8,128)(2,1)} %bitcast.32), calls=%async_computation.4 | async-start | bytes 1310720 | tf_op jit(solution)/shard_map/all_to_all | solution.py:105
  243.3 2.0 broadcast_select_fusion.1
  248.3 2.1 copy.128
  250.5 3.7 %all-to-all-done.4 = bf16[8,80,448]{2,1,0:T(8,128)(2,1)S(1)} async-done(((bf16[8,80,448]{2,1,0:T(8,128)(2,1)}), bf16[8,80,448]{2,1,0:T(8,128)(2,1)S(1)}, u32[]{:S(2)}, u32[]{:S(2)}) %all-to-all-start.4) | async-done | bytes 573472 | tf_op jit(solution)/shard_map/all_to_all | solution.py:105
  254.2 4.2 %all-to-all-start.6 = ((bf16[8,80,448]{2,1,0:T(8,128)(2,1)}), bf16[8,80,448]{2,1,0:T(8,128)(2,1)}, u32[]{:S(2)}, u32[]{:S(2)}) async-start(bf16[8,80,448]{2,1,0:T(8,128)(2,1)} %bitcast.40), calls=%async_computation.6 | async-start | bytes 1310720 | tf_op jit(solution)/shard_map/all_to_all | solution.py:105
  261.7 6.7 %all-to-all-done.6 = bf16[8,80,448]{2,1,0:T(8,128)(2,1)} async-done(((bf16[8,80,448]{2,1,0:T(8,128)(2,1)}), bf16[8,80,448]{2,1,0:T(8,128)(2,1)}, u32[]{:S(2)}, u32[]{:S(2)}) %all-to-all-start.6) | async-done | bytes 573472 | tf_op jit(solution)/shard_map/all_to_all | solution.py:105
  268.4 3.4 %all-to-all-start.5 = ((bf16[8,32,448]{2,1,0:T(8,128)(2,1)}), bf16[8,32,448]{2,1,0:T(8,128)(2,1)S(1)}, u32[]{:S(2)}, u32[]{:S(2)}) async-start(bf16[8,32,448]{2,1,0:T(8,128)(2,1)} %bitcast.35), calls=%async_computation.5 | async-start | bytes 524288 | tf_op jit(solution)/shard_map/all_to_all | solution.py:102
  274.2 7.0 %all-to-all-done.5 = bf16[8,32,448]{2,1,0:T(8,128)(2,1)S(1)} async-done(((bf16[8,32,448]{2,1,0:T(8,128)(2,1)}), bf16[8,32,448]{2,1,0:T(8,128)(2,1)S(1)}, u32[]{:S(2)}, u32[]{:S(2)}) %all-to-all-start.5) | async-done | bytes 229408 | tf_op jit(solution)/shard_map/all_to_all | solution.py:102
  281.1 3.4 %all-to-all-start.7 = ((bf16[8,32,448]{2,1,0:T(8,128)(2,1)}), bf16[8,32,448]{2,1,0:T(8,128)(2,1)S(1)}, u32[]{:S(2)}, u32[]{:S(2)}) async-start(bf16[8,32,448]{2,1,0:T(8,128)(2,1)} %bitcast.42), calls=%async_computation.7 | async-start | bytes 524288 | tf_op jit(solution)/shard_map/all_to_all | solution.py:102
  284.6 3.0 %fusion.1 = bf16[1,448,1024]{2,1,0:T(8,128)(2,1)} fusion(bf16[640,448]{1,0:T(8,128)(2,1)} %bitcast.112, bf16[320,2048]{1,0:T(8,128)(2,1)S(1)} %get-tuple-element.7, bf16[320,2048]{1,0:T(8,128)(2,1)S(1)} %get-tuple-element.6), kind=kOutput, calls=%fused_computation.17 | convolution fusion | flops 590282752 | bytes 4112384 | tf_op jit(solution)/shard_map/dot_general | solution.py:12
  287.5 1.8 fusion
  290.0 4.0 %all-to-all-done.7 = bf16[8,32,448]{2,1,0:T(8,128)(2,1)S(1)} async-done(((bf16[8,32,448]{2,1,0:T(8,128)(2,1)}), bf16[8,32,448]{2,1,0:T(8,128)(2,1)S(1)}, u32[]{:S(2)}, u32[]{:S(2)}) %all-to-all-start.7) | async-done | bytes 229408 | tf_op jit(solution)/shard_map/all_to_all | solution.py:102
  (146 shorter events, 47.7 us)
Async XLA Ops:
  3.1 8.6 %copy-start.14 = (bf16[3,448,16]{1,2,0:T(8,128)(2,1)S(1)}, bf16[3,448,16]{1,2,0:T(8,128)(2,1)}, u32[]{:S(2)}) copy-start(bf16[3,448,16]{1,2,0:T(8,128)(2,1)} %param.17) | copy-start | bytes 129028
  3.2 8.7 %copy-start.15 = (bf16[32,448]{1,0:T(8,128)(2,1)S(1)}, bf16[32,448]{1,0:T(8,128)(2,1)}, u32[]{:S(2)}) copy-start(bf16[32,448]{1,0:T(8,128)(2,1)} %param.10) | copy-start | bytes 86020
  3.2 8.7 %copy-start.16 = (bf16[32,448]{1,0:T(8,128)(2,1)S(1)}, bf16[32,448]{1,0:T(8,128)(2,1)}, u32[]{:S(2)}) copy-start(bf16[32,448]{1,0:T(8,128)(2,1)} %param.9) | copy-start | bytes 86020
  12.9 25.7 %all-to-all-start = ((bf16[8,40,1024]{2,1,0:T(8,128)(2,1)}), bf16[8,40,1024]{2,1,0:T(8,128)(2,1)S(1)}, u32[]{:S(2)}, u32[]{:S(2)}) async-start(bf16[8,40,1024]{2,1,0:T(8,128)(2,1)} %fusion.19), calls=%async_computation | async-start | bytes 1310720 | tf_op jit(solution)/shard_map/all_to_all | solution.py:102
  38.6 5.3 %copy-start.7 = (bf16[8,40,1024]{2,1,0:T(8,128)(2,1)}, bf16[8,40,1024]{2,1,0:T(8,128)(2,1)S(1)}, u32[]{:S(2)}) copy-start(bf16[8,40,1024]{2,1,0:T(8,128)(2,1)S(1)} %all-to-all-done) | copy-start | bytes 1966084
  39.4 12.8 %all-to-all-start.1 = ((bf16[8,32,448]{2,1,0:T(8,128)(2,1)}), bf16[8,32,448]{2,1,0:T(8,128)(2,1)S(1)}, u32[]{:S(2)}, u32[]{:S(2)}) async-start(bf16[8,32,448]{2,1,0:T(8,128)(2,1)} %broadcast_in_dim.92), calls=%async_computation.1 | async-start | bytes 524288 | tf_op jit(solution)/shard_map/all_to_all | solution.py:102
  42.8 0.6 copy-start.8
  54.2 44.1 %all-to-all-start.2 = ((bf16[8,336,448]{2,1,0:T(8,128)(2,1)}), bf16[8,336,448]{2,1,0:T(8,128)(2,1)S(1)}, u32[]{:S(2)}, u32[]{:S(2)}) async-start(bf16[8,336,448]{2,1,0:T(8,128)(2,1)} %pad_maximum_fusion), calls=%async_computation.2 | async-start | bytes 5505024 | tf_op jit(solution)/shard_map/all_to_all | solution.py:105
  98.4 24.8 %all-to-all-start.3 = ((bf16[8,208,448]{2,1,0:T(8,128)(2,1)}), bf16[8,208,448]{2,1,0:T(8,128)(2,1)}, u32[]{:S(2)}, u32[]{:S(2)}) async-start(bf16[8,208,448]{2,1,0:T(8,128)(2,1)} %pad_maximum_fusion.1), calls=%async_computation.3 | async-start | bytes 3407872 | tf_op jit(solution)/shard_map/all_to_all | solution.py:105
  108.3 1.2 copy-start.3
  109.5 2.0 copy-start.12
  109.7 1.1 copy-start.9
  109.7 1.7 copy-start.4
  111.6 1.0 copy-start.5
  112.5 1.5 copy-start
  112.5 5.5 %copy-start.11 = (bf16[1,1024,448]{1,2,0:T(8,128)(2,1)S(1)}, bf16[1,1024,448]{1,2,0:T(8,128)(2,1)}, u32[]{:S(2)}) copy-start(bf16[1,1024,448]{1,2,0:T(8,128)(2,1)} %param.16) | copy-start | bytes 2752516
  114.0 18.0 %collective-permute-start = (bf16[320,2048]{1,0:T(8,128)(2,1)}, bf16[320,2048]{1,0:T(8,128)(2,1)}, u32[]{:S(2)}, u32[]{:S(2)}) collective-permute-start(bf16[320,2048]{1,0:T(8,128)(2,1)} %fusion.5), channel_id=1, source_target_pairs={{0,64},{64,0},{128,192},{192,128},{256,320},{320,256},{384,448},{4... | collective-permute-start | bytes 3932168 | tf_op jit(solution)/shard_map/ppermute | solution.py:27
  126.8 5.3 %copy-start.1 = (bf16[640,1024]{1,0:T(8,128)(2,1)S(1)}, bf16[640,1024]{1,0:T(8,128)(2,1)}, u32[]{:S(2)}) copy-start(bf16[640,1024]{1,0:T(8,128)(2,1)} %copy-done) | copy-start | bytes 3932164
  126.8 18.8 %collective-permute-start.10 = (bf16[320,1024]{1,0:T(8,128)(2,1)S(1)}, bf16[320,1024]{1,0:T(8,128)(2,1)S(1)}, u32[]{:S(2)}, u32[]{:S(2)}) collective-permute-start(bf16[320,1024]{1,0:T(8,128)(2,1)S(1)} %constant_dynamic-slice_fusion.4), channel_id=1, source_target_pairs={{0,64},{64,0},{128,192},{192,128},{256,320},{320,256},{384,448},{4... | collective-permute-start | bytes 1966088 | tf_op jit(solution)/shard_map/ppermute | solution.py:27
  133.9 19.4 %collective-permute-start.1 = (bf16[40,2048]{1,0:T(8,128)(2,1)S(1)}, bf16[40,2048]{1,0:T(8,128)(2,1)S(1)}, u32[]{:S(2)}, u32[]{:S(2)}) collective-permute-start(bf16[40,2048]{1,0:T(8,128)(2,1)S(1)} %get-tuple-element.16), channel_id=1, source_target_pairs={{0,128},{64,192},{128,256},{192,320},{256,384},{320,448},{384,0},{... | collective-permute-start | bytes 491528 | tf_op jit(solution)/shard_map/ppermute | solution.py:31
  139.8 14.1 %collective-permute-start.3 = (bf16[40,2048]{1,0:T(8,128)(2,1)S(1)}, bf16[40,2048]{1,0:T(8,128)(2,1)S(1)}, u32[]{:S(2)}, u32[]{:S(2)}) collective-permute-start(bf16[40,2048]{1,0:T(8,128)(2,1)S(1)} %get-tuple-element.18), channel_id=1, source_target_pairs={{0,384},{64,448},{128,0},{192,64},{256,128},{320,192},{384,256},{4... | collective-permute-start | bytes 491528 | tf_op jit(solution)/shard_map/ppermute | solution.py:31
  145.9 15.4 %collective-permute-start.11 = (bf16[40,1024]{1,0:T(8,128)(2,1)S(1)}, bf16[40,1024]{1,0:T(8,128)(2,1)S(1)}, u32[]{:S(2)}, u32[]{:S(2)}) collective-permute-start(bf16[40,1024]{1,0:T(8,128)(2,1)S(1)} %get-tuple-element.22), channel_id=1, source_target_pairs={{0,128},{64,192},{128,256},{192,320},{256,384},{320,448},{384,0},{... | collective-permute-start | bytes 245768 | tf_op jit(solution)/shard_map/ppermute | solution.py:31
  148.1 13.3 %collective-permute-start.13 = (bf16[40,1024]{1,0:T(8,128)(2,1)S(1)}, bf16[40,1024]{1,0:T(8,128)(2,1)S(1)}, u32[]{:S(2)}, u32[]{:S(2)}) collective-permute-start(bf16[40,1024]{1,0:T(8,128)(2,1)S(1)} %get-tuple-element.24), channel_id=1, source_target_pairs={{0,384},{64,448},{128,0},{192,64},{256,128},{320,192},{384,256},{4... | collective-permute-start | bytes 245768 | tf_op jit(solution)/shard_map/ppermute | solution.py:31
  154.0 24.2 %collective-permute-start.4 = (bf16[80,2048]{1,0:T(8,128)(2,1)S(1)}, bf16[80,2048]{1,0:T(8,128)(2,1)S(1)}, u32[]{:S(2)}, u32[]{:S(2)}) collective-permute-start(bf16[80,2048]{1,0:T(8,128)(2,1)S(1)} %pad_maximum_fusion.4), channel_id=1, source_target_pairs={{0,384},{64,448},{128,0},{192,64},{256,128},{320,192},{384,256},{4... | collective-permute-start | bytes 983048 | tf_op jit(solution)/shard_map/ppermute | solution.py:31
  159.2 23.7 %collective-permute-start.2 = (bf16[80,2048]{1,0:T(8,128)(2,1)S(1)}, bf16[80,2048]{1,0:T(8,128)(2,1)S(1)}, u32[]{:S(2)}, u32[]{:S(2)}) collective-permute-start(bf16[80,2048]{1,0:T(8,128)(2,1)S(1)} %pad_maximum_fusion.3), channel_id=1, source_target_pairs={{0,128},{64,192},{128,256},{192,320},{256,384},{320,448},{384,0},{... | collective-permute-start | bytes 983048 | tf_op jit(solution)/shard_map/ppermute | solution.py:31
  161.5 30.6 %collective-permute-start.14 = (bf16[80,1024]{1,0:T(8,128)(2,1)S(1)}, bf16[80,1024]{1,0:T(8,128)(2,1)S(1)}, u32[]{:S(2)}, u32[]{:S(2)}) collective-permute-start(bf16[80,1024]{1,0:T(8,128)(2,1)S(1)} %pad_maximum_fusion.9), channel_id=1, source_target_pairs={{0,384},{64,448},{128,0},{192,64},{256,128},{320,192},{384,256},{4... | collective-permute-start | bytes 491528 | tf_op jit(solution)/shard_map/ppermute | solution.py:31
  166.7 25.3 %collective-permute-start.12 = (bf16[80,1024]{1,0:T(8,128)(2,1)S(1)}, bf16[80,1024]{1,0:T(8,128)(2,1)S(1)}, u32[]{:S(2)}, u32[]{:S(2)}) collective-permute-start(bf16[80,1024]{1,0:T(8,128)(2,1)S(1)} %pad_maximum_fusion.8), channel_id=1, source_target_pairs={{0,128},{64,192},{128,256},{192,320},{256,384},{320,448},{384,0},{... | collective-permute-start | bytes 491528 | tf_op jit(solution)/shard_map/ppermute | solution.py:31
  184.7 17.2 %collective-permute-start.5 = (bf16[80,1024]{1,0:T(8,128)(2,1)S(1)}, bf16[80,1024]{1,0:T(8,128)(2,1)S(1)}, u32[]{:S(2)}, u32[]{:S(2)}) collective-permute-start(bf16[80,1024]{1,0:T(8,128)(2,1)S(1)} %get-tuple-element.5), channel_id=1, source_target_pairs={{0,128},{64,192},{128,256},{192,320},{256,384},{320,448},{384,0},{... | collective-permute-start | bytes 491528 | tf_op jit(solution)/shard_map/ppermute | solution.py:31
  186.6 12.1 %collective-permute-start.6 = (bf16[80,1024]{1,0:T(8,128)(2,1)S(1)}, bf16[80,1024]{1,0:T(8,128)(2,1)S(1)}, u32[]{:S(2)}, u32[]{:S(2)}) collective-permute-start(bf16[80,1024]{1,0:T(8,128)(2,1)S(1)} %get-tuple-element.5), channel_id=1, source_target_pairs={{0,384},{64,448},{128,0},{192,64},{256,128},{320,192},{384,256},{4... | collective-permute-start | bytes 491528 | tf_op jit(solution)/shard_map/ppermute | solution.py:31
  192.5 13.8 %collective-permute-start.16 = (bf16[80,2048]{1,0:T(8,128)(2,1)S(1)}, bf16[80,2048]{1,0:T(8,128)(2,1)S(1)}, u32[]{:S(2)}, u32[]{:S(2)}) collective-permute-start(bf16[80,2048]{1,0:T(8,128)(2,1)S(1)} %get-tuple-element.28), channel_id=1, source_target_pairs={{0,384},{64,448},{128,0},{192,64},{256,128},{320,192},{384,256},{4... | collective-permute-start | bytes 983048 | tf_op jit(solution)/shard_map/ppermute | solution.py:31
  194.4 17.2 %collective-permute-start.15 = (bf16[80,2048]{1,0:T(8,128)(2,1)S(1)}, bf16[80,2048]{1,0:T(8,128)(2,1)S(1)}, u32[]{:S(2)}, u32[]{:S(2)}) collective-permute-start(bf16[80,2048]{1,0:T(8,128)(2,1)S(1)} %get-tuple-element.28), channel_id=1, source_target_pairs={{0,128},{64,192},{128,256},{192,320},{256,384},{320,448},{384,0},{... | collective-permute-start | bytes 983048 | tf_op jit(solution)/shard_map/ppermute | solution.py:31
  198.7 29.3 %collective-permute-start.8 = (bf16[40,1024]{1,0:T(8,128)(2,1)S(1)}, bf16[40,1024]{1,0:T(8,128)(2,1)S(1)}, u32[]{:S(2)}, u32[]{:S(2)}) collective-permute-start(bf16[40,1024]{1,0:T(8,128)(2,1)S(1)} %slice.175), channel_id=1, source_target_pairs={{0,384},{64,448},{128,0},{192,64},{256,128},{320,192},{384,256},{4... | collective-permute-start | bytes 245768 | tf_op jit(solution)/shard_map/ppermute | solution.py:31
  201.9 26.1 %collective-permute-start.7 = (bf16[40,1024]{1,0:T(8,128)(2,1)S(1)}, bf16[40,1024]{1,0:T(8,128)(2,1)S(1)}, u32[]{:S(2)}, u32[]{:S(2)}) collective-permute-start(bf16[40,1024]{1,0:T(8,128)(2,1)S(1)} %slice.174), channel_id=1, source_target_pairs={{0,128},{64,192},{128,256},{192,320},{256,384},{320,448},{384,0},{... | collective-permute-start | bytes 245768 | tf_op jit(solution)/shard_map/ppermute | solution.py:31
  206.3 8.9 %collective-permute-start.18 = (bf16[40,2048]{1,0:T(8,128)(2,1)S(1)}, bf16[40,2048]{1,0:T(8,128)(2,1)S(1)}, u32[]{:S(2)}, u32[]{:S(2)}) collective-permute-start(bf16[40,2048]{1,0:T(8,128)(2,1)S(1)} %slice.183), channel_id=1, source_target_pairs={{0,384},{64,448},{128,0},{192,64},{256,128},{320,192},{384,256},{4... | collective-permute-start | bytes 491528 | tf_op jit(solution)/shard_map/ppermute | solution.py:31
  211.7 8.2 %collective-permute-start.17 = (bf16[40,2048]{1,0:T(8,128)(2,1)S(1)}, bf16[40,2048]{1,0:T(8,128)(2,1)S(1)}, u32[]{:S(2)}, u32[]{:S(2)}) collective-permute-start(bf16[40,2048]{1,0:T(8,128)(2,1)S(1)} %slice.182), channel_id=1, source_target_pairs={{0,128},{64,192},{128,256},{192,320},{256,384},{320,448},{384,0},{... | collective-permute-start | bytes 491528 | tf_op jit(solution)/shard_map/ppermute | solution.py:31
  219.9 14.5 %copy-start.2 = (bf16[320,2048]{1,0:T(8,128)(2,1)}, bf16[320,2048]{1,0:T(8,128)(2,1)S(1)}, u32[]{:S(2)}) copy-start(bf16[320,2048]{1,0:T(8,128)(2,1)S(1)} %maximum_dynamic-update-slice_fusion) | copy-start | bytes 3932164
  219.9 23.4 %collective-permute-start.19 = (bf16[320,2048]{1,0:T(8,128)(2,1)S(1)}, bf16[320,2048]{1,0:T(8,128)(2,1)}, u32[]{:S(2)}, u32[]{:S(2)}) collective-permute-start(bf16[320,2048]{1,0:T(8,128)(2,1)S(1)} %maximum_dynamic-update-slice_fusion), channel_id=1, source_target_pairs={{0,64},{64,0},{128,192},{192,128},{256,320},{320,256},{384,448},{4... | collective-permute-start | bytes 3932168 | tf_op jit(solution)/shard_map/ppermute | solution.py:27
  228.7 4.3 %collective-permute-start.9 = (bf16[320,1024]{1,0:T(8,128)(2,1)}, bf16[320,1024]{1,0:T(8,128)(2,1)}, u32[]{:S(2)}, u32[]{:S(2)}) collective-permute-start(bf16[320,1024]{1,0:T(8,128)(2,1)} %maximum_dynamic-update-slice_fusion.1), channel_id=1, source_target_pairs={{0,64},{64,0},{128,192},{192,128},{256,320},{320,256},{384,448},{4... | collective-permute-start | bytes 1966088 | tf_op jit(solution)/shard_map/ppermute | solution.py:27
  236.5 17.7 %all-to-all-start.4 = ((bf16[8,80,448]{2,1,0:T(8,128)(2,1)}), bf16[8,80,448]{2,1,0:T(8,128)(2,1)S(1)}, u32[]{:S(2)}, u32[]{:S(2)}) async-start(bf16[8,80,448]{2,1,0:T(8,128)(2,1)} %bitcast.32), calls=%async_computation.4 | async-start | bytes 1310720 | tf_op jit(solution)/shard_map/all_to_all | solution.py:105
  243.3 2.0 copy-start.6
  245.3 1.2 copy-start.10
  254.2 14.2 %all-to-all-start.6 = ((bf16[8,80,448]{2,1,0:T(8,128)(2,1)}), bf16[8,80,448]{2,1,0:T(8,128)(2,1)}, u32[]{:S(2)}, u32[]{:S(2)}) async-start(bf16[8,80,448]{2,1,0:T(8,128)(2,1)} %bitcast.40), calls=%async_computation.6 | async-start | bytes 1310720 | tf_op jit(solution)/shard_map/all_to_all | solution.py:105
  268.4 12.8 %all-to-all-start.5 = ((bf16[8,32,448]{2,1,0:T(8,128)(2,1)}), bf16[8,32,448]{2,1,0:T(8,128)(2,1)S(1)}, u32[]{:S(2)}, u32[]{:S(2)}) async-start(bf16[8,32,448]{2,1,0:T(8,128)(2,1)} %bitcast.35), calls=%async_computation.5 | async-start | bytes 524288 | tf_op jit(solution)/shard_map/all_to_all | solution.py:102
  281.1 12.9 %all-to-all-start.7 = ((bf16[8,32,448]{2,1,0:T(8,128)(2,1)}), bf16[8,32,448]{2,1,0:T(8,128)(2,1)S(1)}, u32[]{:S(2)}, u32[]{:S(2)}) async-start(bf16[8,32,448]{2,1,0:T(8,128)(2,1)} %bitcast.42), calls=%async_computation.7 | async-start | bytes 524288 | tf_op jit(solution)/shard_map/all_to_all | solution.py:102
  284.6 3.0 %copy-start.13 = (bf16[8,80,448]{2,1,0:T(8,128)(2,1)S(1)}, bf16[8,80,448]{2,1,0:T(8,128)(2,1)}, u32[]{:S(2)}) copy-start(bf16[8,80,448]{2,1,0:T(8,128)(2,1)} %copy-done.12) | copy-start | bytes 1720324

commit v2 on v0

v2 whole, which is shorter than its diff:
```python
import functools

import jax
import jax.numpy as jnp
import numpy as np
from jax import lax
from jax.experimental import pallas as pl
from jax.experimental.pallas import tpu as pltpu
from jax.sharding import PartitionSpec as P

BF = jnp.bfloat16
F32 = jnp.float32
GRID = {64: (4, 8, 2), 8: (2, 2, 2)}
NN = (((1,), (0,)), ((), ()))
NT = (((1,), (1,)), ((), ()))
TN = (((0,), (0,)), ((), ()))
LANES = 1152
TILE = 256


def dot(a, b, dims=NN):
    return lax.dot_general(a, b, dims, preferred_element_type=F32)


def call(kernel, outs, scratch=(), scalars=0, operands=0, megabytes=32):
    def of(shape, dtype=BF):
        return jax.ShapeDtypeStruct(shape, dtype)

    specs = [pl.BlockSpec(memory_space=pltpu.SMEM)] * scalars
    specs += [pl.BlockSpec(memory_space=pltpu.VMEM)] * operands
    return pl.pallas_call(
        kernel,
        out_shape=[of(*s) if isinstance(s[0], tuple) else of(s) for s in outs],
        in_specs=specs,
        out_specs=[pl.BlockSpec(memory_space=pltpu.VMEM)] * len(outs),
        scratch_shapes=list(scratch),
        compiler_params=pltpu.CompilerParams(vmem_limit_bytes=megabytes << 20),
    )


def pack_kernel(grid, ids_ref, weight_ref, tok_ref, cot_ref, saved_ref, out_ref):
    nx, ny, nz = grid
    nxz, ranks = nx * nz, nx * ny * nz
    tok, topk = ids_ref.shape
    ids = ids_ref[...]
    x, y, z = lax.div(ids, ny * nz), lax.rem(lax.div(ids, nz), ny), lax.rem(ids, nz)
    column = y * nxz + x * nz + z
    lane = lax.broadcasted_iota(jnp.int32, (tok, ranks), 1)
    member = jnp.zeros((tok, ranks), F32)
    share = jnp.zeros((tok, ranks), F32)
    for k in range(topk):
        same = column[:, k : k + 1] == lane
        member = member + jnp.where(same, 1.0, 0.0)
        share = share + jnp.where(same, weight_ref[:, k : k + 1], 0.0)
    row = lax.broadcasted_iota(jnp.int32, (tok, tok), 0)
    col = lax.broadcasted_iota(jnp.int32, (tok, tok), 1)
    before = dot(jnp.where(col <= row, 1.0, 0.0).astype(BF), member.astype(BF))
    place = jnp.where(member > 0.5, before - 1.0, -1.0).astype(BF)
    hi = share.astype(BF)
    lo = (share - hi.astype(F32)).astype(BF)
    source = lax.broadcasted_iota(jnp.int32, (ranks, ny * 128), 0)
    target = lax.broadcasted_iota(jnp.int32, (ranks, ny * 128), 1)
    base = lax.div(source, nxz) * 128 + lax.rem(source, nxz) + 64
    meta = jnp.zeros((tok, ny * 128), F32)
    for k, part in enumerate((place, hi, lo)):
        meta = meta + dot(part, jnp.where(target == base + k * nxz, 1.0, 0.0).astype(BF))
    feat = tok_ref.shape[1]
    assert feat == 448
    last = jnp.concatenate([tok_ref[:, 384:448].astype(F32), jnp.zeros((tok, 64), F32)], axis=1)
    n = saved_ref.shape[1]
    for i in range(ny):
        out_ref[i, 0:tok, 0:384] = tok_ref[:, 0:384]
        out_ref[i, 0:tok, 384:512] = (meta[:, i * 128 : (i + 1) * 128] + last).astype(BF)
        out_ref[i, 0:tok, 512 : 512 + feat] = cot_ref[...]
        out_ref[i, tok : tok + n, 0:feat] = saved_ref[0]
        out_ref[i, tok : tok + n, 512 : 512 + feat] = saved_ref[1]
        for k in range(3):
            out_ref[i, k * n : (k + 1) * n, 1024:1152] = saved_ref[2, :, k * 128 : (k + 1) * 128]
        out_ref[i, 2 * n : 3 * n, 960:1024] = saved_ref[2, :, 384:448]


def select_kernel(first_ref, want_ref, out_ref, pick_ref, hi_ref, lo_ref):
    nxz, _, width = out_ref.shape
    feat = width // 2
    ny, rows, _ = first_ref.shape
    n = 16
    tok = rows - n
    seen = ny * tok
    out_rows = want_ref.shape[0]
    tokens = first_ref[:, 0:tok, 0:feat].reshape(seen, feat)
    cots = first_ref[:, 0:tok, 512 : 512 + feat].reshape(seen, feat)
    meta = jnp.transpose(first_ref[:, 0:tok, 384:512].reshape(seen, 128).astype(F32))
    want = want_ref[...]
    both = jnp.concatenate([cots, cots], axis=0)
    gate = first_ref[:, tok : tok + n, 0:feat].reshape(ny * n, feat)
    up = first_ref[:, tok : tok + n, 512 : 512 + feat].reshape(ny * n, feat)
    half = ny // 2
    for q in range(nxz):
        hit = meta[64 + q : 65 + q] == want
        pick = jnp.where(hit, 1.0, 0.0).astype(BF)
        hi = jnp.where(hit, meta[64 + nxz + q : 65 + nxz + q], 0.0).astype(BF)
        lo = jnp.where(hit, meta[64 + 2 * nxz + q : 65 + 2 * nxz + q], 0.0).astype(BF)
        span = pl.ds(q * out_rows, out_rows)
        pick_ref[span, :] = pick
        hi_ref[span, :] = hi
        lo_ref[span, :] = lo
        out_ref[q, 0:out_rows, 0:feat] = dot(pick, tokens).astype(BF)
        weighted = dot(jnp.concatenate([hi, lo], axis=1), both)
        out_ref[q, 0:out_rows, feat:width] = weighted.astype(BF)
        r = out_rows
        out_ref[q, r : r + ny * n, 0:feat] = gate
        out_ref[q, r : r + ny * n, feat:width] = up
        r += ny * n
        for k in range(3):
            piece = first_ref[:, k * n : (k + 1) * n, 1024:1152]
            at = k * 128
            out_ref[q, r : r + half * n, at : at + 128] = piece[:half].reshape(half * n, 128)
            out_ref[q, r : r + half * n, feat + at : feat + at + 128] = piece[half:].reshape(half * n, 128)
        piece = first_ref[:, 2 * n : 3 * n, 960:1024]
        out_ref[q, r : r + half * n, 384:448] = piece[:half].reshape(half * n, 64)
        out_ref[q, r : r + half * n, feat + 384 : feat + 448] = piece[half:].reshape(half * n, 64)


def chunk_at(h, c, p):
    half = c if p < 4 else 1 - c
    return half * 4 + lax.rem(h + (2, 0, 1, 3)[p % 4], 4)


def products_kernel(
    grid, who_ref, recv_ref, gate_ref, up_ref, down_ref,
    rows_ref, far_ref, rest_ref, far_out_ref, rest_out_ref, restored_ref, grads_ref,
):
    nx, ny, nz = grid
    feat, ff = gate_ref.shape
    chunk = far_ref.shape[0]
    n = 16
    target, h, c = who_ref[0], who_ref[1], who_ref[2]
    for p in range(8):
        g = chunk_at(h, c, p)
        rows_ref[p * chunk : (p + 1) * chunk, :] = recv_ref[g, 0:chunk, 0:feat]
        grads_ref[p * chunk : (p + 1) * chunk, :] = recv_ref[g, 0:chunk, feat : 2 * feat]

    def store(k, j, value):
        at = pl.ds(pl.multiple_of(k * ff + j * TILE, TILE), TILE)
        value = value.astype(BF)
        far_ref[:, at] = value[0:chunk]
        rest_ref[:, at] = value[chunk : 4 * chunk]
        far_out_ref[:, at] = value[4 * chunk : 5 * chunk]
        rest_out_ref[:, at] = value[5 * chunk :]

    tiles = ff // TILE

    @pl.when(target == 0)
    def _():
        @pl.loop(0, tiles)
        def _(j):
            at = pl.ds(pl.multiple_of(j * TILE, TILE), TILE)
            store(0, j, dot(rows_ref[...], gate_ref[:, at]))
            store(1, j, dot(rows_ref[...], up_ref[:, at]))
            store(2, j, dot(grads_ref[...], down_ref[:, at]))

    @pl.when(target == 1)
    def _():
        for x in range(nx):
            for z in range(nz):
                q = x * nz + z
                for y in range(ny):
                    to = pl.ds(((x * ny + y) * nz + z) * n, n)
                    r = chunk + y * n
                    restored_ref[0, to, :] = recv_ref[q, r : r + n, 0:feat]
                    restored_ref[1, to, :] = recv_ref[q, r : r + n, feat : 2 * feat]
                    r = chunk + ny * n + (y % (ny // 2)) * n
                    s = 0 if y < ny // 2 else feat
                    restored_ref[2, to, :] = recv_ref[q, r : r + n, s : s + feat]

        @pl.loop(0, tiles)
        def _(j):
            at = pl.ds(pl.multiple_of(j * TILE, TILE), TILE)
            store(0, j, dot(rows_ref[...], restored_ref[0, at, :], NT))
            store(1, j, dot(rows_ref[...], restored_ref[1, at, :], NT))
            store(2, j, dot(grads_ref[...], restored_ref[2, at, :], NT))


def activate_kernel(own_ref, other_ref, left_ref, right_ref, out_ref):
    ff = out_ref.shape[1] // 3
    rows = out_ref.shape[0]

    @pl.loop(0, ff // TILE)
    def _(j):
        def total(k):
            at = pl.ds(pl.multiple_of(k * ff + j * TILE, TILE), TILE)
            near = own_ref[0:rows, at].astype(F32) + other_ref[0:rows, at].astype(F32)
            return near + (left_ref[:, at].astype(F32) + right_ref[:, at].astype(F32))

        gate, up, dh = total(0), total(1), total(2)
        sig = jax.nn.sigmoid(gate)
        values = (
            gate * sig * up,
            dh * up * sig * (1.0 + gate * (1.0 - sig)),
            dh * gate * sig,
        )
        for k, value in enumerate(values):
            at = pl.ds(pl.multiple_of(k * ff + j * TILE, TILE), TILE)
            out_ref[:, at] = value.astype(BF)


def back_kernel(*refs):
    who_ref, parts = refs[0], refs[1:9]
    gate_ref, up_ref, down_ref, restored_ref, out_ref, grads_ref, hidden_ref, y_ref, dx_ref = refs[9:]
    feat, ff = gate_ref.shape
    chunk = out_ref.shape[1]
    target, h, c = who_ref[0], who_ref[1], who_ref[2]
    for p in range(8):
        span = slice(p * chunk, (p + 1) * chunk)
        hidden_ref[span, :] = parts[p][:, 0:ff]
        grads_ref[span, :] = parts[p][:, ff : 3 * ff]

    @pl.when(target == 0)
    def _():
        y_ref[...] = dot(hidden_ref[...], down_ref[...], NT).astype(BF)
        dx_ref[...] = (
            dot(grads_ref[:, 0:ff], gate_ref[...], NT) + dot(grads_ref[:, ff : 2 * ff], up_ref[...], NT)
        ).astype(BF)

    @pl.when(target == 1)
    def _():
        y_ref[...] = dot(hidden_ref[...], restored_ref[2]).astype(BF)
        dx_ref[...] = (
            dot(grads_ref[:, 0:ff], restored_ref[0]) + dot(grads_ref[:, ff : 2 * ff], restored_ref[1])
        ).astype(BF)

    for p in range(8):
        g = chunk_at(h, c, p)
        span = slice(p * chunk, (p + 1) * chunk)
        out_ref[g, :, 0:feat] = y_ref[span, :]
        out_ref[g, :, feat : 2 * feat] = dx_ref[span, :]


def combine_kernel(recv_ref, pick_ref, hi_ref, lo_ref, out_ref):
    nxz, out_rows, width = recv_ref.shape
    feat = width // 2
    rows = recv_ref[...].reshape(nxz * out_rows, width)
    y = dot(hi_ref[...], rows[:, 0:feat], TN) + dot(lo_ref[...], rows[:, 0:feat], TN)
    out_ref[:, 0:feat] = y.astype(BF)
    out_ref[:, feat:width] = dot(pick_ref[...], rows[:, feat:width], TN).astype(BF)


def finish_kernel(recv_ref, out_ref, grad_ref):
    feat = out_ref.shape[1]
    total = jnp.sum(recv_ref[...].astype(F32), axis=0)
    out_ref[...] = total[:, 0:feat].astype(BF)
    grad_ref[...] = total[:, feat : 2 * feat].astype(BF)


def core_swap(x):
    return lax.ppermute(x, "dp", [(i, i ^ 1) for i in range(8)])


def shift(x, k):
    return lax.ppermute(
        x, "dp", [(2 * h + c, 2 * ((h + k) % 4) + c) for h in range(4) for c in range(2)]
    )


def add(a, b):
    return (a.astype(F32) + b.astype(F32)).astype(BF)


def body(
    tokens,
    cotangent,
    expert_ids,
    route_weight,
    replaced,
    gate_weight,
    up_weight,
    down_weight,
    backup,
):
    ranks = lax.axis_size("expert")
    grid = nx, ny, nz = GRID[ranks]
    nxz = nx * nz
    along_y = [
        [(x * ny + y) * nz + z for y in range(ny)] for x in range(nx) for z in range(nz)
    ]
    along_xz = [
        [(x * ny + y) * nz + z for x in range(nx) for z in range(nz)] for y in range(ny)
    ]

    def exchange(v, groups):
        flat = v.reshape(-1, v.shape[-1])
        flat = lax.all_to_all(flat, "expert", 0, 0, axis_index_groups=groups, tiled=True)
        return flat.reshape(v.shape)

    tok, topk = expert_ids.shape
    feat = tokens.shape[1]
    ff = gate_weight.shape[2]
    ffr = ff // ranks
    capacity = min(tok, 5 * tok * topk // (2 * ranks))
    chunk = ranks * capacity // 8
    me = lax.axis_index("dp")
    who = jnp.stack(
        [(lax.axis_index("expert") == replaced[0]).astype(jnp.int32), me // 2, me % 2]
    ).astype(jnp.int32)

    saved = jnp.transpose(backup, (0, 2, 1))
    (first,) = call(
        functools.partial(pack_kernel, grid), [(ny, tok + ffr, LANES)], operands=5
    )(expert_ids, route_weight, tokens, cotangent, saved)
    first = exchange(first, along_y)

    out_rows, seen = ny * capacity, ny * tok
    row, col = np.arange(out_rows)[:, None], np.arange(seen)[None, :]
    want = np.where(row // capacity == col // tok, row % capacity, -2).astype(np.float32)
    table = (nxz * out_rows, seen)
    send, pick, pick_hi, pick_lo = call(
        select_kernel,
        [(nxz, out_rows + ny * ffr * 3 // 2, 2 * feat), table, table, table],
        operands=2,
    )(first, want)
    recv = exchange(send, along_xz)

    w_gate, w_up, w_down = gate_weight[0], up_weight[0], jnp.transpose(down_weight[0])
    wide = 3 * ff
    rows, far, rest, far_out, rest_out, restored = call(
        functools.partial(products_kernel, grid),
        [
            (8 * chunk, feat), (chunk, wide), (3 * chunk, wide),
            (chunk, wide), (3 * chunk, wide), (3, ff, feat),
        ],
        scratch=[pltpu.VMEM((8 * chunk, feat), BF)],
        scalars=1,
        operands=4,
        megabytes=40,
    )(who, recv, w_gate, w_up, w_down)

    mid = chunk // 2
    far = add(far, core_swap(far_out))
    rest_in = core_swap(rest_out)
    from_left, from_right = shift(far[:mid], 1), shift(far[mid:], -1)
    sides = add(rest[chunk:], rest_in[chunk:])
    right, left = sides[:chunk], sides[chunk:]
    right = jnp.concatenate([add(right[:mid], from_left), right[mid:]], axis=0)
    left = jnp.concatenate([left[:mid], add(left[mid:], from_right)], axis=0)
    from_left, from_right = shift(right, 1), shift(left, -1)
    (own,) = call(activate_kernel, [(chunk, wide)], operands=4)(
        rest, rest_in, from_left, from_right
    )

    left, right = shift(own, 1), shift(own, -1)
    far = jnp.concatenate([shift(left[:mid], 1), shift(right[mid:], -1)], axis=0)
    mine = (far, own, right, left)
    other = tuple(core_swap(v) for v in mine)

    out, grads = call(
        back_kernel,
        [(8, chunk, 2 * feat), (8 * chunk, 2 * ff)],
        scratch=[
            pltpu.VMEM((8 * chunk, ff), BF),
            pltpu.VMEM((8 * chunk, feat), BF),
            pltpu.VMEM((8 * chunk, feat), BF),
        ],
        scalars=1,
        operands=12,
        megabytes=40,
    )(who, *mine, *other, w_gate, w_up, w_down, restored)

    out = exchange(out.reshape(nxz, out_rows, 2 * feat), along_xz)
    gate_grad = dot(rows, grads[:, :ff], TN).astype(BF)
    up_grad = dot(rows, grads[:, ff:], TN).astype(BF)
    (part,) = call(combine_kernel, [(seen, 2 * feat)], operands=4)(out, pick, pick_hi, pick_lo)
    part = exchange(part.reshape(ny, tok, 2 * feat), along_y)
    combined, token_grad = call(finish_kernel, [(tok, feat), (tok, feat)], operands=1)(part)
    return (combined, token_grad, gate_grad[None], up_grad[None])


def solution(mesh):
    placed = (
        P("expert", "dp"),
        P("expert", "dp"),
        P("expert", None),
        P("expert", None),
        P(),
        P("expert", "dp", None),
        P("expert", "dp", None),
        P("expert", None, "dp"),
        P(None, "dp", "expert"),
    )
    return jax.shard_map(
        body,
        mesh=mesh,
        in_specs=placed,
        out_specs=(
            P("expert", "dp"),
            P("expert", "dp"),
            P("expert", "dp", None),
            P("expert", "dp", None),
        ),
        check_vma=False,
    )
```

time: 542 us -> 254 us (0.47)
  waiting for transfers between devices: 436 us -> 82.5 us
  blocking collectives: 0 us -> 52.7 us
  starting transfers between devices: 40.8 us -> 90 us
  matrix products: 25.7 us -> 5.12 us
  between operations: 15.1 us -> 1.64 us
  Pallas kernels: 0 us -> 13.2 us
  local copies, waits for them, and re-layouts: 19 us -> 6.66 us
    all_gather x1 -> x0, waiting for transfers between devices: 193 us -> none  [body(): restored = lax.all_gather(backup, 'expert', axis=2, tiled=True)]
    psum x1 -> x0, waiting for transfers between devices: 154 us -> none  [body(): lax.psum(part_up.astype(jnp.bfloat16), 'dp').astype(jnp.float32)]
    ppermute x0 -> x14, starting transfers between devices: none -> 78.9 us  [the longest x8 43.4 us: shift(): lax.ppermute(x, 'dp', [(2 * h + c, 2 * ((h + k) % 4) + c) for h in range(...]
    all_to_all x0 -> x2, blocking collectives: none -> 52.7 us  [exchange(): lax.all_to_all(flat, 'expert', 0, 0, axis_index_groups=groups, tiled=True)]
    all_to_all x4 -> x2, waiting for transfers between devices: 88.4 us -> 52.8 us  [exchange(): lax.all_to_all(flat, 'expert', 0, 0, axis_index_groups=groups, tiled=True)]
    ppermute x0 -> x14, waiting for transfers between devices: none -> 29.8 us  [the longest x8 28.3 us: shift(): lax.ppermute(x, 'dp', [(2 * h + c, 2 * ((h + k) % 4) + c) for h in range(...]
    all_to_all x4 -> x2, starting transfers between devices: 40.5 us -> 11.1 us  [exchange(): lax.all_to_all(flat, 'expert', 0, 0, axis_index_groups=groups, tiled=True)]
    dot_general x12 -> x2, matrix products: 25.7 us -> 5.12 us  [dot(): return lax.dot_general(a, b, dims, preferred_element_type=F32)]
  transfers between devices with their start and end apart: 6 -> 16, of which waited for: 6 -> 9; matrix products, arithmetic and copies ran while one was open for 4% -> 2% of each run, Pallas kernels for 0% -> 0%
where the time goes in v2:
time: 254 us; the launch traced here: 252 us
  starting transfers between devices  90 us (35%)
  waiting for transfers between devices  82.5 us (32%)
  blocking collectives  52.7 us (21%)
  Pallas kernels  13.2 us (5%)
  local copies, waits for them, and re-layouts  6.66 us (3%)
  matrix products  5.12 us (2%)
    all_to_all x2, waiting for transfers between devices, exchange(): lax.all_to_all(flat, 'expert', 0, 0, axis_index_groups=groups, tiled=True)  52.8 us
    all_to_all x2, blocking collectives, exchange(): lax.all_to_all(flat, 'expert', 0, 0, axis_index_groups=groups, tiled=True)  52.7 us
    ppermute x8, starting transfers between devices, shift(): lax.ppermute(x, 'dp', [(2 * h + c, 2 * ((h + k) % 4) + c) for h in range(...  43.4 us
    ppermute x6, starting transfers between devices, core_swap(): return lax.ppermute(x, 'dp', [(i, i ^ 1) for i in range(8)])  35.5 us
    ppermute x8, waiting for transfers between devices, shift(): lax.ppermute(x, 'dp', [(2 * h + c, 2 * ((h + k) % 4) + c) for h in range(...  28.3 us
    all_to_all x2, starting transfers between devices, exchange(): lax.all_to_all(flat, 'expert', 0, 0, axis_index_groups=groups, tiled=True)  11.1 us
    unnamed x31, local copies, waits for them, and re-layouts  6.54 us
    pallas_call x1, Pallas kernels, body(): call(functools.partial(products_kernel, grid), [(8 * chunk, feat), (chunk...  5.19 us
  transfers between devices with their start and end apart: 16, of which 9 were waited for; matrix products, arithmetic and copies ran while one was open for 2% of the time, Pallas kernels for 0%

profile of v2, /device:TPU:1, one launch (start us, length us, event | category | flops | bytes accessed | tf_op | source)
XLA Modules:
  0.0 252.5 jit_solution(15788486478359601843)
XLA Ops:
  0.6 0.0 copy-start.6
  0.6 0.8 copy.14.ids_ref
  1.4 0.8 copy.15.weight_ref
  2.2 0.8 copy-done.7
  3.0 0.8 copy-done.8
  3.8 0.8 copy-done.9
  4.5 0.4 shard_map.129
  4.9 30.1 %all_to_all.27.first_ref = bf16[8,48,1152]{2,1,0:T(8,128)(2,1)S(1)} all-to-all(bf16[8,48,1152]{2,1,0:T(8,128)(2,1)S(1)} %shard_map.129), channel_id=1, replica_groups={{0,2,4,6,8,10,12,14},{1,3,5,7,9,11,13,15},{16,18,20,22,24,26,28,30},{17..., dimensions={0} | all-to-all | bytes 1769472 | tf_op jit(solution)/shard_map/all_to_all | solution.py:292
  35.0 1.5 shard_map.130
  36.5 1.9 copy-done
  38.4 0.7 copy-done.4
  39.1 7.7 %all-to-all-start.1 = ((bf16[8,272,896]{2,1,0:T(8,128)(2,1)}), bf16[8,272,896]{2,1,0:T(8,128)(2,1)}, u32[]{:S(2)}, u32[]{:S(2)}) async-start(bf16[8,272,896]{2,1,0:T(8,128)(2,1)} %copy-done), calls=%async_computation.1 | async-start | bytes 7798784 | tf_op jit(solution)/shard_map/all_to_all | solution.py:292
  47.4 0.1 pad_add_fusion.who_ref.refs_0_
  47.5 43.4 %all-to-all-done.1.recv_ref = bf16[8,272,896]{2,1,0:T(8,128)(2,1)} async-done(((bf16[8,272,896]{2,1,0:T(8,128)(2,1)}), bf16[8,272,896]{2,1,0:T(8,128)(2,1)}, u32[]{:S(2)}, u32[]{:S(2)}) %all-to-all-start.1) | async-done | bytes 3899424 | tf_op jit(solution)/shard_map/all_to_all | solution.py:292
  90.9 5.2 %shard_map.131 = (bf16[640,448]{1,0:T(8,128)(2,1)S(1)}, bf16[80,3072]{1,0:T(8,128)(2,1)S(1)}, bf16[240,3072]{1,0:T(8,128)(2,1)S(1)}, bf16[80,3072]{1,0:T(8,128)(...) custom-call(s32[3]{0:T(128)S(1)} %pad_add_fusion.who_ref.refs_0_, ...), custom_call_target="tpu_custom_call" | custom-call | tf_op jit(solution)/shard_map/pallas_call | solution.py:325
  96.1 5.1 %collective-permute-start.1 = (bf16[80,3072]{1,0:T(8,128)(2,1)S(1)}, bf16[80,3072]{1,0:T(8,128)(2,1)S(1)}, u32[]{:S(2)}, u32[]{:S(2)}) collective-permute-start(bf16[80,3072]{1,0:T(8,128)(2,1)S(1)} %get-tuple-element.22), channel_id=1, source_target_pairs={{0,64},{64,0},{128,192},{192,128},{256,320},{320,256},{384,448},{4... | collective-permute-start | bytes 1474568 | tf_op jit(solution)/shard_map/ppermute | solution.py:256
  101.3 1.9 collective-permute-start
  103.2 0.1 add_convert_fusion.1
  103.4 9.8 %collective-permute-start.4 = (bf16[40,3072]{1,0:T(8,128)(2,1)S(1)}, bf16[40,3072]{1,0:T(8,128)(2,1)S(1)}, u32[]{:S(2)}, u32[]{:S(2)}) collective-permute-start(bf16[40,3072]{1,0:T(8,128)(2,1)S(1)} %get-tuple-element.36), channel_id=1, source_target_pairs={{0,384},{64,448},{128,0},{192,64},{256,128},{320,192},{384,256},{4... | collective-permute-start | bytes 737288 | tf_op jit(solution)/shard_map/ppermute | solution.py:260
  113.2 1.9 collective-permute-start.2
  115.1 0.3 add_convert_fusion
  115.5 5.3 %collective-permute-done.4 = bf16[40,3072]{1,0:T(8,128)(2,1)S(1)} collective-permute-done((bf16[40,3072]{1,0:T(8,128)(2,1)S(1)}, bf16[40,3072]{1,0:T(8,128)(2,1)S(1)}, u32[]{:S(2)}, u32[]{:S(2)}) %collective-permute-start.4) | collective-permute-done | bytes 245792 | tf_op jit(solution)/shard_map/ppermute | solution.py:260
  120.7 4.9 %collective-permute-done.2 = bf16[40,3072]{1,0:T(8,128)(2,1)S(1)} collective-permute-done((bf16[40,3072]{1,0:T(8,128)(2,1)S(1)}, bf16[40,3072]{1,0:T(8,128)(2,1)S(1)}, u32[]{:S(2)}, u32[]{:S(2)}) %collective-permute-start.2) | collective-permute-done | bytes 245792 | tf_op jit(solution)/shard_map/ppermute | solution.py:260
  125.6 0.1 add_convert_fusion.2
  125.8 1.9 collective-permute-start.3
  127.8 5.5 %collective-permute-start.5 = (bf16[80,3072]{1,0:T(8,128)(2,1)S(1)}, bf16[80,3072]{1,0:T(8,128)(2,1)S(1)}, u32[]{:S(2)}, u32[]{:S(2)}) collective-permute-start(bf16[80,3072]{1,0:T(8,128)(2,1)S(1)} %pad_maximum_fusion.1), channel_id=1, source_target_pairs={{0,384},{64,448},{128,0},{192,64},{256,128},{320,192},{384,256},{4... | collective-permute-start | bytes 1474568 | tf_op jit(solution)/shard_map/ppermute | solution.py:260
  133.3 5.7 %collective-permute-done.3.left_ref = bf16[80,3072]{1,0:T(8,128)(2,1)S(1)} collective-permute-done((bf16[80,3072]{1,0:T(8,128)(2,1)S(1)}, bf16[80,3072]{1,0:T(8,128)(2,1)S(1)}, u32[]{:S(2)}, u32[]{:S(2)}) %collective-permute-start.3) | collective-permute-done | bytes 491552 | tf_op jit(solution)/shard_map/ppermute | solution.py:260
  139.0 0.8 collective-permute-done.5.right_ref
  139.7 0.4 shard_map.132.refs_2_
  140.2 5.2 %collective-permute-start.6 = (bf16[80,3072]{1,0:T(8,128)(2,1)S(1)}, bf16[80,3072]{1,0:T(8,128)(2,1)S(1)}, u32[]{:S(2)}, u32[]{:S(2)}) collective-permute-start(bf16[80,3072]{1,0:T(8,128)(2,1)S(1)} %shard_map.132.refs_2_), channel_id=1, source_target_pairs={{0,128},{64,192},{128,256},{192,320},{256,384},{320,448},{384,0},{... | collective-permute-start | bytes 1474568 | tf_op jit(solution)/shard_map/ppermute | solution.py:260
  145.4 3.1 %collective-permute-start.8 = (bf16[80,3072]{1,0:T(8,128)(2,1)S(1)}, bf16[80,3072]{1,0:T(8,128)(2,1)S(1)}, u32[]{:S(2)}, u32[]{:S(2)}) collective-permute-start(bf16[80,3072]{1,0:T(8,128)(2,1)S(1)} %shard_map.132.refs_2_), channel_id=1, source_target_pairs={{0,384},{64,448},{128,0},{192,64},{256,128},{320,192},{384,256},{4... | collective-permute-start | bytes 1474568 | tf_op jit(solution)/shard_map/ppermute | solution.py:260
  148.5 10.2 %collective-permute-done.6.refs_4_ = bf16[80,3072]{1,0:T(8,128)(2,1)S(1)} collective-permute-done((bf16[80,3072]{1,0:T(8,128)(2,1)S(1)}, bf16[80,3072]{1,0:T(8,128)(2,1)S(1)}, u32[]{:S(2)}, u32[]{:S(2)}) %collective-permute-start.6) | collective-permute-done | bytes 491552 | tf_op jit(solution)/shard_map/ppermute | solution.py:260
  158.7 5.4 %collective-permute-start.7 = (bf16[40,3072]{1,0:T(8,128)(2,1)S(1)}, bf16[40,3072]{1,0:T(8,128)(2,1)S(1)}, u32[]{:S(2)}, u32[]{:S(2)}) collective-permute-start(bf16[40,3072]{1,0:T(8,128)(2,1)S(1)} %slice.61), channel_id=1, source_target_pairs={{0,128},{64,192},{128,256},{192,320},{256,384},{320,448},{384,0},{... | collective-permute-start | bytes 737288 | tf_op jit(solution)/shard_map/ppermute | solution.py:260
  164.1 21.6 %collective-permute-start.11 = (bf16[80,3072]{1,0:T(8,128)(2,1)S(1)}, bf16[80,3072]{1,0:T(8,128)(2,1)S(1)}, u32[]{:S(2)}, u32[]{:S(2)}) collective-permute-start(bf16[80,3072]{1,0:T(8,128)(2,1)S(1)} %shard_map.132.refs_2_), channel_id=1, source_target_pairs={{0,64},{64,0},{128,192},{192,128},{256,320},{320,256},{384,448},{4... | collective-permute-start | bytes 1474568 | tf_op jit(solution)/shard_map/ppermute | solution.py:256
  185.7 10.7 %collective-permute-start.9 = (bf16[40,3072]{1,0:T(8,128)(2,1)S(1)}, bf16[40,3072]{1,0:T(8,128)(2,1)S(1)}, u32[]{:S(2)}, u32[]{:S(2)}) collective-permute-start(bf16[40,3072]{1,0:T(8,128)(2,1)S(1)} %slice.62), channel_id=1, source_target_pairs={{0,384},{64,448},{128,0},{192,64},{256,128},{320,192},{384,256},{4... | collective-permute-start | bytes 737288 | tf_op jit(solution)/shard_map/ppermute | solution.py:260
  196.4 2.2 collective-permute-start.12
  198.6 2.1 collective-permute-start.13
  200.8 1.5 collective-permute-done.9
  202.3 2.5 collective-permute-start.10
  204.8 1.4 collective-permute-done.10.refs_5_
  206.2 3.3 %shard_map.133 = (bf16[8,80,896]{2,1,0:T(8,128)(2,1)S(1)}, bf16[640,2048]{1,0:T(8,128)(2,1)S(1)}) custom-call(s32[3]{0:T(128)S(1)} %pad_add_fusion.who_ref.refs_0_, bf16[80,3072]{1,0:T(8,128)(2,1)S(1)} %constant_dynamic-update-slice_fusion.refs_1_, bf16[80,3072]{1,0:T(8,128)(2,1)S(1)} %shard_map.132.refs_2_, ...), custom_call_target="tpu_custom_call" | custom-call | tf_op jit(solution)/shard_map/pallas_call | solution.py:355
  209.5 22.6 %all_to_all.28.recv_ref = bf16[8,80,896]{2,1,0:T(8,128)(2,1)S(1)} all-to-all(bf16[8,80,896]{2,1,0:T(8,128)(2,1)S(1)} %get-tuple-element.24), channel_id=1, replica_groups={{0,1,16,17,32,33,48,49},{2,3,18,19,34,35,50,51},{4,5,20,21,36,37,52,53}..., dimensions={0} | all-to-all | bytes 2293760 | tf_op jit(solution)/shard_map/all_to_all | solution.py:292
  232.1 1.7 shard_map.134
  233.8 3.5 %all-to-all-start.3 = ((bf16[8,32,896]{2,1,0:T(8,128)(2,1)}), bf16[8,32,896]{2,1,0:T(8,128)(2,1)S(1)}, u32[]{:S(2)}, u32[]{:S(2)}) async-start(bf16[8,32,896]{2,1,0:T(8,128)(2,1)} %bitcast.9), calls=%async_computation.3 | async-start | bytes 917504 | tf_op jit(solution)/shard_map/all_to_all | solution.py:292
  237.3 3.3 %fusion.1 = bf16[1,448,1024]{2,1,0:T(8,128)(2,1)} fusion(bf16[640,448]{1,0:T(8,128)(2,1)S(1)} %copy-done.13, bf16[640,2048]{1,0:T(8,128)(2,1)} %copy-done.10), kind=kOutput, calls=%fused_computation.4 | convolution fusion | flops 587661312 | bytes 2801664 | tf_op jit(solution)/shard_map/dot_general | solution.py:22
  240.6 1.8 fusion
  242.4 9.4 %all-to-all-done.3.recv_ref = bf16[8,32,896]{2,1,0:T(8,128)(2,1)S(1)} async-done(((bf16[8,32,896]{2,1,0:T(8,128)(2,1)}), bf16[8,32,896]{2,1,0:T(8,128)(2,1)S(1)}, u32[]{:S(2)}, u32[]{:S(2)}) %all-to-all-start.3) | async-done | bytes 458784 | tf_op jit(solution)/shard_map/all_to_all | solution.py:292
  251.8 0.7 shard_map.135
  (37 shorter events, 0.3 us)
Async XLA Ops:
  0.6 34.4 %copy-start.6 = (f32[80,256]{1,0:T(8,128)S(1)}, f32[80,256]{1,0:T(8,128)}, u32[]{:S(2)}) copy-start(f32[80,256]{1,0:T(8,128)} %constant.35.clone.want_ref) | copy-start | bytes 245764
  2.2 0.8 copy-start.7
  3.0 0.8 copy-start.8
  3.8 0.8 copy-start.9
  36.5 1.9 copy-start
  38.4 0.7 copy-start.4
  39.1 51.8 %copy-start.1 = (bf16[1,448,1024]{2,1,0:T(8,128)(2,1)S(1)}, bf16[1,448,1024]{2,1,0:T(8,128)(2,1)}, u32[]{:S(2)}) copy-start(bf16[1,448,1024]{2,1,0:T(8,128)(2,1)} %param.15) | copy-start | bytes 2752516
  39.1 51.8 %copy-start.2 = (bf16[1,448,1024]{2,1,0:T(8,128)(2,1)S(1)}, bf16[1,448,1024]{2,1,0:T(8,128)(2,1)}, u32[]{:S(2)}) copy-start(bf16[1,448,1024]{2,1,0:T(8,128)(2,1)} %param.16) | copy-start | bytes 2752516
  39.1 51.8 %copy-start.3 = (bf16[1,1024,448]{1,2,0:T(8,128)(2,1)S(1)}, bf16[1,1024,448]{1,2,0:T(8,128)(2,1)}, u32[]{:S(2)}) copy-start(bf16[1,1024,448]{1,2,0:T(8,128)(2,1)} %param.17) | copy-start | bytes 2752516
  39.1 51.8 %all-to-all-start.1 = ((bf16[8,272,896]{2,1,0:T(8,128)(2,1)}), bf16[8,272,896]{2,1,0:T(8,128)(2,1)}, u32[]{:S(2)}, u32[]{:S(2)}) async-start(bf16[8,272,896]{2,1,0:T(8,128)(2,1)} %copy-done), calls=%async_computation.1 | async-start | bytes 7798784 | tf_op jit(solution)/shard_map/all_to_all | solution.py:292
  96.1 19.3 %copy-start.12 = (bf16[640,448]{1,0:T(8,128)(2,1)}, bf16[640,448]{1,0:T(8,128)(2,1)S(1)}, u32[]{:S(2)}) copy-start(bf16[640,448]{1,0:T(8,128)(2,1)S(1)} %get-tuple-element.30) | copy-start | bytes 1720324
  96.1 7.1 %collective-permute-start.1 = (bf16[80,3072]{1,0:T(8,128)(2,1)S(1)}, bf16[80,3072]{1,0:T(8,128)(2,1)S(1)}, u32[]{:S(2)}, u32[]{:S(2)}) collective-permute-start(bf16[80,3072]{1,0:T(8,128)(2,1)S(1)} %get-tuple-element.22), channel_id=1, source_target_pairs={{0,64},{64,0},{128,192},{192,128},{256,320},{320,256},{384,448},{4... | collective-permute-start | bytes 1474568 | tf_op jit(solution)/shard_map/ppermute | solution.py:256
  101.3 13.8 %collective-permute-start = (bf16[240,3072]{1,0:T(8,128)(2,1)S(1)}, bf16[240,3072]{1,0:T(8,128)(2,1)S(1)}, u32[]{:S(2)}, u32[]{:S(2)}) collective-permute-start(bf16[240,3072]{1,0:T(8,128)(2,1)S(1)} %get-tuple-element.20), channel_id=1, source_target_pairs={{0,64},{64,0},{128,192},{192,128},{256,320},{320,256},{384,448},{4... | collective-permute-start | bytes 4423688 | tf_op jit(solution)/shard_map/ppermute | solution.py:256
  103.4 17.3 %collective-permute-start.4 = (bf16[40,3072]{1,0:T(8,128)(2,1)S(1)}, bf16[40,3072]{1,0:T(8,128)(2,1)S(1)}, u32[]{:S(2)}, u32[]{:S(2)}) collective-permute-start(bf16[40,3072]{1,0:T(8,128)(2,1)S(1)} %get-tuple-element.36), channel_id=1, source_target_pairs={{0,384},{64,448},{128,0},{192,64},{256,128},{320,192},{384,256},{4... | collective-permute-start | bytes 737288 | tf_op jit(solution)/shard_map/ppermute | solution.py:260
  113.2 12.5 %collective-permute-start.2 = (bf16[40,3072]{1,0:T(8,128)(2,1)S(1)}, bf16[40,3072]{1,0:T(8,128)(2,1)S(1)}, u32[]{:S(2)}, u32[]{:S(2)}) collective-permute-start(bf16[40,3072]{1,0:T(8,128)(2,1)S(1)} %get-tuple-element.37), channel_id=1, source_target_pairs={{0,128},{64,192},{128,256},{192,320},{256,384},{320,448},{384,0},{... | collective-permute-start | bytes 737288 | tf_op jit(solution)/shard_map/ppermute | solution.py:260
  125.8 13.2 %collective-permute-start.3 = (bf16[80,3072]{1,0:T(8,128)(2,1)S(1)}, bf16[80,3072]{1,0:T(8,128)(2,1)S(1)}, u32[]{:S(2)}, u32[]{:S(2)}) collective-permute-start(bf16[80,3072]{1,0:T(8,128)(2,1)S(1)} %pad_maximum_fusion), channel_id=1, source_target_pairs={{0,128},{64,192},{128,256},{192,320},{256,384},{320,448},{384,0},{... | collective-permute-start | bytes 1474568 | tf_op jit(solution)/shard_map/ppermute | solution.py:260
  127.8 12.0 %collective-permute-start.5 = (bf16[80,3072]{1,0:T(8,128)(2,1)S(1)}, bf16[80,3072]{1,0:T(8,128)(2,1)S(1)}, u32[]{:S(2)}, u32[]{:S(2)}) collective-permute-start(bf16[80,3072]{1,0:T(8,128)(2,1)S(1)} %pad_maximum_fusion.1), channel_id=1, source_target_pairs={{0,384},{64,448},{128,0},{192,64},{256,128},{320,192},{384,256},{4... | collective-permute-start | bytes 1474568 | tf_op jit(solution)/shard_map/ppermute | solution.py:260
  140.2 18.5 %collective-permute-start.6 = (bf16[80,3072]{1,0:T(8,128)(2,1)S(1)}, bf16[80,3072]{1,0:T(8,128)(2,1)S(1)}, u32[]{:S(2)}, u32[]{:S(2)}) collective-permute-start(bf16[80,3072]{1,0:T(8,128)(2,1)S(1)} %shard_map.132.refs_2_), channel_id=1, source_target_pairs={{0,128},{64,192},{128,256},{192,320},{256,384},{320,448},{384,0},{... | collective-permute-start | bytes 1474568 | tf_op jit(solution)/shard_map/ppermute | solution.py:260
  145.4 40.3 %collective-permute-start.8 = (bf16[80,3072]{1,0:T(8,128)(2,1)S(1)}, bf16[80,3072]{1,0:T(8,128)(2,1)S(1)}, u32[]{:S(2)}, u32[]{:S(2)}) collective-permute-start(bf16[80,3072]{1,0:T(8,128)(2,1)S(1)} %shard_map.132.refs_2_), channel_id=1, source_target_pairs={{0,384},{64,448},{128,0},{192,64},{256,128},{320,192},{384,256},{4... | collective-permute-start | bytes 1474568 | tf_op jit(solution)/shard_map/ppermute | solution.py:260
  158.7 42.1 %collective-permute-start.7 = (bf16[40,3072]{1,0:T(8,128)(2,1)S(1)}, bf16[40,3072]{1,0:T(8,128)(2,1)S(1)}, u32[]{:S(2)}, u32[]{:S(2)}) collective-permute-start(bf16[40,3072]{1,0:T(8,128)(2,1)S(1)} %slice.61), channel_id=1, source_target_pairs={{0,128},{64,192},{128,256},{192,320},{256,384},{320,448},{384,0},{... | collective-permute-start | bytes 737288 | tf_op jit(solution)/shard_map/ppermute | solution.py:260
  164.1 40.7 %collective-permute-start.11 = (bf16[80,3072]{1,0:T(8,128)(2,1)S(1)}, bf16[80,3072]{1,0:T(8,128)(2,1)S(1)}, u32[]{:S(2)}, u32[]{:S(2)}) collective-permute-start(bf16[80,3072]{1,0:T(8,128)(2,1)S(1)} %shard_map.132.refs_2_), channel_id=1, source_target_pairs={{0,64},{64,0},{128,192},{192,128},{256,320},{320,256},{384,448},{4... | collective-permute-start | bytes 1474568 | tf_op jit(solution)/shard_map/ppermute | solution.py:256
  185.7 16.5 %collective-permute-start.9 = (bf16[40,3072]{1,0:T(8,128)(2,1)S(1)}, bf16[40,3072]{1,0:T(8,128)(2,1)S(1)}, u32[]{:S(2)}, u32[]{:S(2)}) collective-permute-start(bf16[40,3072]{1,0:T(8,128)(2,1)S(1)} %slice.62), channel_id=1, source_target_pairs={{0,384},{64,448},{128,0},{192,64},{256,128},{320,192},{384,256},{4... | collective-permute-start | bytes 737288 | tf_op jit(solution)/shard_map/ppermute | solution.py:260
  196.4 8.4 %collective-permute-start.12 = (bf16[80,3072]{1,0:T(8,128)(2,1)S(1)}, bf16[80,3072]{1,0:T(8,128)(2,1)S(1)}, u32[]{:S(2)}, u32[]{:S(2)}) collective-permute-start(bf16[80,3072]{1,0:T(8,128)(2,1)S(1)} %collective-permute-done.8.refs_3_), channel_id=1, source_target_pairs={{0,64},{64,0},{128,192},{192,128},{256,320},{320,256},{384,448},{4... | collective-permute-start | bytes 1474568 | tf_op jit(solution)/shard_map/ppermute | solution.py:256
  198.6 6.2 %collective-permute-start.13 = (bf16[80,3072]{1,0:T(8,128)(2,1)S(1)}, bf16[80,3072]{1,0:T(8,128)(2,1)S(1)}, u32[]{:S(2)}, u32[]{:S(2)}) collective-permute-start(bf16[80,3072]{1,0:T(8,128)(2,1)S(1)} %collective-permute-done.6.refs_4_), channel_id=1, source_target_pairs={{0,64},{64,0},{128,192},{192,128},{256,320},{320,256},{384,448},{4... | collective-permute-start | bytes 1474568 | tf_op jit(solution)/shard_map/ppermute | solution.py:256
  202.3 4.0 %collective-permute-start.10 = (bf16[80,3072]{1,0:T(8,128)(2,1)S(1)}, bf16[80,3072]{1,0:T(8,128)(2,1)S(1)}, u32[]{:S(2)}, u32[]{:S(2)}) collective-permute-start(bf16[80,3072]{1,0:T(8,128)(2,1)S(1)} %constant_dynamic-update-slice_fusion.refs_1_), channel_id=1, source_target_pairs={{0,64},{64,0},{128,192},{192,128},{256,320},{320,256},{384,448},{4... | collective-permute-start | bytes 1474568 | tf_op jit(solution)/shard_map/ppermute | solution.py:256
  209.5 24.3 %copy-start.10 = (bf16[640,2048]{1,0:T(8,128)(2,1)}, bf16[640,2048]{1,0:T(8,128)(2,1)S(1)}, u32[]{:S(2)}) copy-start(bf16[640,2048]{1,0:T(8,128)(2,1)S(1)} %get-tuple-element.31) | copy-start | bytes 7864324
  209.5 22.6 %copy-start.5 = (bf16[640,256]{1,0:T(8,128)(2,1)S(1)}, bf16[640,256]{1,0:T(8,128)(2,1)}, u32[]{:S(2)}) copy-start(bf16[640,256]{1,0:T(8,128)(2,1)} %copy-done.4) | copy-start | bytes 983044
  232.1 5.1 %copy-start.13 = (bf16[640,448]{1,0:T(8,128)(2,1)S(1)}, bf16[640,448]{1,0:T(8,128)(2,1)}, u32[]{:S(2)}) copy-start(bf16[640,448]{1,0:T(8,128)(2,1)} %copy-done.12) | copy-start | bytes 1720324
  233.8 18.0 %all-to-all-start.3 = ((bf16[8,32,896]{2,1,0:T(8,128)(2,1)}), bf16[8,32,896]{2,1,0:T(8,128)(2,1)S(1)}, u32[]{:S(2)}, u32[]{:S(2)}) async-start(bf16[8,32,896]{2,1,0:T(8,128)(2,1)} %bitcast.9), calls=%async_computation.3 | async-start | bytes 917504 | tf_op jit(solution)/shard_map/all_to_all | solution.py:292
  237.3 3.3 %copy-start.11 = (bf16[640,2048]{1,0:T(8,128)(2,1)S(1)}, bf16[640,2048]{1,0:T(8,128)(2,1)}, u32[]{:S(2)}) copy-start(bf16[640,2048]{1,0:T(8,128)(2,1)} %copy-done.10) | copy-start | bytes 7864324

commit v3 on v2

v3 whole, which is shorter than its diff:
```python
import functools

import jax
import jax.numpy as jnp
import numpy as np
from jax import lax
from jax.experimental import pallas as pl
from jax.experimental.pallas import tpu as pltpu
from jax.sharding import PartitionSpec as P

BF = jnp.bfloat16
F32 = jnp.float32
GRID = {64: (4, 8, 2), 8: (2, 2, 2)}
NN = (((1,), (0,)), ((), ()))
NT = (((1,), (1,)), ((), ()))
TN = (((0,), (0,)), ((), ()))
LANES = 1280
TILE = 256


def dot(a, b, dims=NN):
    return lax.dot_general(a, b, dims, preferred_element_type=F32)


def call(kernel, outs, scratch=(), scalars=0, operands=0, megabytes=32):
    def of(shape, dtype=BF):
        return jax.ShapeDtypeStruct(shape, dtype)

    specs = [pl.BlockSpec(memory_space=pltpu.SMEM)] * scalars
    specs += [pl.BlockSpec(memory_space=pltpu.VMEM)] * operands
    return pl.pallas_call(
        kernel,
        out_shape=[of(*s) if isinstance(s[0], tuple) else of(s) for s in outs],
        in_specs=specs,
        out_specs=[pl.BlockSpec(memory_space=pltpu.VMEM)] * len(outs),
        scratch_shapes=list(scratch),
        compiler_params=pltpu.CompilerParams(vmem_limit_bytes=megabytes << 20),
    )


def pack_kernel(grid, ids_ref, weight_ref, tok_ref, cot_ref, saved_ref, out_ref):
    nx, ny, nz = grid
    nxz, ranks = nx * nz, nx * ny * nz
    tok, topk = ids_ref.shape
    ids = ids_ref[...]
    x, y, z = lax.div(ids, ny * nz), lax.rem(lax.div(ids, nz), ny), lax.rem(ids, nz)
    column = y * nxz + x * nz + z
    lane = lax.broadcasted_iota(jnp.int32, (tok, ranks), 1)
    member = jnp.zeros((tok, ranks), F32)
    share = jnp.zeros((tok, ranks), F32)
    for k in range(topk):
        same = column[:, k : k + 1] == lane
        member = member + jnp.where(same, 1.0, 0.0)
        share = share + jnp.where(same, weight_ref[:, k : k + 1], 0.0)
    row = lax.broadcasted_iota(jnp.int32, (tok, tok), 0)
    col = lax.broadcasted_iota(jnp.int32, (tok, tok), 1)
    before = dot(jnp.where(col <= row, 1.0, 0.0).astype(BF), member.astype(BF))
    place = jnp.where(member > 0.5, before - 1.0, -1.0).astype(BF)
    hi = share.astype(BF)
    lo = (share - hi.astype(F32)).astype(BF)
    source = lax.broadcasted_iota(jnp.int32, (ranks, ny * 128), 0)
    target = lax.broadcasted_iota(jnp.int32, (ranks, ny * 128), 1)
    base = lax.div(source, nxz) * 128 + lax.rem(source, nxz) + 64
    meta = jnp.zeros((tok, ny * 128), F32)
    for k, part in enumerate((place, hi, lo)):
        meta = meta + dot(part, jnp.where(target == base + k * nxz, 1.0, 0.0).astype(BF))
    feat = tok_ref.shape[1]
    assert feat == 448
    last = jnp.concatenate([tok_ref[:, 384:448].astype(F32), jnp.zeros((tok, 64), F32)], axis=1)
    n = saved_ref.shape[0]
    for i in range(ny):
        out_ref[i, :, 0:384] = tok_ref[:, 0:384]
        out_ref[i, :, 384:512] = (meta[:, i * 128 : (i + 1) * 128] + last).astype(BF)
        out_ref[i, :, 512 : 512 + feat] = cot_ref[...]
        for k in range(4):
            at, wide = 1024 + 128 * (k // 2), min(128, feat - 128 * k)
            out_ref[i, (k % 2) * n : (k % 2 + 1) * n, at : at + wide] = saved_ref[:, 128 * k : 128 * k + wide]


def select_kernel(first_ref, want_ref, out_ref, pick_ref, hi_ref, lo_ref):
    nxz = out_ref.shape[0]
    ny, tok, _ = first_ref.shape
    n = tok // 2
    seen = ny * tok
    rows = want_ref.shape[0]
    saved = ny * n
    cots = first_ref[:, :, 512:960].reshape(seen, 448)
    meta = jnp.transpose(first_ref[:, :, 384:512].reshape(seen, 128).astype(F32))
    want = want_ref[...]
    both = jnp.concatenate([cots, cots], axis=0)
    split = saved - rows
    for q in range(nxz):
        hit = meta[64 + q : 65 + q] == want
        hi = jnp.where(hit, meta[64 + nxz + q : 65 + nxz + q], 0.0).astype(BF)
        lo = jnp.where(hit, meta[64 + 2 * nxz + q : 65 + 2 * nxz + q], 0.0).astype(BF)
        span = pl.ds(q * rows, rows)
        pick_ref[span, :] = jnp.where(hit, 1.0, 0.0).astype(BF)
        hi_ref[span, :] = hi
        lo_ref[span, :] = lo
        value = dot(jnp.concatenate([hi, lo], axis=1), both).astype(BF)
        out_ref[q, 0:rows, 512:640] = value[:, 0:128]
        out_ref[q, 0:rows, 640:768] = value[:, 128:256]
        out_ref[q, rows : rows + split, 512:640] = value[0:split, 256:384]
        out_ref[q, rows : 2 * rows - split, 640:768] = value[split:, 256:384]
        out_ref[q, 0:rows, 448:512] = value[:, 384:448]
        for k in range(4):
            at, wide = 1024 + 128 * (k // 2), min(128, 448 - 128 * k)
            piece = first_ref[:, (k % 2) * n : (k % 2 + 1) * n, at : at + wide]
            out_ref[q, 0:saved, 128 * k : 128 * k + wide] = piece.reshape(saved, wide)


def pick_kernel(first_ref, pick_ref, out_ref):
    ny, tok, _ = first_ref.shape
    nxz, rows, feat = out_ref.shape
    tokens = first_ref[:, :, 0:feat].reshape(ny * tok, feat)
    out_ref[...] = dot(pick_ref[...], tokens).astype(BF).reshape(nxz, rows, feat)


def chunk_at(h, c, p):
    half = c if p < 4 else 1 - c
    return half * 4 + lax.rem(h + (2, 0, 1, 3)[p % 4], 4)


def store(outs, chunk, at, value):
    value = value.astype(BF)
    outs[0][:, at] = value[0:chunk]
    outs[1][:, at] = value[chunk : 4 * chunk]
    outs[2][:, at] = value[4 * chunk : 5 * chunk]
    outs[3][:, at] = value[5 * chunk :]


def down_kernel(grid, who_ref, recv_ref, down_ref, o0, o1, o2, o3, restored_ref, grads_ref):
    nx, ny, nz = grid
    ff = down_ref.shape[1]
    chunk = o0.shape[0]
    outs = (o0, o1, o2, o3)
    saved = recv_ref.shape[1]
    n = saved // ny
    split = saved - chunk
    target, h, c = who_ref[0], who_ref[1], who_ref[2]
    for p in range(8):
        g = chunk_at(h, c, p)
        at = p * chunk
        grads_ref[at : at + chunk, 0:128] = recv_ref[g, 0:chunk, 512:640]
        grads_ref[at : at + chunk, 128:256] = recv_ref[g, 0:chunk, 640:768]
        grads_ref[at : at + split, 256:384] = recv_ref[g, chunk : chunk + split, 512:640]
        grads_ref[at + split : at + chunk, 256:384] = recv_ref[g, chunk : 2 * chunk - split, 640:768]
        grads_ref[at : at + chunk, 384:448] = recv_ref[g, 0:chunk, 448:512]

    @pl.when(target == 0)
    def _():
        @pl.loop(0, ff // TILE)
        def _(j):
            at = pl.ds(pl.multiple_of(j * TILE, TILE), TILE)
            store(outs, chunk, at, dot(grads_ref[...], down_ref[:, at]))

    @pl.when(target == 1)
    def _():
        for x in range(nx):
            for z in range(nz):
                for y in range(ny):
                    to = pl.ds(((x * ny + y) * nz + z) * n, n)
                    restored_ref[to, :] = recv_ref[x * nz + z, y * n : (y + 1) * n, 0:448]

        @pl.loop(0, ff // TILE)
        def _(j):
            at = pl.ds(pl.multiple_of(j * TILE, TILE), TILE)
            store(outs, chunk, at, dot(grads_ref[...], restored_ref[at, :], NT))


def gate_up_kernel(
    grid, who_ref, recv_ref, saved_ref, gate_ref, up_ref, rows_ref, o0, o1, o2, o3, restored_ref
):
    nx, ny, nz = grid
    feat, ff = gate_ref.shape
    chunk = o0.shape[0]
    outs = (o0, o1, o2, o3)
    n = saved_ref.shape[0] // (nx * ny * nz)
    target, h, c, my_x, my_z = (who_ref[i] for i in range(5))
    for p in range(8):
        rows_ref[p * chunk : (p + 1) * chunk, :] = recv_ref[chunk_at(h, c, p)]

    def tile(k, j):
        return pl.ds(pl.multiple_of(k * ff + j * TILE, TILE), TILE)

    @pl.when(target == 0)
    def _():
        @pl.loop(0, ff // TILE)
        def _(j):
            store(outs, chunk, tile(0, j), dot(rows_ref[...], gate_ref[:, tile(0, j)]))
            store(outs, chunk, tile(1, j), dot(rows_ref[...], up_ref[:, tile(0, j)]))

    @pl.when(target == 1)
    def _():
        for y in range(ny):
            for k in range(nx):
                for other in range(nz):
                    x = lax.rem(my_x - k + nx, nx)
                    z = 1 - my_z if other else my_z
                    to = pl.ds(pl.multiple_of(((x * ny + y) * nz + z) * n, n), n)
                    r = ((y * nx + k) * nz + other) * n
                    restored_ref[0, to, :] = saved_ref[r : r + n, 0:feat]
                    restored_ref[1, to, :] = saved_ref[r : r + n, feat : 2 * feat]

        @pl.loop(0, ff // TILE)
        def _(j):
            store(outs, chunk, tile(0, j), dot(rows_ref[...], restored_ref[0, tile(0, j), :], NT))
            store(outs, chunk, tile(1, j), dot(rows_ref[...], restored_ref[1, tile(0, j), :], NT))


def activate_kernel(*refs):
    gate_up, grads, out_ref = refs[0:4], refs[4:8], refs[8]
    ff = out_ref.shape[1] // 3
    rows = out_ref.shape[0]

    @pl.loop(0, ff // TILE)
    def _(j):
        def total(parts, k):
            at = pl.ds(pl.multiple_of(k * ff + j * TILE, TILE), TILE)
            near = parts[0][0:rows, at].astype(F32) + parts[1][0:rows, at].astype(F32)
            return near + (parts[2][:, at].astype(F32) + parts[3][:, at].astype(F32))

        gate, up, dh = total(gate_up, 0), total(gate_up, 1), total(grads, 0)
        sig = jax.nn.sigmoid(gate)
        values = (
            gate * sig * up,
            dh * up * sig * (1.0 + gate * (1.0 - sig)),
            dh * gate * sig,
        )
        for k, value in enumerate(values):
            at = pl.ds(pl.multiple_of(k * ff + j * TILE, TILE), TILE)
            out_ref[:, at] = value.astype(BF)


def back_kernel(*refs):
    who_ref, parts = refs[0], refs[1:9]
    gate_ref, up_ref, down_ref, restored_ref, restored_down_ref = refs[9:14]
    out_ref, grads_ref, hidden_ref, y_ref, dx_ref = refs[14:]
    feat, ff = gate_ref.shape
    chunk = out_ref.shape[1]
    target, h, c = who_ref[0], who_ref[1], who_ref[2]
    for p in range(8):
        span = slice(p * chunk, (p + 1) * chunk)
        hidden_ref[span, :] = parts[p][:, 0:ff]
        grads_ref[span, :] = parts[p][:, ff : 3 * ff]

    @pl.when(target == 0)
    def _():
        y_ref[...] = dot(hidden_ref[...], down_ref[...], NT).astype(BF)
        dx_ref[...] = (
            dot(grads_ref[:, 0:ff], gate_ref[...], NT) + dot(grads_ref[:, ff : 2 * ff], up_ref[...], NT)
        ).astype(BF)

    @pl.when(target == 1)
    def _():
        y_ref[...] = dot(hidden_ref[...], restored_down_ref[...]).astype(BF)
        dx_ref[...] = (
            dot(grads_ref[:, 0:ff], restored_ref[0]) + dot(grads_ref[:, ff : 2 * ff], restored_ref[1])
        ).astype(BF)

    for p in range(8):
        g = chunk_at(h, c, p)
        span = slice(p * chunk, (p + 1) * chunk)
        out_ref[g, :, 0:feat] = y_ref[span, :]
        out_ref[g, :, feat : 2 * feat] = dx_ref[span, :]


def combine_kernel(recv_ref, pick_ref, hi_ref, lo_ref, out_ref):
    nxz, out_rows, width = recv_ref.shape
    feat = width // 2
    rows = recv_ref[...].reshape(nxz * out_rows, width)
    y = dot(hi_ref[...], rows[:, 0:feat], TN) + dot(lo_ref[...], rows[:, 0:feat], TN)
    out_ref[:, 0:feat] = y.astype(BF)
    out_ref[:, feat:width] = dot(pick_ref[...], rows[:, feat:width], TN).astype(BF)


def finish_kernel(recv_ref, out_ref, grad_ref):
    feat = out_ref.shape[1]
    total = jnp.sum(recv_ref[...].astype(F32), axis=0)
    out_ref[...] = total[:, 0:feat].astype(BF)
    grad_ref[...] = total[:, feat : 2 * feat].astype(BF)


def core_swap(x):
    return lax.ppermute(x, "dp", [(i, i ^ 1) for i in range(8)])


def shift(x, k):
    return lax.ppermute(
        x, "dp", [(2 * h + c, 2 * ((h + k) % 4) + c) for h in range(4) for c in range(2)]
    )


def add(a, b):
    return (a.astype(F32) + b.astype(F32)).astype(BF)


def body(
    tokens,
    cotangent,
    expert_ids,
    route_weight,
    replaced,
    gate_weight,
    up_weight,
    down_weight,
    backup,
):
    ranks = lax.axis_size("expert")
    grid = nx, ny, nz = GRID[ranks]
    nxz = nx * nz
    along_y = [
        [(x * ny + y) * nz + z for y in range(ny)] for x in range(nx) for z in range(nz)
    ]
    along_xz = [
        [(x * ny + y) * nz + z for x in range(nx) for z in range(nz)] for y in range(ny)
    ]

    def exchange(v, groups):
        flat = v.reshape(-1, v.shape[-1])
        flat = lax.all_to_all(flat, "expert", 0, 0, axis_index_groups=groups, tiled=True)
        return flat.reshape(v.shape)

    def rank(x, y, z):
        return ((x % nx) * ny + y) * nz + z % nz

    def step(v, dx, dz):
        pairs = [
            (rank(x, y, z), rank(x + dx, y, z + dz))
            for x in range(nx) for y in range(ny) for z in range(nz)
        ]
        return lax.ppermute(v, "expert", pairs)

    tok, topk = expert_ids.shape
    feat = tokens.shape[1]
    ff = gate_weight.shape[2]
    ffr = ff // ranks
    capacity = min(tok, 5 * tok * topk // (2 * ranks))
    chunk = ranks * capacity // 8
    mid = chunk // 2
    me, expert = lax.axis_index("dp"), lax.axis_index("expert")
    who = jnp.stack(
        [
            (expert == replaced[0]).astype(jnp.int32),
            me // 2,
            me % 2,
            expert // (ny * nz),
            expert % nz,
        ]
    ).astype(jnp.int32)

    saved = jnp.transpose(backup, (0, 2, 1))
    pair = jnp.concatenate([saved[0], saved[1]], axis=1)
    pair = jnp.concatenate([pair, step(pair, 0, 1)], axis=0)
    (first,) = call(functools.partial(pack_kernel, grid), [(ny, tok, LANES)], operands=5)(
        expert_ids, route_weight, tokens, cotangent, saved[2]
    )
    pair, first = lax.optimization_barrier((pair, first))
    first = exchange(first, along_y)

    line = jnp.concatenate([pair] + [step(pair, k, 0) for k in range(1, nx)], axis=0)
    line, first = lax.optimization_barrier((line, first))
    saved_gate_up = lax.all_gather(
        line, "expert", axis=0, axis_index_groups=along_y, tiled=True
    )

    out_rows, seen = ny * capacity, ny * tok
    row, col = np.arange(out_rows)[:, None], np.arange(seen)[None, :]
    want = np.where(row // capacity == col // tok, row % capacity, -2).astype(np.float32)
    table = (nxz * out_rows, seen)
    send, pick, pick_hi, pick_lo = call(
        select_kernel, [(nxz, ny * ffr, 768), table, table, table], operands=2
    )(first, want)
    recv_grads = exchange(send, along_xz)
    (send,) = call(pick_kernel, [(nxz, out_rows, feat)], operands=2)(first, pick)
    recv_rows = exchange(send, along_xz)

    def sum_parts(far, rest, far_out, rest_out):
        far = add(far, core_swap(far_out))
        rest_in = core_swap(rest_out)
        from_left, from_right = shift(far[:mid], 1), shift(far[mid:], -1)
        sides = add(rest[chunk:], rest_in[chunk:])
        right, left = sides[:chunk], sides[chunk:]
        right = jnp.concatenate([add(right[:mid], from_left), right[mid:]], axis=0)
        left = jnp.concatenate([left[:mid], add(left[mid:], from_right)], axis=0)
        return rest, rest_in, shift(right, 1), shift(left, -1)

    def parts_of(width):
        return [(chunk, width), (3 * chunk, width)] * 2

    w_gate, w_up, w_down = gate_weight[0], up_weight[0], jnp.transpose(down_weight[0])
    *parts, restored_down = call(
        functools.partial(down_kernel, grid),
        parts_of(ff) + [(ff, feat)],
        scratch=[pltpu.VMEM((8 * chunk, feat), BF)],
        scalars=1,
        operands=2,
    )(who, recv_grads, w_down)
    grad_parts = sum_parts(*parts)
    rows, *parts, restored = call(
        functools.partial(gate_up_kernel, grid),
        [(8 * chunk, feat)] + parts_of(2 * ff) + [(2, ff, feat)],
        scalars=1,
        operands=4,
    )(who, recv_rows, saved_gate_up, w_gate, w_up)
    (own,) = call(activate_kernel, [(chunk, 3 * ff)], operands=8)(*sum_parts(*parts), *grad_parts)

    left, right, own_other = lax.optimization_barrier((shift(own, 1), shift(own, -1), core_swap(own)))
    far = (shift(left[:mid], 1), shift(right[mid:], -1))
    low, high, right_other, left_other = lax.optimization_barrier(
        (*far, core_swap(right), core_swap(left))
    )
    far = jnp.concatenate([low, high], axis=0)
    mine = (far, own, right, left)
    other = (core_swap(far), own_other, right_other, left_other)

    out, grads = call(
        back_kernel,
        [(8, chunk, 2 * feat), (8 * chunk, 2 * ff)],
        scratch=[
            pltpu.VMEM((8 * chunk, ff), BF),
            pltpu.VMEM((8 * chunk, feat), BF),
            pltpu.VMEM((8 * chunk, feat), BF),
        ],
        scalars=1,
        operands=13,
        megabytes=40,
    )(who, *mine, *other, w_gate, w_up, w_down, restored, restored_down)

    out = exchange(out.reshape(nxz, out_rows, 2 * feat), along_xz)
    gate_grad = dot(rows, grads[:, :ff], TN).astype(BF)
    up_grad = dot(rows, grads[:, ff:], TN).astype(BF)
    (part,) = call(combine_kernel, [(seen, 2 * feat)], operands=4)(out, pick, pick_hi, pick_lo)
    part = exchange(part.reshape(ny, tok, 2 * feat), along_y)
    combined, token_grad = call(finish_kernel, [(tok, feat), (tok, feat)], operands=1)(part)
    return (combined, token_grad, gate_grad[None], up_grad[None])


def solution(mesh):
    placed = (
        P("expert", "dp"),
        P("expert", "dp"),
        P("expert", None),
        P("expert", None),
        P(),
        P("expert", "dp", None),
        P("expert", "dp", None),
        P("expert", None, "dp"),
        P(None, "dp", "expert"),
    )
    return jax.shard_map(
        body,
        mesh=mesh,
        in_specs=placed,
        out_specs=(
            P("expert", "dp"),
            P("expert", "dp"),
            P("expert", "dp", None),
            P("expert", "dp", None),
        ),
        check_vma=False,
    )
```

time: 254 us -> 275 us (1.083)
  blocking collectives: 52.7 us -> 23.3 us
  waiting for transfers between devices: 82.5 us -> 96.9 us
  starting transfers between devices: 90 us -> 104 us
  between operations: 1.64 us -> 15.3 us
  local copies, waits for them, and re-layouts: 6.66 us -> 11.2 us
    all_to_all x2 -> x1, blocking collectives: 52.7 us -> 23.3 us  [exchange(): lax.all_to_all(flat, 'expert', 0, 0, axis_index_groups=groups, tiled=True)]
    ppermute x8 -> x12, waiting for transfers between devices: 28.3 us -> 55.9 us  [shift(): lax.ppermute(x, 'dp', [(2 * h + c, 2 * ((h + k) % 4) + c) for h in range(...]
    all_to_all x2 -> x4, waiting for transfers between devices: 52.8 us -> 34.4 us  [exchange(): lax.all_to_all(flat, 'expert', 0, 0, axis_index_groups=groups, tiled=True)]
    ppermute x0 -> x4, starting transfers between devices: none -> 14.1 us  [step(): return lax.ppermute(v, 'expert', pairs)]
    ppermute x6 -> x8, starting transfers between devices: 35.5 us -> 22.6 us  [core_swap(): return lax.ppermute(x, 'dp', [(i, i ^ 1) for i in range(8)])]
    all_to_all x2 -> x4, starting transfers between devices: 11.1 us -> 18.5 us  [exchange(): lax.all_to_all(flat, 'expert', 0, 0, axis_index_groups=groups, tiled=True)]
    ppermute x8 -> x12, starting transfers between devices: 43.4 us -> 48.4 us  [shift(): lax.ppermute(x, 'dp', [(2 * h + c, 2 * ((h + k) % 4) + c) for h in range(...]
    ppermute x0 -> x4, waiting for transfers between devices: none -> 4.43 us  [step(): return lax.ppermute(v, 'expert', pairs)]
  transfers between devices with their start and end apart: 16 -> 29, of which waited for: 9 -> 14; matrix products, arithmetic and copies ran while one was open for 2% -> 3% of each run, Pallas kernels for 0% -> 3%
where the time goes in v3:
time: 275 us; the launch traced here: 274 us
  starting transfers between devices  104 us (38%)
  waiting for transfers between devices  96.9 us (35%)
  blocking collectives  23.3 us (8%)
  Pallas kernels  15.8 us (6%)
  between operations  15.3 us (6%)
  local copies, waits for them, and re-layouts  11.2 us (4%)
  matrix products  5.11 us (2%)
    ppermute x12, waiting for transfers between devices, shift(): lax.ppermute(x, 'dp', [(2 * h + c, 2 * ((h + k) % 4) + c) for h in range(...  55.9 us
    ppermute x12, starting transfers between devices, shift(): lax.ppermute(x, 'dp', [(2 * h + c, 2 * ((h + k) % 4) + c) for h in range(...  48.4 us
    all_to_all x4, waiting for transfers between devices, exchange(): lax.all_to_all(flat, 'expert', 0, 0, axis_index_groups=groups, tiled=True)  34.4 us
    all_to_all x1, blocking collectives, exchange(): lax.all_to_all(flat, 'expert', 0, 0, axis_index_groups=groups, tiled=True)  23.3 us
    ppermute x8, starting transfers between devices, core_swap(): return lax.ppermute(x, 'dp', [(i, i ^ 1) for i in range(8)])  22.6 us
    all_to_all x4, starting transfers between devices, exchange(): lax.all_to_all(flat, 'expert', 0, 0, axis_index_groups=groups, tiled=True)  18.5 us
    ppermute x4, starting transfers between devices, step(): return lax.ppermute(v, 'expert', pairs)  14.1 us
    unnamed x45, local copies, waits for them, and re-layouts  10.2 us
  transfers between devices with their start and end apart: 29, of which 14 were waited for; matrix products, arithmetic and copies ran while one was open for 3% of the time, Pallas kernels for 3%

profile of v3, /device:TPU:1, one launch (start us, length us, event | category | flops | bytes accessed | tf_op | source)
XLA Modules:
  0.0 273.6 jit_solution(6340728184851980090)
XLA Ops:
  8.0 4.8 %collective-permute-start = (bf16[16,896]{1,0:T(8,128)(2,1)S(1)}, bf16[16,896]{1,0:T(8,128)(2,1)S(1)}, u32[]{:S(2)}, u32[]{:S(2)}) collective-permute-start(bf16[16,896]{1,0:T(8,128)(2,1)S(1)} %pad_maximum_fusion.6), channel_id=1, source_target_pairs={{0,1},{1,0},{2,3},{3,2},{4,5},{5,4},{6,7},{7,6},{8,9},{9,8},{10,11... | collective-permute-start | bytes 86024 | tf_op jit(solution)/shard_map/ppermute | solution.py:332
  17.3 6.8 %all-to-all-start = ((bf16[8,32,1280]{2,1,0:T(8,128)(2,1)}), bf16[8,32,1280]{2,1,0:T(8,128)(2,1)S(1)}, u32[]{:S(2)}, u32[]{:S(2)}) async-start(bf16[8,32,1280]{2,1,0:T(8,128)(2,1)} %shard_map.129), calls=%async_computation | async-start | bytes 1310720 | tf_op jit(solution)/shard_map/all_to_all | solution.py:321
  24.1 4.4 %collective-permute-start.3 = (bf16[32,896]{1,0:T(8,128)(2,1)S(1)}, bf16[32,896]{1,0:T(8,128)(2,1)S(1)}, u32[]{:S(2)}, u32[]{:S(2)}) collective-permute-start(bf16[32,896]{1,0:T(8,128)(2,1)S(1)} %pad_maximum_fusion.5), channel_id=1, source_target_pairs={{0,48},{1,49},{2,50},{3,51},{4,52},{5,53},{6,54},{7,55},{8,56},{9,... | collective-permute-start | bytes 172040 | tf_op jit(solution)/shard_map/ppermute | solution.py:332
  28.5 2.4 collective-permute-start.2
  30.9 2.5 collective-permute-start.1
  33.4 1.8 collective-permute-done.2
  35.2 2.7 collective-permute-done.1
  38.6 6.3 %all-to-all-done.first_ref = bf16[8,32,1280]{2,1,0:T(8,128)(2,1)S(1)} async-done(((bf16[8,32,1280]{2,1,0:T(8,128)(2,1)}), bf16[8,32,1280]{2,1,0:T(8,128)(2,1)S(1)}, u32[]{:S(2)}, u32[]{:S(2)}) %all-to-all-start) | async-done | bytes 655392 | tf_op jit(solution)/shard_map/all_to_all | solution.py:321
  48.6 4.0 %all-to-all-start.2 = ((bf16[8,128,768]{2,1,0:T(8,128)(2,1)}), bf16[8,128,768]{2,1,0:T(8,128)(2,1)S(1)}, u32[]{:S(2)}, u32[]{:S(2)}) async-start(bf16[8,128,768]{2,1,0:T(8,128)(2,1)} %copy-done.5), calls=%async_computation.2 | async-start | bytes 3145728 | tf_op jit(solution)/shard_map/all_to_all | solution.py:321
  54.5 18.7 %all-to-all-done.2.recv_ref = bf16[8,128,768]{2,1,0:T(8,128)(2,1)S(1)} async-done(((bf16[8,128,768]{2,1,0:T(8,128)(2,1)}), bf16[8,128,768]{2,1,0:T(8,128)(2,1)S(1)}, u32[]{:S(2)}, u32[]{:S(2)}) %all-to-all-start.2) | async-done | bytes 1572896 | tf_op jit(solution)/shard_map/all_to_all | solution.py:321
  73.2 4.2 %all-to-all-start.1 = ((bf16[8,80,448]{2,1,0:T(8,128)(2,1)}), bf16[8,80,448]{2,1,0:T(8,128)(2,1)}, u32[]{:S(2)}, u32[]{:S(2)}) async-start(bf16[8,80,448]{2,1,0:T(8,128)(2,1)} %shard_map.131), calls=%async_computation.1 | async-start | bytes 1310720 | tf_op jit(solution)/shard_map/all_to_all | solution.py:321
  79.4 2.9 %shard_map.133 = (bf16[80,1024]{1,0:T(8,128)(2,1)S(1)}, bf16[240,1024]{1,0:T(8,128)(2,1)S(1)}, bf16[80,1024]{1,0:T(8,128)(2,1)S(1)}, bf16[240,1024]{1,0:T(8,128)(2,1)}, bf16[1024,448]{1,0:T(8,128)(2,1)S(1)}) custom-call(s32[5]{0:T(128)S(1)} %stack.27.who_ref.refs_0_, bf16[8,128,768]{2,1,0:T(8,128)(2,1)S(1)} %all-to-all-done.2.recv_ref, ...), custom_call_target="tpu_custom_call" | custom-call | tf_op jit(solution)/shard_map/pallas_call | solution.py:392
  84.0 3.6 %collective-permute-start.11 = (bf16[80,1024]{1,0:T(8,128)(2,1)S(1)}, bf16[80,1024]{1,0:T(8,128)(2,1)S(1)}, u32[]{:S(2)}, u32[]{:S(2)}) collective-permute-start(bf16[80,1024]{1,0:T(8,128)(2,1)S(1)} %get-tuple-element.47), channel_id=1, source_target_pairs={{0,64},{64,0},{128,192},{192,128},{256,320},{320,256},{384,448},{4... | collective-permute-start | bytes 491528 | tf_op jit(solution)/shard_map/ppermute | solution.py:285
  87.6 1.9 collective-permute-start.10
  89.6 9.8 %collective-permute-start.14 = (bf16[40,1024]{1,0:T(8,128)(2,1)S(1)}, bf16[40,1024]{1,0:T(8,128)(2,1)}, u32[]{:S(2)}, u32[]{:S(2)}) collective-permute-start(bf16[40,1024]{1,0:T(8,128)(2,1)S(1)} %get-tuple-element.74), channel_id=1, source_target_pairs={{0,384},{64,448},{128,0},{192,64},{256,128},{320,192},{384,256},{4... | collective-permute-start | bytes 245768 | tf_op jit(solution)/shard_map/ppermute | solution.py:289
  99.4 1.9 collective-permute-start.12
  101.4 1.5 copy-done.4
  102.9 3.3 %shard_map.132 = (bf16[640,448]{1,0:T(8,128)(2,1)S(1)}, bf16[80,2048]{1,0:T(8,128)(2,1)S(1)}, bf16[240,2048]{1,0:T(8,128)(2,1)S(1)}, bf16[80,2048]{1,0:T(8,128)(...) custom-call(s32[5]{0:T(128)S(1)} %stack.27.who_ref.refs_0_, ...), custom_call_target="tpu_custom_call" | custom-call | tf_op jit(solution)/shard_map/pallas_call | solution.py:400
  106.2 2.7 collective-permute-start.5
  108.9 1.9 collective-permute-start.4
  112.1 5.8 %collective-permute-start.8 = (bf16[40,2048]{1,0:T(8,128)(2,1)S(1)}, bf16[40,2048]{1,0:T(8,128)(2,1)S(1)}, u32[]{:S(2)}, u32[]{:S(2)}) collective-permute-start(bf16[40,2048]{1,0:T(8,128)(2,1)S(1)} %get-tuple-element.72), channel_id=1, source_target_pairs={{0,384},{64,448},{128,0},{192,64},{256,128},{320,192},{384,256},{4... | collective-permute-start | bytes 491528 | tf_op jit(solution)/shard_map/ppermute | solution.py:289
  117.8 1.9 collective-permute-start.6
  120.0 4.2 %collective-permute-done.8 = bf16[40,2048]{1,0:T(8,128)(2,1)S(1)} collective-permute-done((bf16[40,2048]{1,0:T(8,128)(2,1)S(1)}, bf16[40,2048]{1,0:T(8,128)(2,1)S(1)}, u32[]{:S(2)}, u32[]{:S(2)}) %collective-permute-start.8) | collective-permute-done | bytes 163872 | tf_op jit(solution)/shard_map/ppermute | solution.py:289
  124.3 6.0 %collective-permute-done.6 = bf16[40,2048]{1,0:T(8,128)(2,1)S(1)} collective-permute-done((bf16[40,2048]{1,0:T(8,128)(2,1)S(1)}, bf16[40,2048]{1,0:T(8,128)(2,1)S(1)}, u32[]{:S(2)}, u32[]{:S(2)}) %collective-permute-start.6) | collective-permute-done | bytes 163872 | tf_op jit(solution)/shard_map/ppermute | solution.py:289
  130.3 1.9 collective-permute-start.7
  132.3 5.5 %collective-permute-start.9 = (bf16[80,2048]{1,0:T(8,128)(2,1)S(1)}, bf16[80,2048]{1,0:T(8,128)(2,1)S(1)}, u32[]{:S(2)}, u32[]{:S(2)}) collective-permute-start(bf16[80,2048]{1,0:T(8,128)(2,1)S(1)} %pad_maximum_fusion.1), channel_id=1, source_target_pairs={{0,384},{64,448},{128,0},{192,64},{256,128},{320,192},{384,256},{4... | collective-permute-start | bytes 983048 | tf_op jit(solution)/shard_map/ppermute | solution.py:289
  137.8 1.9 collective-permute-start.13
  139.8 5.5 %collective-permute-start.15 = (bf16[80,1024]{1,0:T(8,128)(2,1)S(1)}, bf16[80,1024]{1,0:T(8,128)(2,1)S(1)}, u32[]{:S(2)}, u32[]{:S(2)}) collective-permute-start(bf16[80,1024]{1,0:T(8,128)(2,1)S(1)} %pad_maximum_fusion.4), channel_id=1, source_target_pairs={{0,384},{64,448},{128,0},{192,64},{256,128},{320,192},{384,256},{4... | collective-permute-start | bytes 491528 | tf_op jit(solution)/shard_map/ppermute | solution.py:289
  145.2 10.9 %collective-permute-done.13.refs_6_ = bf16[80,1024]{1,0:T(8,128)(2,1)S(1)} collective-permute-done((bf16[80,1024]{1,0:T(8,128)(2,1)S(1)}, bf16[80,1024]{1,0:T(8,128)(2,1)S(1)}, u32[]{:S(2)}, u32[]{:S(2)}) %collective-permute-start.13) | collective-permute-done | bytes 163872 | tf_op jit(solution)/shard_map/ppermute | solution.py:289
  157.6 4.7 %collective-permute-start.18 = (bf16[80,3072]{1,0:T(8,128)(2,1)S(1)}, bf16[80,3072]{1,0:T(8,128)(2,1)S(1)}, u32[]{:S(2)}, u32[]{:S(2)}) collective-permute-start(bf16[80,3072]{1,0:T(8,128)(2,1)S(1)} %shard_map.134.refs_2_), channel_id=1, source_target_pairs={{0,64},{64,0},{128,192},{192,128},{256,320},{320,256},{384,448},{4... | collective-permute-start | bytes 1474568 | tf_op jit(solution)/shard_map/ppermute | solution.py:285
  162.3 6.2 %collective-permute-start.17 = (bf16[80,3072]{1,0:T(8,128)(2,1)S(1)}, bf16[80,3072]{1,0:T(8,128)(2,1)S(1)}, u32[]{:S(2)}, u32[]{:S(2)}) collective-permute-start(bf16[80,3072]{1,0:T(8,128)(2,1)S(1)} %shard_map.134.refs_2_), channel_id=1, source_target_pairs={{0,384},{64,448},{128,0},{192,64},{256,128},{320,192},{384,256},{4... | collective-permute-start | bytes 1474568 | tf_op jit(solution)/shard_map/ppermute | solution.py:289
  168.5 1.9 collective-permute-start.16
  170.4 19.3 %collective-permute-done.17.refs_3_ = bf16[80,3072]{1,0:T(8,128)(2,1)S(1)} collective-permute-done((bf16[80,3072]{1,0:T(8,128)(2,1)S(1)}, bf16[80,3072]{1,0:T(8,128)(2,1)S(1)}, u32[]{:S(2)}, u32[]{:S(2)}) %collective-permute-start.17) | collective-permute-done | bytes 491552 | tf_op jit(solution)/shard_map/ppermute | solution.py:289
  189.7 4.1 %collective-permute-done.16.refs_4_ = bf16[80,3072]{1,0:T(8,128)(2,1)S(1)} collective-permute-done((bf16[80,3072]{1,0:T(8,128)(2,1)S(1)}, bf16[80,3072]{1,0:T(8,128)(2,1)S(1)}, u32[]{:S(2)}, u32[]{:S(2)}) %collective-permute-start.16) | collective-permute-done | bytes 491552 | tf_op jit(solution)/shard_map/ppermute | solution.py:289
  193.8 2.4 collective-permute-start.22
  196.3 1.9 collective-permute-start.21
  198.2 3.1 %collective-permute-start.20 = (bf16[40,3072]{1,0:T(8,128)(2,1)S(1)}, bf16[40,3072]{1,0:T(8,128)(2,1)S(1)}, u32[]{:S(2)}, u32[]{:S(2)}) collective-permute-start(bf16[40,3072]{1,0:T(8,128)(2,1)S(1)} %slice.101), channel_id=1, source_target_pairs={{0,384},{64,448},{128,0},{192,64},{256,128},{320,192},{384,256},{4... | collective-permute-start | bytes 737288 | tf_op jit(solution)/shard_map/ppermute | solution.py:289
  201.4 3.1 %collective-permute-start.19 = (bf16[40,3072]{1,0:T(8,128)(2,1)S(1)}, bf16[40,3072]{1,0:T(8,128)(2,1)S(1)}, u32[]{:S(2)}, u32[]{:S(2)}) collective-permute-start(bf16[40,3072]{1,0:T(8,128)(2,1)S(1)} %slice.100), channel_id=1, source_target_pairs={{0,128},{64,192},{128,256},{192,320},{256,384},{320,448},{384,0},{... | collective-permute-start | bytes 737288 | tf_op jit(solution)/shard_map/ppermute | solution.py:289
  204.4 4.5 %collective-permute-done.20 = bf16[40,3072]{1,0:T(8,128)(2,1)S(1)} collective-permute-done((bf16[40,3072]{1,0:T(8,128)(2,1)S(1)}, bf16[40,3072]{1,0:T(8,128)(2,1)S(1)}, u32[]{:S(2)}, u32[]{:S(2)}) %collective-permute-start.20) | collective-permute-done | bytes 245792 | tf_op jit(solution)/shard_map/ppermute | solution.py:289
  209.0 5.9 %collective-permute-done.19 = bf16[40,3072]{1,0:T(8,128)(2,1)S(1)} collective-permute-done((bf16[40,3072]{1,0:T(8,128)(2,1)S(1)}, bf16[40,3072]{1,0:T(8,128)(2,1)S(1)}, u32[]{:S(2)}, u32[]{:S(2)}) %collective-permute-start.19) | collective-permute-done | bytes 245792 | tf_op jit(solution)/shard_map/ppermute | solution.py:289
  214.9 3.4 %collective-permute-start.23 = (bf16[80,3072]{1,0:T(8,128)(2,1)S(1)}, bf16[80,3072]{1,0:T(8,128)(2,1)S(1)}, u32[]{:S(2)}, u32[]{:S(2)}) collective-permute-start(bf16[80,3072]{1,0:T(8,128)(2,1)S(1)} %constant_dynamic-update-slice_fusion.refs_1_), channel_id=1, source_target_pairs={{0,64},{64,0},{128,192},{192,128},{256,320},{320,256},{384,448},{4... | collective-permute-start | bytes 1474568 | tf_op jit(solution)/shard_map/ppermute | solution.py:285
  219.8 3.2 %shard_map.135 = (bf16[8,80,896]{2,1,0:T(8,128)(2,1)S(1)}, bf16[640,2048]{1,0:T(8,128)(2,1)S(1)}) custom-call(s32[5]{0:T(128)S(1)} %stack.27.who_ref.refs_0_, bf16[80,3072]{1,0:T(8,128)(2,1)S(1)} %constant_dynamic-update-slice_fusion.refs_1_, bf16[80,3072]{1,0:T(8,128)(2,1)S(1)} %shard_map.134.refs_2_, bf16[80,3072]{1,0:T(8,128)(2,1)S(1)} %collective-permute-done.17.refs_3_, ...), custom_call_target="tpu_custom_call" | custom-call | tf_op jit(solution)/shard_map/pallas_call | solution.py:417
  223.1 23.3 %all_to_all.33.recv_ref = bf16[8,80,896]{2,1,0:T(8,128)(2,1)S(1)} all-to-all(bf16[8,80,896]{2,1,0:T(8,128)(2,1)S(1)} %get-tuple-element.57), channel_id=1, replica_groups={{0,1,16,17,32,33,48,49},{2,3,18,19,34,35,50,51},{4,5,20,21,36,37,52,53}..., dimensions={0} | all-to-all | bytes 2293760 | tf_op jit(solution)/shard_map/all_to_all | solution.py:321
  246.4 1.7 shard_map.136
  248.1 3.5 %all-to-all-start.4 = ((bf16[8,32,896]{2,1,0:T(8,128)(2,1)}), bf16[8,32,896]{2,1,0:T(8,128)(2,1)S(1)}, u32[]{:S(2)}, u32[]{:S(2)}) async-start(bf16[8,32,896]{2,1,0:T(8,128)(2,1)} %bitcast.14), calls=%async_computation.4 | async-start | bytes 917504 | tf_op jit(solution)/shard_map/all_to_all | solution.py:321
  251.6 3.3 %fusion.1 = bf16[1,448,1024]{2,1,0:T(8,128)(2,1)} fusion(bf16[640,448]{1,0:T(8,128)(2,1)S(1)} %get-tuple-element.62, bf16[640,2048]{1,0:T(8,128)(2,1)} %copy-done.19), kind=kOutput, calls=%fused_computation.3 | convolution fusion | flops 587661312 | bytes 2801664 | tf_op jit(solution)/shard_map/dot_general | solution.py:22
  254.8 1.8 fusion
  256.7 9.4 %all-to-all-done.4.recv_ref = bf16[8,32,896]{2,1,0:T(8,128)(2,1)S(1)} async-done(((bf16[8,32,896]{2,1,0:T(8,128)(2,1)}), bf16[8,32,896]{2,1,0:T(8,128)(2,1)S(1)}, u32[]{:S(2)}, u32[]{:S(2)}) %all-to-all-start.4) | async-done | bytes 458784 | tf_op jit(solution)/shard_map/all_to_all | solution.py:321
  (90 shorter events, 20.0 us)
Async XLA Ops:
  7.2 37.7 %copy-start.16 = (f32[80,256]{1,0:T(8,128)S(1)}, f32[80,256]{1,0:T(8,128)}, u32[]{:S(2)}) copy-start(f32[80,256]{1,0:T(8,128)} %constant.50.clone.want_ref) | copy-start | bytes 245764
  8.0 9.1 %collective-permute-start = (bf16[16,896]{1,0:T(8,128)(2,1)S(1)}, bf16[16,896]{1,0:T(8,128)(2,1)S(1)}, u32[]{:S(2)}, u32[]{:S(2)}) collective-permute-start(bf16[16,896]{1,0:T(8,128)(2,1)S(1)} %pad_maximum_fusion.6), channel_id=1, source_target_pairs={{0,1},{1,0},{2,3},{3,2},{4,5},{5,4},{6,7},{7,6},{8,9},{9,8},{10,11... | collective-permute-start | bytes 86024 | tf_op jit(solution)/shard_map/ppermute | solution.py:332
  14.4 0.8 copy-start.17
  15.2 0.8 copy-start.18
  17.3 27.6 %all-to-all-start = ((bf16[8,32,1280]{2,1,0:T(8,128)(2,1)}), bf16[8,32,1280]{2,1,0:T(8,128)(2,1)S(1)}, u32[]{:S(2)}, u32[]{:S(2)}) async-start(bf16[8,32,1280]{2,1,0:T(8,128)(2,1)} %shard_map.129), calls=%async_computation | async-start | bytes 1310720 | tf_op jit(solution)/shard_map/all_to_all | solution.py:321
  24.1 9.3 %collective-permute-start.3 = (bf16[32,896]{1,0:T(8,128)(2,1)S(1)}, bf16[32,896]{1,0:T(8,128)(2,1)S(1)}, u32[]{:S(2)}, u32[]{:S(2)}) collective-permute-start(bf16[32,896]{1,0:T(8,128)(2,1)S(1)} %pad_maximum_fusion.5), channel_id=1, source_target_pairs={{0,48},{1,49},{2,50},{3,51},{4,52},{5,53},{6,54},{7,55},{8,56},{9,... | collective-permute-start | bytes 172040 | tf_op jit(solution)/shard_map/ppermute | solution.py:332
  28.5 6.7 %collective-permute-start.2 = (bf16[32,896]{1,0:T(8,128)(2,1)S(1)}, bf16[32,896]{1,0:T(8,128)(2,1)S(1)}, u32[]{:S(2)}, u32[]{:S(2)}) collective-permute-start(bf16[32,896]{1,0:T(8,128)(2,1)S(1)} %pad_maximum_fusion.5), channel_id=1, source_target_pairs={{0,32},{1,33},{2,34},{3,35},{4,36},{5,37},{6,38},{7,39},{8,40},{9,... | collective-permute-start | bytes 172040 | tf_op jit(solution)/shard_map/ppermute | solution.py:332
  30.9 7.0 %collective-permute-start.1 = (bf16[32,896]{1,0:T(8,128)(2,1)S(1)}, bf16[32,896]{1,0:T(8,128)(2,1)S(1)}, u32[]{:S(2)}, u32[]{:S(2)}) collective-permute-start(bf16[32,896]{1,0:T(8,128)(2,1)S(1)} %pad_maximum_fusion.5), channel_id=1, source_target_pairs={{0,16},{1,17},{2,18},{3,19},{4,20},{5,21},{6,22},{7,23},{8,24},{9,... | collective-permute-start | bytes 172040 | tf_op jit(solution)/shard_map/ppermute | solution.py:332
  45.9 1.2 copy-start.5
  48.6 4.8 %copy-start.8 = (bf16[640,256]{1,0:T(8,128)(2,1)}, bf16[640,256]{1,0:T(8,128)(2,1)S(1)}, u32[]{:S(2)}) copy-start(bf16[640,256]{1,0:T(8,128)(2,1)S(1)} %get-tuple-element.37.pick_ref) | copy-start | bytes 983044
  48.6 24.7 %all-to-all-start.2 = ((bf16[8,128,768]{2,1,0:T(8,128)(2,1)}), bf16[8,128,768]{2,1,0:T(8,128)(2,1)S(1)}, u32[]{:S(2)}, u32[]{:S(2)}) async-start(bf16[8,128,768]{2,1,0:T(8,128)(2,1)} %copy-done.5), calls=%async_computation.2 | async-start | bytes 3145728 | tf_op jit(solution)/shard_map/all_to_all | solution.py:321
  52.6 48.7 %all-gather.2.cloned.1.call-start = ((), (), s32[]{:S(2)}) async-start(), calls=%async_computation.5 | async-start | bytes 2064384 | tf_op jit(solution)/shard_map/all_gather | solution.py:363
  73.2 28.1 %all-to-all-start.1 = ((bf16[8,80,448]{2,1,0:T(8,128)(2,1)}), bf16[8,80,448]{2,1,0:T(8,128)(2,1)}, u32[]{:S(2)}, u32[]{:S(2)}) async-start(bf16[8,80,448]{2,1,0:T(8,128)(2,1)} %shard_map.131), calls=%async_computation.1 | async-start | bytes 1310720 | tf_op jit(solution)/shard_map/all_to_all | solution.py:321
  78.2 1.2 copy-start.2
  79.4 21.9 %copy-start = (bf16[1,448,1024]{2,1,0:T(8,128)(2,1)S(1)}, bf16[1,448,1024]{2,1,0:T(8,128)(2,1)}, u32[]{:S(2)}) copy-start(bf16[1,448,1024]{2,1,0:T(8,128)(2,1)} %param.15) | copy-start | bytes 2752516
  79.4 22.0 %copy-start.1 = (bf16[1,448,1024]{2,1,0:T(8,128)(2,1)S(1)}, bf16[1,448,1024]{2,1,0:T(8,128)(2,1)}, u32[]{:S(2)}) copy-start(bf16[1,448,1024]{2,1,0:T(8,128)(2,1)} %param.16) | copy-start | bytes 2752516
  82.3 0.8 copy-start.6
  83.0 1.0 copy-start.10
  84.0 5.5 %collective-permute-start.11 = (bf16[80,1024]{1,0:T(8,128)(2,1)S(1)}, bf16[80,1024]{1,0:T(8,128)(2,1)S(1)}, u32[]{:S(2)}, u32[]{:S(2)}) collective-permute-start(bf16[80,1024]{1,0:T(8,128)(2,1)S(1)} %get-tuple-element.47), channel_id=1, source_target_pairs={{0,64},{64,0},{128,192},{192,128},{256,320},{320,256},{384,448},{4... | collective-permute-start | bytes 491528 | tf_op jit(solution)/shard_map/ppermute | solution.py:285
  87.6 23.2 %collective-permute-start.10 = (bf16[240,1024]{1,0:T(8,128)(2,1)}, bf16[240,1024]{1,0:T(8,128)(2,1)S(1)}, u32[]{:S(2)}, u32[]{:S(2)}) collective-permute-start(bf16[240,1024]{1,0:T(8,128)(2,1)} %get-tuple-element.45), channel_id=1, source_target_pairs={{0,64},{64,0},{128,192},{192,128},{256,320},{320,256},{384,448},{4... | collective-permute-start | bytes 1474568 | tf_op jit(solution)/shard_map/ppermute | solution.py:285
  89.6 21.4 %collective-permute-start.14 = (bf16[40,1024]{1,0:T(8,128)(2,1)S(1)}, bf16[40,1024]{1,0:T(8,128)(2,1)}, u32[]{:S(2)}, u32[]{:S(2)}) collective-permute-start(bf16[40,1024]{1,0:T(8,128)(2,1)S(1)} %get-tuple-element.74), channel_id=1, source_target_pairs={{0,384},{64,448},{128,0},{192,64},{256,128},{320,192},{384,256},{4... | collective-permute-start | bytes 245768 | tf_op jit(solution)/shard_map/ppermute | solution.py:289
  99.4 11.6 %collective-permute-start.12 = (bf16[40,1024]{1,0:T(8,128)(2,1)S(1)}, bf16[40,1024]{1,0:T(8,128)(2,1)}, u32[]{:S(2)}, u32[]{:S(2)}) collective-permute-start(bf16[40,1024]{1,0:T(8,128)(2,1)S(1)} %get-tuple-element.75), channel_id=1, source_target_pairs={{0,128},{64,192},{128,256},{192,320},{256,384},{320,448},{384,0},{... | collective-permute-start | bytes 245768 | tf_op jit(solution)/shard_map/ppermute | solution.py:289
  101.4 1.5 copy-start.4
  102.9 8.0 %copy-start.7 = (bf16[240,1024]{1,0:T(8,128)(2,1)S(1)}, bf16[240,1024]{1,0:T(8,128)(2,1)}, u32[]{:S(2)}) copy-start(bf16[240,1024]{1,0:T(8,128)(2,1)} %copy-done.6) | copy-start | bytes 1474564
  106.2 5.8 %collective-permute-start.5 = (bf16[80,2048]{1,0:T(8,128)(2,1)S(1)}, bf16[80,2048]{1,0:T(8,128)(2,1)S(1)}, u32[]{:S(2)}, u32[]{:S(2)}) collective-permute-start(bf16[80,2048]{1,0:T(8,128)(2,1)S(1)} %get-tuple-element.42), channel_id=1, source_target_pairs={{0,64},{64,0},{128,192},{192,128},{256,320},{320,256},{384,448},{4... | collective-permute-start | bytes 983048 | tf_op jit(solution)/shard_map/ppermute | solution.py:285
  108.9 10.9 %collective-permute-start.4 = (bf16[240,2048]{1,0:T(8,128)(2,1)S(1)}, bf16[240,2048]{1,0:T(8,128)(2,1)S(1)}, u32[]{:S(2)}, u32[]{:S(2)}) collective-permute-start(bf16[240,2048]{1,0:T(8,128)(2,1)S(1)} %get-tuple-element.40), channel_id=1, source_target_pairs={{0,64},{64,0},{128,192},{192,128},{256,320},{320,256},{384,448},{4... | collective-permute-start | bytes 2949128 | tf_op jit(solution)/shard_map/ppermute | solution.py:285
  112.1 12.2 %collective-permute-start.8 = (bf16[40,2048]{1,0:T(8,128)(2,1)S(1)}, bf16[40,2048]{1,0:T(8,128)(2,1)S(1)}, u32[]{:S(2)}, u32[]{:S(2)}) collective-permute-start(bf16[40,2048]{1,0:T(8,128)(2,1)S(1)} %get-tuple-element.72), channel_id=1, source_target_pairs={{0,384},{64,448},{128,0},{192,64},{256,128},{320,192},{384,256},{4... | collective-permute-start | bytes 491528 | tf_op jit(solution)/shard_map/ppermute | solution.py:289
  117.8 12.4 %collective-permute-start.6 = (bf16[40,2048]{1,0:T(8,128)(2,1)S(1)}, bf16[40,2048]{1,0:T(8,128)(2,1)S(1)}, u32[]{:S(2)}, u32[]{:S(2)}) collective-permute-start(bf16[40,2048]{1,0:T(8,128)(2,1)S(1)} %get-tuple-element.73), channel_id=1, source_target_pairs={{0,128},{64,192},{128,256},{192,320},{256,384},{320,448},{384,0},{... | collective-permute-start | bytes 491528 | tf_op jit(solution)/shard_map/ppermute | solution.py:289
  130.3 26.8 %collective-permute-start.7 = (bf16[80,2048]{1,0:T(8,128)(2,1)S(1)}, bf16[80,2048]{1,0:T(8,128)(2,1)S(1)}, u32[]{:S(2)}, u32[]{:S(2)}) collective-permute-start(bf16[80,2048]{1,0:T(8,128)(2,1)S(1)} %pad_maximum_fusion), channel_id=1, source_target_pairs={{0,128},{64,192},{128,256},{192,320},{256,384},{320,448},{384,0},{... | collective-permute-start | bytes 983048 | tf_op jit(solution)/shard_map/ppermute | solution.py:289
  132.3 24.8 %collective-permute-start.9 = (bf16[80,2048]{1,0:T(8,128)(2,1)S(1)}, bf16[80,2048]{1,0:T(8,128)(2,1)S(1)}, u32[]{:S(2)}, u32[]{:S(2)}) collective-permute-start(bf16[80,2048]{1,0:T(8,128)(2,1)S(1)} %pad_maximum_fusion.1), channel_id=1, source_target_pairs={{0,384},{64,448},{128,0},{192,64},{256,128},{320,192},{384,256},{4... | collective-permute-start | bytes 983048 | tf_op jit(solution)/shard_map/ppermute | solution.py:289
  137.8 18.3 %collective-permute-start.13 = (bf16[80,1024]{1,0:T(8,128)(2,1)S(1)}, bf16[80,1024]{1,0:T(8,128)(2,1)S(1)}, u32[]{:S(2)}, u32[]{:S(2)}) collective-permute-start(bf16[80,1024]{1,0:T(8,128)(2,1)S(1)} %pad_maximum_fusion.3), channel_id=1, source_target_pairs={{0,128},{64,192},{128,256},{192,320},{256,384},{320,448},{384,0},{... | collective-permute-start | bytes 491528 | tf_op jit(solution)/shard_map/ppermute | solution.py:289
  139.8 17.4 %collective-permute-start.15 = (bf16[80,1024]{1,0:T(8,128)(2,1)S(1)}, bf16[80,1024]{1,0:T(8,128)(2,1)S(1)}, u32[]{:S(2)}, u32[]{:S(2)}) collective-permute-start(bf16[80,1024]{1,0:T(8,128)(2,1)S(1)} %pad_maximum_fusion.4), channel_id=1, source_target_pairs={{0,384},{64,448},{128,0},{192,64},{256,128},{320,192},{384,256},{4... | collective-permute-start | bytes 491528 | tf_op jit(solution)/shard_map/ppermute | solution.py:289
  157.6 62.3 %copy-start.3 = (bf16[1,1024,448]{1,2,0:T(8,128)(2,1)S(1)}, bf16[1,1024,448]{1,2,0:T(8,128)(2,1)}, u32[]{:S(2)}) copy-start(bf16[1,1024,448]{1,2,0:T(8,128)(2,1)} %param.17) | copy-start | bytes 2752516
  157.6 62.3 %copy-start.11 = (bf16[1024,448]{1,0:T(8,128)(2,1)S(1)}, bf16[1024,448]{1,0:T(8,128)(2,1)}, u32[]{:S(2)}) copy-start(bf16[1024,448]{1,0:T(8,128)(2,1)} %copy-done.10) | copy-start | bytes 2752516
  157.6 12.9 %collective-permute-start.18 = (bf16[80,3072]{1,0:T(8,128)(2,1)S(1)}, bf16[80,3072]{1,0:T(8,128)(2,1)S(1)}, u32[]{:S(2)}, u32[]{:S(2)}) collective-permute-start(bf16[80,3072]{1,0:T(8,128)(2,1)S(1)} %shard_map.134.refs_2_), channel_id=1, source_target_pairs={{0,64},{64,0},{128,192},{192,128},{256,320},{320,256},{384,448},{4... | collective-permute-start | bytes 1474568 | tf_op jit(solution)/shard_map/ppermute | solution.py:285
  162.3 27.4 %collective-permute-start.17 = (bf16[80,3072]{1,0:T(8,128)(2,1)S(1)}, bf16[80,3072]{1,0:T(8,128)(2,1)S(1)}, u32[]{:S(2)}, u32[]{:S(2)}) collective-permute-start(bf16[80,3072]{1,0:T(8,128)(2,1)S(1)} %shard_map.134.refs_2_), channel_id=1, source_target_pairs={{0,384},{64,448},{128,0},{192,64},{256,128},{320,192},{384,256},{4... | collective-permute-start | bytes 1474568 | tf_op jit(solution)/shard_map/ppermute | solution.py:289
  168.5 25.3 %collective-permute-start.16 = (bf16[80,3072]{1,0:T(8,128)(2,1)S(1)}, bf16[80,3072]{1,0:T(8,128)(2,1)S(1)}, u32[]{:S(2)}, u32[]{:S(2)}) collective-permute-start(bf16[80,3072]{1,0:T(8,128)(2,1)S(1)} %shard_map.134.refs_2_), channel_id=1, source_target_pairs={{0,128},{64,192},{128,256},{192,320},{256,384},{320,448},{384,0},{... | collective-permute-start | bytes 1474568 | tf_op jit(solution)/shard_map/ppermute | solution.py:289
  193.8 21.0 %collective-permute-start.22 = (bf16[80,3072]{1,0:T(8,128)(2,1)S(1)}, bf16[80,3072]{1,0:T(8,128)(2,1)S(1)}, u32[]{:S(2)}, u32[]{:S(2)}) collective-permute-start(bf16[80,3072]{1,0:T(8,128)(2,1)S(1)} %collective-permute-done.16.refs_4_), channel_id=1, source_target_pairs={{0,64},{64,0},{128,192},{192,128},{256,320},{320,256},{384,448},{4... | collective-permute-start | bytes 1474568 | tf_op jit(solution)/shard_map/ppermute | solution.py:285
  196.3 18.6 %collective-permute-start.21 = (bf16[80,3072]{1,0:T(8,128)(2,1)S(1)}, bf16[80,3072]{1,0:T(8,128)(2,1)S(1)}, u32[]{:S(2)}, u32[]{:S(2)}) collective-permute-start(bf16[80,3072]{1,0:T(8,128)(2,1)S(1)} %collective-permute-done.17.refs_3_), channel_id=1, source_target_pairs={{0,64},{64,0},{128,192},{192,128},{256,320},{320,256},{384,448},{4... | collective-permute-start | bytes 1474568 | tf_op jit(solution)/shard_map/ppermute | solution.py:285
  198.2 10.7 %collective-permute-start.20 = (bf16[40,3072]{1,0:T(8,128)(2,1)S(1)}, bf16[40,3072]{1,0:T(8,128)(2,1)S(1)}, u32[]{:S(2)}, u32[]{:S(2)}) collective-permute-start(bf16[40,3072]{1,0:T(8,128)(2,1)S(1)} %slice.101), channel_id=1, source_target_pairs={{0,384},{64,448},{128,0},{192,64},{256,128},{320,192},{384,256},{4... | collective-permute-start | bytes 737288 | tf_op jit(solution)/shard_map/ppermute | solution.py:289
  201.4 13.5 %collective-permute-start.19 = (bf16[40,3072]{1,0:T(8,128)(2,1)S(1)}, bf16[40,3072]{1,0:T(8,128)(2,1)S(1)}, u32[]{:S(2)}, u32[]{:S(2)}) collective-permute-start(bf16[40,3072]{1,0:T(8,128)(2,1)S(1)} %slice.100), channel_id=1, source_target_pairs={{0,128},{64,192},{128,256},{192,320},{256,384},{320,448},{384,0},{... | collective-permute-start | bytes 737288 | tf_op jit(solution)/shard_map/ppermute | solution.py:289
  214.9 4.9 %collective-permute-start.23 = (bf16[80,3072]{1,0:T(8,128)(2,1)S(1)}, bf16[80,3072]{1,0:T(8,128)(2,1)S(1)}, u32[]{:S(2)}, u32[]{:S(2)}) collective-permute-start(bf16[80,3072]{1,0:T(8,128)(2,1)S(1)} %constant_dynamic-update-slice_fusion.refs_1_), channel_id=1, source_target_pairs={{0,64},{64,0},{128,192},{192,128},{256,320},{320,256},{384,448},{4... | collective-permute-start | bytes 1474568 | tf_op jit(solution)/shard_map/ppermute | solution.py:285
  223.1 25.0 %copy-start.19 = (bf16[640,2048]{1,0:T(8,128)(2,1)}, bf16[640,2048]{1,0:T(8,128)(2,1)S(1)}, u32[]{:S(2)}) copy-start(bf16[640,2048]{1,0:T(8,128)(2,1)S(1)} %get-tuple-element.63) | copy-start | bytes 7864324
  223.1 23.3 %copy-start.9 = (bf16[640,256]{1,0:T(8,128)(2,1)S(1)}, bf16[640,256]{1,0:T(8,128)(2,1)}, u32[]{:S(2)}) copy-start(bf16[640,256]{1,0:T(8,128)(2,1)} %copy-done.8) | copy-start | bytes 983044
  223.1 23.3 %copy-start.13 = (bf16[640,256]{1,0:T(8,128)(2,1)S(1)}, bf16[640,256]{1,0:T(8,128)(2,1)}, u32[]{:S(2)}) copy-start(bf16[640,256]{1,0:T(8,128)(2,1)} %copy-done.12) | copy-start | bytes 983044
  223.1 23.3 %copy-start.15 = (bf16[640,256]{1,0:T(8,128)(2,1)S(1)}, bf16[640,256]{1,0:T(8,128)(2,1)}, u32[]{:S(2)}) copy-start(bf16[640,256]{1,0:T(8,128)(2,1)} %copy-done.14) | copy-start | bytes 983044
  248.1 18.0 %all-to-all-start.4 = ((bf16[8,32,896]{2,1,0:T(8,128)(2,1)}), bf16[8,32,896]{2,1,0:T(8,128)(2,1)S(1)}, u32[]{:S(2)}, u32[]{:S(2)}) async-start(bf16[8,32,896]{2,1,0:T(8,128)(2,1)} %bitcast.14), calls=%async_computation.4 | async-start | bytes 917504 | tf_op jit(solution)/shard_map/all_to_all | solution.py:321
  251.5 3.3 %copy-start.20 = (bf16[640,2048]{1,0:T(8,128)(2,1)S(1)}, bf16[640,2048]{1,0:T(8,128)(2,1)}, u32[]{:S(2)}) copy-start(bf16[640,2048]{1,0:T(8,128)(2,1)} %copy-done.19) | copy-start | bytes 7864324
  (2 other events, 1.5 us)
Sparse Core Ops, SparseCore 0:
  55.5 37.9 all-gather.1

commit v4 on v2

--- a/solution.py
+++ b/solution.py
@@ -14,7 +14,7 @@
 NN = (((1,), (0,)), ((), ()))
 NT = (((1,), (1,)), ((), ()))
 TN = (((0,), (0,)), ((), ()))
-LANES = 1152
+LANES = 1024
 TILE = 256
 
 
@@ -38,13 +38,13 @@
     )
 
 
-def pack_kernel(grid, ids_ref, weight_ref, tok_ref, cot_ref, saved_ref, out_ref):
+def pack_kernel(grid, ids_ref, weight_ref, tok_ref, cot_ref, out_ref):
     nx, ny, nz = grid
     nxz, ranks = nx * nz, nx * ny * nz
     tok, topk = ids_ref.shape
     ids = ids_ref[...]
     x, y, z = lax.div(ids, ny * nz), lax.rem(lax.div(ids, nz), ny), lax.rem(ids, nz)
-    column = y * nxz + x * nz + z
+    column = (x * nz + z) * ny + y
     lane = lax.broadcasted_iota(jnp.int32, (tok, ranks), 1)
     member = jnp.zeros((tok, ranks), F32)
     share = jnp.zeros((tok, ranks), F32)
@@ -58,67 +58,42 @@
     place = jnp.where(member > 0.5, before - 1.0, -1.0).astype(BF)
     hi = share.astype(BF)
     lo = (share - hi.astype(F32)).astype(BF)
-    source = lax.broadcasted_iota(jnp.int32, (ranks, ny * 128), 0)
-    target = lax.broadcasted_iota(jnp.int32, (ranks, ny * 128), 1)
-    base = lax.div(source, nxz) * 128 + lax.rem(source, nxz) + 64
-    meta = jnp.zeros((tok, ny * 128), F32)
+    source = lax.broadcasted_iota(jnp.int32, (ranks, nxz * 128), 0)
+    target = lax.broadcasted_iota(jnp.int32, (ranks, nxz * 128), 1)
+    base = lax.div(source, ny) * 128 + lax.rem(source, ny) + 64
+    meta = jnp.zeros((tok, nxz * 128), F32)
     for k, part in enumerate((place, hi, lo)):
-        meta = meta + dot(part, jnp.where(target == base + k * nxz, 1.0, 0.0).astype(BF))
+        meta = meta + dot(part, jnp.where(target == base + k * ny, 1.0, 0.0).astype(BF))
     feat = tok_ref.shape[1]
     assert feat == 448
     last = jnp.concatenate([tok_ref[:, 384:448].astype(F32), jnp.zeros((tok, 64), F32)], axis=1)
-    n = saved_ref.shape[1]
-    for i in range(ny):
-        out_ref[i, 0:tok, 0:384] = tok_ref[:, 0:384]
-        out_ref[i, 0:tok, 384:512] = (meta[:, i * 128 : (i + 1) * 128] + last).astype(BF)
-        out_ref[i, 0:tok, 512 : 512 + feat] = cot_ref[...]
-        out_ref[i, tok : tok + n, 0:feat] = saved_ref[0]
-        out_ref[i, tok : tok + n, 512 : 512 + feat] = saved_ref[1]
-        for k in range(3):
-            out_ref[i, k * n : (k + 1) * n, 1024:1152] = saved_ref[2, :, k * 128 : (k + 1) * 128]
-        out_ref[i, 2 * n : 3 * n, 960:1024] = saved_ref[2, :, 384:448]
+    for i in range(nxz):
+        out_ref[i, :, 0:384] = tok_ref[:, 0:384]
+        out_ref[i, :, 384:512] = (meta[:, i * 128 : (i + 1) * 128] + last).astype(BF)
+        out_ref[i, :, 512 : 512 + feat] = cot_ref[...]
 
 
 def select_kernel(first_ref, want_ref, out_ref, pick_ref, hi_ref, lo_ref):
-    nxz, _, width = out_ref.shape
+    ny, rows, width = out_ref.shape
     feat = width // 2
-    ny, rows, _ = first_ref.shape
-    n = 16
-    tok = rows - n
-    seen = ny * tok
-    out_rows = want_ref.shape[0]
-    tokens = first_ref[:, 0:tok, 0:feat].reshape(seen, feat)
-    cots = first_ref[:, 0:tok, 512 : 512 + feat].reshape(seen, feat)
-    meta = jnp.transpose(first_ref[:, 0:tok, 384:512].reshape(seen, 128).astype(F32))
+    nxz, tok, _ = first_ref.shape
+    seen = nxz * tok
+    tokens = first_ref[:, :, 0:feat].reshape(seen, feat)
+    cots = first_ref[:, :, 512 : 512 + feat].reshape(seen, feat)
+    meta = jnp.transpose(first_ref[:, :, 384:512].reshape(seen, 128).astype(F32))
     want = want_ref[...]
     both = jnp.concatenate([cots, cots], axis=0)
-    gate = first_ref[:, tok : tok + n, 0:feat].reshape(ny * n, feat)
-    up = first_ref[:, tok : tok + n, 512 : 512 + feat].reshape(ny * n, feat)
-    half = ny // 2
-    for q in range(nxz):
+    for q in range(ny):
         hit = meta[64 + q : 65 + q] == want
         pick = jnp.where(hit, 1.0, 0.0).astype(BF)
-        hi = jnp.where(hit, meta[64 + nxz + q : 65 + nxz + q], 0.0).astype(BF)
-        lo = jnp.where(hit, meta[64 + 2 * nxz + q : 65 + 2 * nxz + q], 0.0).astype(BF)
-        span = pl.ds(q * out_rows, out_rows)
+        hi = jnp.where(hit, meta[64 + ny + q : 65 + ny + q], 0.0).astype(BF)
+        lo = jnp.where(hit, meta[64 + 2 * ny + q : 65 + 2 * ny + q], 0.0).astype(BF)
+        span = pl.ds(q * rows, rows)
         pick_ref[span, :] = pick
         hi_ref[span, :] = hi
         lo_ref[span, :] = lo
-        out_ref[q, 0:out_rows, 0:feat] = dot(pick, tokens).astype(BF)
-        weighted = dot(jnp.concatenate([hi, lo], axis=1), both)
-        out_ref[q, 0:out_rows, feat:width] = weighted.astype(BF)
-        r = out_rows
-        out_ref[q, r : r + ny * n, 0:feat] = gate
-        out_ref[q, r : r + ny * n, feat:width] = up
-        r += ny * n
-        for k in range(3):
-            piece = first_ref[:, k * n : (k + 1) * n, 1024:1152]
-            at = k * 128
-            out_ref[q, r : r + half * n, at : at + 128] = piece[:half].reshape(half * n, 128)
-            out_ref[q, r : r + half * n, feat + at : feat + at + 128] = piece[half:].reshape(half * n, 128)
-        piece = first_ref[:, 2 * n : 3 * n, 960:1024]
-        out_ref[q, r : r + half * n, 384:448] = piece[:half].reshape(half * n, 64)
-        out_ref[q, r : r + half * n, feat + 384 : feat + 448] = piece[half:].reshape(half * n, 64)
+        out_ref[q, :, 0:feat] = dot(pick, tokens).astype(BF)
+        out_ref[q, :, feat:width] = dot(jnp.concatenate([hi, lo], axis=1), both).astype(BF)
 
 
 def chunk_at(h, c, p):
@@ -126,19 +101,25 @@
     return half * 4 + lax.rem(h + (2, 0, 1, 3)[p % 4], 4)
 
 
+def block_of(ref, g, chunk):
+    per = ref.shape[1] // chunk
+    if per == 1:
+        return ref.at[g]
+    return ref.at[lax.div(g, per), pl.ds(lax.rem(g, per) * chunk, chunk)]
+
+
 def products_kernel(
-    grid, who_ref, recv_ref, gate_ref, up_ref, down_ref,
+    grid, who_ref, recv_ref, s0, s1, s2a, s2b, s3, gate_ref, up_ref, down_ref,
     rows_ref, far_ref, rest_ref, far_out_ref, rest_out_ref, restored_ref, grads_ref,
 ):
     nx, ny, nz = grid
     feat, ff = gate_ref.shape
     chunk = far_ref.shape[0]
-    n = 16
-    target, h, c = who_ref[0], who_ref[1], who_ref[2]
+    target, h, c, my_x, my_z = (who_ref[i] for i in range(5))
     for p in range(8):
-        g = chunk_at(h, c, p)
-        rows_ref[p * chunk : (p + 1) * chunk, :] = recv_ref[g, 0:chunk, 0:feat]
-        grads_ref[p * chunk : (p + 1) * chunk, :] = recv_ref[g, 0:chunk, feat : 2 * feat]
+        block = block_of(recv_ref, chunk_at(h, c, p), chunk)
+        rows_ref[p * chunk : (p + 1) * chunk, :] = block[:, 0:feat]
+        grads_ref[p * chunk : (p + 1) * chunk, :] = block[:, feat : 2 * feat]
 
     def store(k, j, value):
         at = pl.ds(pl.multiple_of(k * ff + j * TILE, TILE), TILE)
@@ -161,17 +142,19 @@
 
     @pl.when(target == 1)
     def _():
-        for x in range(nx):
-            for z in range(nz):
-                q = x * nz + z
+        n = s0.shape[0] // (nz * ny)
+        half = ny * n
+        for k in range(nx):
+            for other in range(nz):
+                x = lax.rem(my_x - k + nx, nx)
+                z = 1 - my_z if other else my_z
+                source = ((s0, s0), (s1, s1), (s2a, s2b), (s3, s3))[k][other]
+                start = 0 if k == 2 else other * half
                 for y in range(ny):
-                    to = pl.ds(((x * ny + y) * nz + z) * n, n)
-                    r = chunk + y * n
-                    restored_ref[0, to, :] = recv_ref[q, r : r + n, 0:feat]
-                    restored_ref[1, to, :] = recv_ref[q, r : r + n, feat : 2 * feat]
-                    r = chunk + ny * n + (y % (ny // 2)) * n
-                    s = 0 if y < ny // 2 else feat
-                    restored_ref[2, to, :] = recv_ref[q, r : r + n, s : s + feat]
+                    to = pl.ds(pl.multiple_of(((x * ny + y) * nz + z) * n, n), n)
+                    r = start + y * n
+                    for m in range(3):
+                        restored_ref[m, to, :] = source[r : r + n, m * feat : (m + 1) * feat]
 
         @pl.loop(0, tiles)
         def _(j):
@@ -208,7 +191,7 @@
     who_ref, parts = refs[0], refs[1:9]
     gate_ref, up_ref, down_ref, restored_ref, out_ref, grads_ref, hidden_ref, y_ref, dx_ref = refs[9:]
     feat, ff = gate_ref.shape
-    chunk = out_ref.shape[1]
+    chunk = parts[0].shape[0]
     target, h, c = who_ref[0], who_ref[1], who_ref[2]
     for p in range(8):
         span = slice(p * chunk, (p + 1) * chunk)
@@ -230,16 +213,16 @@
         ).astype(BF)
 
     for p in range(8):
-        g = chunk_at(h, c, p)
+        block = block_of(out_ref, chunk_at(h, c, p), chunk)
         span = slice(p * chunk, (p + 1) * chunk)
-        out_ref[g, :, 0:feat] = y_ref[span, :]
-        out_ref[g, :, feat : 2 * feat] = dx_ref[span, :]
+        block[:, 0:feat] = y_ref[span, :]
+        block[:, feat : 2 * feat] = dx_ref[span, :]
 
 
 def combine_kernel(recv_ref, pick_ref, hi_ref, lo_ref, out_ref):
-    nxz, out_rows, width = recv_ref.shape
+    blocks, out_rows, width = recv_ref.shape
     feat = width // 2
-    rows = recv_ref[...].reshape(nxz * out_rows, width)
+    rows = recv_ref[...].reshape(blocks * out_rows, width)
     y = dot(hi_ref[...], rows[:, 0:feat], TN) + dot(lo_ref[...], rows[:, 0:feat], TN)
     out_ref[:, 0:feat] = y.astype(BF)
     out_ref[:, feat:width] = dot(pick_ref[...], rows[:, feat:width], TN).astype(BF)
@@ -292,33 +275,54 @@
         flat = lax.all_to_all(flat, "expert", 0, 0, axis_index_groups=groups, tiled=True)
         return flat.reshape(v.shape)
 
+    def rank(x, y, z):
+        return ((x % nx) * ny + y) * nz + z % nz
+
+    def step(v, dx, dz):
+        pairs = [
+            (rank(x, y, z), rank(x + dx, y, z + dz))
+            for x in range(nx) for y in range(ny) for z in range(nz)
+        ]
+        return lax.ppermute(v, "expert", pairs)
+
     tok, topk = expert_ids.shape
     feat = tokens.shape[1]
     ff = gate_weight.shape[2]
     ffr = ff // ranks
     capacity = min(tok, 5 * tok * topk // (2 * ranks))
     chunk = ranks * capacity // 8
-    me = lax.axis_index("dp")
+    me, expert = lax.axis_index("dp"), lax.axis_index("expert")
     who = jnp.stack(
-        [(lax.axis_index("expert") == replaced[0]).astype(jnp.int32), me // 2, me % 2]
+        [
+            (expert == replaced[0]).astype(jnp.int32),
+            me // 2,
+            me % 2,
+            expert // (ny * nz),
+            expert % nz,
+        ]
     ).astype(jnp.int32)
 
-    saved = jnp.transpose(backup, (0, 2, 1))
-    (first,) = call(
-        functools.partial(pack_kernel, grid), [(ny, tok + ffr, LANES)], operands=5
-    )(expert_ids, route_weight, tokens, cotangent, saved)
-    first = exchange(first, along_y)
-
-    out_rows, seen = ny * capacity, ny * tok
+    saved = jnp.transpose(backup, (2, 0, 1)).reshape(ffr, 3 * feat)
+    saved = exchange(jnp.broadcast_to(saved, (ny, ffr, 3 * feat)), along_y)
+    saved = saved.reshape(ny * ffr, 3 * feat)
+    both_z = jnp.concatenate([saved, step(saved, 0, 1)], axis=0)
+
+    (first,) = call(functools.partial(pack_kernel, grid), [(nxz, tok, LANES)], operands=4)(
+        expert_ids, route_weight, tokens, cotangent
+    )
+    first, saved = lax.optimization_barrier((first, saved))
+    first = exchange(first, along_xz)
+
+    out_rows, seen = nxz * capacity, nxz * tok
     row, col = np.arange(out_rows)[:, None], np.arange(seen)[None, :]
     want = np.where(row // capacity == col // tok, row % capacity, -2).astype(np.float32)
-    table = (nxz * out_rows, seen)
+    table = (ny * out_rows, seen)
     send, pick, pick_hi, pick_lo = call(
-        select_kernel,
-        [(nxz, out_rows + ny * ffr * 3 // 2, 2 * feat), table, table, table],
-        operands=2,
+        select_kernel, [(ny, out_rows, 2 * feat), table, table, table], operands=2
     )(first, want)
-    recv = exchange(send, along_xz)
+    recv = exchange(send, along_y)
+    before, after = step(both_z, 1, 0), step(both_z, -1, 0)
+    two_before = step(before[: ny * ffr], 1, 0), step(after[ny * ffr :], -1, 0)
 
     w_gate, w_up, w_down = gate_weight[0], up_weight[0], jnp.transpose(down_weight[0])
     wide = 3 * ff
@@ -330,9 +334,9 @@
         ],
         scratch=[pltpu.VMEM((8 * chunk, feat), BF)],
         scalars=1,
-        operands=4,
+        operands=9,
         megabytes=40,
-    )(who, recv, w_gate, w_up, w_down)
+    )(who, recv, both_z, before, *two_before, after, w_gate, w_up, w_down)
 
     mid = chunk // 2
     far = add(far, core_swap(far_out))
@@ -347,14 +351,18 @@
         rest, rest_in, from_left, from_right
     )
 
-    left, right = shift(own, 1), shift(own, -1)
-    far = jnp.concatenate([shift(left[:mid], 1), shift(right[mid:], -1)], axis=0)
+    left, right, own_other = lax.optimization_barrier((shift(own, 1), shift(own, -1), core_swap(own)))
+    far = (shift(left[:mid], 1), shift(right[mid:], -1))
+    low, high, right_other, left_other = lax.optimization_barrier(
+        (*far, core_swap(right), core_swap(left))
+    )
+    far = jnp.concatenate([low, high], axis=0)
     mine = (far, own, right, left)
-    other = tuple(core_swap(v) for v in mine)
+    other = (core_swap(far), own_other, right_other, left_other)
 
     out, grads = call(
         back_kernel,
-        [(8, chunk, 2 * feat), (8 * chunk, 2 * ff)],
+        [(ny, out_rows, 2 * feat), (8 * chunk, 2 * ff)],
         scratch=[
             pltpu.VMEM((8 * chunk, ff), BF),
             pltpu.VMEM((8 * chunk, feat), BF),
@@ -365,11 +373,11 @@
         megabytes=40,
     )(who, *mine, *other, w_gate, w_up, w_down, restored)
 
-    out = exchange(out.reshape(nxz, out_rows, 2 * feat), along_xz)
+    out = exchange(out, along_y)
     gate_grad = dot(rows, grads[:, :ff], TN).astype(BF)
     up_grad = dot(rows, grads[:, ff:], TN).astype(BF)
     (part,) = call(combine_kernel, [(seen, 2 * feat)], operands=4)(out, pick, pick_hi, pick_lo)
-    part = exchange(part.reshape(ny, tok, 2 * feat), along_y)
+    part = exchange(part.reshape(nxz, tok, 2 * feat), along_xz)
     combined, token_grad = call(finish_kernel, [(tok, feat), (tok, feat)], operands=1)(part)
     return (combined, token_grad, gate_grad[None], up_grad[None])
 

time: 254 us -> 272 us (1.071)
  local copies, waits for them, and re-layouts: 6.66 us -> 15.4 us
  starting transfers between devices: 90 us -> 97.3 us
    all_to_all x2 -> x3, waiting for transfers between devices: 52.8 us -> 9.32 us  [exchange(): lax.all_to_all(flat, 'expert', 0, 0, axis_index_groups=groups, tiled=True)]
    ppermute x8, waiting for transfers between devices: 28.3 us -> 52 us  [shift(): lax.ppermute(x, 'dp', [(2 * h + c, 2 * ((h + k) % 4) + c) for h in range(...]
    ppermute x0 -> x5, waiting for transfers between devices: none -> 22.3 us  [step(): return lax.ppermute(v, 'expert', pairs)]
    ppermute x0 -> x5, starting transfers between devices: none -> 13.8 us  [step(): return lax.ppermute(v, 'expert', pairs)]
    ppermute x8, starting transfers between devices: 43.4 us -> 33.4 us  [shift(): lax.ppermute(x, 'dp', [(2 * h + c, 2 * ((h + k) % 4) + c) for h in range(...]
    all_to_all x2 -> x3, starting transfers between devices: 11.1 us -> 14.7 us  [exchange(): lax.all_to_all(flat, 'expert', 0, 0, axis_index_groups=groups, tiled=True)]
    ppermute x0 -> x2, local copies, waits for them, and re-layouts: none -> 2.88 us  [step(): return lax.ppermute(v, 'expert', pairs)]
    unnamed x31 -> x37, local copies, waits for them, and re-layouts: 6.54 us -> 8.82 us
  transfers between devices with their start and end apart: 16 -> 22, of which waited for: 9 -> 14; matrix products, arithmetic and copies ran while one was open for 2% -> 4% of each run, Pallas kernels for 0% -> 0%
where the time goes in v4:
time: 272 us; the launch traced here: 270 us
  starting transfers between devices  97.3 us (36%)
  waiting for transfers between devices  85.1 us (31%)
  blocking collectives  51.9 us (19%)
  local copies, waits for them, and re-layouts  15.4 us (6%)
  Pallas kernels  13.1 us (5%)
  matrix products  4.8 us (2%)
    ppermute x8, waiting for transfers between devices, shift(): lax.ppermute(x, 'dp', [(2 * h + c, 2 * ((h + k) % 4) + c) for h in range(...  52 us
    all_to_all x2, blocking collectives, exchange(): lax.all_to_all(flat, 'expert', 0, 0, axis_index_groups=groups, tiled=True)  51.9 us
    ppermute x6, starting transfers between devices, core_swap(): return lax.ppermute(x, 'dp', [(i, i ^ 1) for i in range(8)])  35.4 us
    ppermute x8, starting transfers between devices, shift(): lax.ppermute(x, 'dp', [(2 * h + c, 2 * ((h + k) % 4) + c) for h in range(...  33.4 us
    ppermute x5, waiting for transfers between devices, step(): return lax.ppermute(v, 'expert', pairs)  22.3 us
    all_to_all x3, starting transfers between devices, exchange(): lax.all_to_all(flat, 'expert', 0, 0, axis_index_groups=groups, tiled=True)  14.7 us
    ppermute x5, starting transfers between devices, step(): return lax.ppermute(v, 'expert', pairs)  13.8 us
    all_to_all x3, waiting for transfers between devices, exchange(): lax.all_to_all(flat, 'expert', 0, 0, axis_index_groups=groups, tiled=True)  9.32 us
  transfers between devices with their start and end apart: 22, of which 14 were waited for; matrix products, arithmetic and copies ran while one was open for 4% of the time, Pallas kernels for 0%

profile of v4, /device:TPU:1, one launch (start us, length us, event | category | flops | bytes accessed | tf_op | source)
XLA Modules:
  0.0 270.0 jit_solution(17115931826862619091)
XLA Ops:
  2.4 7.7 %all-to-all-start = ((bf16[8,16,1344]{2,1,0:T(8,128)(2,1)}), bf16[8,16,1344]{2,1,0:T(8,128)(2,1)S(1)}, u32[]{:S(2)}, u32[]{:S(2)}) async-start(bf16[8,16,1344]{2,1,0:T(8,128)(2,1)} %broadcast_in_dim.9), calls=%async_computation | async-start | bytes 720896 | tf_op jit(solution)/shard_map/all_to_all | solution.py:275
  13.5 6.9 %all-to-all-done = bf16[8,16,1344]{2,1,0:T(8,128)(2,1)S(1)} async-done(((bf16[8,16,1344]{2,1,0:T(8,128)(2,1)}), bf16[8,16,1344]{2,1,0:T(8,128)(2,1)S(1)}, u32[]{:S(2)}, u32[]{:S(2)}) %all-to-all-start) | async-done | bytes 344096 | tf_op jit(solution)/shard_map/all_to_all | solution.py:275
  20.4 15.7 %all_to_all.36.first_ref = bf16[8,32,1024]{2,1,0:T(8,128)(2,1)S(1)} all-to-all(bf16[8,32,1024]{2,1,0:T(8,128)(2,1)S(1)} %shard_map.129), channel_id=1, replica_groups={{0,1,16,17,32,33,48,49},{2,3,18,19,34,35,50,51},{4,5,20,21,36,37,52,53}..., dimensions={0} | all-to-all | bytes 1048576 | tf_op jit(solution)/shard_map/all_to_all | solution.py:275
  36.1 2.4 shard_map.130
  40.7 3.6 %all-to-all-start.2 = ((bf16[8,80,896]{2,1,0:T(8,128)(2,1)}), bf16[8,80,896]{2,1,0:T(8,128)(2,1)S(1)}, u32[]{:S(2)}, u32[]{:S(2)}) async-start(bf16[8,80,896]{2,1,0:T(8,128)(2,1)} %get-tuple-element.27), calls=%async_computation.2 | async-start | bytes 2293760 | tf_op jit(solution)/shard_map/all_to_all | solution.py:275
  44.3 2.5 collective-permute-start
  46.8 6.0 %collective-permute-done = bf16[128,1344]{1,0:T(8,128)(2,1)S(1)} collective-permute-done((bf16[128,1344]{1,0:T(8,128)(2,1)S(1)}, bf16[128,1344]{1,0:T(8,128)(2,1)S(1)}, u32[]{:S(2)}, u32[]{:S(2)}) %collective-permute-start) | collective-permute-done | bytes 344096 | tf_op jit(solution)/shard_map/ppermute | solution.py:286
  53.1 2.8 %collective-permute-start.3 = (bf16[256,1344]{0,1:T(8,128)(2,1)S(1)}, bf16[256,1344]{0,1:T(8,128)(2,1)}, u32[]{:S(2)}, u32[]{:S(2)}) collective-permute-start(bf16[256,1344]{0,1:T(8,128)(2,1)S(1)} %copy.22), channel_id=1, source_target_pairs={{0,48},{1,49},{2,50},{3,51},{4,52},{5,53},{6,54},{7,55},{8,56},{9,... | collective-permute-start | bytes 2064392 | tf_op jit(solution)/shard_map/ppermute | solution.py:286
  55.9 2.5 collective-permute-start.1
  58.4 9.3 %collective-permute-done.3 = bf16[256,1344]{0,1:T(8,128)(2,1)} collective-permute-done((bf16[256,1344]{0,1:T(8,128)(2,1)S(1)}, bf16[256,1344]{0,1:T(8,128)(2,1)}, u32[]{:S(2)}, u32[]{:S(2)}) %collective-permute-start.3) | collective-permute-done | bytes 688160 | tf_op jit(solution)/shard_map/ppermute | solution.py:286
  67.7 1.4 copy.25.s3
  69.9 4.1 %collective-permute-start.4 = (bf16[128,1344]{1,0:T(8,128)(2,1)}, bf16[128,1344]{1,0:T(8,128)(2,1)}, u32[]{:S(2)}, u32[]{:S(2)}) collective-permute-start(bf16[128,1344]{1,0:T(8,128)(2,1)} %slice.63), channel_id=1, source_target_pairs={{0,48},{1,49},{2,50},{3,51},{4,52},{5,53},{6,54},{7,55},{8,56},{9,... | collective-permute-start | bytes 1032200 | tf_op jit(solution)/shard_map/ppermute | solution.py:286
  74.1 1.4 copy.26.s1
  76.3 1.9 collective-permute-start.2
  78.9 7.0 %collective-permute-done.2.s2a = bf16[128,1344]{1,0:T(8,128)(2,1)} collective-permute-done((bf16[128,1344]{1,0:T(8,128)(2,1)}, bf16[128,1344]{1,0:T(8,128)(2,1)}, u32[]{:S(2)}, u32[]{:S(2)}) %collective-permute-start.2) | collective-permute-done | bytes 344096 | tf_op jit(solution)/shard_map/ppermute | solution.py:286
  85.9 1.2 copy-done
  87.1 1.2 copy-done.2
  88.3 1.2 copy-done.4
  89.5 4.2 %shard_map.131 = (bf16[640,448]{1,0:T(8,128)(2,1)S(1)}, bf16[80,3072]{1,0:T(8,128)(2,1)S(1)}, bf16[240,3072]{1,0:T(8,128)(2,1)S(1)}, bf16[80,3072]{1,0:T(8,128)(...) custom-call(s32[5]{0:T(128)S(1)} %stack.27.who_ref.refs_0_, ...), custom_call_target="tpu_custom_call" | custom-call | tf_op jit(solution)/shard_map/pallas_call | solution.py:329
  93.7 8.4 %collective-permute-start.6 = (bf16[80,3072]{1,0:T(8,128)(2,1)S(1)}, bf16[80,3072]{1,0:T(8,128)(2,1)S(1)}, u32[]{:S(2)}, u32[]{:S(2)}) collective-permute-start(bf16[80,3072]{1,0:T(8,128)(2,1)S(1)} %get-tuple-element.31), channel_id=1, source_target_pairs={{0,64},{64,0},{128,192},{192,128},{256,320},{320,256},{384,448},{4... | collective-permute-start | bytes 1474568 | tf_op jit(solution)/shard_map/ppermute | solution.py:239
  102.1 1.9 collective-permute-start.5
  104.2 9.8 %collective-permute-start.9 = (bf16[40,3072]{1,0:T(8,128)(2,1)S(1)}, bf16[40,3072]{1,0:T(8,128)(2,1)S(1)}, u32[]{:S(2)}, u32[]{:S(2)}) collective-permute-start(bf16[40,3072]{1,0:T(8,128)(2,1)S(1)} %get-tuple-element.52), channel_id=1, source_target_pairs={{0,384},{64,448},{128,0},{192,64},{256,128},{320,192},{384,256},{4... | collective-permute-start | bytes 737288 | tf_op jit(solution)/shard_map/ppermute | solution.py:243
  114.0 1.9 collective-permute-start.7
  116.3 5.2 %collective-permute-done.9 = bf16[40,3072]{1,0:T(8,128)(2,1)S(1)} collective-permute-done((bf16[40,3072]{1,0:T(8,128)(2,1)S(1)}, bf16[40,3072]{1,0:T(8,128)(2,1)S(1)}, u32[]{:S(2)}, u32[]{:S(2)}) %collective-permute-start.9) | collective-permute-done | bytes 245792 | tf_op jit(solution)/shard_map/ppermute | solution.py:243
  121.5 4.9 %collective-permute-done.7 = bf16[40,3072]{1,0:T(8,128)(2,1)S(1)} collective-permute-done((bf16[40,3072]{1,0:T(8,128)(2,1)S(1)}, bf16[40,3072]{1,0:T(8,128)(2,1)S(1)}, u32[]{:S(2)}, u32[]{:S(2)}) %collective-permute-start.7) | collective-permute-done | bytes 245792 | tf_op jit(solution)/shard_map/ppermute | solution.py:243
  126.6 1.9 collective-permute-start.8
  128.5 5.5 %collective-permute-start.10 = (bf16[80,3072]{1,0:T(8,128)(2,1)S(1)}, bf16[80,3072]{1,0:T(8,128)(2,1)S(1)}, u32[]{:S(2)}, u32[]{:S(2)}) collective-permute-start(bf16[80,3072]{1,0:T(8,128)(2,1)S(1)} %pad_maximum_fusion.2), channel_id=1, source_target_pairs={{0,384},{64,448},{128,0},{192,64},{256,128},{320,192},{384,256},{4... | collective-permute-start | bytes 1474568 | tf_op jit(solution)/shard_map/ppermute | solution.py:243
  134.0 5.6 %collective-permute-done.8.left_ref = bf16[80,3072]{1,0:T(8,128)(2,1)S(1)} collective-permute-done((bf16[80,3072]{1,0:T(8,128)(2,1)S(1)}, bf16[80,3072]{1,0:T(8,128)(2,1)S(1)}, u32[]{:S(2)}, u32[]{:S(2)}) %collective-permute-start.8) | collective-permute-done | bytes 491552 | tf_op jit(solution)/shard_map/ppermute | solution.py:243
  140.8 17.7 %collective-permute-start.13 = (bf16[80,3072]{1,0:T(8,128)(2,1)S(1)}, bf16[80,3072]{1,0:T(8,128)(2,1)S(1)}, u32[]{:S(2)}, u32[]{:S(2)}) collective-permute-start(bf16[80,3072]{1,0:T(8,128)(2,1)S(1)} %shard_map.132.refs_2_), channel_id=1, source_target_pairs={{0,64},{64,0},{128,192},{192,128},{256,320},{320,256},{384,448},{4... | collective-permute-start | bytes 1474568 | tf_op jit(solution)/shard_map/ppermute | solution.py:239
  158.5 6.2 %collective-permute-start.12 = (bf16[80,3072]{1,0:T(8,128)(2,1)S(1)}, bf16[80,3072]{1,0:T(8,128)(2,1)S(1)}, u32[]{:S(2)}, u32[]{:S(2)}) collective-permute-start(bf16[80,3072]{1,0:T(8,128)(2,1)S(1)} %shard_map.132.refs_2_), channel_id=1, source_target_pairs={{0,384},{64,448},{128,0},{192,64},{256,128},{320,192},{384,256},{4... | collective-permute-start | bytes 1474568 | tf_op jit(solution)/shard_map/ppermute | solution.py:243
  164.7 1.9 collective-permute-start.11
  166.7 19.2 %collective-permute-done.12.refs_3_ = bf16[80,3072]{1,0:T(8,128)(2,1)S(1)} collective-permute-done((bf16[80,3072]{1,0:T(8,128)(2,1)S(1)}, bf16[80,3072]{1,0:T(8,128)(2,1)S(1)}, u32[]{:S(2)}, u32[]{:S(2)}) %collective-permute-start.12) | collective-permute-done | bytes 491552 | tf_op jit(solution)/shard_map/ppermute | solution.py:243
  185.8 5.8 %collective-permute-done.11.refs_4_ = bf16[80,3072]{1,0:T(8,128)(2,1)S(1)} collective-permute-done((bf16[80,3072]{1,0:T(8,128)(2,1)S(1)}, bf16[80,3072]{1,0:T(8,128)(2,1)S(1)}, u32[]{:S(2)}, u32[]{:S(2)}) %collective-permute-start.11) | collective-permute-done | bytes 491552 | tf_op jit(solution)/shard_map/ppermute | solution.py:243
  191.6 3.0 %collective-permute-start.17 = (bf16[80,3072]{1,0:T(8,128)(2,1)S(1)}, bf16[80,3072]{1,0:T(8,128)(2,1)S(1)}, u32[]{:S(2)}, u32[]{:S(2)}) collective-permute-start(bf16[80,3072]{1,0:T(8,128)(2,1)S(1)} %collective-permute-done.11.refs_4_), channel_id=1, source_target_pairs={{0,64},{64,0},{128,192},{192,128},{256,320},{320,256},{384,448},{4... | collective-permute-start | bytes 1474568 | tf_op jit(solution)/shard_map/ppermute | solution.py:239
  194.6 1.9 collective-permute-start.16
  196.6 1.9 collective-permute-start.15
  198.5 4.3 %collective-permute-start.14 = (bf16[40,3072]{1,0:T(8,128)(2,1)S(1)}, bf16[40,3072]{1,0:T(8,128)(2,1)S(1)}, u32[]{:S(2)}, u32[]{:S(2)}) collective-permute-start(bf16[40,3072]{1,0:T(8,128)(2,1)S(1)} %slice.58), channel_id=1, source_target_pairs={{0,128},{64,192},{128,256},{192,320},{256,384},{320,448},{384,0},{... | collective-permute-start | bytes 737288 | tf_op jit(solution)/shard_map/ppermute | solution.py:243
  202.8 3.7 %collective-permute-done.15 = bf16[40,3072]{1,0:T(8,128)(2,1)S(1)} collective-permute-done((bf16[40,3072]{1,0:T(8,128)(2,1)S(1)}, bf16[40,3072]{1,0:T(8,128)(2,1)S(1)}, u32[]{:S(2)}, u32[]{:S(2)}) %collective-permute-start.15) | collective-permute-done | bytes 245792 | tf_op jit(solution)/shard_map/ppermute | solution.py:243
  206.4 7.0 %collective-permute-done.14 = bf16[40,3072]{1,0:T(8,128)(2,1)S(1)} collective-permute-done((bf16[40,3072]{1,0:T(8,128)(2,1)S(1)}, bf16[40,3072]{1,0:T(8,128)(2,1)S(1)}, u32[]{:S(2)}, u32[]{:S(2)}) %collective-permute-start.14) | collective-permute-done | bytes 245792 | tf_op jit(solution)/shard_map/ppermute | solution.py:243
  213.5 2.5 collective-permute-start.18
  216.0 1.5 collective-permute-done.18.refs_5_
  217.4 3.2 %shard_map.133 = (bf16[8,80,896]{2,1,0:T(8,128)(2,1)S(1)}, bf16[640,2048]{1,0:T(8,128)(2,1)S(1)}) custom-call(s32[5]{0:T(128)S(1)} %stack.27.who_ref.refs_0_, bf16[80,3072]{1,0:T(8,128)(2,1)S(1)} %constant_dynamic-update-slice_fusion.refs_1_, bf16[80,3072]{1,0:T(8,128)(2,1)S(1)} %shard_map.132.refs_2_, bf16[80,3072]{1,0:T(8,128)(2,1)S(1)} %collective-permute-done.12.refs_3_, ...), custom_call_target="tpu_custom_call" | custom-call | tf_op jit(solution)/shard_map/pallas_call | solution.py:363
  220.7 36.1 %all_to_all.37.recv_ref = bf16[8,80,896]{2,1,0:T(8,128)(2,1)S(1)} all-to-all(bf16[8,80,896]{2,1,0:T(8,128)(2,1)S(1)} %get-tuple-element.40), channel_id=1, replica_groups={{0,2,4,6,8,10,12,14},{1,3,5,7,9,11,13,15},{16,18,20,22,24,26,28,30},{17..., dimensions={0} | all-to-all | bytes 2293760 | tf_op jit(solution)/shard_map/all_to_all | solution.py:275
  256.8 1.7 shard_map.134
  258.5 3.5 %all-to-all-start.4 = ((bf16[8,32,896]{2,1,0:T(8,128)(2,1)}), bf16[8,32,896]{2,1,0:T(8,128)(2,1)S(1)}, u32[]{:S(2)}, u32[]{:S(2)}) async-start(bf16[8,32,896]{2,1,0:T(8,128)(2,1)} %bitcast.12), calls=%async_computation.4 | async-start | bytes 917504 | tf_op jit(solution)/shard_map/all_to_all | solution.py:275
  262.0 3.0 %fusion.1 = bf16[1,448,1024]{2,1,0:T(8,128)(2,1)} fusion(bf16[640,448]{1,0:T(8,128)(2,1)} %copy-done.15, bf16[640,2048]{1,0:T(8,128)(2,1)S(1)} %get-tuple-element.47), kind=kOutput, calls=%fused_computation.4 | convolution fusion | flops 587661312 | bytes 2801664 | tf_op jit(solution)/shard_map/dot_general | solution.py:22
  265.0 1.8 fusion
  266.8 2.4 all-to-all-done.4.recv_ref
  (64 shorter events, 12.0 us)
Async XLA Ops:
  1.5 34.6 %copy-start.12 = (f32[80,256]{1,0:T(8,128)S(1)}, f32[80,256]{1,0:T(8,128)}, u32[]{:S(2)}) copy-start(f32[80,256]{1,0:T(8,128)} %constant.50.clone.want_ref) | copy-start | bytes 245764
  2.4 18.0 %all-to-all-start = ((bf16[8,16,1344]{2,1,0:T(8,128)(2,1)}), bf16[8,16,1344]{2,1,0:T(8,128)(2,1)S(1)}, u32[]{:S(2)}, u32[]{:S(2)}) async-start(bf16[8,16,1344]{2,1,0:T(8,128)(2,1)} %broadcast_in_dim.9), calls=%async_computation | async-start | bytes 720896 | tf_op jit(solution)/shard_map/all_to_all | solution.py:275
  11.5 0.8 copy-start.13
  12.3 0.8 copy-start.14
  38.5 0.7 copy-start.6
  39.2 0.7 copy-start.8
  40.0 0.7 copy-start.10
  40.7 45.2 %all-to-all-start.2 = ((bf16[8,80,896]{2,1,0:T(8,128)(2,1)}), bf16[8,80,896]{2,1,0:T(8,128)(2,1)S(1)}, u32[]{:S(2)}, u32[]{:S(2)}) async-start(bf16[8,80,896]{2,1,0:T(8,128)(2,1)} %get-tuple-element.27), calls=%async_computation.2 | async-start | bytes 2293760 | tf_op jit(solution)/shard_map/all_to_all | solution.py:275
  44.3 8.5 %collective-permute-start = (bf16[128,1344]{1,0:T(8,128)(2,1)S(1)}, bf16[128,1344]{1,0:T(8,128)(2,1)S(1)}, u32[]{:S(2)}, u32[]{:S(2)}) collective-permute-start(bf16[128,1344]{1,0:T(8,128)(2,1)S(1)} %bitcast.27), channel_id=1, source_target_pairs={{0,1},{1,0},{2,3},{3,2},{4,5},{5,4},{6,7},{7,6},{8,9},{9,8},{10,11... | collective-permute-start | bytes 1032200 | tf_op jit(solution)/shard_map/ppermute | solution.py:286
  53.1 14.6 %collective-permute-start.3 = (bf16[256,1344]{0,1:T(8,128)(2,1)S(1)}, bf16[256,1344]{0,1:T(8,128)(2,1)}, u32[]{:S(2)}, u32[]{:S(2)}) collective-permute-start(bf16[256,1344]{0,1:T(8,128)(2,1)S(1)} %copy.22), channel_id=1, source_target_pairs={{0,48},{1,49},{2,50},{3,51},{4,52},{5,53},{6,54},{7,55},{8,56},{9,... | collective-permute-start | bytes 2064392 | tf_op jit(solution)/shard_map/ppermute | solution.py:286
  55.9 18.2 %collective-permute-start.1 = (bf16[256,1344]{0,1:T(8,128)(2,1)S(1)}, bf16[256,1344]{0,1:T(8,128)(2,1)}, u32[]{:S(2)}, u32[]{:S(2)}) collective-permute-start(bf16[256,1344]{0,1:T(8,128)(2,1)S(1)} %copy.22), channel_id=1, source_target_pairs={{0,16},{1,17},{2,18},{3,19},{4,20},{5,21},{6,22},{7,23},{8,24},{9,... | collective-permute-start | bytes 2064392 | tf_op jit(solution)/shard_map/ppermute | solution.py:286
  69.9 9.1 %collective-permute-start.4 = (bf16[128,1344]{1,0:T(8,128)(2,1)}, bf16[128,1344]{1,0:T(8,128)(2,1)}, u32[]{:S(2)}, u32[]{:S(2)}) collective-permute-start(bf16[128,1344]{1,0:T(8,128)(2,1)} %slice.63), channel_id=1, source_target_pairs={{0,48},{1,49},{2,50},{3,51},{4,52},{5,53},{6,54},{7,55},{8,56},{9,... | collective-permute-start | bytes 1032200 | tf_op jit(solution)/shard_map/ppermute | solution.py:286
  76.3 9.7 %collective-permute-start.2 = (bf16[128,1344]{1,0:T(8,128)(2,1)}, bf16[128,1344]{1,0:T(8,128)(2,1)}, u32[]{:S(2)}, u32[]{:S(2)}) collective-permute-start(bf16[128,1344]{1,0:T(8,128)(2,1)} %slice.62), channel_id=1, source_target_pairs={{0,16},{1,17},{2,18},{3,19},{4,20},{5,21},{6,22},{7,23},{8,24},{9,... | collective-permute-start | bytes 1032200 | tf_op jit(solution)/shard_map/ppermute | solution.py:286
  85.9 1.2 copy-start
  87.1 1.2 copy-start.2
  88.3 1.2 copy-start.4
  93.7 22.6 %copy-start.15 = (bf16[640,448]{1,0:T(8,128)(2,1)}, bf16[640,448]{1,0:T(8,128)(2,1)S(1)}, u32[]{:S(2)}) copy-start(bf16[640,448]{1,0:T(8,128)(2,1)S(1)} %get-tuple-element.46) | copy-start | bytes 1720324
  93.7 10.4 %collective-permute-start.6 = (bf16[80,3072]{1,0:T(8,128)(2,1)S(1)}, bf16[80,3072]{1,0:T(8,128)(2,1)S(1)}, u32[]{:S(2)}, u32[]{:S(2)}) collective-permute-start(bf16[80,3072]{1,0:T(8,128)(2,1)S(1)} %get-tuple-element.31), channel_id=1, source_target_pairs={{0,64},{64,0},{128,192},{192,128},{256,320},{320,256},{384,448},{4... | collective-permute-start | bytes 1474568 | tf_op jit(solution)/shard_map/ppermute | solution.py:239
  102.1 13.8 %collective-permute-start.5 = (bf16[240,3072]{1,0:T(8,128)(2,1)S(1)}, bf16[240,3072]{1,0:T(8,128)(2,1)S(1)}, u32[]{:S(2)}, u32[]{:S(2)}) collective-permute-start(bf16[240,3072]{1,0:T(8,128)(2,1)S(1)} %get-tuple-element.29), channel_id=1, source_target_pairs={{0,64},{64,0},{128,192},{192,128},{256,320},{320,256},{384,448},{4... | collective-permute-start | bytes 4423688 | tf_op jit(solution)/shard_map/ppermute | solution.py:239
  104.2 17.3 %collective-permute-start.9 = (bf16[40,3072]{1,0:T(8,128)(2,1)S(1)}, bf16[40,3072]{1,0:T(8,128)(2,1)S(1)}, u32[]{:S(2)}, u32[]{:S(2)}) collective-permute-start(bf16[40,3072]{1,0:T(8,128)(2,1)S(1)} %get-tuple-element.52), channel_id=1, source_target_pairs={{0,384},{64,448},{128,0},{192,64},{256,128},{320,192},{384,256},{4... | collective-permute-start | bytes 737288 | tf_op jit(solution)/shard_map/ppermute | solution.py:243
  114.0 12.4 %collective-permute-start.7 = (bf16[40,3072]{1,0:T(8,128)(2,1)S(1)}, bf16[40,3072]{1,0:T(8,128)(2,1)S(1)}, u32[]{:S(2)}, u32[]{:S(2)}) collective-permute-start(bf16[40,3072]{1,0:T(8,128)(2,1)S(1)} %get-tuple-element.53), channel_id=1, source_target_pairs={{0,128},{64,192},{128,256},{192,320},{256,384},{320,448},{384,0},{... | collective-permute-start | bytes 737288 | tf_op jit(solution)/shard_map/ppermute | solution.py:243
  126.6 13.0 %collective-permute-start.8 = (bf16[80,3072]{1,0:T(8,128)(2,1)S(1)}, bf16[80,3072]{1,0:T(8,128)(2,1)S(1)}, u32[]{:S(2)}, u32[]{:S(2)}) collective-permute-start(bf16[80,3072]{1,0:T(8,128)(2,1)S(1)} %pad_maximum_fusion.1), channel_id=1, source_target_pairs={{0,128},{64,192},{128,256},{192,320},{256,384},{320,448},{384,0},{... | collective-permute-start | bytes 1474568 | tf_op jit(solution)/shard_map/ppermute | solution.py:243
  128.5 11.8 %collective-permute-start.10 = (bf16[80,3072]{1,0:T(8,128)(2,1)S(1)}, bf16[80,3072]{1,0:T(8,128)(2,1)S(1)}, u32[]{:S(2)}, u32[]{:S(2)}) collective-permute-start(bf16[80,3072]{1,0:T(8,128)(2,1)S(1)} %pad_maximum_fusion.2), channel_id=1, source_target_pairs={{0,384},{64,448},{128,0},{192,64},{256,128},{320,192},{384,256},{4... | collective-permute-start | bytes 1474568 | tf_op jit(solution)/shard_map/ppermute | solution.py:243
  140.3 77.1 %copy-start.5 = (bf16[1,1024,448]{1,2,0:T(8,128)(2,1)S(1)}, bf16[1,1024,448]{1,2,0:T(8,128)(2,1)}, u32[]{:S(2)}) copy-start(bf16[1,1024,448]{1,2,0:T(8,128)(2,1)} %param.17) | copy-start | bytes 2752516
  140.8 76.7 %copy-start.1 = (bf16[1,448,1024]{2,1,0:T(8,128)(2,1)S(1)}, bf16[1,448,1024]{2,1,0:T(8,128)(2,1)}, u32[]{:S(2)}) copy-start(bf16[1,448,1024]{2,1,0:T(8,128)(2,1)} %param.15) | copy-start | bytes 2752516
  140.8 76.7 %copy-start.3 = (bf16[1,448,1024]{2,1,0:T(8,128)(2,1)S(1)}, bf16[1,448,1024]{2,1,0:T(8,128)(2,1)}, u32[]{:S(2)}) copy-start(bf16[1,448,1024]{2,1,0:T(8,128)(2,1)} %param.16) | copy-start | bytes 2752516
  140.8 25.9 %collective-permute-start.13 = (bf16[80,3072]{1,0:T(8,128)(2,1)S(1)}, bf16[80,3072]{1,0:T(8,128)(2,1)S(1)}, u32[]{:S(2)}, u32[]{:S(2)}) collective-permute-start(bf16[80,3072]{1,0:T(8,128)(2,1)S(1)} %shard_map.132.refs_2_), channel_id=1, source_target_pairs={{0,64},{64,0},{128,192},{192,128},{256,320},{320,256},{384,448},{4... | collective-permute-start | bytes 1474568 | tf_op jit(solution)/shard_map/ppermute | solution.py:239
  158.5 27.3 %collective-permute-start.12 = (bf16[80,3072]{1,0:T(8,128)(2,1)S(1)}, bf16[80,3072]{1,0:T(8,128)(2,1)S(1)}, u32[]{:S(2)}, u32[]{:S(2)}) collective-permute-start(bf16[80,3072]{1,0:T(8,128)(2,1)S(1)} %shard_map.132.refs_2_), channel_id=1, source_target_pairs={{0,384},{64,448},{128,0},{192,64},{256,128},{320,192},{384,256},{4... | collective-permute-start | bytes 1474568 | tf_op jit(solution)/shard_map/ppermute | solution.py:243
  164.7 26.9 %collective-permute-start.11 = (bf16[80,3072]{1,0:T(8,128)(2,1)S(1)}, bf16[80,3072]{1,0:T(8,128)(2,1)S(1)}, u32[]{:S(2)}, u32[]{:S(2)}) collective-permute-start(bf16[80,3072]{1,0:T(8,128)(2,1)S(1)} %shard_map.132.refs_2_), channel_id=1, source_target_pairs={{0,128},{64,192},{128,256},{192,320},{256,384},{320,448},{384,0},{... | collective-permute-start | bytes 1474568 | tf_op jit(solution)/shard_map/ppermute | solution.py:243
  191.6 21.9 %collective-permute-start.17 = (bf16[80,3072]{1,0:T(8,128)(2,1)S(1)}, bf16[80,3072]{1,0:T(8,128)(2,1)S(1)}, u32[]{:S(2)}, u32[]{:S(2)}) collective-permute-start(bf16[80,3072]{1,0:T(8,128)(2,1)S(1)} %collective-permute-done.11.refs_4_), channel_id=1, source_target_pairs={{0,64},{64,0},{128,192},{192,128},{256,320},{320,256},{384,448},{4... | collective-permute-start | bytes 1474568 | tf_op jit(solution)/shard_map/ppermute | solution.py:239
  194.6 18.9 %collective-permute-start.16 = (bf16[80,3072]{1,0:T(8,128)(2,1)S(1)}, bf16[80,3072]{1,0:T(8,128)(2,1)S(1)}, u32[]{:S(2)}, u32[]{:S(2)}) collective-permute-start(bf16[80,3072]{1,0:T(8,128)(2,1)S(1)} %collective-permute-done.12.refs_3_), channel_id=1, source_target_pairs={{0,64},{64,0},{128,192},{192,128},{256,320},{320,256},{384,448},{4... | collective-permute-start | bytes 1474568 | tf_op jit(solution)/shard_map/ppermute | solution.py:239
  196.6 9.9 %collective-permute-start.15 = (bf16[40,3072]{1,0:T(8,128)(2,1)S(1)}, bf16[40,3072]{1,0:T(8,128)(2,1)S(1)}, u32[]{:S(2)}, u32[]{:S(2)}) collective-permute-start(bf16[40,3072]{1,0:T(8,128)(2,1)S(1)} %slice.59), channel_id=1, source_target_pairs={{0,384},{64,448},{128,0},{192,64},{256,128},{320,192},{384,256},{4... | collective-permute-start | bytes 737288 | tf_op jit(solution)/shard_map/ppermute | solution.py:243
  198.5 14.9 %collective-permute-start.14 = (bf16[40,3072]{1,0:T(8,128)(2,1)S(1)}, bf16[40,3072]{1,0:T(8,128)(2,1)S(1)}, u32[]{:S(2)}, u32[]{:S(2)}) collective-permute-start(bf16[40,3072]{1,0:T(8,128)(2,1)S(1)} %slice.58), channel_id=1, source_target_pairs={{0,128},{64,192},{128,256},{192,320},{256,384},{320,448},{384,0},{... | collective-permute-start | bytes 737288 | tf_op jit(solution)/shard_map/ppermute | solution.py:243
  213.5 3.9 %collective-permute-start.18 = (bf16[80,3072]{1,0:T(8,128)(2,1)S(1)}, bf16[80,3072]{1,0:T(8,128)(2,1)S(1)}, u32[]{:S(2)}, u32[]{:S(2)}) collective-permute-start(bf16[80,3072]{1,0:T(8,128)(2,1)S(1)} %constant_dynamic-update-slice_fusion.refs_1_), channel_id=1, source_target_pairs={{0,64},{64,0},{128,192},{192,128},{256,320},{320,256},{384,448},{4... | collective-permute-start | bytes 1474568 | tf_op jit(solution)/shard_map/ppermute | solution.py:239
  220.7 36.2 %copy-start.7 = (bf16[640,256]{1,0:T(8,128)(2,1)S(1)}, bf16[640,256]{1,0:T(8,128)(2,1)}, u32[]{:S(2)}) copy-start(bf16[640,256]{1,0:T(8,128)(2,1)} %copy-done.6) | copy-start | bytes 983044
  220.7 36.1 %copy-start.9 = (bf16[640,256]{1,0:T(8,128)(2,1)S(1)}, bf16[640,256]{1,0:T(8,128)(2,1)}, u32[]{:S(2)}) copy-start(bf16[640,256]{1,0:T(8,128)(2,1)} %copy-done.8) | copy-start | bytes 983044
  220.7 36.1 %copy-start.11 = (bf16[640,256]{1,0:T(8,128)(2,1)S(1)}, bf16[640,256]{1,0:T(8,128)(2,1)}, u32[]{:S(2)}) copy-start(bf16[640,256]{1,0:T(8,128)(2,1)} %copy-done.10) | copy-start | bytes 983044
  258.5 10.7 %all-to-all-start.4 = ((bf16[8,32,896]{2,1,0:T(8,128)(2,1)}), bf16[8,32,896]{2,1,0:T(8,128)(2,1)S(1)}, u32[]{:S(2)}, u32[]{:S(2)}) async-start(bf16[8,32,896]{2,1,0:T(8,128)(2,1)} %bitcast.12), calls=%async_computation.4 | async-start | bytes 917504 | tf_op jit(solution)/shard_map/all_to_all | solution.py:275
  262.0 3.0 %copy-start.16 = (bf16[640,448]{1,0:T(8,128)(2,1)S(1)}, bf16[640,448]{1,0:T(8,128)(2,1)}, u32[]{:S(2)}) copy-start(bf16[640,448]{1,0:T(8,128)(2,1)} %copy-done.15) | copy-start | bytes 1720324

commit v5 on v4

--- a/solution.py
+++ b/solution.py
@@ -44,7 +44,7 @@
     tok, topk = ids_ref.shape
     ids = ids_ref[...]
     x, y, z = lax.div(ids, ny * nz), lax.rem(lax.div(ids, nz), ny), lax.rem(ids, nz)
-    column = (x * nz + z) * ny + y
+    column = y * nxz + x * nz + z
     lane = lax.broadcasted_iota(jnp.int32, (tok, ranks), 1)
     member = jnp.zeros((tok, ranks), F32)
     share = jnp.zeros((tok, ranks), F32)
@@ -58,40 +58,41 @@
     place = jnp.where(member > 0.5, before - 1.0, -1.0).astype(BF)
     hi = share.astype(BF)
     lo = (share - hi.astype(F32)).astype(BF)
-    source = lax.broadcasted_iota(jnp.int32, (ranks, nxz * 128), 0)
-    target = lax.broadcasted_iota(jnp.int32, (ranks, nxz * 128), 1)
-    base = lax.div(source, ny) * 128 + lax.rem(source, ny) + 64
-    meta = jnp.zeros((tok, nxz * 128), F32)
+    source = lax.broadcasted_iota(jnp.int32, (ranks, ny * 128), 0)
+    target = lax.broadcasted_iota(jnp.int32, (ranks, ny * 128), 1)
+    base = lax.div(source, nxz) * 128 + lax.rem(source, nxz) + 64
+    meta = jnp.zeros((tok, ny * 128), F32)
     for k, part in enumerate((place, hi, lo)):
-        meta = meta + dot(part, jnp.where(target == base + k * ny, 1.0, 0.0).astype(BF))
+        meta = meta + dot(part, jnp.where(target == base + k * nxz, 1.0, 0.0).astype(BF))
     feat = tok_ref.shape[1]
     assert feat == 448
     last = jnp.concatenate([tok_ref[:, 384:448].astype(F32), jnp.zeros((tok, 64), F32)], axis=1)
-    for i in range(nxz):
+    for i in range(ny):
         out_ref[i, :, 0:384] = tok_ref[:, 0:384]
         out_ref[i, :, 384:512] = (meta[:, i * 128 : (i + 1) * 128] + last).astype(BF)
         out_ref[i, :, 512 : 512 + feat] = cot_ref[...]
 
 
-def select_kernel(first_ref, want_ref, out_ref, pick_ref, hi_ref, lo_ref):
-    ny, rows, width = out_ref.shape
+def tables(meta_ref, want, q, count):
+    hit = meta_ref[q : q + 1, :] == want
+    hi = jnp.where(hit, meta_ref[count + q : count + q + 1, :], 0.0).astype(BF)
+    lo = jnp.where(hit, meta_ref[2 * count + q : 2 * count + q + 1, :], 0.0).astype(BF)
+    return jnp.where(hit, 1.0, 0.0).astype(BF), hi, lo
+
+
+def select_kernel(first_ref, want_ref, out_ref, meta_ref):
+    nxz, rows, width = out_ref.shape
     feat = width // 2
-    nxz, tok, _ = first_ref.shape
-    seen = nxz * tok
+    ny, tok, _ = first_ref.shape
+    seen = ny * tok
     tokens = first_ref[:, :, 0:feat].reshape(seen, feat)
     cots = first_ref[:, :, 512 : 512 + feat].reshape(seen, feat)
     meta = jnp.transpose(first_ref[:, :, 384:512].reshape(seen, 128).astype(F32))
+    meta_ref[...] = meta[64:128]
     want = want_ref[...]
     both = jnp.concatenate([cots, cots], axis=0)
-    for q in range(ny):
-        hit = meta[64 + q : 65 + q] == want
-        pick = jnp.where(hit, 1.0, 0.0).astype(BF)
-        hi = jnp.where(hit, meta[64 + ny + q : 65 + ny + q], 0.0).astype(BF)
-        lo = jnp.where(hit, meta[64 + 2 * ny + q : 65 + 2 * ny + q], 0.0).astype(BF)
-        span = pl.ds(q * rows, rows)
-        pick_ref[span, :] = pick
-        hi_ref[span, :] = hi
-        lo_ref[span, :] = lo
+    for q in range(nxz):
+        pick, hi, lo = tables(meta_ref, want, q, nxz)
         out_ref[q, :, 0:feat] = dot(pick, tokens).astype(BF)
         out_ref[q, :, feat:width] = dot(jnp.concatenate([hi, lo], axis=1), both).astype(BF)
 
@@ -101,15 +102,8 @@
     return half * 4 + lax.rem(h + (2, 0, 1, 3)[p % 4], 4)
 
 
-def block_of(ref, g, chunk):
-    per = ref.shape[1] // chunk
-    if per == 1:
-        return ref.at[g]
-    return ref.at[lax.div(g, per), pl.ds(lax.rem(g, per) * chunk, chunk)]
-
-
 def products_kernel(
-    grid, who_ref, recv_ref, s0, s1, s2a, s2b, s3, gate_ref, up_ref, down_ref,
+    grid, who_ref, recv_ref, s0, t0, s1, t1, s2, t2, s3, t3, gate_ref, up_ref, down_ref,
     rows_ref, far_ref, rest_ref, far_out_ref, rest_out_ref, restored_ref, grads_ref,
 ):
     nx, ny, nz = grid
@@ -117,9 +111,9 @@
     chunk = far_ref.shape[0]
     target, h, c, my_x, my_z = (who_ref[i] for i in range(5))
     for p in range(8):
-        block = block_of(recv_ref, chunk_at(h, c, p), chunk)
-        rows_ref[p * chunk : (p + 1) * chunk, :] = block[:, 0:feat]
-        grads_ref[p * chunk : (p + 1) * chunk, :] = block[:, feat : 2 * feat]
+        g = chunk_at(h, c, p)
+        rows_ref[p * chunk : (p + 1) * chunk, :] = recv_ref[g, :, 0:feat]
+        grads_ref[p * chunk : (p + 1) * chunk, :] = recv_ref[g, :, feat : 2 * feat]
 
     def store(k, j, value):
         at = pl.ds(pl.multiple_of(k * ff + j * TILE, TILE), TILE)
@@ -142,19 +136,15 @@
 
     @pl.when(target == 1)
     def _():
-        n = s0.shape[0] // (nz * ny)
-        half = ny * n
-        for k in range(nx):
+        n = s0.shape[0] // ny
+        for k, sources in enumerate(((s0, t0), (s1, t1), (s2, t2), (s3, t3))):
             for other in range(nz):
                 x = lax.rem(my_x - k + nx, nx)
                 z = 1 - my_z if other else my_z
-                source = ((s0, s0), (s1, s1), (s2a, s2b), (s3, s3))[k][other]
-                start = 0 if k == 2 else other * half
                 for y in range(ny):
                     to = pl.ds(pl.multiple_of(((x * ny + y) * nz + z) * n, n), n)
-                    r = start + y * n
                     for m in range(3):
-                        restored_ref[m, to, :] = source[r : r + n, m * feat : (m + 1) * feat]
+                        restored_ref[m, to, :] = sources[other][y * n : (y + 1) * n, m * feat : (m + 1) * feat]
 
         @pl.loop(0, tiles)
         def _(j):
@@ -191,7 +181,7 @@
     who_ref, parts = refs[0], refs[1:9]
     gate_ref, up_ref, down_ref, restored_ref, out_ref, grads_ref, hidden_ref, y_ref, dx_ref = refs[9:]
     feat, ff = gate_ref.shape
-    chunk = parts[0].shape[0]
+    chunk = out_ref.shape[1]
     target, h, c = who_ref[0], who_ref[1], who_ref[2]
     for p in range(8):
         span = slice(p * chunk, (p + 1) * chunk)
@@ -213,17 +203,23 @@
         ).astype(BF)
 
     for p in range(8):
-        block = block_of(out_ref, chunk_at(h, c, p), chunk)
+        g = chunk_at(h, c, p)
         span = slice(p * chunk, (p + 1) * chunk)
-        block[:, 0:feat] = y_ref[span, :]
-        block[:, feat : 2 * feat] = dx_ref[span, :]
-
-
-def combine_kernel(recv_ref, pick_ref, hi_ref, lo_ref, out_ref):
-    blocks, out_rows, width = recv_ref.shape
+        out_ref[g, :, 0:feat] = y_ref[span, :]
+        out_ref[g, :, feat : 2 * feat] = dx_ref[span, :]
+
+
+def combine_kernel(recv_ref, meta_ref, want_ref, out_ref, pick_ref, share_ref):
+    nxz, out_rows, width = recv_ref.shape
     feat = width // 2
-    rows = recv_ref[...].reshape(blocks * out_rows, width)
-    y = dot(hi_ref[...], rows[:, 0:feat], TN) + dot(lo_ref[...], rows[:, 0:feat], TN)
+    total = nxz * out_rows
+    for q in range(nxz):
+        span = pl.ds(q * out_rows, out_rows)
+        pick_ref[span, :], share_ref[0, span, :], share_ref[1, span, :] = tables(
+            meta_ref, want_ref[...], q, nxz
+        )
+    rows = recv_ref[...].reshape(total, width)
+    y = dot(share_ref[0], rows[:, 0:feat], TN) + dot(share_ref[1], rows[:, 0:feat], TN)
     out_ref[:, 0:feat] = y.astype(BF)
     out_ref[:, feat:width] = dot(pick_ref[...], rows[:, feat:width], TN).astype(BF)
 
@@ -303,26 +299,29 @@
     ).astype(jnp.int32)
 
     saved = jnp.transpose(backup, (2, 0, 1)).reshape(ffr, 3 * feat)
-    saved = exchange(jnp.broadcast_to(saved, (ny, ffr, 3 * feat)), along_y)
-    saved = saved.reshape(ny * ffr, 3 * feat)
-    both_z = jnp.concatenate([saved, step(saved, 0, 1)], axis=0)
-
-    (first,) = call(functools.partial(pack_kernel, grid), [(nxz, tok, LANES)], operands=4)(
+    saved = jnp.pad(saved, ((0, 0), (0, -3 * feat % 128)))
+    saved = exchange(jnp.broadcast_to(saved, (ny, *saved.shape)), along_y)
+    saved = saved.reshape(ny * ffr, -1)
+    (first,) = call(functools.partial(pack_kernel, grid), [(ny, tok, LANES)], operands=4)(
         expert_ids, route_weight, tokens, cotangent
     )
     first, saved = lax.optimization_barrier((first, saved))
-    first = exchange(first, along_xz)
-
-    out_rows, seen = nxz * capacity, nxz * tok
+    other_z = step(saved, 0, 1)
+    before, after = step(saved, 1, 0), step(saved, -1, 0)
+    first = exchange(first, along_y)
+    first, other_z, before, after = lax.optimization_barrier((first, other_z, before, after))
+    before_z, after_z = step(other_z, 1, 0), step(other_z, -1, 0)
+    blocks = (
+        saved, other_z, before, before_z, step(before, 1, 0), step(after_z, -1, 0), after, after_z,
+    )
+
+    out_rows, seen = ny * capacity, ny * tok
     row, col = np.arange(out_rows)[:, None], np.arange(seen)[None, :]
     want = np.where(row // capacity == col // tok, row % capacity, -2).astype(np.float32)
-    table = (ny * out_rows, seen)
-    send, pick, pick_hi, pick_lo = call(
-        select_kernel, [(ny, out_rows, 2 * feat), table, table, table], operands=2
+    send, meta = call(
+        select_kernel, [(nxz, out_rows, 2 * feat), ((64, seen), F32)], operands=2
     )(first, want)
-    recv = exchange(send, along_y)
-    before, after = step(both_z, 1, 0), step(both_z, -1, 0)
-    two_before = step(before[: ny * ffr], 1, 0), step(after[ny * ffr :], -1, 0)
+    recv = exchange(send, along_xz)
 
     w_gate, w_up, w_down = gate_weight[0], up_weight[0], jnp.transpose(down_weight[0])
     wide = 3 * ff
@@ -334,9 +333,9 @@
         ],
         scratch=[pltpu.VMEM((8 * chunk, feat), BF)],
         scalars=1,
-        operands=9,
+        operands=12,
         megabytes=40,
-    )(who, recv, both_z, before, *two_before, after, w_gate, w_up, w_down)
+    )(who, recv, *blocks, w_gate, w_up, w_down)
 
     mid = chunk // 2
     far = add(far, core_swap(far_out))
@@ -351,18 +350,14 @@
         rest, rest_in, from_left, from_right
     )
 
-    left, right, own_other = lax.optimization_barrier((shift(own, 1), shift(own, -1), core_swap(own)))
-    far = (shift(left[:mid], 1), shift(right[mid:], -1))
-    low, high, right_other, left_other = lax.optimization_barrier(
-        (*far, core_swap(right), core_swap(left))
-    )
-    far = jnp.concatenate([low, high], axis=0)
+    left, right = shift(own, 1), shift(own, -1)
+    far = jnp.concatenate([shift(left[:mid], 1), shift(right[mid:], -1)], axis=0)
     mine = (far, own, right, left)
-    other = (core_swap(far), own_other, right_other, left_other)
+    other = tuple(core_swap(v) for v in mine)
 
     out, grads = call(
         back_kernel,
-        [(ny, out_rows, 2 * feat), (8 * chunk, 2 * ff)],
+        [(8, chunk, 2 * feat), (8 * chunk, 2 * ff)],
         scratch=[
             pltpu.VMEM((8 * chunk, ff), BF),
             pltpu.VMEM((8 * chunk, feat), BF),
@@ -373,11 +368,19 @@
         megabytes=40,
     )(who, *mine, *other, w_gate, w_up, w_down, restored)
 
-    out = exchange(out, along_y)
+    out = exchange(out.reshape(nxz, out_rows, 2 * feat), along_xz)
     gate_grad = dot(rows, grads[:, :ff], TN).astype(BF)
     up_grad = dot(rows, grads[:, ff:], TN).astype(BF)
-    (part,) = call(combine_kernel, [(seen, 2 * feat)], operands=4)(out, pick, pick_hi, pick_lo)
-    part = exchange(part.reshape(nxz, tok, 2 * feat), along_xz)
+    (part,) = call(
+        combine_kernel,
+        [(seen, 2 * feat)],
+        scratch=[
+            pltpu.VMEM((nxz * out_rows, seen), BF),
+            pltpu.VMEM((2, nxz * out_rows, seen), BF),
+        ],
+        operands=3,
+    )(out, meta, want)
+    part = exchange(part.reshape(ny, tok, 2 * feat), along_y)
     combined, token_grad = call(finish_kernel, [(tok, feat), (tok, feat)], operands=1)(part)
     return (combined, token_grad, gate_grad[None], up_grad[None])
 

time: 272 us -> 248 us (0.912)
  blocking collectives: 51.9 us -> 21.7 us
  starting transfers between devices: 97.3 us -> 124 us
  waiting for transfers between devices: 85.1 us -> 71.2 us
  local copies, waits for them, and re-layouts: 15.4 us -> 9.17 us
    all_to_all x2 -> x1, blocking collectives: 51.9 us -> 21.7 us  [exchange(): lax.all_to_all(flat, 'expert', 0, 0, axis_index_groups=groups, tiled=True)]
    ppermute x8, waiting for transfers between devices: 52 us -> 30.8 us  [shift(): lax.ppermute(x, 'dp', [(2 * h + c, 2 * ((h + k) % 4) + c) for h in range(...]
    ppermute x5 -> x7, starting transfers between devices: 13.8 us -> 26.9 us  [step(): return lax.ppermute(v, 'expert', pairs)]
    all_to_all x3 -> x4, waiting for transfers between devices: 9.32 us -> 16.6 us  [exchange(): lax.all_to_all(flat, 'expert', 0, 0, axis_index_groups=groups, tiled=True)]
    all_to_all x3 -> x4, starting transfers between devices: 14.7 us -> 20.6 us  [exchange(): lax.all_to_all(flat, 'expert', 0, 0, axis_index_groups=groups, tiled=True)]
    ppermute x6, starting transfers between devices: 35.4 us -> 40 us  [core_swap(): return lax.ppermute(x, 'dp', [(i, i ^ 1) for i in range(8)])]
    ppermute x8, starting transfers between devices: 33.4 us -> 36.4 us  [shift(): lax.ppermute(x, 'dp', [(2 * h + c, 2 * ((h + k) % 4) + c) for h in range(...]
    ppermute x2 -> x0, local copies, waits for them, and re-layouts: 2.88 us -> none  [step(): return lax.ppermute(v, 'expert', pairs)]
  transfers between devices with their start and end apart: 22 -> 25, of which waited for: 14 -> 14; matrix products, arithmetic and copies ran while one was open for 4% -> 3% of each run, Pallas kernels for 0% -> 0%
where the time goes in v5:
time: 248 us; the launch traced here: 247 us
  starting transfers between devices  124 us (50%)
  waiting for transfers between devices  71.2 us (29%)
  blocking collectives  21.7 us (9%)
  Pallas kernels  13.2 us (5%)
  local copies, waits for them, and re-layouts  9.17 us (4%)
  matrix products  5.11 us (2%)
    ppermute x6, starting transfers between devices, core_swap(): return lax.ppermute(x, 'dp', [(i, i ^ 1) for i in range(8)])  40 us
    ppermute x8, starting transfers between devices, shift(): lax.ppermute(x, 'dp', [(2 * h + c, 2 * ((h + k) % 4) + c) for h in range(...  36.4 us
    ppermute x8, waiting for transfers between devices, shift(): lax.ppermute(x, 'dp', [(2 * h + c, 2 * ((h + k) % 4) + c) for h in range(...  30.8 us
    ppermute x7, starting transfers between devices, step(): return lax.ppermute(v, 'expert', pairs)  26.9 us
    ppermute x7, waiting for transfers between devices, step(): return lax.ppermute(v, 'expert', pairs)  22.3 us
    all_to_all x1, blocking collectives, exchange(): lax.all_to_all(flat, 'expert', 0, 0, axis_index_groups=groups, tiled=True)  21.7 us
    all_to_all x4, starting transfers between devices, exchange(): lax.all_to_all(flat, 'expert', 0, 0, axis_index_groups=groups, tiled=True)  20.6 us
    all_to_all x4, waiting for transfers between devices, exchange(): lax.all_to_all(flat, 'expert', 0, 0, axis_index_groups=groups, tiled=True)  16.6 us
  transfers between devices with their start and end apart: 25, of which 14 were waited for; matrix products, arithmetic and copies ran while one was open for 3% of the time, Pallas kernels for 0%

profile of v5, /device:TPU:1, one launch (start us, length us, event | category | flops | bytes accessed | tf_op | source)
XLA Modules:
  0.0 246.5 jit_solution(2958910245982113495)
XLA Ops:
  2.4 7.7 %all-to-all-start = ((bf16[8,16,1408]{2,1,0:T(8,128)(2,1)}), bf16[8,16,1408]{2,1,0:T(8,128)(2,1)S(1)}, u32[]{:S(2)}, u32[]{:S(2)}) async-start(bf16[8,16,1408]{2,1,0:T(8,128)(2,1)} %broadcast_in_dim.9), calls=%async_computation | async-start | bytes 720896 | tf_op jit(solution)/shard_map/all_to_all | solution.py:271
  11.6 1.2 shard_map.129
  12.8 7.6 %all-to-all-done = bf16[8,16,1408]{2,1,0:T(8,128)(2,1)S(1)} async-done(((bf16[8,16,1408]{2,1,0:T(8,128)(2,1)}), bf16[8,16,1408]{2,1,0:T(8,128)(2,1)S(1)}, u32[]{:S(2)}, u32[]{:S(2)}) %all-to-all-start) | async-done | bytes 360480 | tf_op jit(solution)/shard_map/all_to_all | solution.py:271
  20.4 3.6 %all-to-all-start.1 = ((bf16[8,32,1024]{2,1,0:T(8,128)(2,1)}), bf16[8,32,1024]{2,1,0:T(8,128)(2,1)S(1)}, u32[]{:S(2)}, u32[]{:S(2)}) async-start(bf16[8,32,1024]{2,1,0:T(8,128)(2,1)} %shard_map.129), calls=%async_computation.1 | async-start | bytes 1048576 | tf_op jit(solution)/shard_map/all_to_all | solution.py:271
  24.0 7.0 %collective-permute-start.2 = (bf16[128,1408]{1,0:T(8,128)(2,1)S(1)}, bf16[128,1408]{1,0:T(8,128)(2,1)S(1)}, u32[]{:S(2)}, u32[]{:S(2)}) collective-permute-start(bf16[128,1408]{1,0:T(8,128)(2,1)S(1)} %bitcast.27), channel_id=1, source_target_pairs={{0,48},{1,49},{2,50},{3,51},{4,52},{5,53},{6,54},{7,55},{8,56},{9,... | collective-permute-start | bytes 1081352 | tf_op jit(solution)/shard_map/ppermute | solution.py:282
  31.0 1.9 collective-permute-start.1
  32.9 4.0 %collective-permute-start = (bf16[128,1408]{1,0:T(8,128)(2,1)S(1)}, bf16[128,1408]{1,0:T(8,128)(2,1)}, u32[]{:S(2)}, u32[]{:S(2)}) collective-permute-start(bf16[128,1408]{1,0:T(8,128)(2,1)S(1)} %bitcast.29), channel_id=1, source_target_pairs={{0,1},{1,0},{2,3},{3,2},{4,5},{5,4},{6,7},{7,6},{8,9},{9,8},{10,11... | collective-permute-start | bytes 1081352 | tf_op jit(solution)/shard_map/ppermute | solution.py:282
  37.7 4.0 %collective-permute-done.1.s1 = bf16[128,1408]{1,0:T(8,128)(2,1)S(1)} collective-permute-done((bf16[128,1408]{1,0:T(8,128)(2,1)S(1)}, bf16[128,1408]{1,0:T(8,128)(2,1)S(1)}, u32[]{:S(2)}, u32[]{:S(2)}) %collective-permute-start.1) | collective-permute-done | bytes 360480 | tf_op jit(solution)/shard_map/ppermute | solution.py:282
  43.5 1.4 shard_map.130
  44.9 1.0 copy-done.3
  45.9 4.6 %all-to-all-start.2 = ((bf16[8,80,896]{2,1,0:T(8,128)(2,1)}), bf16[8,80,896]{2,1,0:T(8,128)(2,1)S(1)}, u32[]{:S(2)}, u32[]{:S(2)}) async-start(bf16[8,80,896]{2,1,0:T(8,128)(2,1)} %copy-done.3), calls=%async_computation.2 | async-start | bytes 2293760 | tf_op jit(solution)/shard_map/all_to_all | solution.py:271
  50.4 4.6 %collective-permute-start.5 = (bf16[128,1408]{1,0:T(8,128)(2,1)}, bf16[128,1408]{1,0:T(8,128)(2,1)}, u32[]{:S(2)}, u32[]{:S(2)}) collective-permute-start(bf16[128,1408]{1,0:T(8,128)(2,1)} %collective-permute-done.t0), channel_id=1, source_target_pairs={{0,48},{1,49},{2,50},{3,51},{4,52},{5,53},{6,54},{7,55},{8,56},{9,... | collective-permute-start | bytes 1081352 | tf_op jit(solution)/shard_map/ppermute | solution.py:282
  55.0 1.9 collective-permute-start.3
  56.9 2.2 collective-permute-start.4
  59.1 11.9 %collective-permute-done.5.t3 = bf16[128,1408]{1,0:T(8,128)(2,1)} collective-permute-done((bf16[128,1408]{1,0:T(8,128)(2,1)}, bf16[128,1408]{1,0:T(8,128)(2,1)}, u32[]{:S(2)}, u32[]{:S(2)}) %collective-permute-start.5) | collective-permute-done | bytes 360480 | tf_op jit(solution)/shard_map/ppermute | solution.py:282
  71.0 5.3 %collective-permute-start.6 = (bf16[128,1408]{1,0:T(8,128)(2,1)}, bf16[128,1408]{1,0:T(8,128)(2,1)}, u32[]{:S(2)}, u32[]{:S(2)}) collective-permute-start(bf16[128,1408]{1,0:T(8,128)(2,1)} %collective-permute-done.5.t3), channel_id=1, source_target_pairs={{0,48},{1,49},{2,50},{3,51},{4,52},{5,53},{6,54},{7,55},{8,56},{9,... | collective-permute-start | bytes 1081352 | tf_op jit(solution)/shard_map/ppermute | solution.py:282
  77.0 4.3 %collective-permute-done.4.s2 = bf16[128,1408]{1,0:T(8,128)(2,1)} collective-permute-done((bf16[128,1408]{1,0:T(8,128)(2,1)}, bf16[128,1408]{1,0:T(8,128)(2,1)}, u32[]{:S(2)}, u32[]{:S(2)}) %collective-permute-start.4) | collective-permute-done | bytes 360480 | tf_op jit(solution)/shard_map/ppermute | solution.py:282
  81.3 1.2 collective-permute-done.6.t2
  82.5 1.2 copy-done.2
  85.7 4.5 %shard_map.131 = (bf16[640,448]{1,0:T(8,128)(2,1)S(1)}, bf16[80,3072]{1,0:T(8,128)(2,1)S(1)}, bf16[240,3072]{1,0:T(8,128)(2,1)S(1)}, bf16[80,3072]{1,0:T(8,128)(...) custom-call(s32[5]{0:T(128)S(1)} %stack.27.who_ref.refs_0_, ...), custom_call_target="tpu_custom_call" | custom-call | tf_op jit(solution)/shard_map/pallas_call | solution.py:328
  90.2 4.6 %collective-permute-start.8 = (bf16[80,3072]{1,0:T(8,128)(2,1)S(1)}, bf16[80,3072]{1,0:T(8,128)(2,1)S(1)}, u32[]{:S(2)}, u32[]{:S(2)}) collective-permute-start(bf16[80,3072]{1,0:T(8,128)(2,1)S(1)} %get-tuple-element.32), channel_id=1, source_target_pairs={{0,64},{64,0},{128,192},{192,128},{256,320},{320,256},{384,448},{4... | collective-permute-start | bytes 1474568 | tf_op jit(solution)/shard_map/ppermute | solution.py:235
  94.8 1.9 collective-permute-start.7
  96.9 9.8 %collective-permute-start.11 = (bf16[40,3072]{1,0:T(8,128)(2,1)S(1)}, bf16[40,3072]{1,0:T(8,128)(2,1)S(1)}, u32[]{:S(2)}, u32[]{:S(2)}) collective-permute-start(bf16[40,3072]{1,0:T(8,128)(2,1)S(1)} %get-tuple-element.44), channel_id=1, source_target_pairs={{0,384},{64,448},{128,0},{192,64},{256,128},{320,192},{384,256},{4... | collective-permute-start | bytes 737288 | tf_op jit(solution)/shard_map/ppermute | solution.py:239
  106.7 1.9 collective-permute-start.9
  109.0 4.9 %collective-permute-done.11 = bf16[40,3072]{1,0:T(8,128)(2,1)S(1)} collective-permute-done((bf16[40,3072]{1,0:T(8,128)(2,1)S(1)}, bf16[40,3072]{1,0:T(8,128)(2,1)S(1)}, u32[]{:S(2)}, u32[]{:S(2)}) %collective-permute-start.11) | collective-permute-done | bytes 245792 | tf_op jit(solution)/shard_map/ppermute | solution.py:239
  113.9 3.8 %collective-permute-done.9 = bf16[40,3072]{1,0:T(8,128)(2,1)S(1)} collective-permute-done((bf16[40,3072]{1,0:T(8,128)(2,1)S(1)}, bf16[40,3072]{1,0:T(8,128)(2,1)S(1)}, u32[]{:S(2)}, u32[]{:S(2)}) %collective-permute-start.9) | collective-permute-done | bytes 245792 | tf_op jit(solution)/shard_map/ppermute | solution.py:239
  117.8 2.3 collective-permute-start.10
  120.2 5.1 %collective-permute-start.12 = (bf16[80,3072]{1,0:T(8,128)(2,1)S(1)}, bf16[80,3072]{1,0:T(8,128)(2,1)S(1)}, u32[]{:S(2)}, u32[]{:S(2)}) collective-permute-start(bf16[80,3072]{1,0:T(8,128)(2,1)S(1)} %pad_maximum_fusion.1), channel_id=1, source_target_pairs={{0,384},{64,448},{128,0},{192,64},{256,128},{320,192},{384,256},{4... | collective-permute-start | bytes 1474568 | tf_op jit(solution)/shard_map/ppermute | solution.py:239
  125.3 4.5 %collective-permute-done.10.left_ref = bf16[80,3072]{1,0:T(8,128)(2,1)S(1)} collective-permute-done((bf16[80,3072]{1,0:T(8,128)(2,1)S(1)}, bf16[80,3072]{1,0:T(8,128)(2,1)S(1)}, u32[]{:S(2)}, u32[]{:S(2)}) %collective-permute-start.10) | collective-permute-done | bytes 491552 | tf_op jit(solution)/shard_map/ppermute | solution.py:239
  129.8 1.2 collective-permute-done.12.right_ref
  131.5 7.8 %collective-permute-start.13 = (bf16[80,3072]{1,0:T(8,128)(2,1)S(1)}, bf16[80,3072]{1,0:T(8,128)(2,1)S(1)}, u32[]{:S(2)}, u32[]{:S(2)}) collective-permute-start(bf16[80,3072]{1,0:T(8,128)(2,1)S(1)} %shard_map.132.refs_2_), channel_id=1, source_target_pairs={{0,128},{64,192},{128,256},{192,320},{256,384},{320,448},{384,0},{... | collective-permute-start | bytes 1474568 | tf_op jit(solution)/shard_map/ppermute | solution.py:239
  139.2 1.9 collective-permute-start.15
  141.2 10.6 %collective-permute-done.13.refs_4_ = bf16[80,3072]{1,0:T(8,128)(2,1)S(1)} collective-permute-done((bf16[80,3072]{1,0:T(8,128)(2,1)S(1)}, bf16[80,3072]{1,0:T(8,128)(2,1)S(1)}, u32[]{:S(2)}, u32[]{:S(2)}) %collective-permute-start.13) | collective-permute-done | bytes 491552 | tf_op jit(solution)/shard_map/ppermute | solution.py:239
  151.8 1.9 collective-permute-start.14
  153.7 26.7 %collective-permute-start.18 = (bf16[80,3072]{1,0:T(8,128)(2,1)S(1)}, bf16[80,3072]{1,0:T(8,128)(2,1)S(1)}, u32[]{:S(2)}, u32[]{:S(2)}) collective-permute-start(bf16[80,3072]{1,0:T(8,128)(2,1)S(1)} %shard_map.132.refs_2_), channel_id=1, source_target_pairs={{0,64},{64,0},{128,192},{192,128},{256,320},{320,256},{384,448},{4... | collective-permute-start | bytes 1474568 | tf_op jit(solution)/shard_map/ppermute | solution.py:235
  180.4 5.8 %collective-permute-start.16 = (bf16[40,3072]{1,0:T(8,128)(2,1)S(1)}, bf16[40,3072]{1,0:T(8,128)(2,1)S(1)}, u32[]{:S(2)}, u32[]{:S(2)}) collective-permute-start(bf16[40,3072]{1,0:T(8,128)(2,1)S(1)} %slice.62), channel_id=1, source_target_pairs={{0,384},{64,448},{128,0},{192,64},{256,128},{320,192},{384,256},{4... | collective-permute-start | bytes 737288 | tf_op jit(solution)/shard_map/ppermute | solution.py:239
  186.2 2.2 collective-permute-start.19
  188.4 2.1 collective-permute-start.20
  190.6 5.7 %collective-permute-done.16 = bf16[40,3072]{1,0:T(8,128)(2,1)S(1)} collective-permute-done((bf16[40,3072]{1,0:T(8,128)(2,1)S(1)}, bf16[40,3072]{1,0:T(8,128)(2,1)S(1)}, u32[]{:S(2)}, u32[]{:S(2)}) %collective-permute-start.16) | collective-permute-done | bytes 245792 | tf_op jit(solution)/shard_map/ppermute | solution.py:239
  196.3 2.5 %collective-permute-start.17 = (bf16[80,3072]{1,0:T(8,128)(2,1)S(1)}, bf16[80,3072]{1,0:T(8,128)(2,1)S(1)}, u32[]{:S(2)}, u32[]{:S(2)}) collective-permute-start(bf16[80,3072]{1,0:T(8,128)(2,1)S(1)} %constant_dynamic-update-slice_fusion.refs_1_), channel_id=1, source_target_pairs={{0,64},{64,0},{128,192},{192,128},{256,320},{320,256},{384,448},{4... | collective-permute-start | bytes 1474568 | tf_op jit(solution)/shard_map/ppermute | solution.py:235
  198.8 1.4 collective-permute-done.17.refs_5_
  200.3 3.2 %shard_map.133 = (bf16[8,80,896]{2,1,0:T(8,128)(2,1)S(1)}, bf16[640,2048]{1,0:T(8,128)(2,1)S(1)}) custom-call(s32[5]{0:T(128)S(1)} %stack.27.who_ref.refs_0_, bf16[80,3072]{1,0:T(8,128)(2,1)S(1)} %constant_dynamic-update-slice_fusion.refs_1_, bf16[80,3072]{1,0:T(8,128)(2,1)S(1)} %shard_map.132.refs_2_, bf16[80,3072]{1,0:T(8,128)(2,1)S(1)} %collective-permute-done.15.refs_3_, ...), custom_call_target="tpu_custom_call" | custom-call | tf_op jit(solution)/shard_map/pallas_call | solution.py:358
  203.5 21.7 %all_to_all.36.recv_ref = bf16[8,80,896]{2,1,0:T(8,128)(2,1)S(1)} all-to-all(bf16[8,80,896]{2,1,0:T(8,128)(2,1)S(1)} %get-tuple-element.34), channel_id=1, replica_groups={{0,1,16,17,32,33,48,49},{2,3,18,19,34,35,50,51},{4,5,20,21,36,37,52,53}..., dimensions={0} | all-to-all | bytes 2293760 | tf_op jit(solution)/shard_map/all_to_all | solution.py:271
  225.2 1.7 shard_map.134
  226.9 4.8 %all-to-all-start.4 = ((bf16[8,32,896]{2,1,0:T(8,128)(2,1)}), bf16[8,32,896]{2,1,0:T(8,128)(2,1)S(1)}, u32[]{:S(2)}, u32[]{:S(2)}) async-start(bf16[8,32,896]{2,1,0:T(8,128)(2,1)} %bitcast.12), calls=%async_computation.4 | async-start | bytes 917504 | tf_op jit(solution)/shard_map/all_to_all | solution.py:271
  231.7 3.3 %fusion.1 = bf16[1,448,1024]{2,1,0:T(8,128)(2,1)} fusion(bf16[640,448]{1,0:T(8,128)(2,1)S(1)} %copy-done.14, bf16[640,2048]{1,0:T(8,128)(2,1)} %copy-done.11), kind=kOutput, calls=%fused_computation.4 | convolution fusion | flops 587661312 | bytes 2801664 | tf_op jit(solution)/shard_map/dot_general | solution.py:22
  235.0 1.8 fusion
  236.8 9.0 %all-to-all-done.4.recv_ref = bf16[8,32,896]{2,1,0:T(8,128)(2,1)S(1)} async-done(((bf16[8,32,896]{2,1,0:T(8,128)(2,1)}), bf16[8,32,896]{2,1,0:T(8,128)(2,1)S(1)}, u32[]{:S(2)}, u32[]{:S(2)}) %all-to-all-start.4) | async-done | bytes 458784 | tf_op jit(solution)/shard_map/all_to_all | solution.py:271
  (60 shorter events, 9.8 us)
Async XLA Ops:
  0.6 10.9 %copy-start.10 = (bf16[32,448]{1,0:T(8,128)(2,1)S(1)}, bf16[32,448]{1,0:T(8,128)(2,1)}, u32[]{:S(2)}) copy-start(bf16[32,448]{1,0:T(8,128)(2,1)} %cot_ref.1) | copy-start | bytes 86020
  0.6 10.9 %copy-start.9 = (bf16[32,448]{1,0:T(8,128)(2,1)S(1)}, bf16[32,448]{1,0:T(8,128)(2,1)}, u32[]{:S(2)}) copy-start(bf16[32,448]{1,0:T(8,128)(2,1)} %tok_ref.1) | copy-start | bytes 86020
  1.6 41.9 %copy-start.8 = (f32[80,256]{1,0:T(8,128)S(1)}, f32[80,256]{1,0:T(8,128)}, u32[]{:S(2)}) copy-start(f32[80,256]{1,0:T(8,128)} %constant.53.clone.want_ref) | copy-start | bytes 245764
  2.4 18.0 %all-to-all-start = ((bf16[8,16,1408]{2,1,0:T(8,128)(2,1)}), bf16[8,16,1408]{2,1,0:T(8,128)(2,1)S(1)}, u32[]{:S(2)}, u32[]{:S(2)}) async-start(bf16[8,16,1408]{2,1,0:T(8,128)(2,1)} %broadcast_in_dim.9), calls=%async_computation | async-start | bytes 720896 | tf_op jit(solution)/shard_map/all_to_all | solution.py:271
  20.4 23.1 %all-to-all-start.1 = ((bf16[8,32,1024]{2,1,0:T(8,128)(2,1)}), bf16[8,32,1024]{2,1,0:T(8,128)(2,1)S(1)}, u32[]{:S(2)}, u32[]{:S(2)}) async-start(bf16[8,32,1024]{2,1,0:T(8,128)(2,1)} %shard_map.129), calls=%async_computation.1 | async-start | bytes 1048576 | tf_op jit(solution)/shard_map/all_to_all | solution.py:271
  24.0 58.5 %copy-start = (bf16[1,448,1024]{2,1,0:T(8,128)(2,1)S(1)}, bf16[1,448,1024]{2,1,0:T(8,128)(2,1)}, u32[]{:S(2)}) copy-start(bf16[1,448,1024]{2,1,0:T(8,128)(2,1)} %param.15) | copy-start | bytes 2752516
  24.0 58.5 %copy-start.1 = (bf16[1,448,1024]{2,1,0:T(8,128)(2,1)S(1)}, bf16[1,448,1024]{2,1,0:T(8,128)(2,1)}, u32[]{:S(2)}) copy-start(bf16[1,448,1024]{2,1,0:T(8,128)(2,1)} %param.16) | copy-start | bytes 2752516
  24.0 13.0 %collective-permute-start.2 = (bf16[128,1408]{1,0:T(8,128)(2,1)S(1)}, bf16[128,1408]{1,0:T(8,128)(2,1)S(1)}, u32[]{:S(2)}, u32[]{:S(2)}) collective-permute-start(bf16[128,1408]{1,0:T(8,128)(2,1)S(1)} %bitcast.27), channel_id=1, source_target_pairs={{0,48},{1,49},{2,50},{3,51},{4,52},{5,53},{6,54},{7,55},{8,56},{9,... | collective-permute-start | bytes 1081352 | tf_op jit(solution)/shard_map/ppermute | solution.py:282
  31.0 10.7 %collective-permute-start.1 = (bf16[128,1408]{1,0:T(8,128)(2,1)S(1)}, bf16[128,1408]{1,0:T(8,128)(2,1)S(1)}, u32[]{:S(2)}, u32[]{:S(2)}) collective-permute-start(bf16[128,1408]{1,0:T(8,128)(2,1)S(1)} %bitcast.28), channel_id=1, source_target_pairs={{0,16},{1,17},{2,18},{3,19},{4,20},{5,21},{6,22},{7,23},{8,24},{9,... | collective-permute-start | bytes 1081352 | tf_op jit(solution)/shard_map/ppermute | solution.py:282
  32.9 10.5 %collective-permute-start = (bf16[128,1408]{1,0:T(8,128)(2,1)S(1)}, bf16[128,1408]{1,0:T(8,128)(2,1)}, u32[]{:S(2)}, u32[]{:S(2)}) collective-permute-start(bf16[128,1408]{1,0:T(8,128)(2,1)S(1)} %bitcast.29), channel_id=1, source_target_pairs={{0,1},{1,0},{2,3},{3,2},{4,5},{5,4},{6,7},{7,6},{8,9},{9,8},{10,11... | collective-permute-start | bytes 1081352 | tf_op jit(solution)/shard_map/ppermute | solution.py:282
  37.0 0.8 copy-start.4
  41.7 0.7 copy-start.6
  44.8 1.0 copy-start.3
  45.9 36.6 %all-to-all-start.2 = ((bf16[8,80,896]{2,1,0:T(8,128)(2,1)}), bf16[8,80,896]{2,1,0:T(8,128)(2,1)S(1)}, u32[]{:S(2)}, u32[]{:S(2)}) async-start(bf16[8,80,896]{2,1,0:T(8,128)(2,1)} %copy-done.3), calls=%async_computation.2 | async-start | bytes 2293760 | tf_op jit(solution)/shard_map/all_to_all | solution.py:271
  50.4 20.5 %collective-permute-start.5 = (bf16[128,1408]{1,0:T(8,128)(2,1)}, bf16[128,1408]{1,0:T(8,128)(2,1)}, u32[]{:S(2)}, u32[]{:S(2)}) collective-permute-start(bf16[128,1408]{1,0:T(8,128)(2,1)} %collective-permute-done.t0), channel_id=1, source_target_pairs={{0,48},{1,49},{2,50},{3,51},{4,52},{5,53},{6,54},{7,55},{8,56},{9,... | collective-permute-start | bytes 1081352 | tf_op jit(solution)/shard_map/ppermute | solution.py:282
  55.0 26.3 %collective-permute-start.3 = (bf16[128,1408]{1,0:T(8,128)(2,1)}, bf16[128,1408]{1,0:T(8,128)(2,1)}, u32[]{:S(2)}, u32[]{:S(2)}) collective-permute-start(bf16[128,1408]{1,0:T(8,128)(2,1)} %collective-permute-done.t0), channel_id=1, source_target_pairs={{0,16},{1,17},{2,18},{3,19},{4,20},{5,21},{6,22},{7,23},{8,24},{9,... | collective-permute-start | bytes 1081352 | tf_op jit(solution)/shard_map/ppermute | solution.py:282
  56.9 24.4 %collective-permute-start.4 = (bf16[128,1408]{1,0:T(8,128)(2,1)}, bf16[128,1408]{1,0:T(8,128)(2,1)}, u32[]{:S(2)}, u32[]{:S(2)}) collective-permute-start(bf16[128,1408]{1,0:T(8,128)(2,1)} %copy-done.6), channel_id=1, source_target_pairs={{0,16},{1,17},{2,18},{3,19},{4,20},{5,21},{6,22},{7,23},{8,24},{9,... | collective-permute-start | bytes 1081352 | tf_op jit(solution)/shard_map/ppermute | solution.py:282
  71.0 11.6 %collective-permute-start.6 = (bf16[128,1408]{1,0:T(8,128)(2,1)}, bf16[128,1408]{1,0:T(8,128)(2,1)}, u32[]{:S(2)}, u32[]{:S(2)}) collective-permute-start(bf16[128,1408]{1,0:T(8,128)(2,1)} %collective-permute-done.5.t3), channel_id=1, source_target_pairs={{0,48},{1,49},{2,50},{3,51},{4,52},{5,53},{6,54},{7,55},{8,56},{9,... | collective-permute-start | bytes 1081352 | tf_op jit(solution)/shard_map/ppermute | solution.py:282
  82.5 1.2 copy-start.2
  83.7 1.0 copy-start.5
  84.7 1.0 copy-start.7
  90.2 18.7 %copy-start.13 = (bf16[640,448]{1,0:T(8,128)(2,1)}, bf16[640,448]{1,0:T(8,128)(2,1)S(1)}, u32[]{:S(2)}) copy-start(bf16[640,448]{1,0:T(8,128)(2,1)S(1)} %get-tuple-element.38) | copy-start | bytes 1720324
  90.2 6.5 %collective-permute-start.8 = (bf16[80,3072]{1,0:T(8,128)(2,1)S(1)}, bf16[80,3072]{1,0:T(8,128)(2,1)S(1)}, u32[]{:S(2)}, u32[]{:S(2)}) collective-permute-start(bf16[80,3072]{1,0:T(8,128)(2,1)S(1)} %get-tuple-element.32), channel_id=1, source_target_pairs={{0,64},{64,0},{128,192},{192,128},{256,320},{320,256},{384,448},{4... | collective-permute-start | bytes 1474568 | tf_op jit(solution)/shard_map/ppermute | solution.py:235
  94.8 13.8 %collective-permute-start.7 = (bf16[240,3072]{1,0:T(8,128)(2,1)S(1)}, bf16[240,3072]{1,0:T(8,128)(2,1)S(1)}, u32[]{:S(2)}, u32[]{:S(2)}) collective-permute-start(bf16[240,3072]{1,0:T(8,128)(2,1)S(1)} %get-tuple-element.30), channel_id=1, source_target_pairs={{0,64},{64,0},{128,192},{192,128},{256,320},{320,256},{384,448},{4... | collective-permute-start | bytes 4423688 | tf_op jit(solution)/shard_map/ppermute | solution.py:235
  96.9 17.0 %collective-permute-start.11 = (bf16[40,3072]{1,0:T(8,128)(2,1)S(1)}, bf16[40,3072]{1,0:T(8,128)(2,1)S(1)}, u32[]{:S(2)}, u32[]{:S(2)}) collective-permute-start(bf16[40,3072]{1,0:T(8,128)(2,1)S(1)} %get-tuple-element.44), channel_id=1, source_target_pairs={{0,384},{64,448},{128,0},{192,64},{256,128},{320,192},{384,256},{4... | collective-permute-start | bytes 737288 | tf_op jit(solution)/shard_map/ppermute | solution.py:239
  106.7 11.0 %collective-permute-start.9 = (bf16[40,3072]{1,0:T(8,128)(2,1)S(1)}, bf16[40,3072]{1,0:T(8,128)(2,1)S(1)}, u32[]{:S(2)}, u32[]{:S(2)}) collective-permute-start(bf16[40,3072]{1,0:T(8,128)(2,1)S(1)} %get-tuple-element.45), channel_id=1, source_target_pairs={{0,128},{64,192},{128,256},{192,320},{256,384},{320,448},{384,0},{... | collective-permute-start | bytes 737288 | tf_op jit(solution)/shard_map/ppermute | solution.py:239
  117.8 12.0 %collective-permute-start.10 = (bf16[80,3072]{1,0:T(8,128)(2,1)S(1)}, bf16[80,3072]{1,0:T(8,128)(2,1)S(1)}, u32[]{:S(2)}, u32[]{:S(2)}) collective-permute-start(bf16[80,3072]{1,0:T(8,128)(2,1)S(1)} %pad_maximum_fusion), channel_id=1, source_target_pairs={{0,128},{64,192},{128,256},{192,320},{256,384},{320,448},{384,0},{... | collective-permute-start | bytes 1474568 | tf_op jit(solution)/shard_map/ppermute | solution.py:239
  120.2 10.8 %collective-permute-start.12 = (bf16[80,3072]{1,0:T(8,128)(2,1)S(1)}, bf16[80,3072]{1,0:T(8,128)(2,1)S(1)}, u32[]{:S(2)}, u32[]{:S(2)}) collective-permute-start(bf16[80,3072]{1,0:T(8,128)(2,1)S(1)} %pad_maximum_fusion.1), channel_id=1, source_target_pairs={{0,384},{64,448},{128,0},{192,64},{256,128},{320,192},{384,256},{4... | collective-permute-start | bytes 1474568 | tf_op jit(solution)/shard_map/ppermute | solution.py:239
  131.5 20.3 %collective-permute-start.13 = (bf16[80,3072]{1,0:T(8,128)(2,1)S(1)}, bf16[80,3072]{1,0:T(8,128)(2,1)S(1)}, u32[]{:S(2)}, u32[]{:S(2)}) collective-permute-start(bf16[80,3072]{1,0:T(8,128)(2,1)S(1)} %shard_map.132.refs_2_), channel_id=1, source_target_pairs={{0,128},{64,192},{128,256},{192,320},{256,384},{320,448},{384,0},{... | collective-permute-start | bytes 1474568 | tf_op jit(solution)/shard_map/ppermute | solution.py:239
  139.2 41.2 %collective-permute-start.15 = (bf16[80,3072]{1,0:T(8,128)(2,1)S(1)}, bf16[80,3072]{1,0:T(8,128)(2,1)S(1)}, u32[]{:S(2)}, u32[]{:S(2)}) collective-permute-start(bf16[80,3072]{1,0:T(8,128)(2,1)S(1)} %shard_map.132.refs_2_), channel_id=1, source_target_pairs={{0,384},{64,448},{128,0},{192,64},{256,128},{320,192},{384,256},{4... | collective-permute-start | bytes 1474568 | tf_op jit(solution)/shard_map/ppermute | solution.py:239
  151.8 38.7 %collective-permute-start.14 = (bf16[40,3072]{1,0:T(8,128)(2,1)S(1)}, bf16[40,3072]{1,0:T(8,128)(2,1)S(1)}, u32[]{:S(2)}, u32[]{:S(2)}) collective-permute-start(bf16[40,3072]{1,0:T(8,128)(2,1)S(1)} %slice.61), channel_id=1, source_target_pairs={{0,128},{64,192},{128,256},{192,320},{256,384},{320,448},{384,0},{... | collective-permute-start | bytes 737288 | tf_op jit(solution)/shard_map/ppermute | solution.py:239
  153.7 45.1 %collective-permute-start.18 = (bf16[80,3072]{1,0:T(8,128)(2,1)S(1)}, bf16[80,3072]{1,0:T(8,128)(2,1)S(1)}, u32[]{:S(2)}, u32[]{:S(2)}) collective-permute-start(bf16[80,3072]{1,0:T(8,128)(2,1)S(1)} %shard_map.132.refs_2_), channel_id=1, source_target_pairs={{0,64},{64,0},{128,192},{192,128},{256,320},{320,256},{384,448},{4... | collective-permute-start | bytes 1474568 | tf_op jit(solution)/shard_map/ppermute | solution.py:235
  180.4 15.8 %collective-permute-start.16 = (bf16[40,3072]{1,0:T(8,128)(2,1)S(1)}, bf16[40,3072]{1,0:T(8,128)(2,1)S(1)}, u32[]{:S(2)}, u32[]{:S(2)}) collective-permute-start(bf16[40,3072]{1,0:T(8,128)(2,1)S(1)} %slice.62), channel_id=1, source_target_pairs={{0,384},{64,448},{128,0},{192,64},{256,128},{320,192},{384,256},{4... | collective-permute-start | bytes 737288 | tf_op jit(solution)/shard_map/ppermute | solution.py:239
  186.2 12.6 %collective-permute-start.19 = (bf16[80,3072]{1,0:T(8,128)(2,1)S(1)}, bf16[80,3072]{1,0:T(8,128)(2,1)S(1)}, u32[]{:S(2)}, u32[]{:S(2)}) collective-permute-start(bf16[80,3072]{1,0:T(8,128)(2,1)S(1)} %collective-permute-done.15.refs_3_), channel_id=1, source_target_pairs={{0,64},{64,0},{128,192},{192,128},{256,320},{320,256},{384,448},{4... | collective-permute-start | bytes 1474568 | tf_op jit(solution)/shard_map/ppermute | solution.py:235
  188.4 10.4 %collective-permute-start.20 = (bf16[80,3072]{1,0:T(8,128)(2,1)S(1)}, bf16[80,3072]{1,0:T(8,128)(2,1)S(1)}, u32[]{:S(2)}, u32[]{:S(2)}) collective-permute-start(bf16[80,3072]{1,0:T(8,128)(2,1)S(1)} %collective-permute-done.13.refs_4_), channel_id=1, source_target_pairs={{0,64},{64,0},{128,192},{192,128},{256,320},{320,256},{384,448},{4... | collective-permute-start | bytes 1474568 | tf_op jit(solution)/shard_map/ppermute | solution.py:235
  196.3 4.0 %collective-permute-start.17 = (bf16[80,3072]{1,0:T(8,128)(2,1)S(1)}, bf16[80,3072]{1,0:T(8,128)(2,1)S(1)}, u32[]{:S(2)}, u32[]{:S(2)}) collective-permute-start(bf16[80,3072]{1,0:T(8,128)(2,1)S(1)} %constant_dynamic-update-slice_fusion.refs_1_), channel_id=1, source_target_pairs={{0,64},{64,0},{128,192},{192,128},{256,320},{320,256},{384,448},{4... | collective-permute-start | bytes 1474568 | tf_op jit(solution)/shard_map/ppermute | solution.py:235
  203.5 23.4 %copy-start.11 = (bf16[640,2048]{1,0:T(8,128)(2,1)}, bf16[640,2048]{1,0:T(8,128)(2,1)S(1)}, u32[]{:S(2)}) copy-start(bf16[640,2048]{1,0:T(8,128)(2,1)S(1)} %get-tuple-element.39) | copy-start | bytes 7864324
  225.2 6.5 %copy-start.14 = (bf16[640,448]{1,0:T(8,128)(2,1)S(1)}, bf16[640,448]{1,0:T(8,128)(2,1)}, u32[]{:S(2)}) copy-start(bf16[640,448]{1,0:T(8,128)(2,1)} %copy-done.13) | copy-start | bytes 1720324
  226.9 18.9 %all-to-all-start.4 = ((bf16[8,32,896]{2,1,0:T(8,128)(2,1)}), bf16[8,32,896]{2,1,0:T(8,128)(2,1)S(1)}, u32[]{:S(2)}, u32[]{:S(2)}) async-start(bf16[8,32,896]{2,1,0:T(8,128)(2,1)} %bitcast.12), calls=%async_computation.4 | async-start | bytes 917504 | tf_op jit(solution)/shard_map/all_to_all | solution.py:271
  231.7 3.3 %copy-start.12 = (bf16[640,2048]{1,0:T(8,128)(2,1)S(1)}, bf16[640,2048]{1,0:T(8,128)(2,1)}, u32[]{:S(2)}) copy-start(bf16[640,2048]{1,0:T(8,128)(2,1)} %copy-done.11) | copy-start | bytes 7864324

commit v6 on v5

--- a/solution.py
+++ b/solution.py
@@ -22,11 +22,12 @@
     return lax.dot_general(a, b, dims, preferred_element_type=F32)
 
 
-def call(kernel, outs, scratch=(), scalars=0, operands=0, megabytes=32):
+def call(kernel, outs, scratch=(), scalars=0, left=0, operands=0, megabytes=12):
     def of(shape, dtype=BF):
         return jax.ShapeDtypeStruct(shape, dtype)
 
     specs = [pl.BlockSpec(memory_space=pltpu.SMEM)] * scalars
+    specs += [pl.BlockSpec(memory_space=pltpu.HBM)] * left
     specs += [pl.BlockSpec(memory_space=pltpu.VMEM)] * operands
     return pl.pallas_call(
         kernel,
@@ -102,14 +103,35 @@
     return half * 4 + lax.rem(h + (2, 0, 1, 3)[p % 4], 4)
 
 
+def restore_kernel(grid, who_ref, *refs):
+    nx, ny, nz = grid
+    *blocks, restored_ref, saved_ref, sems = refs
+    feat = restored_ref.shape[2]
+    n = saved_ref.shape[1] // ny
+
+    @pl.when(who_ref[0] == 1)
+    def _():
+        my_x, my_z = who_ref[3], who_ref[4]
+        copies = [pltpu.make_async_copy(b, saved_ref.at[i], sems.at[i]) for i, b in enumerate(blocks)]
+        for copy in copies:
+            copy.start()
+        for i, copy in enumerate(copies):
+            copy.wait()
+            x = lax.rem(my_x - i % nx + nx, nx)
+            z = my_z if i < nx else 1 - my_z
+            for y in range(ny):
+                to = pl.ds(pl.multiple_of(((x * ny + y) * nz + z) * n, n), n)
+                for m in range(3):
+                    restored_ref[m, to, :] = saved_ref[i, y * n : (y + 1) * n, m * feat : (m + 1) * feat]
+
+
 def products_kernel(
-    grid, who_ref, recv_ref, s0, t0, s1, t1, s2, t2, s3, t3, gate_ref, up_ref, down_ref,
-    rows_ref, far_ref, rest_ref, far_out_ref, rest_out_ref, restored_ref, grads_ref,
+    who_ref, recv_ref, restored_ref, gate_ref, up_ref, down_ref,
+    rows_ref, far_ref, rest_ref, far_out_ref, rest_out_ref, grads_ref,
 ):
-    nx, ny, nz = grid
     feat, ff = gate_ref.shape
     chunk = far_ref.shape[0]
-    target, h, c, my_x, my_z = (who_ref[i] for i in range(5))
+    target, h, c = who_ref[0], who_ref[1], who_ref[2]
     for p in range(8):
         g = chunk_at(h, c, p)
         rows_ref[p * chunk : (p + 1) * chunk, :] = recv_ref[g, :, 0:feat]
@@ -136,16 +158,6 @@
 
     @pl.when(target == 1)
     def _():
-        n = s0.shape[0] // ny
-        for k, sources in enumerate(((s0, t0), (s1, t1), (s2, t2), (s3, t3))):
-            for other in range(nz):
-                x = lax.rem(my_x - k + nx, nx)
-                z = 1 - my_z if other else my_z
-                for y in range(ny):
-                    to = pl.ds(pl.multiple_of(((x * ny + y) * nz + z) * n, n), n)
-                    for m in range(3):
-                        restored_ref[m, to, :] = sources[other][y * n : (y + 1) * n, m * feat : (m + 1) * feat]
-
         @pl.loop(0, tiles)
         def _(j):
             at = pl.ds(pl.multiple_of(j * TILE, TILE), TILE)
@@ -307,13 +319,10 @@
     )
     first, saved = lax.optimization_barrier((first, saved))
     other_z = step(saved, 0, 1)
-    before, after = step(saved, 1, 0), step(saved, -1, 0)
+    along_x = [step(saved, k, 0) for k in range(1, nx)]
     first = exchange(first, along_y)
-    first, other_z, before, after = lax.optimization_barrier((first, other_z, before, after))
-    before_z, after_z = step(other_z, 1, 0), step(other_z, -1, 0)
-    blocks = (
-        saved, other_z, before, before_z, step(before, 1, 0), step(after_z, -1, 0), after, after_z,
-    )
+    first, other_z, along_x = lax.optimization_barrier((first, other_z, along_x))
+    blocks = [saved, *along_x, other_z, step(other_z, 1, 0), step(along_x[1], 0, 1), step(other_z, 3, 0)]
 
     out_rows, seen = ny * capacity, ny * tok
     row, col = np.arange(out_rows)[:, None], np.arange(seen)[None, :]
@@ -325,17 +334,25 @@
 
     w_gate, w_up, w_down = gate_weight[0], up_weight[0], jnp.transpose(down_weight[0])
     wide = 3 * ff
-    rows, far, rest, far_out, rest_out, restored = call(
-        functools.partial(products_kernel, grid),
+    (restored,) = call(
+        functools.partial(restore_kernel, grid),
+        [(3, ff, feat)],
+        scratch=[pltpu.VMEM((8, *saved.shape), BF), pltpu.SemaphoreType.DMA((8,))],
+        scalars=1,
+        left=8,
+        megabytes=52,
+    )(who, *blocks)
+    rows, far, rest, far_out, rest_out = call(
+        products_kernel,
         [
             (8 * chunk, feat), (chunk, wide), (3 * chunk, wide),
-            (chunk, wide), (3 * chunk, wide), (3, ff, feat),
+            (chunk, wide), (3 * chunk, wide),
         ],
         scratch=[pltpu.VMEM((8 * chunk, feat), BF)],
         scalars=1,
-        operands=12,
-        megabytes=40,
-    )(who, recv, *blocks, w_gate, w_up, w_down)
+        operands=5,
+        megabytes=14,
+    )(who, recv, restored, w_gate, w_up, w_down)
 
     mid = chunk // 2
     far = add(far, core_swap(far_out))
@@ -365,7 +382,7 @@
         ],
         scalars=1,
         operands=12,
-        megabytes=40,
+        megabytes=14,
     )(who, *mine, *other, w_gate, w_up, w_down, restored)
 
     out = exchange(out.reshape(nxz, out_rows, 2 * feat), along_xz)

time: 248 us -> 251 us (1.012)
  waiting for transfers between devices: 71.2 us -> 75.4 us
  starting transfers between devices: 124 us -> 120 us
    ppermute x6, starting transfers between devices: 40 us -> 35.9 us  [core_swap(): return lax.ppermute(x, 'dp', [(i, i ^ 1) for i in range(8)])]
    ppermute x7, waiting for transfers between devices: 22.3 us -> 26 us  [step(): return lax.ppermute(v, 'expert', pairs)]
    ppermute x8, starting transfers between devices: 36.4 us -> 39 us  [shift(): lax.ppermute(x, 'dp', [(2 * h + c, 2 * ((h + k) % 4) + c) for h in range(...]
    pallas_call x1 -> x2, Pallas kernels: 4.5 us -> 5.86 us  [the longest x1 3.62 us: body(): call(products_kernel, [(8 * chunk, feat), (chunk, wide), (3 * chunk, wide...]
    unnamed x33 -> x35, local copies, waits for them, and re-layouts: 7.24 us -> 7.35 us
  transfers between devices with their start and end apart: 25 -> 25, of which waited for: 14 -> 13; matrix products, arithmetic and copies ran while one was open for 3% -> 3% of each run, Pallas kernels for 0% -> 1%
where the time goes in v6:
time: 251 us; the launch traced here: 250 us
  starting transfers between devices  120 us (48%)
  waiting for transfers between devices  75.4 us (30%)
  blocking collectives  22.3 us (9%)
  Pallas kernels  15.5 us (6%)
  local copies, waits for them, and re-layouts  9.28 us (4%)
  matrix products  5.11 us (2%)
    ppermute x8, starting transfers between devices, shift(): lax.ppermute(x, 'dp', [(2 * h + c, 2 * ((h + k) % 4) + c) for h in range(...  39 us
    ppermute x6, starting transfers between devices, core_swap(): return lax.ppermute(x, 'dp', [(i, i ^ 1) for i in range(8)])  35.9 us
    ppermute x8, waiting for transfers between devices, shift(): lax.ppermute(x, 'dp', [(2 * h + c, 2 * ((h + k) % 4) + c) for h in range(...  31.4 us
    ppermute x7, waiting for transfers between devices, step(): return lax.ppermute(v, 'expert', pairs)  26 us
    ppermute x7, starting transfers between devices, step(): return lax.ppermute(v, 'expert', pairs)  25.3 us
    all_to_all x1, blocking collectives, exchange(): lax.all_to_all(flat, 'expert', 0, 0, axis_index_groups=groups, tiled=True)  22.3 us
    all_to_all x4, starting transfers between devices, exchange(): lax.all_to_all(flat, 'expert', 0, 0, axis_index_groups=groups, tiled=True)  19.3 us
    all_to_all x4, waiting for transfers between devices, exchange(): lax.all_to_all(flat, 'expert', 0, 0, axis_index_groups=groups, tiled=True)  16.6 us
  transfers between devices with their start and end apart: 25, of which 13 were waited for; matrix products, arithmetic and copies ran while one was open for 3% of the time, Pallas kernels for 1%

profile of v6, /device:TPU:1, one launch (start us, length us, event | category | flops | bytes accessed | tf_op | source)
XLA Modules:
  0.0 249.5 jit_solution(16259665905552937752)
XLA Ops:
  2.4 7.7 %all-to-all-start = ((bf16[8,16,1408]{2,1,0:T(8,128)(2,1)}), bf16[8,16,1408]{2,1,0:T(8,128)(2,1)S(1)}, u32[]{:S(2)}, u32[]{:S(2)}) async-start(bf16[8,16,1408]{2,1,0:T(8,128)(2,1)} %broadcast_in_dim.9), calls=%async_computation | async-start | bytes 720896 | tf_op jit(solution)/shard_map/all_to_all | solution.py:283
  11.6 1.2 shard_map.129
  12.8 7.6 %all-to-all-done = bf16[8,16,1408]{2,1,0:T(8,128)(2,1)S(1)} async-done(((bf16[8,16,1408]{2,1,0:T(8,128)(2,1)}), bf16[8,16,1408]{2,1,0:T(8,128)(2,1)S(1)}, u32[]{:S(2)}, u32[]{:S(2)}) %all-to-all-start) | async-done | bytes 360480 | tf_op jit(solution)/shard_map/all_to_all | solution.py:283
  20.4 3.6 %all-to-all-start.1 = ((bf16[8,32,1024]{2,1,0:T(8,128)(2,1)}), bf16[8,32,1024]{2,1,0:T(8,128)(2,1)S(1)}, u32[]{:S(2)}, u32[]{:S(2)}) async-start(bf16[8,32,1024]{2,1,0:T(8,128)(2,1)} %shard_map.129), calls=%async_computation.1 | async-start | bytes 1048576 | tf_op jit(solution)/shard_map/all_to_all | solution.py:283
  24.0 6.9 %collective-permute-start.3 = (bf16[128,1408]{1,0:T(8,128)(2,1)S(1)}, bf16[128,1408]{1,0:T(8,128)(2,1)S(1)}, u32[]{:S(2)}, u32[]{:S(2)}) collective-permute-start(bf16[128,1408]{1,0:T(8,128)(2,1)S(1)} %bitcast.27), channel_id=1, source_target_pairs={{0,48},{1,49},{2,50},{3,51},{4,52},{5,53},{6,54},{7,55},{8,56},{9,... | collective-permute-start | bytes 1081352 | tf_op jit(solution)/shard_map/ppermute | solution.py:294
  30.9 2.4 collective-permute-start.2
  33.3 2.5 %collective-permute-start.1 = (bf16[128,1408]{1,0:T(8,128)(2,1)S(1)}, bf16[128,1408]{1,0:T(8,128)(2,1)S(1)}, u32[]{:S(2)}, u32[]{:S(2)}) collective-permute-start(bf16[128,1408]{1,0:T(8,128)(2,1)S(1)} %bitcast.29), channel_id=1, source_target_pairs={{0,16},{1,17},{2,18},{3,19},{4,20},{5,21},{6,22},{7,23},{8,24},{9,... | collective-permute-start | bytes 1081352 | tf_op jit(solution)/shard_map/ppermute | solution.py:294
  35.8 4.0 %collective-permute-start = (bf16[128,1408]{1,0:T(8,128)(2,1)S(1)}, bf16[128,1408]{1,0:T(8,128)(2,1)}, u32[]{:S(2)}, u32[]{:S(2)}) collective-permute-start(bf16[128,1408]{1,0:T(8,128)(2,1)S(1)} %bitcast.30), channel_id=1, source_target_pairs={{0,1},{1,0},{2,3},{3,2},{4,5},{5,4},{6,7},{7,6},{8,9},{9,8},{10,11... | collective-permute-start | bytes 1081352 | tf_op jit(solution)/shard_map/ppermute | solution.py:294
  39.9 2.2 collective-permute-done.2.refs_2_
  42.0 10.2 %collective-permute-done.1.refs_1_ = bf16[128,1408]{1,0:T(8,128)(2,1)S(1)} collective-permute-done((bf16[128,1408]{1,0:T(8,128)(2,1)S(1)}, bf16[128,1408]{1,0:T(8,128)(2,1)S(1)}, u32[]{:S(2)}, u32[]{:S(2)}) %collective-permute-start.1) | collective-permute-done | bytes 360480 | tf_op jit(solution)/shard_map/ppermute | solution.py:294
  53.0 2.4 shard_map.130
  55.4 3.6 %all-to-all-start.2 = ((bf16[8,80,896]{2,1,0:T(8,128)(2,1)}), bf16[8,80,896]{2,1,0:T(8,128)(2,1)S(1)}, u32[]{:S(2)}, u32[]{:S(2)}) async-start(bf16[8,80,896]{2,1,0:T(8,128)(2,1)} %get-tuple-element.25), calls=%async_computation.2 | async-start | bytes 2293760 | tf_op jit(solution)/shard_map/all_to_all | solution.py:283
  59.0 4.0 %collective-permute-start.5 = (bf16[128,1408]{1,0:T(8,128)(2,1)}, bf16[128,1408]{1,0:T(8,128)(2,1)}, u32[]{:S(2)}, u32[]{:S(2)}) collective-permute-start(bf16[128,1408]{1,0:T(8,128)(2,1)} %collective-permute-done.2.refs_2_), channel_id=1, source_target_pairs={{0,1},{1,0},{2,3},{3,2},{4,5},{5,4},{6,7},{7,6},{8,9},{9,8},{10,11... | collective-permute-start | bytes 1081352 | tf_op jit(solution)/shard_map/ppermute | solution.py:294
  62.9 3.6 %collective-permute-start.6 = (bf16[128,1408]{1,0:T(8,128)(2,1)}, bf16[128,1408]{1,0:T(8,128)(2,1)}, u32[]{:S(2)}, u32[]{:S(2)}) collective-permute-start(bf16[128,1408]{1,0:T(8,128)(2,1)} %collective-permute-done.refs_4_), channel_id=1, source_target_pairs={{0,48},{1,49},{2,50},{3,51},{4,52},{5,53},{6,54},{7,55},{8,56},{9,... | collective-permute-start | bytes 1081352 | tf_op jit(solution)/shard_map/ppermute | solution.py:294
  66.6 1.9 collective-permute-start.4
  69.3 12.9 %collective-permute-done.5.refs_6_ = bf16[128,1408]{1,0:T(8,128)(2,1)} collective-permute-done((bf16[128,1408]{1,0:T(8,128)(2,1)}, bf16[128,1408]{1,0:T(8,128)(2,1)}, u32[]{:S(2)}, u32[]{:S(2)}) %collective-permute-start.5) | collective-permute-done | bytes 360480 | tf_op jit(solution)/shard_map/ppermute | solution.py:294
  84.9 2.2 shard_map.131.restored_ref.refs_12_
  87.2 1.9 copy-done
  89.0 1.2 copy-done.4
  90.2 3.6 %shard_map.132 = (bf16[640,448]{1,0:T(8,128)(2,1)S(1)}, bf16[80,3072]{1,0:T(8,128)(2,1)S(1)}, bf16[240,3072]{1,0:T(8,128)(2,1)S(1)}, bf16[80,3072]{1,0:T(8,128)(2,1)S(1)}, bf16[240,3072]{1,0:T(8,128)(2,1)S(1)}) custom-call(s32[5]{0:T(128)S(1)} %stack.27.who_ref.refs_0_, bf16[8,80,896]{2,1,0:T(8,128)(2,1)S(1)} %all-to-all-done.2.recv_ref, ...), custom_call_target="tpu_custom_call" | custom-call | tf_op jit(solution)/shard_map/pallas_call | solution.py:345
  93.9 2.9 %collective-permute-start.8 = (bf16[80,3072]{1,0:T(8,128)(2,1)S(1)}, bf16[80,3072]{1,0:T(8,128)(2,1)S(1)}, u32[]{:S(2)}, u32[]{:S(2)}) collective-permute-start(bf16[80,3072]{1,0:T(8,128)(2,1)S(1)} %get-tuple-element.33), channel_id=1, source_target_pairs={{0,64},{64,0},{128,192},{192,128},{256,320},{320,256},{384,448},{4... | collective-permute-start | bytes 1474568 | tf_op jit(solution)/shard_map/ppermute | solution.py:247
  96.8 1.9 collective-permute-start.7
  98.9 10.8 %collective-permute-start.11 = (bf16[40,3072]{1,0:T(8,128)(2,1)S(1)}, bf16[40,3072]{1,0:T(8,128)(2,1)S(1)}, u32[]{:S(2)}, u32[]{:S(2)}) collective-permute-start(bf16[40,3072]{1,0:T(8,128)(2,1)S(1)} %get-tuple-element.44), channel_id=1, source_target_pairs={{0,384},{64,448},{128,0},{192,64},{256,128},{320,192},{384,256},{4... | collective-permute-start | bytes 737288 | tf_op jit(solution)/shard_map/ppermute | solution.py:251
  109.7 1.9 collective-permute-start.9
  112.0 4.0 %collective-permute-done.11 = bf16[40,3072]{1,0:T(8,128)(2,1)S(1)} collective-permute-done((bf16[40,3072]{1,0:T(8,128)(2,1)S(1)}, bf16[40,3072]{1,0:T(8,128)(2,1)S(1)}, u32[]{:S(2)}, u32[]{:S(2)}) %collective-permute-start.11) | collective-permute-done | bytes 245792 | tf_op jit(solution)/shard_map/ppermute | solution.py:251
  116.0 5.1 %collective-permute-done.9 = bf16[40,3072]{1,0:T(8,128)(2,1)S(1)} collective-permute-done((bf16[40,3072]{1,0:T(8,128)(2,1)S(1)}, bf16[40,3072]{1,0:T(8,128)(2,1)S(1)}, u32[]{:S(2)}, u32[]{:S(2)}) %collective-permute-start.9) | collective-permute-done | bytes 245792 | tf_op jit(solution)/shard_map/ppermute | solution.py:251
  121.3 2.0 collective-permute-start.10
  123.4 5.4 %collective-permute-start.12 = (bf16[80,3072]{1,0:T(8,128)(2,1)S(1)}, bf16[80,3072]{1,0:T(8,128)(2,1)S(1)}, u32[]{:S(2)}, u32[]{:S(2)}) collective-permute-start(bf16[80,3072]{1,0:T(8,128)(2,1)S(1)} %pad_maximum_fusion.1), channel_id=1, source_target_pairs={{0,384},{64,448},{128,0},{192,64},{256,128},{320,192},{384,256},{4... | collective-permute-start | bytes 1474568 | tf_op jit(solution)/shard_map/ppermute | solution.py:251
  128.7 4.4 %collective-permute-done.10.left_ref = bf16[80,3072]{1,0:T(8,128)(2,1)S(1)} collective-permute-done((bf16[80,3072]{1,0:T(8,128)(2,1)S(1)}, bf16[80,3072]{1,0:T(8,128)(2,1)S(1)}, u32[]{:S(2)}, u32[]{:S(2)}) %collective-permute-start.10) | collective-permute-done | bytes 491552 | tf_op jit(solution)/shard_map/ppermute | solution.py:251
  133.1 1.4 collective-permute-done.12.right_ref
  134.9 9.1 %collective-permute-start.13 = (bf16[80,3072]{1,0:T(8,128)(2,1)S(1)}, bf16[80,3072]{1,0:T(8,128)(2,1)S(1)}, u32[]{:S(2)}, u32[]{:S(2)}) collective-permute-start(bf16[80,3072]{1,0:T(8,128)(2,1)S(1)} %shard_map.133.refs_2_), channel_id=1, source_target_pairs={{0,128},{64,192},{128,256},{192,320},{256,384},{320,448},{384,0},{... | collective-permute-start | bytes 1474568 | tf_op jit(solution)/shard_map/ppermute | solution.py:251
  144.1 1.9 collective-permute-start.15
  146.0 8.7 %collective-permute-done.13.refs_4_ = bf16[80,3072]{1,0:T(8,128)(2,1)S(1)} collective-permute-done((bf16[80,3072]{1,0:T(8,128)(2,1)S(1)}, bf16[80,3072]{1,0:T(8,128)(2,1)S(1)}, u32[]{:S(2)}, u32[]{:S(2)}) %collective-permute-start.13) | collective-permute-done | bytes 491552 | tf_op jit(solution)/shard_map/ppermute | solution.py:251
  154.7 3.5 %collective-permute-start.14 = (bf16[40,3072]{1,0:T(8,128)(2,1)S(1)}, bf16[40,3072]{1,0:T(8,128)(2,1)S(1)}, u32[]{:S(2)}, u32[]{:S(2)}) collective-permute-start(bf16[40,3072]{1,0:T(8,128)(2,1)S(1)} %slice.61), channel_id=1, source_target_pairs={{0,128},{64,192},{128,256},{192,320},{256,384},{320,448},{384,0},{... | collective-permute-start | bytes 737288 | tf_op jit(solution)/shard_map/ppermute | solution.py:251
  158.2 24.4 %collective-permute-start.18 = (bf16[80,3072]{1,0:T(8,128)(2,1)S(1)}, bf16[80,3072]{1,0:T(8,128)(2,1)S(1)}, u32[]{:S(2)}, u32[]{:S(2)}) collective-permute-start(bf16[80,3072]{1,0:T(8,128)(2,1)S(1)} %shard_map.133.refs_2_), channel_id=1, source_target_pairs={{0,64},{64,0},{128,192},{192,128},{256,320},{320,256},{384,448},{4... | collective-permute-start | bytes 1474568 | tf_op jit(solution)/shard_map/ppermute | solution.py:247
  182.7 4.3 %collective-permute-start.16 = (bf16[40,3072]{1,0:T(8,128)(2,1)S(1)}, bf16[40,3072]{1,0:T(8,128)(2,1)S(1)}, u32[]{:S(2)}, u32[]{:S(2)}) collective-permute-start(bf16[40,3072]{1,0:T(8,128)(2,1)S(1)} %slice.62), channel_id=1, source_target_pairs={{0,384},{64,448},{128,0},{192,64},{256,128},{320,192},{384,256},{4... | collective-permute-start | bytes 737288 | tf_op jit(solution)/shard_map/ppermute | solution.py:251
  187.0 2.2 collective-permute-start.19
  189.2 2.1 collective-permute-start.20
  191.4 7.8 %collective-permute-done.16 = bf16[40,3072]{1,0:T(8,128)(2,1)S(1)} collective-permute-done((bf16[40,3072]{1,0:T(8,128)(2,1)S(1)}, bf16[40,3072]{1,0:T(8,128)(2,1)S(1)}, u32[]{:S(2)}, u32[]{:S(2)}) %collective-permute-start.16) | collective-permute-done | bytes 245792 | tf_op jit(solution)/shard_map/ppermute | solution.py:251
  199.2 2.3 collective-permute-start.17
  201.5 1.4 collective-permute-done.17.refs_5_
  203.0 3.2 %shard_map.134 = (bf16[8,80,896]{2,1,0:T(8,128)(2,1)S(1)}, bf16[640,2048]{1,0:T(8,128)(2,1)S(1)}) custom-call(s32[5]{0:T(128)S(1)} %stack.27.who_ref.refs_0_, bf16[80,3072]{1,0:T(8,128)(2,1)S(1)} %constant_dynamic-update-slice_fusion.refs_1_, bf16[80,3072]{1,0:T(8,128)(2,1)S(1)} %shard_map.133.refs_2_, bf16[80,3072]{1,0:T(8,128)(2,1)S(1)} %collective-permute-done.15.refs_3_, ...), custom_call_target="tpu_custom_call" | custom-call | tf_op jit(solution)/shard_map/pallas_call | solution.py:375
  206.2 22.3 %all_to_all.36.recv_ref = bf16[8,80,896]{2,1,0:T(8,128)(2,1)S(1)} all-to-all(bf16[8,80,896]{2,1,0:T(8,128)(2,1)S(1)} %get-tuple-element.34), channel_id=1, replica_groups={{0,1,16,17,32,33,48,49},{2,3,18,19,34,35,50,51},{4,5,20,21,36,37,52,53}..., dimensions={0} | all-to-all | bytes 2293760 | tf_op jit(solution)/shard_map/all_to_all | solution.py:283
  228.5 1.7 shard_map.135
  230.1 4.5 %all-to-all-start.4 = ((bf16[8,32,896]{2,1,0:T(8,128)(2,1)}), bf16[8,32,896]{2,1,0:T(8,128)(2,1)S(1)}, u32[]{:S(2)}, u32[]{:S(2)}) async-start(bf16[8,32,896]{2,1,0:T(8,128)(2,1)} %bitcast.12), calls=%async_computation.4 | async-start | bytes 917504 | tf_op jit(solution)/shard_map/all_to_all | solution.py:283
  234.7 3.3 %fusion.1 = bf16[1,448,1024]{2,1,0:T(8,128)(2,1)} fusion(bf16[640,448]{1,0:T(8,128)(2,1)S(1)} %copy-done.15, bf16[640,2048]{1,0:T(8,128)(2,1)} %copy-done.12), kind=kOutput, calls=%fused_computation.4 | convolution fusion | flops 587661312 | bytes 2801664 | tf_op jit(solution)/shard_map/dot_general | solution.py:22
  238.0 1.8 fusion
  239.8 9.0 %all-to-all-done.4.recv_ref = bf16[8,32,896]{2,1,0:T(8,128)(2,1)S(1)} async-done(((bf16[8,32,896]{2,1,0:T(8,128)(2,1)}), bf16[8,32,896]{2,1,0:T(8,128)(2,1)S(1)}, u32[]{:S(2)}, u32[]{:S(2)}) %all-to-all-start.4) | async-done | bytes 458784 | tf_op jit(solution)/shard_map/all_to_all | solution.py:283
  (63 shorter events, 8.7 us)
Async XLA Ops:
  0.6 10.9 %copy-start.11 = (bf16[32,448]{1,0:T(8,128)(2,1)S(1)}, bf16[32,448]{1,0:T(8,128)(2,1)}, u32[]{:S(2)}) copy-start(bf16[32,448]{1,0:T(8,128)(2,1)} %cot_ref.1) | copy-start | bytes 86020
  0.6 10.9 %copy-start.10 = (bf16[32,448]{1,0:T(8,128)(2,1)S(1)}, bf16[32,448]{1,0:T(8,128)(2,1)}, u32[]{:S(2)}) copy-start(bf16[32,448]{1,0:T(8,128)(2,1)} %tok_ref.1) | copy-start | bytes 86020
  1.6 51.4 %copy-start.9 = (f32[80,256]{1,0:T(8,128)S(1)}, f32[80,256]{1,0:T(8,128)}, u32[]{:S(2)}) copy-start(f32[80,256]{1,0:T(8,128)} %constant.53.clone.want_ref) | copy-start | bytes 245764
  2.4 18.0 %all-to-all-start = ((bf16[8,16,1408]{2,1,0:T(8,128)(2,1)}), bf16[8,16,1408]{2,1,0:T(8,128)(2,1)S(1)}, u32[]{:S(2)}, u32[]{:S(2)}) async-start(bf16[8,16,1408]{2,1,0:T(8,128)(2,1)} %broadcast_in_dim.9), calls=%async_computation | async-start | bytes 720896 | tf_op jit(solution)/shard_map/all_to_all | solution.py:283
  20.4 32.6 %all-to-all-start.1 = ((bf16[8,32,1024]{2,1,0:T(8,128)(2,1)}), bf16[8,32,1024]{2,1,0:T(8,128)(2,1)S(1)}, u32[]{:S(2)}, u32[]{:S(2)}) async-start(bf16[8,32,1024]{2,1,0:T(8,128)(2,1)} %shard_map.129), calls=%async_computation.1 | async-start | bytes 1048576 | tf_op jit(solution)/shard_map/all_to_all | solution.py:283
  24.0 15.9 %collective-permute-start.3 = (bf16[128,1408]{1,0:T(8,128)(2,1)S(1)}, bf16[128,1408]{1,0:T(8,128)(2,1)S(1)}, u32[]{:S(2)}, u32[]{:S(2)}) collective-permute-start(bf16[128,1408]{1,0:T(8,128)(2,1)S(1)} %bitcast.27), channel_id=1, source_target_pairs={{0,48},{1,49},{2,50},{3,51},{4,52},{5,53},{6,54},{7,55},{8,56},{9,... | collective-permute-start | bytes 1081352 | tf_op jit(solution)/shard_map/ppermute | solution.py:294
  30.9 11.1 %collective-permute-start.2 = (bf16[128,1408]{1,0:T(8,128)(2,1)S(1)}, bf16[128,1408]{1,0:T(8,128)(2,1)}, u32[]{:S(2)}, u32[]{:S(2)}) collective-permute-start(bf16[128,1408]{1,0:T(8,128)(2,1)S(1)} %bitcast.28), channel_id=1, source_target_pairs={{0,32},{1,33},{2,34},{3,35},{4,36},{5,37},{6,38},{7,39},{8,40},{9,... | collective-permute-start | bytes 1081352 | tf_op jit(solution)/shard_map/ppermute | solution.py:294
  33.3 18.9 %collective-permute-start.1 = (bf16[128,1408]{1,0:T(8,128)(2,1)S(1)}, bf16[128,1408]{1,0:T(8,128)(2,1)S(1)}, u32[]{:S(2)}, u32[]{:S(2)}) collective-permute-start(bf16[128,1408]{1,0:T(8,128)(2,1)S(1)} %bitcast.29), channel_id=1, source_target_pairs={{0,16},{1,17},{2,18},{3,19},{4,20},{5,21},{6,22},{7,23},{8,24},{9,... | collective-permute-start | bytes 1081352 | tf_op jit(solution)/shard_map/ppermute | solution.py:294
  35.8 17.2 %collective-permute-start = (bf16[128,1408]{1,0:T(8,128)(2,1)S(1)}, bf16[128,1408]{1,0:T(8,128)(2,1)}, u32[]{:S(2)}, u32[]{:S(2)}) collective-permute-start(bf16[128,1408]{1,0:T(8,128)(2,1)S(1)} %bitcast.30), channel_id=1, source_target_pairs={{0,1},{1,0},{2,3},{3,2},{4,5},{5,4},{6,7},{7,6},{8,9},{9,8},{10,11... | collective-permute-start | bytes 1081352 | tf_op jit(solution)/shard_map/ppermute | solution.py:294
  39.8 15.5 %copy-start.5 = (bf16[128,1408]{1,0:T(8,128)(2,1)}, bf16[128,1408]{1,0:T(8,128)(2,1)S(1)}, u32[]{:S(2)}) copy-start(bf16[128,1408]{1,0:T(8,128)(2,1)S(1)} %collective-permute-done.3.refs_3_) | copy-start | bytes 1081348
  52.3 0.7 copy-start.7
  55.4 31.7 %all-to-all-start.2 = ((bf16[8,80,896]{2,1,0:T(8,128)(2,1)}), bf16[8,80,896]{2,1,0:T(8,128)(2,1)S(1)}, u32[]{:S(2)}, u32[]{:S(2)}) async-start(bf16[8,80,896]{2,1,0:T(8,128)(2,1)} %get-tuple-element.25), calls=%async_computation.2 | async-start | bytes 2293760 | tf_op jit(solution)/shard_map/all_to_all | solution.py:283
  59.0 23.2 %collective-permute-start.5 = (bf16[128,1408]{1,0:T(8,128)(2,1)}, bf16[128,1408]{1,0:T(8,128)(2,1)}, u32[]{:S(2)}, u32[]{:S(2)}) collective-permute-start(bf16[128,1408]{1,0:T(8,128)(2,1)} %collective-permute-done.2.refs_2_), channel_id=1, source_target_pairs={{0,1},{1,0},{2,3},{3,2},{4,5},{5,4},{6,7},{7,6},{8,9},{9,8},{10,11... | collective-permute-start | bytes 1081352 | tf_op jit(solution)/shard_map/ppermute | solution.py:294
  62.9 19.2 %collective-permute-start.6 = (bf16[128,1408]{1,0:T(8,128)(2,1)}, bf16[128,1408]{1,0:T(8,128)(2,1)}, u32[]{:S(2)}, u32[]{:S(2)}) collective-permute-start(bf16[128,1408]{1,0:T(8,128)(2,1)} %collective-permute-done.refs_4_), channel_id=1, source_target_pairs={{0,48},{1,49},{2,50},{3,51},{4,52},{5,53},{6,54},{7,55},{8,56},{9,... | collective-permute-start | bytes 1081352 | tf_op jit(solution)/shard_map/ppermute | solution.py:294
  66.6 16.3 %collective-permute-start.4 = (bf16[128,1408]{1,0:T(8,128)(2,1)}, bf16[128,1408]{1,0:T(8,128)(2,1)}, u32[]{:S(2)}, u32[]{:S(2)}) collective-permute-start(bf16[128,1408]{1,0:T(8,128)(2,1)} %collective-permute-done.refs_4_), channel_id=1, source_target_pairs={{0,16},{1,17},{2,18},{3,19},{4,20},{5,21},{6,22},{7,23},{8,24},{9,... | collective-permute-start | bytes 1081352 | tf_op jit(solution)/shard_map/ppermute | solution.py:294
  69.3 17.9 %copy-start.2 = (bf16[1,448,1024]{2,1,0:T(8,128)(2,1)S(1)}, bf16[1,448,1024]{2,1,0:T(8,128)(2,1)}, u32[]{:S(2)}) copy-start(bf16[1,448,1024]{2,1,0:T(8,128)(2,1)} %param.15) | copy-start | bytes 2752516
  69.3 17.9 %copy-start.3 = (bf16[1,448,1024]{2,1,0:T(8,128)(2,1)S(1)}, bf16[1,448,1024]{2,1,0:T(8,128)(2,1)}, u32[]{:S(2)}) copy-start(bf16[1,448,1024]{2,1,0:T(8,128)(2,1)} %param.16) | copy-start | bytes 2752516
  82.9 1.0 copy-start.6
  83.9 1.0 copy-start.8
  87.1 1.9 copy-start
  89.0 1.2 copy-start.4
  93.8 18.1 %copy-start.14 = (bf16[640,448]{1,0:T(8,128)(2,1)}, bf16[640,448]{1,0:T(8,128)(2,1)S(1)}, u32[]{:S(2)}) copy-start(bf16[640,448]{1,0:T(8,128)(2,1)S(1)} %get-tuple-element.38) | copy-start | bytes 1720324
  93.9 4.9 %collective-permute-start.8 = (bf16[80,3072]{1,0:T(8,128)(2,1)S(1)}, bf16[80,3072]{1,0:T(8,128)(2,1)S(1)}, u32[]{:S(2)}, u32[]{:S(2)}) collective-permute-start(bf16[80,3072]{1,0:T(8,128)(2,1)S(1)} %get-tuple-element.33), channel_id=1, source_target_pairs={{0,64},{64,0},{128,192},{192,128},{256,320},{320,256},{384,448},{4... | collective-permute-start | bytes 1474568 | tf_op jit(solution)/shard_map/ppermute | solution.py:247
  96.8 14.8 %collective-permute-start.7 = (bf16[240,3072]{1,0:T(8,128)(2,1)S(1)}, bf16[240,3072]{1,0:T(8,128)(2,1)S(1)}, u32[]{:S(2)}, u32[]{:S(2)}) collective-permute-start(bf16[240,3072]{1,0:T(8,128)(2,1)S(1)} %get-tuple-element.31), channel_id=1, source_target_pairs={{0,64},{64,0},{128,192},{192,128},{256,320},{320,256},{384,448},{4... | collective-permute-start | bytes 4423688 | tf_op jit(solution)/shard_map/ppermute | solution.py:247
  98.9 17.1 %collective-permute-start.11 = (bf16[40,3072]{1,0:T(8,128)(2,1)S(1)}, bf16[40,3072]{1,0:T(8,128)(2,1)S(1)}, u32[]{:S(2)}, u32[]{:S(2)}) collective-permute-start(bf16[40,3072]{1,0:T(8,128)(2,1)S(1)} %get-tuple-element.44), channel_id=1, source_target_pairs={{0,384},{64,448},{128,0},{192,64},{256,128},{320,192},{384,256},{4... | collective-permute-start | bytes 737288 | tf_op jit(solution)/shard_map/ppermute | solution.py:251
  109.7 11.4 %collective-permute-start.9 = (bf16[40,3072]{1,0:T(8,128)(2,1)S(1)}, bf16[40,3072]{1,0:T(8,128)(2,1)S(1)}, u32[]{:S(2)}, u32[]{:S(2)}) collective-permute-start(bf16[40,3072]{1,0:T(8,128)(2,1)S(1)} %get-tuple-element.45), channel_id=1, source_target_pairs={{0,128},{64,192},{128,256},{192,320},{256,384},{320,448},{384,0},{... | collective-permute-start | bytes 737288 | tf_op jit(solution)/shard_map/ppermute | solution.py:251
  121.3 11.9 %collective-permute-start.10 = (bf16[80,3072]{1,0:T(8,128)(2,1)S(1)}, bf16[80,3072]{1,0:T(8,128)(2,1)S(1)}, u32[]{:S(2)}, u32[]{:S(2)}) collective-permute-start(bf16[80,3072]{1,0:T(8,128)(2,1)S(1)} %pad_maximum_fusion), channel_id=1, source_target_pairs={{0,128},{64,192},{128,256},{192,320},{256,384},{320,448},{384,0},{... | collective-permute-start | bytes 1474568 | tf_op jit(solution)/shard_map/ppermute | solution.py:251
  123.4 11.2 %collective-permute-start.12 = (bf16[80,3072]{1,0:T(8,128)(2,1)S(1)}, bf16[80,3072]{1,0:T(8,128)(2,1)S(1)}, u32[]{:S(2)}, u32[]{:S(2)}) collective-permute-start(bf16[80,3072]{1,0:T(8,128)(2,1)S(1)} %pad_maximum_fusion.1), channel_id=1, source_target_pairs={{0,384},{64,448},{128,0},{192,64},{256,128},{320,192},{384,256},{4... | collective-permute-start | bytes 1474568 | tf_op jit(solution)/shard_map/ppermute | solution.py:251
  134.5 68.5 %copy-start.1 = (bf16[3,1024,448]{2,1,0:T(8,128)(2,1)S(1)}, bf16[3,1024,448]{2,1,0:T(8,128)(2,1)}, u32[]{:S(2)}) copy-start(bf16[3,1024,448]{2,1,0:T(8,128)(2,1)} %shard_map.131.restored_ref.refs_12_) | copy-start | bytes 8257540
  134.9 19.7 %collective-permute-start.13 = (bf16[80,3072]{1,0:T(8,128)(2,1)S(1)}, bf16[80,3072]{1,0:T(8,128)(2,1)S(1)}, u32[]{:S(2)}, u32[]{:S(2)}) collective-permute-start(bf16[80,3072]{1,0:T(8,128)(2,1)S(1)} %shard_map.133.refs_2_), channel_id=1, source_target_pairs={{0,128},{64,192},{128,256},{192,320},{256,384},{320,448},{384,0},{... | collective-permute-start | bytes 1474568 | tf_op jit(solution)/shard_map/ppermute | solution.py:251
  144.1 38.6 %collective-permute-start.15 = (bf16[80,3072]{1,0:T(8,128)(2,1)S(1)}, bf16[80,3072]{1,0:T(8,128)(2,1)S(1)}, u32[]{:S(2)}, u32[]{:S(2)}) collective-permute-start(bf16[80,3072]{1,0:T(8,128)(2,1)S(1)} %shard_map.133.refs_2_), channel_id=1, source_target_pairs={{0,384},{64,448},{128,0},{192,64},{256,128},{320,192},{384,256},{4... | collective-permute-start | bytes 1474568 | tf_op jit(solution)/shard_map/ppermute | solution.py:251
  154.7 36.7 %collective-permute-start.14 = (bf16[40,3072]{1,0:T(8,128)(2,1)S(1)}, bf16[40,3072]{1,0:T(8,128)(2,1)S(1)}, u32[]{:S(2)}, u32[]{:S(2)}) collective-permute-start(bf16[40,3072]{1,0:T(8,128)(2,1)S(1)} %slice.61), channel_id=1, source_target_pairs={{0,128},{64,192},{128,256},{192,320},{256,384},{320,448},{384,0},{... | collective-permute-start | bytes 737288 | tf_op jit(solution)/shard_map/ppermute | solution.py:251
  158.2 43.3 %collective-permute-start.18 = (bf16[80,3072]{1,0:T(8,128)(2,1)S(1)}, bf16[80,3072]{1,0:T(8,128)(2,1)S(1)}, u32[]{:S(2)}, u32[]{:S(2)}) collective-permute-start(bf16[80,3072]{1,0:T(8,128)(2,1)S(1)} %shard_map.133.refs_2_), channel_id=1, source_target_pairs={{0,64},{64,0},{128,192},{192,128},{256,320},{320,256},{384,448},{4... | collective-permute-start | bytes 1474568 | tf_op jit(solution)/shard_map/ppermute | solution.py:247
  182.7 16.5 %collective-permute-start.16 = (bf16[40,3072]{1,0:T(8,128)(2,1)S(1)}, bf16[40,3072]{1,0:T(8,128)(2,1)S(1)}, u32[]{:S(2)}, u32[]{:S(2)}) collective-permute-start(bf16[40,3072]{1,0:T(8,128)(2,1)S(1)} %slice.62), channel_id=1, source_target_pairs={{0,384},{64,448},{128,0},{192,64},{256,128},{320,192},{384,256},{4... | collective-permute-start | bytes 737288 | tf_op jit(solution)/shard_map/ppermute | solution.py:251
  187.0 14.5 %collective-permute-start.19 = (bf16[80,3072]{1,0:T(8,128)(2,1)S(1)}, bf16[80,3072]{1,0:T(8,128)(2,1)S(1)}, u32[]{:S(2)}, u32[]{:S(2)}) collective-permute-start(bf16[80,3072]{1,0:T(8,128)(2,1)S(1)} %collective-permute-done.15.refs_3_), channel_id=1, source_target_pairs={{0,64},{64,0},{128,192},{192,128},{256,320},{320,256},{384,448},{4... | collective-permute-start | bytes 1474568 | tf_op jit(solution)/shard_map/ppermute | solution.py:247
  189.2 12.3 %collective-permute-start.20 = (bf16[80,3072]{1,0:T(8,128)(2,1)S(1)}, bf16[80,3072]{1,0:T(8,128)(2,1)S(1)}, u32[]{:S(2)}, u32[]{:S(2)}) collective-permute-start(bf16[80,3072]{1,0:T(8,128)(2,1)S(1)} %collective-permute-done.13.refs_4_), channel_id=1, source_target_pairs={{0,64},{64,0},{128,192},{192,128},{256,320},{320,256},{384,448},{4... | collective-permute-start | bytes 1474568 | tf_op jit(solution)/shard_map/ppermute | solution.py:247
  199.2 3.8 %collective-permute-start.17 = (bf16[80,3072]{1,0:T(8,128)(2,1)S(1)}, bf16[80,3072]{1,0:T(8,128)(2,1)S(1)}, u32[]{:S(2)}, u32[]{:S(2)}) collective-permute-start(bf16[80,3072]{1,0:T(8,128)(2,1)S(1)} %constant_dynamic-update-slice_fusion.refs_1_), channel_id=1, source_target_pairs={{0,64},{64,0},{128,192},{192,128},{256,320},{320,256},{384,448},{4... | collective-permute-start | bytes 1474568 | tf_op jit(solution)/shard_map/ppermute | solution.py:247
  206.2 23.9 %copy-start.12 = (bf16[640,2048]{1,0:T(8,128)(2,1)}, bf16[640,2048]{1,0:T(8,128)(2,1)S(1)}, u32[]{:S(2)}) copy-start(bf16[640,2048]{1,0:T(8,128)(2,1)S(1)} %get-tuple-element.39) | copy-start | bytes 7864324
  228.5 6.2 %copy-start.15 = (bf16[640,448]{1,0:T(8,128)(2,1)S(1)}, bf16[640,448]{1,0:T(8,128)(2,1)}, u32[]{:S(2)}) copy-start(bf16[640,448]{1,0:T(8,128)(2,1)} %copy-done.14) | copy-start | bytes 1720324
  230.1 18.6 %all-to-all-start.4 = ((bf16[8,32,896]{2,1,0:T(8,128)(2,1)}), bf16[8,32,896]{2,1,0:T(8,128)(2,1)S(1)}, u32[]{:S(2)}, u32[]{:S(2)}) async-start(bf16[8,32,896]{2,1,0:T(8,128)(2,1)} %bitcast.12), calls=%async_computation.4 | async-start | bytes 917504 | tf_op jit(solution)/shard_map/all_to_all | solution.py:283
  234.7 3.3 %copy-start.13 = (bf16[640,2048]{1,0:T(8,128)(2,1)S(1)}, bf16[640,2048]{1,0:T(8,128)(2,1)}, u32[]{:S(2)}) copy-start(bf16[640,2048]{1,0:T(8,128)(2,1)} %copy-done.12) | copy-start | bytes 7864324

commit v7 on v5

--- a/solution.py
+++ b/solution.py
@@ -22,11 +22,12 @@
     return lax.dot_general(a, b, dims, preferred_element_type=F32)
 
 
-def call(kernel, outs, scratch=(), scalars=0, operands=0, megabytes=32):
+def call(kernel, outs, scratch=(), scalars=0, left=0, operands=0, megabytes=12):
     def of(shape, dtype=BF):
         return jax.ShapeDtypeStruct(shape, dtype)
 
     specs = [pl.BlockSpec(memory_space=pltpu.SMEM)] * scalars
+    specs += [pl.BlockSpec(memory_space=pltpu.HBM)] * left
     specs += [pl.BlockSpec(memory_space=pltpu.VMEM)] * operands
     return pl.pallas_call(
         kernel,
@@ -80,9 +81,8 @@
     return jnp.where(hit, 1.0, 0.0).astype(BF), hi, lo
 
 
-def select_kernel(first_ref, want_ref, out_ref, meta_ref):
-    nxz, rows, width = out_ref.shape
-    feat = width // 2
+def select_kernel(first_ref, want_ref, rows_ref, grads_ref, meta_ref):
+    nxz, rows, feat = rows_ref.shape
     ny, tok, _ = first_ref.shape
     seen = ny * tok
     tokens = first_ref[:, :, 0:feat].reshape(seen, feat)
@@ -93,8 +93,8 @@
     both = jnp.concatenate([cots, cots], axis=0)
     for q in range(nxz):
         pick, hi, lo = tables(meta_ref, want, q, nxz)
-        out_ref[q, :, 0:feat] = dot(pick, tokens).astype(BF)
-        out_ref[q, :, feat:width] = dot(jnp.concatenate([hi, lo], axis=1), both).astype(BF)
+        rows_ref[q] = dot(pick, tokens).astype(BF)
+        grads_ref[q] = dot(jnp.concatenate([hi, lo], axis=1), both).astype(BF)
 
 
 def chunk_at(h, c, p):
@@ -102,18 +102,15 @@
     return half * 4 + lax.rem(h + (2, 0, 1, 3)[p % 4], 4)
 
 
-def products_kernel(
-    grid, who_ref, recv_ref, s0, t0, s1, t1, s2, t2, s3, t3, gate_ref, up_ref, down_ref,
-    rows_ref, far_ref, rest_ref, far_out_ref, rest_out_ref, restored_ref, grads_ref,
-):
+def products_kernel(grid, count, who_ref, recv_ref, *refs):
     nx, ny, nz = grid
-    feat, ff = gate_ref.shape
+    blocks, weights, outs = refs[:nx], refs[nx : nx + count], refs[nx + count :]
+    rows_ref, far_ref, rest_ref, far_out_ref, rest_out_ref, restored_ref = outs
+    feat, ff = weights[0].shape
     chunk = far_ref.shape[0]
     target, h, c, my_x, my_z = (who_ref[i] for i in range(5))
     for p in range(8):
-        g = chunk_at(h, c, p)
-        rows_ref[p * chunk : (p + 1) * chunk, :] = recv_ref[g, :, 0:feat]
-        grads_ref[p * chunk : (p + 1) * chunk, :] = recv_ref[g, :, feat : 2 * feat]
+        rows_ref[p * chunk : (p + 1) * chunk, :] = recv_ref[chunk_at(h, c, p)]
 
     def store(k, j, value):
         at = pl.ds(pl.multiple_of(k * ff + j * TILE, TILE), TILE)
@@ -123,49 +120,47 @@
         far_out_ref[:, at] = value[4 * chunk : 5 * chunk]
         rest_out_ref[:, at] = value[5 * chunk :]
 
-    tiles = ff // TILE
-
     @pl.when(target == 0)
     def _():
-        @pl.loop(0, tiles)
+        @pl.loop(0, ff // TILE)
         def _(j):
             at = pl.ds(pl.multiple_of(j * TILE, TILE), TILE)
-            store(0, j, dot(rows_ref[...], gate_ref[:, at]))
-            store(1, j, dot(rows_ref[...], up_ref[:, at]))
-            store(2, j, dot(grads_ref[...], down_ref[:, at]))
+            for k in range(count):
+                store(k, j, dot(rows_ref[...], weights[k][:, at]))
 
     @pl.when(target == 1)
     def _():
-        n = s0.shape[0] // ny
-        for k, sources in enumerate(((s0, t0), (s1, t1), (s2, t2), (s3, t3))):
+        n = blocks[0].shape[0] // (nz * ny)
+        for i, block in enumerate(blocks):
+            x = lax.rem(my_x - i + nx, nx)
             for other in range(nz):
-                x = lax.rem(my_x - k + nx, nx)
                 z = 1 - my_z if other else my_z
                 for y in range(ny):
                     to = pl.ds(pl.multiple_of(((x * ny + y) * nz + z) * n, n), n)
-                    for m in range(3):
-                        restored_ref[m, to, :] = sources[other][y * n : (y + 1) * n, m * feat : (m + 1) * feat]
-
-        @pl.loop(0, tiles)
+                    r = (other * ny + y) * n
+                    for k in range(count):
+                        restored_ref[k, to, :] = block[r : r + n, k * feat : (k + 1) * feat]
+
+        @pl.loop(0, ff // TILE)
         def _(j):
             at = pl.ds(pl.multiple_of(j * TILE, TILE), TILE)
-            store(0, j, dot(rows_ref[...], restored_ref[0, at, :], NT))
-            store(1, j, dot(rows_ref[...], restored_ref[1, at, :], NT))
-            store(2, j, dot(grads_ref[...], restored_ref[2, at, :], NT))
-
-
-def activate_kernel(own_ref, other_ref, left_ref, right_ref, out_ref):
+            for k in range(count):
+                store(k, j, dot(rows_ref[...], restored_ref[k, at, :], NT))
+
+
+def activate_kernel(*refs):
+    gate_up, grads, out_ref = refs[0:4], refs[4:8], refs[8]
     ff = out_ref.shape[1] // 3
     rows = out_ref.shape[0]
 
     @pl.loop(0, ff // TILE)
     def _(j):
-        def total(k):
+        def total(parts, k):
             at = pl.ds(pl.multiple_of(k * ff + j * TILE, TILE), TILE)
-            near = own_ref[0:rows, at].astype(F32) + other_ref[0:rows, at].astype(F32)
-            return near + (left_ref[:, at].astype(F32) + right_ref[:, at].astype(F32))
-
-        gate, up, dh = total(0), total(1), total(2)
+            near = parts[0][0:rows, at].astype(F32) + parts[1][0:rows, at].astype(F32)
+            return near + (parts[2][:, at].astype(F32) + parts[3][:, at].astype(F32))
+
+        gate, up, dh = total(gate_up, 0), total(gate_up, 1), total(grads, 0)
         sig = jax.nn.sigmoid(gate)
         values = (
             gate * sig * up,
@@ -179,7 +174,8 @@
 
 def back_kernel(*refs):
     who_ref, parts = refs[0], refs[1:9]
-    gate_ref, up_ref, down_ref, restored_ref, out_ref, grads_ref, hidden_ref, y_ref, dx_ref = refs[9:]
+    gate_ref, up_ref, down_ref, restored_ref, restored_down_ref = refs[9:14]
+    out_ref, grads_ref, hidden_ref, y_ref, dx_ref = refs[14:]
     feat, ff = gate_ref.shape
     chunk = out_ref.shape[1]
     target, h, c = who_ref[0], who_ref[1], who_ref[2]
@@ -197,7 +193,7 @@
 
     @pl.when(target == 1)
     def _():
-        y_ref[...] = dot(hidden_ref[...], restored_ref[2]).astype(BF)
+        y_ref[...] = dot(hidden_ref[...], restored_down_ref[0]).astype(BF)
         dx_ref[...] = (
             dot(grads_ref[:, 0:ff], restored_ref[0]) + dot(grads_ref[:, ff : 2 * ff], restored_ref[1])
         ).astype(BF)
@@ -306,49 +302,57 @@
         expert_ids, route_weight, tokens, cotangent
     )
     first, saved = lax.optimization_barrier((first, saved))
-    other_z = step(saved, 0, 1)
-    before, after = step(saved, 1, 0), step(saved, -1, 0)
+    saved_down, saved_gate_up = saved[:, 2 * feat :], saved[:, : 2 * feat]
+    down_z, gate_up_z = (
+        jnp.concatenate([v, step(v, 0, 1)], axis=0) for v in (saved_down, saved_gate_up)
+    )
+    down_blocks = [down_z] + [step(down_z, k, 0) for k in range(1, nx)]
     first = exchange(first, along_y)
-    first, other_z, before, after = lax.optimization_barrier((first, other_z, before, after))
-    before_z, after_z = step(other_z, 1, 0), step(other_z, -1, 0)
-    blocks = (
-        saved, other_z, before, before_z, step(before, 1, 0), step(after_z, -1, 0), after, after_z,
-    )
+    first, gate_up_z, down_blocks = lax.optimization_barrier((first, gate_up_z, down_blocks))
+    gate_up_blocks = [gate_up_z] + [step(gate_up_z, k, 0) for k in range(1, nx)]
 
     out_rows, seen = ny * capacity, ny * tok
     row, col = np.arange(out_rows)[:, None], np.arange(seen)[None, :]
     want = np.where(row // capacity == col // tok, row % capacity, -2).astype(np.float32)
-    send, meta = call(
-        select_kernel, [(nxz, out_rows, 2 * feat), ((64, seen), F32)], operands=2
+    picked = (nxz, out_rows, feat)
+    send_rows, send_grads, meta = call(
+        select_kernel, [picked, picked, ((64, seen), F32)], operands=2
     )(first, want)
-    recv = exchange(send, along_xz)
+    recv_grads = exchange(send_grads, along_xz)
+    recv_grads, *sides = lax.optimization_barrier((recv_grads, gate_up_blocks[1], gate_up_blocks[3]))
+    gate_up_blocks[1], gate_up_blocks[3] = sides
+    recv_rows = exchange(send_rows, along_xz)
+
+    mid = chunk // 2
+
+    def products(recv, blocks, *weights):
+        count = len(weights)
+        parts = [(chunk, count * ff), (3 * chunk, count * ff)]
+        return call(
+            functools.partial(products_kernel, grid, count),
+            [(8 * chunk, feat), *parts, *parts, (count, ff, feat)],
+            scalars=1,
+            operands=1 + nx + count,
+            megabytes=14,
+        )(who, recv, *blocks, *weights)
+
+    def sum_parts(far, rest, far_out, rest_out):
+        far = add(far, core_swap(far_out))
+        rest_in = core_swap(rest_out)
+        from_left, from_right = shift(far[:mid], 1), shift(far[mid:], -1)
+        sides = add(rest[chunk:], rest_in[chunk:])
+        right, left = sides[:chunk], sides[chunk:]
+        right = jnp.concatenate([add(right[:mid], from_left), right[mid:]], axis=0)
+        left = jnp.concatenate([left[:mid], add(left[mid:], from_right)], axis=0)
+        return rest, rest_in, shift(right, 1), shift(left, -1)
 
     w_gate, w_up, w_down = gate_weight[0], up_weight[0], jnp.transpose(down_weight[0])
+    _, *parts, restored_down = products(recv_grads, down_blocks, w_down)
+    grad_parts = sum_parts(*parts)
+    recv_rows, grad_parts = lax.optimization_barrier((recv_rows, grad_parts))
+    rows, *parts, restored = products(recv_rows, gate_up_blocks, w_gate, w_up)
     wide = 3 * ff
-    rows, far, rest, far_out, rest_out, restored = call(
-        functools.partial(products_kernel, grid),
-        [
-            (8 * chunk, feat), (chunk, wide), (3 * chunk, wide),
-            (chunk, wide), (3 * chunk, wide), (3, ff, feat),
-        ],
-        scratch=[pltpu.VMEM((8 * chunk, feat), BF)],
-        scalars=1,
-        operands=12,
-        megabytes=40,
-    )(who, recv, *blocks, w_gate, w_up, w_down)
-
-    mid = chunk // 2
-    far = add(far, core_swap(far_out))
-    rest_in = core_swap(rest_out)
-    from_left, from_right = shift(far[:mid], 1), shift(far[mid:], -1)
-    sides = add(rest[chunk:], rest_in[chunk:])
-    right, left = sides[:chunk], sides[chunk:]
-    right = jnp.concatenate([add(right[:mid], from_left), right[mid:]], axis=0)
-    left = jnp.concatenate([left[:mid], add(left[mid:], from_right)], axis=0)
-    from_left, from_right = shift(right, 1), shift(left, -1)
-    (own,) = call(activate_kernel, [(chunk, wide)], operands=4)(
-        rest, rest_in, from_left, from_right
-    )
+    (own,) = call(activate_kernel, [(chunk, wide)], operands=8)(*sum_parts(*parts), *grad_parts)
 
     left, right = shift(own, 1), shift(own, -1)
     far = jnp.concatenate([shift(left[:mid], 1), shift(right[mid:], -1)], axis=0)
@@ -364,9 +368,9 @@
             pltpu.VMEM((8 * chunk, feat), BF),
         ],
         scalars=1,
-        operands=12,
-        megabytes=40,
-    )(who, *mine, *other, w_gate, w_up, w_down, restored)
+        operands=13,
+        megabytes=14,
+    )(who, *mine, *other, w_gate, w_up, w_down, restored, restored_down)
 
     out = exchange(out.reshape(nxz, out_rows, 2 * feat), along_xz)
     gate_grad = dot(rows, grads[:, :ff], TN).astype(BF)

time: 248 us -> 287 us (1.16)
  blocking collectives: 21.7 us -> 36.6 us
  waiting for transfers between devices: 71.2 us -> 80.4 us
  starting transfers between devices: 124 us -> 130 us
  Pallas kernels: 13.2 us -> 17 us
  other arithmetic: 0.6 us -> 3.83 us
    all_to_all x1, blocking collectives: 21.7 us -> 36.6 us  [exchange(): lax.all_to_all(flat, 'expert', 0, 0, axis_index_groups=groups, tiled=True)]
    ppermute x8 -> x12, starting transfers between devices: 36.4 us -> 49.6 us  [shift(): lax.ppermute(x, 'dp', [(2 * h + c, 2 * ((h + k) % 4) + c) for h in range(...]
    ppermute x6 -> x8, starting transfers between devices: 40 us -> 27.9 us  [core_swap(): return lax.ppermute(x, 'dp', [(i, i ^ 1) for i in range(8)])]
    ppermute x8 -> x12, waiting for transfers between devices: 30.8 us -> 39 us  [shift(): lax.ppermute(x, 'dp', [(2 * h + c, 2 * ((h + k) % 4) + c) for h in range(...]
    all_to_all x4 -> x5, starting transfers between devices: 20.6 us -> 26.3 us  [exchange(): lax.all_to_all(flat, 'expert', 0, 0, axis_index_groups=groups, tiled=True)]
    pallas_call x3 -> x4, Pallas kernels: 6.28 us -> 10.2 us  [the longest x2 6.36 us: products(): call(functools.partial(products_kernel, grid, count), [(8 * chunk, feat),...]
    all_to_all x4 -> x5, waiting for transfers between devices: 16.6 us -> 17.9 us  [exchange(): lax.all_to_all(flat, 'expert', 0, 0, axis_index_groups=groups, tiled=True)]
    ppermute x7 -> x8, starting transfers between devices: 26.9 us -> 26.4 us  [step(): return lax.ppermute(v, 'expert', pairs)]
  transfers between devices with their start and end apart: 25 -> 33, of which waited for: 14 -> 18; matrix products, arithmetic and copies ran while one was open for 3% -> 3% of each run, Pallas kernels for 0% -> 0%
where the time goes in v7:
time: 287 us; the launch traced here: 285 us
  starting transfers between devices  130 us (45%)
  waiting for transfers between devices  80.4 us (28%)
  blocking collectives  36.6 us (13%)
  Pallas kernels  17 us (6%)
  local copies, waits for them, and re-layouts  9.29 us (3%)
  matrix products  5.11 us (2%)
  other arithmetic  3.83 us (1%)
    ppermute x12, starting transfers between devices, shift(): lax.ppermute(x, 'dp', [(2 * h + c, 2 * ((h + k) % 4) + c) for h in range(...  49.6 us
    ppermute x12, waiting for transfers between devices, shift(): lax.ppermute(x, 'dp', [(2 * h + c, 2 * ((h + k) % 4) + c) for h in range(...  39 us
    all_to_all x1, blocking collectives, exchange(): lax.all_to_all(flat, 'expert', 0, 0, axis_index_groups=groups, tiled=True)  36.6 us
    ppermute x8, starting transfers between devices, core_swap(): return lax.ppermute(x, 'dp', [(i, i ^ 1) for i in range(8)])  27.9 us
    ppermute x8, starting transfers between devices, step(): return lax.ppermute(v, 'expert', pairs)  26.4 us
    all_to_all x5, starting transfers between devices, exchange(): lax.all_to_all(flat, 'expert', 0, 0, axis_index_groups=groups, tiled=True)  26.3 us
    ppermute x8, waiting for transfers between devices, step(): return lax.ppermute(v, 'expert', pairs)  22.1 us
    all_to_all x5, waiting for transfers between devices, exchange(): lax.all_to_all(flat, 'expert', 0, 0, axis_index_groups=groups, tiled=True)  17.9 us
  transfers between devices with their start and end apart: 33, of which 18 were waited for; matrix products, arithmetic and copies ran while one was open for 3% of the time, Pallas kernels for 0%

profile of v7, /device:TPU:1, one launch (start us, length us, event | category | flops | bytes accessed | tf_op | source)
XLA Modules:
  0.0 284.6 jit_solution(830427414271429384)
XLA Ops:
  2.4 7.7 %all-to-all-start = ((bf16[8,16,1408]{2,1,0:T(8,128)(2,1)}), bf16[8,16,1408]{2,1,0:T(8,128)(2,1)S(1)}, u32[]{:S(2)}, u32[]{:S(2)}) async-start(bf16[8,16,1408]{2,1,0:T(8,128)(2,1)} %broadcast_in_dim.9), calls=%async_computation | async-start | bytes 720896 | tf_op jit(solution)/shard_map/all_to_all | solution.py:267
  11.5 9.0 %all-to-all-done = bf16[8,16,1408]{2,1,0:T(8,128)(2,1)S(1)} async-done(((bf16[8,16,1408]{2,1,0:T(8,128)(2,1)}), bf16[8,16,1408]{2,1,0:T(8,128)(2,1)S(1)}, u32[]{:S(2)}, u32[]{:S(2)}) %all-to-all-start) | async-done | bytes 360480 | tf_op jit(solution)/shard_map/all_to_all | solution.py:267
  20.4 3.6 %all-to-all-start.1 = ((bf16[8,32,1024]{2,1,0:T(8,128)(2,1)}), bf16[8,32,1024]{2,1,0:T(8,128)(2,1)S(1)}, u32[]{:S(2)}, u32[]{:S(2)}) async-start(bf16[8,32,1024]{2,1,0:T(8,128)(2,1)} %shard_map.129), calls=%async_computation.1 | async-start | bytes 1048576 | tf_op jit(solution)/shard_map/all_to_all | solution.py:267
  24.0 6.5 %collective-permute-start.1 = (bf16[128,512]{1,0:T(8,128)(2,1)S(1)}, bf16[128,512]{1,0:T(8,128)(2,1)S(1)}, u32[]{:S(2)}, u32[]{:S(2)}) collective-permute-start(bf16[128,512]{1,0:T(8,128)(2,1)S(1)} %slice.79), channel_id=1, source_target_pairs={{0,1},{1,0},{2,3},{3,2},{4,5},{5,4},{6,7},{7,6},{8,9},{9,8},{10,11... | collective-permute-start | bytes 393224 | tf_op jit(solution)/shard_map/ppermute | solution.py:278
  30.6 1.9 collective-permute-start
  33.2 4.5 %collective-permute-start.4 = (bf16[256,512]{1,0:T(8,128)(2,1)S(1)}, bf16[256,512]{1,0:T(8,128)(2,1)S(1)}, u32[]{:S(2)}, u32[]{:S(2)}) collective-permute-start(bf16[256,512]{1,0:T(8,128)(2,1)S(1)} %pad_maximum_fusion.3.refs_0_), channel_id=1, source_target_pairs={{0,48},{1,49},{2,50},{3,51},{4,52},{5,53},{6,54},{7,55},{8,56},{9,... | collective-permute-start | bytes 786440 | tf_op jit(solution)/shard_map/ppermute | solution.py:278
  37.7 2.4 collective-permute-start.3
  40.2 2.5 collective-permute-start.2
  43.5 2.9 %collective-permute-done.3.refs_2_ = bf16[256,512]{1,0:T(8,128)(2,1)S(1)} collective-permute-done((bf16[256,512]{1,0:T(8,128)(2,1)S(1)}, bf16[256,512]{1,0:T(8,128)(2,1)S(1)}, u32[]{:S(2)}, u32[]{:S(2)}) %collective-permute-start.3) | collective-permute-done | bytes 262176 | tf_op jit(solution)/shard_map/ppermute | solution.py:278
  46.4 6.0 %collective-permute-done.2.refs_1_ = bf16[256,512]{1,0:T(8,128)(2,1)S(1)} collective-permute-done((bf16[256,512]{1,0:T(8,128)(2,1)S(1)}, bf16[256,512]{1,0:T(8,128)(2,1)S(1)}, u32[]{:S(2)}, u32[]{:S(2)}) %collective-permute-start.2) | collective-permute-done | bytes 262176 | tf_op jit(solution)/shard_map/ppermute | solution.py:278
  52.4 2.3 shard_map.130
  54.7 3.5 %all-to-all-start.3 = ((bf16[8,80,448]{2,1,0:T(8,128)(2,1)}), bf16[8,80,448]{2,1,0:T(8,128)(2,1)S(1)}, u32[]{:S(2)}, u32[]{:S(2)}) async-start(bf16[8,80,448]{2,1,0:T(8,128)(2,1)} %get-tuple-element.42), calls=%async_computation.3 | async-start | bytes 1310720 | tf_op jit(solution)/shard_map/all_to_all | solution.py:267
  58.2 4.5 %collective-permute-start.6 = (bf16[256,896]{1,0:T(8,128)(2,1)}, bf16[256,896]{1,0:T(8,128)(2,1)S(1)}, u32[]{:S(2)}, u32[]{:S(2)}) collective-permute-start(bf16[256,896]{1,0:T(8,128)(2,1)} %pad_maximum_fusion.refs_0_), channel_id=1, source_target_pairs={{0,48},{1,49},{2,50},{3,51},{4,52},{5,53},{6,54},{7,55},{8,56},{9,... | collective-permute-start | bytes 1376264 | tf_op jit(solution)/shard_map/ppermute | solution.py:278
  65.4 10.6 %collective-permute-done.6.refs_3_ = bf16[256,896]{1,0:T(8,128)(2,1)S(1)} collective-permute-done((bf16[256,896]{1,0:T(8,128)(2,1)}, bf16[256,896]{1,0:T(8,128)(2,1)S(1)}, u32[]{:S(2)}, u32[]{:S(2)}) %collective-permute-start.6) | collective-permute-done | bytes 458784 | tf_op jit(solution)/shard_map/ppermute | solution.py:278
  79.1 3.0 %shard_map.131 = (bf16[640,448]{1,0:T(8,128)(2,1)}, bf16[80,1024]{1,0:T(8,128)(2,1)S(1)}, bf16[240,1024]{1,0:T(8,128)(2,1)S(1)}, bf16[80,1024]{1,0:T(8,128)(2,1)...) custom-call(s32[5]{0:T(128)S(1)} %stack.27.who_ref.refs_0_, ...), custom_call_target="tpu_custom_call" | custom-call | tf_op jit(solution)/shard_map/pallas_call | solution.py:331
  84.6 4.8 %collective-permute-start.8 = (bf16[80,1024]{1,0:T(8,128)(2,1)}, bf16[80,1024]{1,0:T(8,128)(2,1)S(1)}, u32[]{:S(2)}, u32[]{:S(2)}) collective-permute-start(bf16[80,1024]{1,0:T(8,128)(2,1)} %get-tuple-element.52), channel_id=1, source_target_pairs={{0,64},{64,0},{128,192},{192,128},{256,320},{320,256},{384,448},{4... | collective-permute-start | bytes 491528 | tf_op jit(solution)/shard_map/ppermute | solution.py:231
  89.4 1.9 collective-permute-start.7
  91.3 2.1 collective-permute-start.13
  93.4 4.0 %all-to-all-start.2 = ((bf16[8,80,448]{2,1,0:T(8,128)(2,1)}), bf16[8,80,448]{2,1,0:T(8,128)(2,1)S(1)}, u32[]{:S(2)}, u32[]{:S(2)}) async-start(bf16[8,80,448]{2,1,0:T(8,128)(2,1)} %get-tuple-element.41), calls=%async_computation.2 | async-start | bytes 1310720 | tf_op jit(solution)/shard_map/all_to_all | solution.py:267
  97.6 9.9 %collective-permute-start.11 = (bf16[40,1024]{1,0:T(8,128)(2,1)S(1)}, bf16[40,1024]{1,0:T(8,128)(2,1)S(1)}, u32[]{:S(2)}, u32[]{:S(2)}) collective-permute-start(bf16[40,1024]{1,0:T(8,128)(2,1)S(1)} %get-tuple-element.82), channel_id=1, source_target_pairs={{0,384},{64,448},{128,0},{192,64},{256,128},{320,192},{384,256},{4... | collective-permute-start | bytes 245768 | tf_op jit(solution)/shard_map/ppermute | solution.py:235
  107.5 1.9 collective-permute-start.9
  110.6 5.0 %collective-permute-done.9 = bf16[40,1024]{1,0:T(8,128)(2,1)S(1)} collective-permute-done((bf16[40,1024]{1,0:T(8,128)(2,1)S(1)}, bf16[40,1024]{1,0:T(8,128)(2,1)S(1)}, u32[]{:S(2)}, u32[]{:S(2)}) %collective-permute-start.9) | collective-permute-done | bytes 81952 | tf_op jit(solution)/shard_map/ppermute | solution.py:235
  118.9 5.5 %collective-permute-start.12 = (bf16[80,1024]{1,0:T(8,128)(2,1)}, bf16[80,1024]{1,0:T(8,128)(2,1)}, u32[]{:S(2)}, u32[]{:S(2)}) collective-permute-start(bf16[80,1024]{1,0:T(8,128)(2,1)} %pad_maximum_fusion.5), channel_id=1, source_target_pairs={{0,384},{64,448},{128,0},{192,64},{256,128},{320,192},{384,256},{4... | collective-permute-start | bytes 491528 | tf_op jit(solution)/shard_map/ppermute | solution.py:235
  129.6 3.3 %shard_map.132 = (bf16[640,448]{1,0:T(8,128)(2,1)S(1)}, bf16[80,2048]{1,0:T(8,128)(2,1)S(1)}, bf16[240,2048]{1,0:T(8,128)(2,1)S(1)}, bf16[80,2048]{1,0:T(8,128)(...) custom-call(s32[5]{0:T(128)S(1)} %copy-done.19, ...), custom_call_target="tpu_custom_call" | custom-call | tf_op jit(solution)/shard_map/pallas_call | solution.py:331
  133.8 8.6 %collective-permute-start.15 = (bf16[80,2048]{1,0:T(8,128)(2,1)S(1)}, bf16[80,2048]{1,0:T(8,128)(2,1)S(1)}, u32[]{:S(2)}, u32[]{:S(2)}) collective-permute-start(bf16[80,2048]{1,0:T(8,128)(2,1)S(1)} %get-tuple-element.59), channel_id=1, source_target_pairs={{0,64},{64,0},{128,192},{192,128},{256,320},{320,256},{384,448},{4... | collective-permute-start | bytes 983048 | tf_op jit(solution)/shard_map/ppermute | solution.py:231
  142.4 1.9 collective-permute-start.14
  144.5 6.2 %collective-permute-start.18 = (bf16[40,2048]{1,0:T(8,128)(2,1)S(1)}, bf16[40,2048]{1,0:T(8,128)(2,1)S(1)}, u32[]{:S(2)}, u32[]{:S(2)}) collective-permute-start(bf16[40,2048]{1,0:T(8,128)(2,1)S(1)} %get-tuple-element.76), channel_id=1, source_target_pairs={{0,384},{64,448},{128,0},{192,64},{256,128},{320,192},{384,256},{4... | collective-permute-start | bytes 491528 | tf_op jit(solution)/shard_map/ppermute | solution.py:235
  150.7 1.9 collective-permute-start.16
  152.9 4.2 %collective-permute-done.18 = bf16[40,2048]{1,0:T(8,128)(2,1)S(1)} collective-permute-done((bf16[40,2048]{1,0:T(8,128)(2,1)S(1)}, bf16[40,2048]{1,0:T(8,128)(2,1)S(1)}, u32[]{:S(2)}, u32[]{:S(2)}) %collective-permute-start.18) | collective-permute-done | bytes 163872 | tf_op jit(solution)/shard_map/ppermute | solution.py:235
  157.0 5.4 %collective-permute-done.16 = bf16[40,2048]{1,0:T(8,128)(2,1)S(1)} collective-permute-done((bf16[40,2048]{1,0:T(8,128)(2,1)S(1)}, bf16[40,2048]{1,0:T(8,128)(2,1)S(1)}, u32[]{:S(2)}, u32[]{:S(2)}) %collective-permute-start.16) | collective-permute-done | bytes 163872 | tf_op jit(solution)/shard_map/ppermute | solution.py:235
  162.6 1.9 collective-permute-start.17
  164.6 5.5 %collective-permute-start.19 = (bf16[80,2048]{1,0:T(8,128)(2,1)S(1)}, bf16[80,2048]{1,0:T(8,128)(2,1)S(1)}, u32[]{:S(2)}, u32[]{:S(2)}) collective-permute-start(bf16[80,2048]{1,0:T(8,128)(2,1)S(1)} %pad_maximum_fusion.2), channel_id=1, source_target_pairs={{0,384},{64,448},{128,0},{192,64},{256,128},{320,192},{384,256},{4... | collective-permute-start | bytes 983048 | tf_op jit(solution)/shard_map/ppermute | solution.py:235
  170.0 9.1 %collective-permute-done.17.refs_2_ = bf16[80,2048]{1,0:T(8,128)(2,1)S(1)} collective-permute-done((bf16[80,2048]{1,0:T(8,128)(2,1)S(1)}, bf16[80,2048]{1,0:T(8,128)(2,1)S(1)}, u32[]{:S(2)}, u32[]{:S(2)}) %collective-permute-start.17) | collective-permute-done | bytes 327712 | tf_op jit(solution)/shard_map/ppermute | solution.py:235
  179.2 2.4 collective-permute-done.19.refs_3_
  183.1 4.2 %collective-permute-start.20 = (bf16[80,3072]{1,0:T(8,128)(2,1)S(1)}, bf16[80,3072]{1,0:T(8,128)(2,1)S(1)}, u32[]{:S(2)}, u32[]{:S(2)}) collective-permute-start(bf16[80,3072]{1,0:T(8,128)(2,1)S(1)} %shard_map.133.refs_2_), channel_id=1, source_target_pairs={{0,128},{64,192},{128,256},{192,320},{256,384},{320,448},{384,0},{... | collective-permute-start | bytes 1474568 | tf_op jit(solution)/shard_map/ppermute | solution.py:235
  187.3 3.4 %collective-permute-start.22 = (bf16[80,3072]{1,0:T(8,128)(2,1)S(1)}, bf16[80,3072]{1,0:T(8,128)(2,1)S(1)}, u32[]{:S(2)}, u32[]{:S(2)}) collective-permute-start(bf16[80,3072]{1,0:T(8,128)(2,1)S(1)} %shard_map.133.refs_2_), channel_id=1, source_target_pairs={{0,384},{64,448},{128,0},{192,64},{256,128},{320,192},{384,256},{4... | collective-permute-start | bytes 1474568 | tf_op jit(solution)/shard_map/ppermute | solution.py:235
  190.7 9.0 %collective-permute-done.20.refs_4_ = bf16[80,3072]{1,0:T(8,128)(2,1)S(1)} collective-permute-done((bf16[80,3072]{1,0:T(8,128)(2,1)S(1)}, bf16[80,3072]{1,0:T(8,128)(2,1)S(1)}, u32[]{:S(2)}, u32[]{:S(2)}) %collective-permute-start.20) | collective-permute-done | bytes 491552 | tf_op jit(solution)/shard_map/ppermute | solution.py:235
  199.6 2.9 %collective-permute-start.21 = (bf16[40,3072]{1,0:T(8,128)(2,1)S(1)}, bf16[40,3072]{1,0:T(8,128)(2,1)S(1)}, u32[]{:S(2)}, u32[]{:S(2)}) collective-permute-start(bf16[40,3072]{1,0:T(8,128)(2,1)S(1)} %slice.114), channel_id=1, source_target_pairs={{0,128},{64,192},{128,256},{192,320},{256,384},{320,448},{384,0},{... | collective-permute-start | bytes 737288 | tf_op jit(solution)/shard_map/ppermute | solution.py:235
  202.5 3.6 %collective-permute-start.25 = (bf16[80,3072]{1,0:T(8,128)(2,1)S(1)}, bf16[80,3072]{1,0:T(8,128)(2,1)S(1)}, u32[]{:S(2)}, u32[]{:S(2)}) collective-permute-start(bf16[80,3072]{1,0:T(8,128)(2,1)S(1)} %shard_map.133.refs_2_), channel_id=1, source_target_pairs={{0,64},{64,0},{128,192},{192,128},{256,320},{320,256},{384,448},{4... | collective-permute-start | bytes 1474568 | tf_op jit(solution)/shard_map/ppermute | solution.py:231
  206.2 4.6 %collective-permute-start.23 = (bf16[40,3072]{1,0:T(8,128)(2,1)S(1)}, bf16[40,3072]{1,0:T(8,128)(2,1)S(1)}, u32[]{:S(2)}, u32[]{:S(2)}) collective-permute-start(bf16[40,3072]{1,0:T(8,128)(2,1)S(1)} %slice.115), channel_id=1, source_target_pairs={{0,384},{64,448},{128,0},{192,64},{256,128},{320,192},{384,256},{4... | collective-permute-start | bytes 737288 | tf_op jit(solution)/shard_map/ppermute | solution.py:235
  210.8 2.2 collective-permute-start.26
  213.0 2.1 collective-permute-start.27
  216.6 2.7 collective-permute-start.24
  220.7 3.2 %shard_map.134 = (bf16[8,80,896]{2,1,0:T(8,128)(2,1)S(1)}, bf16[640,2048]{1,0:T(8,128)(2,1)S(1)}) custom-call(s32[5]{0:T(128)S(1)} %copy-done.20, bf16[80,3072]{1,0:T(8,128)(2,1)S(1)} %constant_dynamic-update-slice_fusion.refs_1_, bf16[80,3072]{1,0:T(8,128)(2,1)S(1)} %shard_map.133.refs_2_, bf16[80,3072]{1,0:T(8,128)(2,1)S(1)} %collective-permute-done.22.refs_3_, ...), custom_call_target="tpu_custom_call" | custom-call | tf_op jit(solution)/shard_map/pallas_call | solution.py:362
  224.0 36.6 %all_to_all.42.recv_ref = bf16[8,80,896]{2,1,0:T(8,128)(2,1)S(1)} all-to-all(bf16[8,80,896]{2,1,0:T(8,128)(2,1)S(1)} %get-tuple-element.66), channel_id=1, replica_groups={{0,1,16,17,32,33,48,49},{2,3,18,19,34,35,50,51},{4,5,20,21,36,37,52,53}..., dimensions={0} | all-to-all | bytes 2293760 | tf_op jit(solution)/shard_map/all_to_all | solution.py:267
  262.3 7.5 %all-to-all-start.5 = ((bf16[8,32,896]{2,1,0:T(8,128)(2,1)}), bf16[8,32,896]{2,1,0:T(8,128)(2,1)S(1)}, u32[]{:S(2)}, u32[]{:S(2)}) async-start(bf16[8,32,896]{2,1,0:T(8,128)(2,1)} %bitcast.12), calls=%async_computation.5 | async-start | bytes 917504 | tf_op jit(solution)/shard_map/all_to_all | solution.py:267
  269.8 3.3 %fusion.1 = bf16[1,448,1024]{2,1,0:T(8,128)(2,1)} fusion(bf16[640,448]{1,0:T(8,128)(2,1)S(1)} %copy-done.24, bf16[640,2048]{1,0:T(8,128)(2,1)} %copy-done.21), kind=kOutput, calls=%fused_computation.3 | convolution fusion | flops 587661312 | bytes 2801664 | tf_op jit(solution)/shard_map/dot_general | solution.py:22
  275.0 8.9 %all-to-all-done.5.recv_ref = bf16[8,32,896]{2,1,0:T(8,128)(2,1)S(1)} async-done(((bf16[8,32,896]{2,1,0:T(8,128)(2,1)}), bf16[8,32,896]{2,1,0:T(8,128)(2,1)S(1)}, u32[]{:S(2)}, u32[]{:S(2)}) %all-to-all-start.5) | async-done | bytes 458784 | tf_op jit(solution)/shard_map/all_to_all | solution.py:267
  (112 shorter events, 32.0 us)
Async XLA Ops:
  0.6 9.4 %copy-start.25 = (s32[32,8]{0,1:T(8,128)S(1)}, s32[32,8]{0,1:T(8,128)}, u32[]{:S(2)}) copy-start(s32[32,8]{0,1:T(8,128)} %param.12) | copy-start | bytes 3076
  0.6 9.5 %copy-start.26 = (f32[32,8]{0,1:T(8,128)S(1)}, f32[32,8]{0,1:T(8,128)}, u32[]{:S(2)}) copy-start(f32[32,8]{0,1:T(8,128)} %param.13) | copy-start | bytes 3076
  0.7 9.6 %copy-start.17 = (bf16[32,448]{1,0:T(8,128)(2,1)S(1)}, bf16[32,448]{1,0:T(8,128)(2,1)}, u32[]{:S(2)}) copy-start(bf16[32,448]{1,0:T(8,128)(2,1)} %cot_ref.1) | copy-start | bytes 86020
  0.7 9.6 %copy-start.16 = (bf16[32,448]{1,0:T(8,128)(2,1)S(1)}, bf16[32,448]{1,0:T(8,128)(2,1)}, u32[]{:S(2)}) copy-start(bf16[32,448]{1,0:T(8,128)(2,1)} %tok_ref.1) | copy-start | bytes 86020
  2.4 18.0 %all-to-all-start = ((bf16[8,16,1408]{2,1,0:T(8,128)(2,1)}), bf16[8,16,1408]{2,1,0:T(8,128)(2,1)S(1)}, u32[]{:S(2)}, u32[]{:S(2)}) async-start(bf16[8,16,1408]{2,1,0:T(8,128)(2,1)} %broadcast_in_dim.9), calls=%async_computation | async-start | bytes 720896 | tf_op jit(solution)/shard_map/all_to_all | solution.py:267
  20.4 31.9 %all-to-all-start.1 = ((bf16[8,32,1024]{2,1,0:T(8,128)(2,1)}), bf16[8,32,1024]{2,1,0:T(8,128)(2,1)S(1)}, u32[]{:S(2)}, u32[]{:S(2)}) async-start(bf16[8,32,1024]{2,1,0:T(8,128)(2,1)} %shard_map.129), calls=%async_computation.1 | async-start | bytes 1048576 | tf_op jit(solution)/shard_map/all_to_all | solution.py:267
  24.0 28.4 %copy-start.11 = (f32[80,256]{1,0:T(8,128)S(1)}, f32[80,256]{1,0:T(8,128)}, u32[]{:S(2)}) copy-start(f32[80,256]{1,0:T(8,128)} %constant.53.clone.want_ref) | copy-start | bytes 245764
  24.0 9.1 %collective-permute-start.1 = (bf16[128,512]{1,0:T(8,128)(2,1)S(1)}, bf16[128,512]{1,0:T(8,128)(2,1)S(1)}, u32[]{:S(2)}, u32[]{:S(2)}) collective-permute-start(bf16[128,512]{1,0:T(8,128)(2,1)S(1)} %slice.79), channel_id=1, source_target_pairs={{0,1},{1,0},{2,3},{3,2},{4,5},{5,4},{6,7},{7,6},{8,9},{9,8},{10,11... | collective-permute-start | bytes 393224 | tf_op jit(solution)/shard_map/ppermute | solution.py:278
  30.6 12.1 %collective-permute-start = (bf16[128,896]{1,0:T(8,128)(2,1)S(1)}, bf16[128,896]{1,0:T(8,128)(2,1)S(1)}, u32[]{:S(2)}, u32[]{:S(2)}) collective-permute-start(bf16[128,896]{1,0:T(8,128)(2,1)S(1)} %slice.78), channel_id=1, source_target_pairs={{0,1},{1,0},{2,3},{3,2},{4,5},{5,4},{6,7},{7,6},{8,9},{9,8},{10,11... | collective-permute-start | bytes 688136 | tf_op jit(solution)/shard_map/ppermute | solution.py:278
  33.2 44.8 %copy-start.2 = (bf16[1,1024,448]{1,2,0:T(8,128)(2,1)S(1)}, bf16[1,1024,448]{1,2,0:T(8,128)(2,1)}, u32[]{:S(2)}) copy-start(bf16[1,1024,448]{1,2,0:T(8,128)(2,1)} %param.17) | copy-start | bytes 2752516
  33.2 10.3 %collective-permute-start.4 = (bf16[256,512]{1,0:T(8,128)(2,1)S(1)}, bf16[256,512]{1,0:T(8,128)(2,1)S(1)}, u32[]{:S(2)}, u32[]{:S(2)}) collective-permute-start(bf16[256,512]{1,0:T(8,128)(2,1)S(1)} %pad_maximum_fusion.3.refs_0_), channel_id=1, source_target_pairs={{0,48},{1,49},{2,50},{3,51},{4,52},{5,53},{6,54},{7,55},{8,56},{9,... | collective-permute-start | bytes 786440 | tf_op jit(solution)/shard_map/ppermute | solution.py:278
  37.7 8.7 %collective-permute-start.3 = (bf16[256,512]{1,0:T(8,128)(2,1)S(1)}, bf16[256,512]{1,0:T(8,128)(2,1)S(1)}, u32[]{:S(2)}, u32[]{:S(2)}) collective-permute-start(bf16[256,512]{1,0:T(8,128)(2,1)S(1)} %pad_maximum_fusion.3.refs_0_), channel_id=1, source_target_pairs={{0,32},{1,33},{2,34},{3,35},{4,36},{5,37},{6,38},{7,39},{8,40},{9,... | collective-permute-start | bytes 786440 | tf_op jit(solution)/shard_map/ppermute | solution.py:278
  40.2 12.2 %collective-permute-start.2 = (bf16[256,512]{1,0:T(8,128)(2,1)S(1)}, bf16[256,512]{1,0:T(8,128)(2,1)S(1)}, u32[]{:S(2)}, u32[]{:S(2)}) collective-permute-start(bf16[256,512]{1,0:T(8,128)(2,1)S(1)} %pad_maximum_fusion.3.refs_0_), channel_id=1, source_target_pairs={{0,16},{1,17},{2,18},{3,19},{4,20},{5,21},{6,22},{7,23},{8,24},{9,... | collective-permute-start | bytes 786440 | tf_op jit(solution)/shard_map/ppermute | solution.py:278
  54.7 23.3 %all-to-all-start.3 = ((bf16[8,80,448]{2,1,0:T(8,128)(2,1)}), bf16[8,80,448]{2,1,0:T(8,128)(2,1)S(1)}, u32[]{:S(2)}, u32[]{:S(2)}) async-start(bf16[8,80,448]{2,1,0:T(8,128)(2,1)} %get-tuple-element.42), calls=%async_computation.3 | async-start | bytes 1310720 | tf_op jit(solution)/shard_map/all_to_all | solution.py:267
  58.2 17.8 %collective-permute-start.6 = (bf16[256,896]{1,0:T(8,128)(2,1)}, bf16[256,896]{1,0:T(8,128)(2,1)S(1)}, u32[]{:S(2)}, u32[]{:S(2)}) collective-permute-start(bf16[256,896]{1,0:T(8,128)(2,1)} %pad_maximum_fusion.refs_0_), channel_id=1, source_target_pairs={{0,48},{1,49},{2,50},{3,51},{4,52},{5,53},{6,54},{7,55},{8,56},{9,... | collective-permute-start | bytes 1376264 | tf_op jit(solution)/shard_map/ppermute | solution.py:278
  62.7 15.2 %collective-permute-start.5 = (bf16[256,896]{1,0:T(8,128)(2,1)}, bf16[256,896]{1,0:T(8,128)(2,1)S(1)}, u32[]{:S(2)}, u32[]{:S(2)}) collective-permute-start(bf16[256,896]{1,0:T(8,128)(2,1)} %pad_maximum_fusion.refs_0_), channel_id=1, source_target_pairs={{0,16},{1,17},{2,18},{3,19},{4,20},{5,21},{6,22},{7,23},{8,24},{9,... | collective-permute-start | bytes 1376264 | tf_op jit(solution)/shard_map/ppermute | solution.py:278
  65.4 16.7 %copy-start.18 = (s32[5]{0:T(128)}, s32[5]{0:T(128)S(1)}, u32[]{:S(2)}) copy-start(s32[5]{0:T(128)S(1)} %stack.27.who_ref.refs_0_) | copy-start | bytes 64
  84.6 12.9 %copy-start.15 = (bf16[80,1024]{1,0:T(8,128)(2,1)S(1)}, bf16[80,1024]{1,0:T(8,128)(2,1)}, u32[]{:S(2)}) copy-start(bf16[80,1024]{1,0:T(8,128)(2,1)} %copy-done.14) | copy-start | bytes 491524
  84.6 12.9 %collective-permute-start.8 = (bf16[80,1024]{1,0:T(8,128)(2,1)}, bf16[80,1024]{1,0:T(8,128)(2,1)S(1)}, u32[]{:S(2)}, u32[]{:S(2)}) collective-permute-start(bf16[80,1024]{1,0:T(8,128)(2,1)} %get-tuple-element.52), channel_id=1, source_target_pairs={{0,64},{64,0},{128,192},{192,128},{256,320},{320,256},{384,448},{4... | collective-permute-start | bytes 491528 | tf_op jit(solution)/shard_map/ppermute | solution.py:231
  89.4 20.0 %collective-permute-start.7 = (bf16[240,1024]{1,0:T(8,128)(2,1)}, bf16[240,1024]{1,0:T(8,128)(2,1)}, u32[]{:S(2)}, u32[]{:S(2)}) collective-permute-start(bf16[240,1024]{1,0:T(8,128)(2,1)} %get-tuple-element.50), channel_id=1, source_target_pairs={{0,64},{64,0},{128,192},{192,128},{256,320},{320,256},{384,448},{4... | collective-permute-start | bytes 1474568 | tf_op jit(solution)/shard_map/ppermute | solution.py:231
  91.3 35.6 %collective-permute-start.13 = (bf16[256,896]{1,0:T(8,128)(2,1)}, bf16[256,896]{1,0:T(8,128)(2,1)}, u32[]{:S(2)}, u32[]{:S(2)}) collective-permute-start(bf16[256,896]{1,0:T(8,128)(2,1)} %pad_maximum_fusion.refs_0_), channel_id=1, source_target_pairs={{0,32},{1,33},{2,34},{3,35},{4,36},{5,37},{6,38},{7,39},{8,40},{9,... | collective-permute-start | bytes 1376264 | tf_op jit(solution)/shard_map/ppermute | solution.py:278
  93.4 30.9 %all-to-all-start.2 = ((bf16[8,80,448]{2,1,0:T(8,128)(2,1)}), bf16[8,80,448]{2,1,0:T(8,128)(2,1)S(1)}, u32[]{:S(2)}, u32[]{:S(2)}) async-start(bf16[8,80,448]{2,1,0:T(8,128)(2,1)} %get-tuple-element.41), calls=%async_computation.2 | async-start | bytes 1310720 | tf_op jit(solution)/shard_map/all_to_all | solution.py:267
  97.6 29.3 %copy-start = (bf16[1,448,1024]{2,1,0:T(8,128)(2,1)S(1)}, bf16[1,448,1024]{2,1,0:T(8,128)(2,1)}, u32[]{:S(2)}) copy-start(bf16[1,448,1024]{2,1,0:T(8,128)(2,1)} %param.15) | copy-start | bytes 2752516
  97.6 29.3 %copy-start.1 = (bf16[1,448,1024]{2,1,0:T(8,128)(2,1)S(1)}, bf16[1,448,1024]{2,1,0:T(8,128)(2,1)}, u32[]{:S(2)}) copy-start(bf16[1,448,1024]{2,1,0:T(8,128)(2,1)} %param.16) | copy-start | bytes 2752516
  97.6 13.0 %collective-permute-start.11 = (bf16[40,1024]{1,0:T(8,128)(2,1)S(1)}, bf16[40,1024]{1,0:T(8,128)(2,1)S(1)}, u32[]{:S(2)}, u32[]{:S(2)}) collective-permute-start(bf16[40,1024]{1,0:T(8,128)(2,1)S(1)} %get-tuple-element.82), channel_id=1, source_target_pairs={{0,384},{64,448},{128,0},{192,64},{256,128},{320,192},{384,256},{4... | collective-permute-start | bytes 245768 | tf_op jit(solution)/shard_map/ppermute | solution.py:235
  107.5 8.1 %collective-permute-start.9 = (bf16[40,1024]{1,0:T(8,128)(2,1)S(1)}, bf16[40,1024]{1,0:T(8,128)(2,1)S(1)}, u32[]{:S(2)}, u32[]{:S(2)}) collective-permute-start(bf16[40,1024]{1,0:T(8,128)(2,1)S(1)} %get-tuple-element.83), channel_id=1, source_target_pairs={{0,128},{64,192},{128,256},{192,320},{256,384},{320,448},{384,0},{... | collective-permute-start | bytes 245768 | tf_op jit(solution)/shard_map/ppermute | solution.py:235
  116.3 9.2 %collective-permute-start.10 = (bf16[80,1024]{1,0:T(8,128)(2,1)}, bf16[80,1024]{1,0:T(8,128)(2,1)}, u32[]{:S(2)}, u32[]{:S(2)}) collective-permute-start(bf16[80,1024]{1,0:T(8,128)(2,1)} %pad_maximum_fusion.4), channel_id=1, source_target_pairs={{0,128},{64,192},{128,256},{192,320},{256,384},{320,448},{384,0},{... | collective-permute-start | bytes 491528 | tf_op jit(solution)/shard_map/ppermute | solution.py:235
  118.9 8.0 %collective-permute-start.12 = (bf16[80,1024]{1,0:T(8,128)(2,1)}, bf16[80,1024]{1,0:T(8,128)(2,1)}, u32[]{:S(2)}, u32[]{:S(2)}) collective-permute-start(bf16[80,1024]{1,0:T(8,128)(2,1)} %pad_maximum_fusion.5), channel_id=1, source_target_pairs={{0,384},{64,448},{128,0},{192,64},{256,128},{320,192},{384,256},{4... | collective-permute-start | bytes 491528 | tf_op jit(solution)/shard_map/ppermute | solution.py:235
  133.8 10.6 %collective-permute-start.15 = (bf16[80,2048]{1,0:T(8,128)(2,1)S(1)}, bf16[80,2048]{1,0:T(8,128)(2,1)S(1)}, u32[]{:S(2)}, u32[]{:S(2)}) collective-permute-start(bf16[80,2048]{1,0:T(8,128)(2,1)S(1)} %get-tuple-element.59), channel_id=1, source_target_pairs={{0,64},{64,0},{128,192},{192,128},{256,320},{320,256},{384,448},{4... | collective-permute-start | bytes 983048 | tf_op jit(solution)/shard_map/ppermute | solution.py:231
  142.4 10.2 %collective-permute-start.14 = (bf16[240,2048]{1,0:T(8,128)(2,1)S(1)}, bf16[240,2048]{1,0:T(8,128)(2,1)S(1)}, u32[]{:S(2)}, u32[]{:S(2)}) collective-permute-start(bf16[240,2048]{1,0:T(8,128)(2,1)S(1)} %get-tuple-element.57), channel_id=1, source_target_pairs={{0,64},{64,0},{128,192},{192,128},{256,320},{320,256},{384,448},{4... | collective-permute-start | bytes 2949128 | tf_op jit(solution)/shard_map/ppermute | solution.py:231
  144.5 12.6 %collective-permute-start.18 = (bf16[40,2048]{1,0:T(8,128)(2,1)S(1)}, bf16[40,2048]{1,0:T(8,128)(2,1)S(1)}, u32[]{:S(2)}, u32[]{:S(2)}) collective-permute-start(bf16[40,2048]{1,0:T(8,128)(2,1)S(1)} %get-tuple-element.76), channel_id=1, source_target_pairs={{0,384},{64,448},{128,0},{192,64},{256,128},{320,192},{384,256},{4... | collective-permute-start | bytes 491528 | tf_op jit(solution)/shard_map/ppermute | solution.py:235
  150.7 11.8 %collective-permute-start.16 = (bf16[40,2048]{1,0:T(8,128)(2,1)S(1)}, bf16[40,2048]{1,0:T(8,128)(2,1)S(1)}, u32[]{:S(2)}, u32[]{:S(2)}) collective-permute-start(bf16[40,2048]{1,0:T(8,128)(2,1)S(1)} %get-tuple-element.77), channel_id=1, source_target_pairs={{0,128},{64,192},{128,256},{192,320},{256,384},{320,448},{384,0},{... | collective-permute-start | bytes 491528 | tf_op jit(solution)/shard_map/ppermute | solution.py:235
  152.9 28.7 %copy-start.4 = (bf16[240,1024]{1,0:T(8,128)(2,1)S(1)}, bf16[240,1024]{1,0:T(8,128)(2,1)}, u32[]{:S(2)}) copy-start(bf16[240,1024]{1,0:T(8,128)(2,1)} %copy-done.3) | copy-start | bytes 1474564
  162.6 16.6 %collective-permute-start.17 = (bf16[80,2048]{1,0:T(8,128)(2,1)S(1)}, bf16[80,2048]{1,0:T(8,128)(2,1)S(1)}, u32[]{:S(2)}, u32[]{:S(2)}) collective-permute-start(bf16[80,2048]{1,0:T(8,128)(2,1)S(1)} %pad_maximum_fusion.1), channel_id=1, source_target_pairs={{0,128},{64,192},{128,256},{192,320},{256,384},{320,448},{384,0},{... | collective-permute-start | bytes 983048 | tf_op jit(solution)/shard_map/ppermute | solution.py:235
  164.6 17.0 %collective-permute-start.19 = (bf16[80,2048]{1,0:T(8,128)(2,1)S(1)}, bf16[80,2048]{1,0:T(8,128)(2,1)S(1)}, u32[]{:S(2)}, u32[]{:S(2)}) collective-permute-start(bf16[80,2048]{1,0:T(8,128)(2,1)S(1)} %pad_maximum_fusion.2), channel_id=1, source_target_pairs={{0,384},{64,448},{128,0},{192,64},{256,128},{320,192},{384,256},{4... | collective-permute-start | bytes 983048 | tf_op jit(solution)/shard_map/ppermute | solution.py:235
  183.1 37.7 %copy-start.6 = (bf16[1,1024,448]{2,1,0:T(8,128)(2,1)S(1)}, bf16[1,1024,448]{2,1,0:T(8,128)(2,1)}, u32[]{:S(2)}) copy-start(bf16[1,1024,448]{2,1,0:T(8,128)(2,1)} %copy-done.5) | copy-start | bytes 2752516
  183.1 37.6 %copy-start.20 = (s32[5]{0:T(128)S(1)}, s32[5]{0:T(128)}, u32[]{:S(2)}) copy-start(s32[5]{0:T(128)} %copy-done.18) | copy-start | bytes 64
  183.1 16.5 %collective-permute-start.20 = (bf16[80,3072]{1,0:T(8,128)(2,1)S(1)}, bf16[80,3072]{1,0:T(8,128)(2,1)S(1)}, u32[]{:S(2)}, u32[]{:S(2)}) collective-permute-start(bf16[80,3072]{1,0:T(8,128)(2,1)S(1)} %shard_map.133.refs_2_), channel_id=1, source_target_pairs={{0,128},{64,192},{128,256},{192,320},{256,384},{320,448},{384,0},{... | collective-permute-start | bytes 1474568 | tf_op jit(solution)/shard_map/ppermute | solution.py:235
  187.3 18.8 %collective-permute-start.22 = (bf16[80,3072]{1,0:T(8,128)(2,1)S(1)}, bf16[80,3072]{1,0:T(8,128)(2,1)S(1)}, u32[]{:S(2)}, u32[]{:S(2)}) collective-permute-start(bf16[80,3072]{1,0:T(8,128)(2,1)S(1)} %shard_map.133.refs_2_), channel_id=1, source_target_pairs={{0,384},{64,448},{128,0},{192,64},{256,128},{320,192},{384,256},{4... | collective-permute-start | bytes 1474568 | tf_op jit(solution)/shard_map/ppermute | solution.py:235
  199.6 16.0 %collective-permute-start.21 = (bf16[40,3072]{1,0:T(8,128)(2,1)S(1)}, bf16[40,3072]{1,0:T(8,128)(2,1)S(1)}, u32[]{:S(2)}, u32[]{:S(2)}) collective-permute-start(bf16[40,3072]{1,0:T(8,128)(2,1)S(1)} %slice.114), channel_id=1, source_target_pairs={{0,128},{64,192},{128,256},{192,320},{256,384},{320,448},{384,0},{... | collective-permute-start | bytes 737288 | tf_op jit(solution)/shard_map/ppermute | solution.py:235
  202.5 16.7 %collective-permute-start.25 = (bf16[80,3072]{1,0:T(8,128)(2,1)S(1)}, bf16[80,3072]{1,0:T(8,128)(2,1)S(1)}, u32[]{:S(2)}, u32[]{:S(2)}) collective-permute-start(bf16[80,3072]{1,0:T(8,128)(2,1)S(1)} %shard_map.133.refs_2_), channel_id=1, source_target_pairs={{0,64},{64,0},{128,192},{192,128},{256,320},{320,256},{384,448},{4... | collective-permute-start | bytes 1474568 | tf_op jit(solution)/shard_map/ppermute | solution.py:231
  206.2 10.4 %collective-permute-start.23 = (bf16[40,3072]{1,0:T(8,128)(2,1)S(1)}, bf16[40,3072]{1,0:T(8,128)(2,1)S(1)}, u32[]{:S(2)}, u32[]{:S(2)}) collective-permute-start(bf16[40,3072]{1,0:T(8,128)(2,1)S(1)} %slice.115), channel_id=1, source_target_pairs={{0,384},{64,448},{128,0},{192,64},{256,128},{320,192},{384,256},{4... | collective-permute-start | bytes 737288 | tf_op jit(solution)/shard_map/ppermute | solution.py:235
  210.8 8.5 %collective-permute-start.26 = (bf16[80,3072]{1,0:T(8,128)(2,1)S(1)}, bf16[80,3072]{1,0:T(8,128)(2,1)S(1)}, u32[]{:S(2)}, u32[]{:S(2)}) collective-permute-start(bf16[80,3072]{1,0:T(8,128)(2,1)S(1)} %collective-permute-done.22.refs_3_), channel_id=1, source_target_pairs={{0,64},{64,0},{128,192},{192,128},{256,320},{320,256},{384,448},{4... | collective-permute-start | bytes 1474568 | tf_op jit(solution)/shard_map/ppermute | solution.py:231
  213.0 6.3 %collective-permute-start.27 = (bf16[80,3072]{1,0:T(8,128)(2,1)S(1)}, bf16[80,3072]{1,0:T(8,128)(2,1)S(1)}, u32[]{:S(2)}, u32[]{:S(2)}) collective-permute-start(bf16[80,3072]{1,0:T(8,128)(2,1)S(1)} %collective-permute-done.20.refs_4_), channel_id=1, source_target_pairs={{0,64},{64,0},{128,192},{192,128},{256,320},{320,256},{384,448},{4... | collective-permute-start | bytes 1474568 | tf_op jit(solution)/shard_map/ppermute | solution.py:231
  216.6 4.2 %collective-permute-start.24 = (bf16[80,3072]{1,0:T(8,128)(2,1)S(1)}, bf16[80,3072]{1,0:T(8,128)(2,1)S(1)}, u32[]{:S(2)}, u32[]{:S(2)}) collective-permute-start(bf16[80,3072]{1,0:T(8,128)(2,1)S(1)} %constant_dynamic-update-slice_fusion.refs_1_), channel_id=1, source_target_pairs={{0,64},{64,0},{128,192},{192,128},{256,320},{320,256},{384,448},{4... | collective-permute-start | bytes 1474568 | tf_op jit(solution)/shard_map/ppermute | solution.py:231
  224.0 38.3 %copy-start.21 = (bf16[640,2048]{1,0:T(8,128)(2,1)}, bf16[640,2048]{1,0:T(8,128)(2,1)S(1)}, u32[]{:S(2)}) copy-start(bf16[640,2048]{1,0:T(8,128)(2,1)S(1)} %get-tuple-element.71) | copy-start | bytes 7864324
  260.6 9.2 %copy-start.24 = (bf16[640,448]{1,0:T(8,128)(2,1)S(1)}, bf16[640,448]{1,0:T(8,128)(2,1)}, u32[]{:S(2)}) copy-start(bf16[640,448]{1,0:T(8,128)(2,1)} %copy-done.23) | copy-start | bytes 1720324
  262.3 21.6 %all-to-all-start.5 = ((bf16[8,32,896]{2,1,0:T(8,128)(2,1)}), bf16[8,32,896]{2,1,0:T(8,128)(2,1)S(1)}, u32[]{:S(2)}, u32[]{:S(2)}) async-start(bf16[8,32,896]{2,1,0:T(8,128)(2,1)} %bitcast.12), calls=%async_computation.5 | async-start | bytes 917504 | tf_op jit(solution)/shard_map/all_to_all | solution.py:267
  (12 other events, 22.9 us)

commit v8 on v5

--- a/solution.py
+++ b/solution.py
@@ -99,11 +99,11 @@
 
 def chunk_at(h, c, p):
     half = c if p < 4 else 1 - c
-    return half * 4 + lax.rem(h + (2, 0, 1, 3)[p % 4], 4)
+    return half * 4 + lax.rem(h + (0, 1, 3, 2)[p % 4], 4)
 
 
 def products_kernel(
-    grid, who_ref, recv_ref, s0, t0, s1, t1, s2, t2, s3, t3, gate_ref, up_ref, down_ref,
+    grid, who_ref, recv_ref, s0, s1, s2a, s2b, s3, gate_ref, up_ref, down_ref,
     rows_ref, far_ref, rest_ref, far_out_ref, rest_out_ref, restored_ref, grads_ref,
 ):
     nx, ny, nz = grid
@@ -118,10 +118,10 @@
     def store(k, j, value):
         at = pl.ds(pl.multiple_of(k * ff + j * TILE, TILE), TILE)
         value = value.astype(BF)
-        far_ref[:, at] = value[0:chunk]
-        rest_ref[:, at] = value[chunk : 4 * chunk]
-        far_out_ref[:, at] = value[4 * chunk : 5 * chunk]
-        rest_out_ref[:, at] = value[5 * chunk :]
+        rest_ref[:, at] = value[0 : 3 * chunk]
+        far_ref[:, at] = value[3 * chunk : 4 * chunk]
+        rest_out_ref[:, at] = value[4 * chunk : 7 * chunk]
+        far_out_ref[:, at] = value[7 * chunk :]
 
     tiles = ff // TILE
 
@@ -136,15 +136,18 @@
 
     @pl.when(target == 1)
     def _():
-        n = s0.shape[0] // ny
-        for k, sources in enumerate(((s0, t0), (s1, t1), (s2, t2), (s3, t3))):
-            for other in range(nz):
-                x = lax.rem(my_x - k + nx, nx)
-                z = 1 - my_z if other else my_z
-                for y in range(ny):
+        n = s0.shape[0] // (ny * nz)
+        half = ny // 2
+        for k in range(nx):
+            x = lax.rem(my_x - k + nx, nx)
+            for y in range(ny):
+                source, first = ((s0, 0), (s1, 0), ((s2a, 0), (s2b, half))[y >= half], (s3, 0))[k]
+                for other in range(nz):
+                    z = 1 - my_z if other else my_z
                     to = pl.ds(pl.multiple_of(((x * ny + y) * nz + z) * n, n), n)
+                    r = ((y - first) * nz + other) * n
                     for m in range(3):
-                        restored_ref[m, to, :] = sources[other][y * n : (y + 1) * n, m * feat : (m + 1) * feat]
+                        restored_ref[m, to, :] = source[r : r + n, m * feat : (m + 1) * feat]
 
         @pl.loop(0, tiles)
         def _(j):
@@ -178,15 +181,15 @@
 
 
 def back_kernel(*refs):
-    who_ref, parts = refs[0], refs[1:9]
-    gate_ref, up_ref, down_ref, restored_ref, out_ref, grads_ref, hidden_ref, y_ref, dx_ref = refs[9:]
+    who_ref, parts = refs[0], refs[1:3]
+    gate_ref, up_ref, down_ref, restored_ref, out_ref, grads_ref, hidden_ref, y_ref, dx_ref = refs[3:]
     feat, ff = gate_ref.shape
     chunk = out_ref.shape[1]
     target, h, c = who_ref[0], who_ref[1], who_ref[2]
-    for p in range(8):
-        span = slice(p * chunk, (p + 1) * chunk)
-        hidden_ref[span, :] = parts[p][:, 0:ff]
-        grads_ref[span, :] = parts[p][:, ff : 3 * ff]
+    for k, part in enumerate(parts):
+        span = slice(4 * chunk * k, 4 * chunk * (k + 1))
+        hidden_ref[span, :] = part[:, 0:ff]
+        grads_ref[span, :] = part[:, ff : 3 * ff]
 
     @pl.when(target == 0)
     def _():
@@ -300,20 +303,19 @@
 
     saved = jnp.transpose(backup, (2, 0, 1)).reshape(ffr, 3 * feat)
     saved = jnp.pad(saved, ((0, 0), (0, -3 * feat % 128)))
+    saved = jnp.concatenate([saved, step(saved, 0, 1)], axis=0)
     saved = exchange(jnp.broadcast_to(saved, (ny, *saved.shape)), along_y)
-    saved = saved.reshape(ny * ffr, -1)
+    saved = saved.reshape(ny * nz * ffr, -1)
+
     (first,) = call(functools.partial(pack_kernel, grid), [(ny, tok, LANES)], operands=4)(
         expert_ids, route_weight, tokens, cotangent
     )
     first, saved = lax.optimization_barrier((first, saved))
-    other_z = step(saved, 0, 1)
     before, after = step(saved, 1, 0), step(saved, -1, 0)
     first = exchange(first, along_y)
-    first, other_z, before, after = lax.optimization_barrier((first, other_z, before, after))
-    before_z, after_z = step(other_z, 1, 0), step(other_z, -1, 0)
-    blocks = (
-        saved, other_z, before, before_z, step(before, 1, 0), step(after_z, -1, 0), after, after_z,
-    )
+    first, before, after = lax.optimization_barrier((first, before, after))
+    half = saved.shape[0] // 2
+    blocks = saved, before, step(before[:half], 1, 0), step(after[half:], -1, 0), after
 
     out_rows, seen = ny * capacity, ny * tok
     row, col = np.arange(out_rows)[:, None], np.arange(seen)[None, :]
@@ -333,8 +335,8 @@
         ],
         scratch=[pltpu.VMEM((8 * chunk, feat), BF)],
         scalars=1,
-        operands=12,
-        megabytes=40,
+        operands=9,
+        megabytes=18,
     )(who, recv, *blocks, w_gate, w_up, w_down)
 
     mid = chunk // 2
@@ -351,9 +353,9 @@
     )
 
     left, right = shift(own, 1), shift(own, -1)
-    far = jnp.concatenate([shift(left[:mid], 1), shift(right[mid:], -1)], axis=0)
-    mine = (far, own, right, left)
-    other = tuple(core_swap(v) for v in mine)
+    far = shift(left[:mid], 1), shift(right[mid:], -1)
+    mine = jnp.concatenate([own, right, left, *far], axis=0)
+    other = core_swap(mine)
 
     out, grads = call(
         back_kernel,
@@ -364,9 +366,9 @@
             pltpu.VMEM((8 * chunk, feat), BF),
         ],
         scalars=1,
-        operands=12,
-        megabytes=40,
-    )(who, *mine, *other, w_gate, w_up, w_down, restored)
+        operands=6,
+        megabytes=18,
+    )(who, mine, other, w_gate, w_up, w_down, restored)
 
     out = exchange(out.reshape(nxz, out_rows, 2 * feat), along_xz)
     gate_grad = dot(rows, grads[:, :ff], TN).astype(BF)

time: 248 us -> 252 us (1.016)
  waiting for transfers between devices: 71.2 us -> 101 us
  starting transfers between devices: 124 us -> 97.1 us
  local copies, waits for them, and re-layouts: 9.17 us -> 11.8 us
    ppermute x6 -> x3, starting transfers between devices: 40 us -> 20.6 us  [core_swap(): return lax.ppermute(x, 'dp', [(i, i ^ 1) for i in range(8)])]
    all_to_all x4, waiting for transfers between devices: 16.6 us -> 26.6 us  [exchange(): lax.all_to_all(flat, 'expert', 0, 0, axis_index_groups=groups, tiled=True)]
    ppermute x8, waiting for transfers between devices: 30.8 us -> 40.8 us  [shift(): lax.ppermute(x, 'dp', [(2 * h + c, 2 * ((h + k) % 4) + c) for h in range(...]
    ppermute x7 -> x5, waiting for transfers between devices: 22.3 us -> 30.2 us  [step(): return lax.ppermute(v, 'expert', pairs)]
    ppermute x7 -> x5, starting transfers between devices: 26.9 us -> 19.2 us  [step(): return lax.ppermute(v, 'expert', pairs)]
    slice x2 -> x4, local copies, waits for them, and re-layouts: 0.03 us -> 3.54 us  [the longest x1 1.76 us: body(): before[:half]]
    unnamed x33 -> x42, local copies, waits for them, and re-layouts: 7.24 us -> 6.23 us
  transfers between devices with their start and end apart: 25 -> 20, of which waited for: 14 -> 16; matrix products, arithmetic and copies ran while one was open for 3% -> 4% of each run, Pallas kernels for 0% -> 0%
where the time goes in v8:
time: 252 us; the launch traced here: 251 us
  waiting for transfers between devices  101 us (40%)
  starting transfers between devices  97.1 us (39%)
  blocking collectives  20 us (8%)
  Pallas kernels  12.9 us (5%)
  local copies, waits for them, and re-layouts  11.8 us (5%)
  matrix products  5.11 us (2%)
    ppermute x8, waiting for transfers between devices, shift(): lax.ppermute(x, 'dp', [(2 * h + c, 2 * ((h + k) % 4) + c) for h in range(...  40.8 us
    ppermute x8, starting transfers between devices, shift(): lax.ppermute(x, 'dp', [(2 * h + c, 2 * ((h + k) % 4) + c) for h in range(...  35.4 us
    ppermute x5, waiting for transfers between devices, step(): return lax.ppermute(v, 'expert', pairs)  30.2 us
    all_to_all x4, waiting for transfers between devices, exchange(): lax.all_to_all(flat, 'expert', 0, 0, axis_index_groups=groups, tiled=True)  26.6 us
    all_to_all x4, starting transfers between devices, exchange(): lax.all_to_all(flat, 'expert', 0, 0, axis_index_groups=groups, tiled=True)  21.9 us
    ppermute x3, starting transfers between devices, core_swap(): return lax.ppermute(x, 'dp', [(i, i ^ 1) for i in range(8)])  20.6 us
    all_to_all x1, blocking collectives, exchange(): lax.all_to_all(flat, 'expert', 0, 0, axis_index_groups=groups, tiled=True)  20 us
    ppermute x5, starting transfers between devices, step(): return lax.ppermute(v, 'expert', pairs)  19.2 us
  transfers between devices with their start and end apart: 20, of which 16 were waited for; matrix products, arithmetic and copies ran while one was open for 4% of the time, Pallas kernels for 0%

profile of v8, /device:TPU:1, one launch (start us, length us, event | category | flops | bytes accessed | tf_op | source)
XLA Modules:
  0.0 250.5 jit_solution(7115185071295946630)
XLA Ops:
  1.7 4.8 %collective-permute-start = (bf16[16,1408]{1,0:T(8,128)(2,1)S(1)}, bf16[16,1408]{1,0:T(8,128)(2,1)S(1)}, u32[]{:S(2)}, u32[]{:S(2)}) collective-permute-start(bf16[16,1408]{1,0:T(8,128)(2,1)S(1)} %pad.4), channel_id=1, source_target_pairs={{0,1},{1,0},{2,3},{3,2},{4,5},{5,4},{6,7},{7,6},{8,9},{9,8},{10,11... | collective-permute-start | bytes 135176 | tf_op jit(solution)/shard_map/ppermute | solution.py:285
  6.5 1.4 collective-permute-done
  8.8 6.8 %all-to-all-start = ((bf16[8,32,1408]{2,1,0:T(8,128)(2,1)}), bf16[8,32,1408]{2,1,0:T(8,128)(2,1)S(1)}, u32[]{:S(2)}, u32[]{:S(2)}) async-start(bf16[8,32,1408]{2,1,0:T(8,128)(2,1)} %broadcast_in_dim.9), calls=%async_computation | async-start | bytes 1441792 | tf_op jit(solution)/shard_map/all_to_all | solution.py:274
  15.8 1.2 shard_map.129
  17.1 17.7 %all-to-all-done = bf16[8,32,1408]{2,1,0:T(8,128)(2,1)S(1)} async-done(((bf16[8,32,1408]{2,1,0:T(8,128)(2,1)}), bf16[8,32,1408]{2,1,0:T(8,128)(2,1)S(1)}, u32[]{:S(2)}, u32[]{:S(2)}) %all-to-all-start) | async-done | bytes 720928 | tf_op jit(solution)/shard_map/all_to_all | solution.py:274
  34.8 3.5 %all-to-all-start.1 = ((bf16[8,32,1024]{2,1,0:T(8,128)(2,1)}), bf16[8,32,1024]{2,1,0:T(8,128)(2,1)S(1)}, u32[]{:S(2)}, u32[]{:S(2)}) async-start(bf16[8,32,1024]{2,1,0:T(8,128)(2,1)} %shard_map.129), calls=%async_computation.1 | async-start | bytes 1048576 | tf_op jit(solution)/shard_map/all_to_all | solution.py:274
  38.3 6.0 %collective-permute-start.2 = (bf16[256,1408]{1,0:T(8,128)(2,1)S(1)}, bf16[256,1408]{1,0:T(8,128)(2,1)S(1)}, u32[]{:S(2)}, u32[]{:S(2)}) collective-permute-start(bf16[256,1408]{1,0:T(8,128)(2,1)S(1)} %bitcast.27), channel_id=1, source_target_pairs={{0,48},{1,49},{2,50},{3,51},{4,52},{5,53},{6,54},{7,55},{8,56},{9,... | collective-permute-start | bytes 2162696 | tf_op jit(solution)/shard_map/ppermute | solution.py:285
  44.3 1.9 collective-permute-start.1
  46.2 11.6 %collective-permute-done.2.s3 = bf16[256,1408]{1,0:T(8,128)(2,1)S(1)} collective-permute-done((bf16[256,1408]{1,0:T(8,128)(2,1)S(1)}, bf16[256,1408]{1,0:T(8,128)(2,1)S(1)}, u32[]{:S(2)}, u32[]{:S(2)}) %collective-permute-start.2) | collective-permute-done | bytes 720928 | tf_op jit(solution)/shard_map/ppermute | solution.py:285
  57.8 5.2 %collective-permute-done.1.s1 = bf16[256,1408]{1,0:T(8,128)(2,1)} collective-permute-done((bf16[256,1408]{1,0:T(8,128)(2,1)S(1)}, bf16[256,1408]{1,0:T(8,128)(2,1)}, u32[]{:S(2)}, u32[]{:S(2)}) %collective-permute-start.1) | collective-permute-done | bytes 720928 | tf_op jit(solution)/shard_map/ppermute | solution.py:285
  63.0 1.4 shard_map.130
  65.4 3.7 %all-to-all-start.2 = ((bf16[8,80,896]{2,1,0:T(8,128)(2,1)}), bf16[8,80,896]{2,1,0:T(8,128)(2,1)S(1)}, u32[]{:S(2)}, u32[]{:S(2)}) async-start(bf16[8,80,896]{2,1,0:T(8,128)(2,1)} %copy-done.8), calls=%async_computation.2 | async-start | bytes 2293760 | tf_op jit(solution)/shard_map/all_to_all | solution.py:274
  69.1 1.8 slice.48
  70.8 1.7 slice.49
  72.6 4.5 %collective-permute-start.4 = (bf16[128,1408]{1,0:T(8,128)(2,1)}, bf16[128,1408]{1,0:T(8,128)(2,1)S(1)}, u32[]{:S(2)}, u32[]{:S(2)}) collective-permute-start(bf16[128,1408]{1,0:T(8,128)(2,1)} %slice.49), channel_id=1, source_target_pairs={{0,48},{1,49},{2,50},{3,51},{4,52},{5,53},{6,54},{7,55},{8,56},{9,... | collective-permute-start | bytes 1081352 | tf_op jit(solution)/shard_map/ppermute | solution.py:285
  77.1 1.9 collective-permute-start.3
  79.8 10.3 %collective-permute-done.4.s2b = bf16[128,1408]{1,0:T(8,128)(2,1)S(1)} collective-permute-done((bf16[128,1408]{1,0:T(8,128)(2,1)}, bf16[128,1408]{1,0:T(8,128)(2,1)S(1)}, u32[]{:S(2)}, u32[]{:S(2)}) %collective-permute-start.4) | collective-permute-done | bytes 360480 | tf_op jit(solution)/shard_map/ppermute | solution.py:285
  90.1 1.8 collective-permute-done.3.s2a
  91.9 1.2 copy-done.2
  93.1 1.1 copy-done.5
  95.3 4.3 %shard_map.131 = (bf16[640,448]{1,0:T(8,128)(2,1)S(1)}, bf16[80,3072]{1,0:T(8,128)(2,1)S(1)}, bf16[240,3072]{1,0:T(8,128)(2,1)S(1)}, bf16[80,3072]{1,0:T(8,128)(...) custom-call(s32[5]{0:T(128)S(1)} %stack.27.who_ref.refs_0_, ...), custom_call_target="tpu_custom_call" | custom-call | tf_op jit(solution)/shard_map/pallas_call | solution.py:330
  99.6 3.9 %collective-permute-start.6 = (bf16[80,3072]{1,0:T(8,128)(2,1)S(1)}, bf16[80,3072]{1,0:T(8,128)(2,1)S(1)}, u32[]{:S(2)}, u32[]{:S(2)}) collective-permute-start(bf16[80,3072]{1,0:T(8,128)(2,1)S(1)} %get-tuple-element.30), channel_id=1, source_target_pairs={{0,64},{64,0},{128,192},{192,128},{256,320},{320,256},{384,448},{4... | collective-permute-start | bytes 1474568 | tf_op jit(solution)/shard_map/ppermute | solution.py:238
  103.5 1.9 collective-permute-start.5
  105.6 9.2 %collective-permute-start.9 = (bf16[40,3072]{1,0:T(8,128)(2,1)S(1)}, bf16[40,3072]{1,0:T(8,128)(2,1)S(1)}, u32[]{:S(2)}, u32[]{:S(2)}) collective-permute-start(bf16[40,3072]{1,0:T(8,128)(2,1)S(1)} %get-tuple-element.42), channel_id=1, source_target_pairs={{0,384},{64,448},{128,0},{192,64},{256,128},{320,192},{384,256},{4... | collective-permute-start | bytes 737288 | tf_op jit(solution)/shard_map/ppermute | solution.py:242
  114.9 1.9 collective-permute-start.7
  117.2 5.5 %collective-permute-done.9 = bf16[40,3072]{1,0:T(8,128)(2,1)S(1)} collective-permute-done((bf16[40,3072]{1,0:T(8,128)(2,1)S(1)}, bf16[40,3072]{1,0:T(8,128)(2,1)S(1)}, u32[]{:S(2)}, u32[]{:S(2)}) %collective-permute-start.9) | collective-permute-done | bytes 245792 | tf_op jit(solution)/shard_map/ppermute | solution.py:242
  122.6 3.0 %collective-permute-done.7 = bf16[40,3072]{1,0:T(8,128)(2,1)S(1)} collective-permute-done((bf16[40,3072]{1,0:T(8,128)(2,1)S(1)}, bf16[40,3072]{1,0:T(8,128)(2,1)S(1)}, u32[]{:S(2)}, u32[]{:S(2)}) %collective-permute-start.7) | collective-permute-done | bytes 245792 | tf_op jit(solution)/shard_map/ppermute | solution.py:242
  125.8 2.3 collective-permute-start.8
  128.2 5.1 %collective-permute-start.10 = (bf16[80,3072]{1,0:T(8,128)(2,1)S(1)}, bf16[80,3072]{1,0:T(8,128)(2,1)S(1)}, u32[]{:S(2)}, u32[]{:S(2)}) collective-permute-start(bf16[80,3072]{1,0:T(8,128)(2,1)S(1)} %pad_maximum_fusion.1), channel_id=1, source_target_pairs={{0,384},{64,448},{128,0},{192,64},{256,128},{320,192},{384,256},{4... | collective-permute-start | bytes 1474568 | tf_op jit(solution)/shard_map/ppermute | solution.py:242
  133.3 4.3 %collective-permute-done.8.left_ref = bf16[80,3072]{1,0:T(8,128)(2,1)S(1)} collective-permute-done((bf16[80,3072]{1,0:T(8,128)(2,1)S(1)}, bf16[80,3072]{1,0:T(8,128)(2,1)S(1)}, u32[]{:S(2)}, u32[]{:S(2)}) %collective-permute-start.8) | collective-permute-done | bytes 491552 | tf_op jit(solution)/shard_map/ppermute | solution.py:242
  137.6 1.4 collective-permute-done.10.right_ref
  139.5 7.4 %collective-permute-start.12 = (bf16[80,3072]{1,0:T(8,128)(2,1)S(1)}, bf16[80,3072]{1,0:T(8,128)(2,1)S(1)}, u32[]{:S(2)}, u32[]{:S(2)}) collective-permute-start(bf16[80,3072]{1,0:T(8,128)(2,1)S(1)} %shard_map.132), channel_id=1, source_target_pairs={{0,128},{64,192},{128,256},{192,320},{256,384},{320,448},{384,0},{... | collective-permute-start | bytes 1474568 | tf_op jit(solution)/shard_map/ppermute | solution.py:242
  146.9 1.9 collective-permute-start.11
  148.9 11.7 %collective-permute-done.12 = bf16[80,3072]{1,0:T(8,128)(2,1)S(1)} collective-permute-done((bf16[80,3072]{1,0:T(8,128)(2,1)S(1)}, bf16[80,3072]{1,0:T(8,128)(2,1)S(1)}, u32[]{:S(2)}, u32[]{:S(2)}) %collective-permute-start.12) | collective-permute-done | bytes 491552 | tf_op jit(solution)/shard_map/ppermute | solution.py:242
  160.5 1.9 collective-permute-start.13
  162.7 5.6 %collective-permute-start.14 = (bf16[40,3072]{1,0:T(8,128)(2,1)S(1)}, bf16[40,3072]{1,0:T(8,128)(2,1)S(1)}, u32[]{:S(2)}, u32[]{:S(2)}) collective-permute-start(bf16[40,3072]{1,0:T(8,128)(2,1)S(1)} %slice.70), channel_id=1, source_target_pairs={{0,384},{64,448},{128,0},{192,64},{256,128},{320,192},{384,256},{4... | collective-permute-start | bytes 737288 | tf_op jit(solution)/shard_map/ppermute | solution.py:242
  168.4 12.1 %collective-permute-done.13 = bf16[40,3072]{1,0:T(8,128)(2,1)S(1)} collective-permute-done((bf16[40,3072]{1,0:T(8,128)(2,1)S(1)}, bf16[40,3072]{1,0:T(8,128)(2,1)S(1)}, u32[]{:S(2)}, u32[]{:S(2)}) %collective-permute-start.13) | collective-permute-done | bytes 245792 | tf_op jit(solution)/shard_map/ppermute | solution.py:242
  180.5 2.6 %collective-permute-done.14 = bf16[40,3072]{1,0:T(8,128)(2,1)S(1)} collective-permute-done((bf16[40,3072]{1,0:T(8,128)(2,1)S(1)}, bf16[40,3072]{1,0:T(8,128)(2,1)S(1)}, u32[]{:S(2)}, u32[]{:S(2)}) %collective-permute-start.14) | collective-permute-done | bytes 245792 | tf_op jit(solution)/shard_map/ppermute | solution.py:242
  183.1 14.8 %collective-permute-start.15 = (bf16[320,3072]{1,0:T(8,128)(2,1)S(1)}, bf16[320,3072]{1,0:T(8,128)(2,1)S(1)}, u32[]{:S(2)}, u32[]{:S(2)}) collective-permute-start(bf16[320,3072]{1,0:T(8,128)(2,1)S(1)} %constant_dynamic-update-slice_fusion.refs_1_), channel_id=1, source_target_pairs={{0,64},{64,0},{128,192},{192,128},{256,320},{320,256},{384,448},{4... | collective-permute-start | bytes 5898248 | tf_op jit(solution)/shard_map/ppermute | solution.py:238
  197.9 3.6 %collective-permute-done.15.refs_2_ = bf16[320,3072]{1,0:T(8,128)(2,1)S(1)} collective-permute-done((bf16[320,3072]{1,0:T(8,128)(2,1)S(1)}, bf16[320,3072]{1,0:T(8,128)(2,1)S(1)}, u32[]{:S(2)}, u32[]{:S(2)}) %collective-permute-start.15) | collective-permute-done | bytes 1966112 | tf_op jit(solution)/shard_map/ppermute | solution.py:238
  201.5 3.2 %shard_map.133 = (bf16[8,80,896]{2,1,0:T(8,128)(2,1)S(1)}, bf16[640,2048]{1,0:T(8,128)(2,1)S(1)}) custom-call(s32[5]{0:T(128)S(1)} %stack.27.who_ref.refs_0_, bf16[320,3072]{1,0:T(8,128)(2,1)S(1)} %constant_dynamic-update-slice_fusion.refs_1_, bf16[320,3072]{1,0:T(8,128)(2,1)S(1)} %collective-permute-done.15.refs_2_, bf16[448,1024]{1,0:T(8,128)(2,1)S(1)} %bitcast.22, ...), custom_call_target="tpu_custom_call" | custom-call | tf_op jit(solution)/shard_map/pallas_call | solution.py:360
  204.7 1.5 copy-done.12
  206.2 20.0 %all_to_all.36.recv_ref = bf16[8,80,896]{2,1,0:T(8,128)(2,1)S(1)} all-to-all(bf16[8,80,896]{2,1,0:T(8,128)(2,1)S(1)} %get-tuple-element.32), channel_id=1, replica_groups={{0,1,16,17,32,33,48,49},{2,3,18,19,34,35,50,51},{4,5,20,21,36,37,52,53}..., dimensions={0} | all-to-all | bytes 2293760 | tf_op jit(solution)/shard_map/all_to_all | solution.py:274
  226.2 1.7 shard_map.134
  227.9 7.9 %all-to-all-start.4 = ((bf16[8,32,896]{2,1,0:T(8,128)(2,1)}), bf16[8,32,896]{2,1,0:T(8,128)(2,1)S(1)}, u32[]{:S(2)}, u32[]{:S(2)}) async-start(bf16[8,32,896]{2,1,0:T(8,128)(2,1)} %bitcast.12), calls=%async_computation.4 | async-start | bytes 917504 | tf_op jit(solution)/shard_map/all_to_all | solution.py:274
  235.7 3.3 %fusion.1 = bf16[1,448,1024]{2,1,0:T(8,128)(2,1)} fusion(bf16[640,448]{1,0:T(8,128)(2,1)S(1)} %copy-done.15, bf16[640,2048]{1,0:T(8,128)(2,1)} %copy-done.12), kind=kOutput, calls=%fused_computation.4 | convolution fusion | flops 587661312 | bytes 2801664 | tf_op jit(solution)/shard_map/dot_general | solution.py:22
  239.0 1.8 fusion
  240.9 8.9 %all-to-all-done.4.recv_ref = bf16[8,32,896]{2,1,0:T(8,128)(2,1)S(1)} async-done(((bf16[8,32,896]{2,1,0:T(8,128)(2,1)}), bf16[8,32,896]{2,1,0:T(8,128)(2,1)S(1)}, u32[]{:S(2)}, u32[]{:S(2)}) %all-to-all-start.4) | async-done | bytes 458784 | tf_op jit(solution)/shard_map/all_to_all | solution.py:274
  (62 shorter events, 6.5 us)
Async XLA Ops:
  0.6 15.0 %copy-start.16 = (s32[32,8]{0,1:T(8,128)S(1)}, s32[32,8]{0,1:T(8,128)}, u32[]{:S(2)}) copy-start(s32[32,8]{0,1:T(8,128)} %param.12) | copy-start | bytes 3076
  0.6 15.1 %copy-start.17 = (f32[32,8]{0,1:T(8,128)S(1)}, f32[32,8]{0,1:T(8,128)}, u32[]{:S(2)}) copy-start(f32[32,8]{0,1:T(8,128)} %param.13) | copy-start | bytes 3076
  0.7 15.2 %copy-start.11 = (bf16[32,448]{1,0:T(8,128)(2,1)S(1)}, bf16[32,448]{1,0:T(8,128)(2,1)}, u32[]{:S(2)}) copy-start(bf16[32,448]{1,0:T(8,128)(2,1)} %cot_ref.1) | copy-start | bytes 86020
  0.7 15.2 %copy-start.10 = (bf16[32,448]{1,0:T(8,128)(2,1)S(1)}, bf16[32,448]{1,0:T(8,128)(2,1)}, u32[]{:S(2)}) copy-start(bf16[32,448]{1,0:T(8,128)(2,1)} %tok_ref.1) | copy-start | bytes 86020
  1.7 6.3 %collective-permute-start = (bf16[16,1408]{1,0:T(8,128)(2,1)S(1)}, bf16[16,1408]{1,0:T(8,128)(2,1)S(1)}, u32[]{:S(2)}, u32[]{:S(2)}) collective-permute-start(bf16[16,1408]{1,0:T(8,128)(2,1)S(1)} %pad.4), channel_id=1, source_target_pairs={{0,1},{1,0},{2,3},{3,2},{4,5},{5,4},{6,7},{7,6},{8,9},{9,8},{10,11... | collective-permute-start | bytes 135176 | tf_op jit(solution)/shard_map/ppermute | solution.py:285
  7.9 55.0 %copy-start.9 = (f32[80,256]{1,0:T(8,128)S(1)}, f32[80,256]{1,0:T(8,128)}, u32[]{:S(2)}) copy-start(f32[80,256]{1,0:T(8,128)} %constant.53.clone.want_ref) | copy-start | bytes 245764
  8.8 25.9 %all-to-all-start = ((bf16[8,32,1408]{2,1,0:T(8,128)(2,1)}), bf16[8,32,1408]{2,1,0:T(8,128)(2,1)S(1)}, u32[]{:S(2)}, u32[]{:S(2)}) async-start(bf16[8,32,1408]{2,1,0:T(8,128)(2,1)} %broadcast_in_dim.9), calls=%async_computation | async-start | bytes 1441792 | tf_op jit(solution)/shard_map/all_to_all | solution.py:274
  34.8 30.6 %copy-start.4 = (bf16[8,32,1408]{2,1,0:T(8,128)(2,1)}, bf16[8,32,1408]{2,1,0:T(8,128)(2,1)S(1)}, u32[]{:S(2)}) copy-start(bf16[8,32,1408]{2,1,0:T(8,128)(2,1)S(1)} %all-to-all-done) | copy-start | bytes 2162692
  34.8 28.2 %all-to-all-start.1 = ((bf16[8,32,1024]{2,1,0:T(8,128)(2,1)}), bf16[8,32,1024]{2,1,0:T(8,128)(2,1)S(1)}, u32[]{:S(2)}, u32[]{:S(2)}) async-start(bf16[8,32,1024]{2,1,0:T(8,128)(2,1)} %shard_map.129), calls=%async_computation.1 | async-start | bytes 1048576 | tf_op jit(solution)/shard_map/all_to_all | solution.py:274
  38.3 19.5 %collective-permute-start.2 = (bf16[256,1408]{1,0:T(8,128)(2,1)S(1)}, bf16[256,1408]{1,0:T(8,128)(2,1)S(1)}, u32[]{:S(2)}, u32[]{:S(2)}) collective-permute-start(bf16[256,1408]{1,0:T(8,128)(2,1)S(1)} %bitcast.27), channel_id=1, source_target_pairs={{0,48},{1,49},{2,50},{3,51},{4,52},{5,53},{6,54},{7,55},{8,56},{9,... | collective-permute-start | bytes 2162696 | tf_op jit(solution)/shard_map/ppermute | solution.py:285
  44.3 18.6 %collective-permute-start.1 = (bf16[256,1408]{1,0:T(8,128)(2,1)S(1)}, bf16[256,1408]{1,0:T(8,128)(2,1)}, u32[]{:S(2)}, u32[]{:S(2)}) collective-permute-start(bf16[256,1408]{1,0:T(8,128)(2,1)S(1)} %bitcast.28), channel_id=1, source_target_pairs={{0,16},{1,17},{2,18},{3,19},{4,20},{5,21},{6,22},{7,23},{8,24},{9,... | collective-permute-start | bytes 2162696 | tf_op jit(solution)/shard_map/ppermute | solution.py:285
  57.8 5.2 %copy-start.6 = (bf16[256,1408]{1,0:T(8,128)(2,1)}, bf16[256,1408]{1,0:T(8,128)(2,1)S(1)}, u32[]{:S(2)}) copy-start(bf16[256,1408]{1,0:T(8,128)(2,1)S(1)} %collective-permute-done.2.s3) | copy-start | bytes 2162692
  64.3 1.0 copy-start.8
  65.3 26.5 %copy-start = (bf16[1,448,1024]{2,1,0:T(8,128)(2,1)S(1)}, bf16[1,448,1024]{2,1,0:T(8,128)(2,1)}, u32[]{:S(2)}) copy-start(bf16[1,448,1024]{2,1,0:T(8,128)(2,1)} %param.15) | copy-start | bytes 2752516
  65.4 26.5 %copy-start.1 = (bf16[1,448,1024]{2,1,0:T(8,128)(2,1)S(1)}, bf16[1,448,1024]{2,1,0:T(8,128)(2,1)}, u32[]{:S(2)}) copy-start(bf16[1,448,1024]{2,1,0:T(8,128)(2,1)} %param.16) | copy-start | bytes 2752516
  65.4 26.5 %all-to-all-start.2 = ((bf16[8,80,896]{2,1,0:T(8,128)(2,1)}), bf16[8,80,896]{2,1,0:T(8,128)(2,1)S(1)}, u32[]{:S(2)}, u32[]{:S(2)}) async-start(bf16[8,80,896]{2,1,0:T(8,128)(2,1)} %copy-done.8), calls=%async_computation.2 | async-start | bytes 2293760 | tf_op jit(solution)/shard_map/all_to_all | solution.py:274
  72.6 17.6 %collective-permute-start.4 = (bf16[128,1408]{1,0:T(8,128)(2,1)}, bf16[128,1408]{1,0:T(8,128)(2,1)S(1)}, u32[]{:S(2)}, u32[]{:S(2)}) collective-permute-start(bf16[128,1408]{1,0:T(8,128)(2,1)} %slice.49), channel_id=1, source_target_pairs={{0,48},{1,49},{2,50},{3,51},{4,52},{5,53},{6,54},{7,55},{8,56},{9,... | collective-permute-start | bytes 1081352 | tf_op jit(solution)/shard_map/ppermute | solution.py:285
  77.1 14.8 %collective-permute-start.3 = (bf16[128,1408]{1,0:T(8,128)(2,1)}, bf16[128,1408]{1,0:T(8,128)(2,1)}, u32[]{:S(2)}, u32[]{:S(2)}) collective-permute-start(bf16[128,1408]{1,0:T(8,128)(2,1)} %slice.48), channel_id=1, source_target_pairs={{0,16},{1,17},{2,18},{3,19},{4,20},{5,21},{6,22},{7,23},{8,24},{9,... | collective-permute-start | bytes 1081352 | tf_op jit(solution)/shard_map/ppermute | solution.py:285
  91.9 1.2 copy-start.2
  93.1 1.1 copy-start.5
  94.2 1.1 copy-start.7
  99.6 17.5 %copy-start.14 = (bf16[640,448]{1,0:T(8,128)(2,1)}, bf16[640,448]{1,0:T(8,128)(2,1)S(1)}, u32[]{:S(2)}) copy-start(bf16[640,448]{1,0:T(8,128)(2,1)S(1)} %get-tuple-element.36) | copy-start | bytes 1720324
  99.6 5.9 %collective-permute-start.6 = (bf16[80,3072]{1,0:T(8,128)(2,1)S(1)}, bf16[80,3072]{1,0:T(8,128)(2,1)S(1)}, u32[]{:S(2)}, u32[]{:S(2)}) collective-permute-start(bf16[80,3072]{1,0:T(8,128)(2,1)S(1)} %get-tuple-element.30), channel_id=1, source_target_pairs={{0,64},{64,0},{128,192},{192,128},{256,320},{320,256},{384,448},{4... | collective-permute-start | bytes 1474568 | tf_op jit(solution)/shard_map/ppermute | solution.py:238
  103.5 13.3 %collective-permute-start.5 = (bf16[240,3072]{1,0:T(8,128)(2,1)S(1)}, bf16[240,3072]{1,0:T(8,128)(2,1)S(1)}, u32[]{:S(2)}, u32[]{:S(2)}) collective-permute-start(bf16[240,3072]{1,0:T(8,128)(2,1)S(1)} %get-tuple-element.28), channel_id=1, source_target_pairs={{0,64},{64,0},{128,192},{192,128},{256,320},{320,256},{384,448},{4... | collective-permute-start | bytes 4423688 | tf_op jit(solution)/shard_map/ppermute | solution.py:238
  105.6 17.0 %collective-permute-start.9 = (bf16[40,3072]{1,0:T(8,128)(2,1)S(1)}, bf16[40,3072]{1,0:T(8,128)(2,1)S(1)}, u32[]{:S(2)}, u32[]{:S(2)}) collective-permute-start(bf16[40,3072]{1,0:T(8,128)(2,1)S(1)} %get-tuple-element.42), channel_id=1, source_target_pairs={{0,384},{64,448},{128,0},{192,64},{256,128},{320,192},{384,256},{4... | collective-permute-start | bytes 737288 | tf_op jit(solution)/shard_map/ppermute | solution.py:242
  114.9 10.8 %collective-permute-start.7 = (bf16[40,3072]{1,0:T(8,128)(2,1)S(1)}, bf16[40,3072]{1,0:T(8,128)(2,1)S(1)}, u32[]{:S(2)}, u32[]{:S(2)}) collective-permute-start(bf16[40,3072]{1,0:T(8,128)(2,1)S(1)} %get-tuple-element.43), channel_id=1, source_target_pairs={{0,128},{64,192},{128,256},{192,320},{256,384},{320,448},{384,0},{... | collective-permute-start | bytes 737288 | tf_op jit(solution)/shard_map/ppermute | solution.py:242
  125.8 11.8 %collective-permute-start.8 = (bf16[80,3072]{1,0:T(8,128)(2,1)S(1)}, bf16[80,3072]{1,0:T(8,128)(2,1)S(1)}, u32[]{:S(2)}, u32[]{:S(2)}) collective-permute-start(bf16[80,3072]{1,0:T(8,128)(2,1)S(1)} %pad_maximum_fusion), channel_id=1, source_target_pairs={{0,128},{64,192},{128,256},{192,320},{256,384},{320,448},{384,0},{... | collective-permute-start | bytes 1474568 | tf_op jit(solution)/shard_map/ppermute | solution.py:242
  128.2 10.8 %collective-permute-start.10 = (bf16[80,3072]{1,0:T(8,128)(2,1)S(1)}, bf16[80,3072]{1,0:T(8,128)(2,1)S(1)}, u32[]{:S(2)}, u32[]{:S(2)}) collective-permute-start(bf16[80,3072]{1,0:T(8,128)(2,1)S(1)} %pad_maximum_fusion.1), channel_id=1, source_target_pairs={{0,384},{64,448},{128,0},{192,64},{256,128},{320,192},{384,256},{4... | collective-permute-start | bytes 1474568 | tf_op jit(solution)/shard_map/ppermute | solution.py:242
  139.5 21.0 %collective-permute-start.12 = (bf16[80,3072]{1,0:T(8,128)(2,1)S(1)}, bf16[80,3072]{1,0:T(8,128)(2,1)S(1)}, u32[]{:S(2)}, u32[]{:S(2)}) collective-permute-start(bf16[80,3072]{1,0:T(8,128)(2,1)S(1)} %shard_map.132), channel_id=1, source_target_pairs={{0,128},{64,192},{128,256},{192,320},{256,384},{320,448},{384,0},{... | collective-permute-start | bytes 1474568 | tf_op jit(solution)/shard_map/ppermute | solution.py:242
  146.9 15.8 %collective-permute-start.11 = (bf16[80,3072]{1,0:T(8,128)(2,1)S(1)}, bf16[80,3072]{1,0:T(8,128)(2,1)S(1)}, u32[]{:S(2)}, u32[]{:S(2)}) collective-permute-start(bf16[80,3072]{1,0:T(8,128)(2,1)S(1)} %shard_map.132), channel_id=1, source_target_pairs={{0,384},{64,448},{128,0},{192,64},{256,128},{320,192},{384,256},{4... | collective-permute-start | bytes 1474568 | tf_op jit(solution)/shard_map/ppermute | solution.py:242
  148.8 52.6 %copy-start.3 = (bf16[1,1024,448]{1,2,0:T(8,128)(2,1)S(1)}, bf16[1,1024,448]{1,2,0:T(8,128)(2,1)}, u32[]{:S(2)}) copy-start(bf16[1,1024,448]{1,2,0:T(8,128)(2,1)} %param.17) | copy-start | bytes 2752516
  160.5 19.9 %collective-permute-start.13 = (bf16[40,3072]{1,0:T(8,128)(2,1)S(1)}, bf16[40,3072]{1,0:T(8,128)(2,1)S(1)}, u32[]{:S(2)}, u32[]{:S(2)}) collective-permute-start(bf16[40,3072]{1,0:T(8,128)(2,1)S(1)} %slice.69), channel_id=1, source_target_pairs={{0,128},{64,192},{128,256},{192,320},{256,384},{320,448},{384,0},{... | collective-permute-start | bytes 737288 | tf_op jit(solution)/shard_map/ppermute | solution.py:242
  162.7 20.5 %collective-permute-start.14 = (bf16[40,3072]{1,0:T(8,128)(2,1)S(1)}, bf16[40,3072]{1,0:T(8,128)(2,1)S(1)}, u32[]{:S(2)}, u32[]{:S(2)}) collective-permute-start(bf16[40,3072]{1,0:T(8,128)(2,1)S(1)} %slice.70), channel_id=1, source_target_pairs={{0,384},{64,448},{128,0},{192,64},{256,128},{320,192},{384,256},{4... | collective-permute-start | bytes 737288 | tf_op jit(solution)/shard_map/ppermute | solution.py:242
  183.1 18.3 %collective-permute-start.15 = (bf16[320,3072]{1,0:T(8,128)(2,1)S(1)}, bf16[320,3072]{1,0:T(8,128)(2,1)S(1)}, u32[]{:S(2)}, u32[]{:S(2)}) collective-permute-start(bf16[320,3072]{1,0:T(8,128)(2,1)S(1)} %constant_dynamic-update-slice_fusion.refs_1_), channel_id=1, source_target_pairs={{0,64},{64,0},{128,192},{192,128},{256,320},{320,256},{384,448},{4... | collective-permute-start | bytes 5898248 | tf_op jit(solution)/shard_map/ppermute | solution.py:238
  204.7 1.5 copy-start.12
  206.2 29.5 %copy-start.15 = (bf16[640,448]{1,0:T(8,128)(2,1)S(1)}, bf16[640,448]{1,0:T(8,128)(2,1)}, u32[]{:S(2)}) copy-start(bf16[640,448]{1,0:T(8,128)(2,1)} %copy-done.14) | copy-start | bytes 1720324
  227.9 21.9 %all-to-all-start.4 = ((bf16[8,32,896]{2,1,0:T(8,128)(2,1)}), bf16[8,32,896]{2,1,0:T(8,128)(2,1)S(1)}, u32[]{:S(2)}, u32[]{:S(2)}) async-start(bf16[8,32,896]{2,1,0:T(8,128)(2,1)} %bitcast.12), calls=%async_computation.4 | async-start | bytes 917504 | tf_op jit(solution)/shard_map/all_to_all | solution.py:274
  235.7 3.3 %copy-start.13 = (bf16[640,2048]{1,0:T(8,128)(2,1)S(1)}, bf16[640,2048]{1,0:T(8,128)(2,1)}, u32[]{:S(2)}) copy-start(bf16[640,2048]{1,0:T(8,128)(2,1)} %copy-done.12) | copy-start | bytes 7864324

commit v9 on v8

--- a/solution.py
+++ b/solution.py
@@ -103,7 +103,7 @@
 
 
 def products_kernel(
-    grid, who_ref, recv_ref, s0, s1, s2a, s2b, s3, gate_ref, up_ref, down_ref,
+    grid, who_ref, recv_ref, s0, t0, s1, t1, s2, t2, s3, t3, gate_ref, up_ref, down_ref,
     rows_ref, far_ref, rest_ref, far_out_ref, rest_out_ref, restored_ref, grads_ref,
 ):
     nx, ny, nz = grid
@@ -136,18 +136,15 @@
 
     @pl.when(target == 1)
     def _():
-        n = s0.shape[0] // (ny * nz)
-        half = ny // 2
-        for k in range(nx):
-            x = lax.rem(my_x - k + nx, nx)
-            for y in range(ny):
-                source, first = ((s0, 0), (s1, 0), ((s2a, 0), (s2b, half))[y >= half], (s3, 0))[k]
-                for other in range(nz):
-                    z = 1 - my_z if other else my_z
+        n = s0.shape[0] // ny
+        for k, sources in enumerate(((s0, t0), (s1, t1), (s2, t2), (s3, t3))):
+            for other in range(nz):
+                x = lax.rem(my_x - k + nx, nx)
+                z = 1 - my_z if other else my_z
+                for y in range(ny):
                     to = pl.ds(pl.multiple_of(((x * ny + y) * nz + z) * n, n), n)
-                    r = ((y - first) * nz + other) * n
                     for m in range(3):
-                        restored_ref[m, to, :] = source[r : r + n, m * feat : (m + 1) * feat]
+                        restored_ref[m, to, :] = sources[other][y * n : (y + 1) * n, m * feat : (m + 1) * feat]
 
         @pl.loop(0, tiles)
         def _(j):
@@ -303,19 +300,20 @@
 
     saved = jnp.transpose(backup, (2, 0, 1)).reshape(ffr, 3 * feat)
     saved = jnp.pad(saved, ((0, 0), (0, -3 * feat % 128)))
-    saved = jnp.concatenate([saved, step(saved, 0, 1)], axis=0)
     saved = exchange(jnp.broadcast_to(saved, (ny, *saved.shape)), along_y)
-    saved = saved.reshape(ny * nz * ffr, -1)
-
+    saved = saved.reshape(ny * ffr, -1)
     (first,) = call(functools.partial(pack_kernel, grid), [(ny, tok, LANES)], operands=4)(
         expert_ids, route_weight, tokens, cotangent
     )
     first, saved = lax.optimization_barrier((first, saved))
+    other_z = step(saved, 0, 1)
     before, after = step(saved, 1, 0), step(saved, -1, 0)
     first = exchange(first, along_y)
-    first, before, after = lax.optimization_barrier((first, before, after))
-    half = saved.shape[0] // 2
-    blocks = saved, before, step(before[:half], 1, 0), step(after[half:], -1, 0), after
+    first, other_z, before, after = lax.optimization_barrier((first, other_z, before, after))
+    before_z, after_z = step(other_z, 1, 0), step(other_z, -1, 0)
+    blocks = (
+        saved, other_z, before, before_z, step(before, 1, 0), step(after_z, -1, 0), after, after_z,
+    )
 
     out_rows, seen = ny * capacity, ny * tok
     row, col = np.arange(out_rows)[:, None], np.arange(seen)[None, :]
@@ -335,7 +333,7 @@
         ],
         scratch=[pltpu.VMEM((8 * chunk, feat), BF)],
         scalars=1,
-        operands=9,
+        operands=12,
         megabytes=18,
     )(who, recv, *blocks, w_gate, w_up, w_down)
 

time: 252 us -> 246 us (0.976)
  waiting for transfers between devices: 101 us -> 80.1 us
  starting transfers between devices: 97.1 us -> 110 us
    all_to_all x4, waiting for transfers between devices: 26.6 us -> 15 us  [exchange(): lax.all_to_all(flat, 'expert', 0, 0, axis_index_groups=groups, tiled=True)]
    ppermute x5 -> x7, waiting for transfers between devices: 30.2 us -> 22.4 us  [step(): return lax.ppermute(v, 'expert', pairs)]
    ppermute x5 -> x7, starting transfers between devices: 19.2 us -> 26.7 us  [step(): return lax.ppermute(v, 'expert', pairs)]
    unnamed x42 -> x38, local copies, waits for them, and re-layouts: 6.23 us -> 10.3 us
    slice x2 -> x0, local copies, waits for them, and re-layouts: 3.51 us -> none  [the longest x1 1.76 us: body(): before[:half]]
    ppermute x3, starting transfers between devices: 20.6 us -> 24 us  [core_swap(): return lax.ppermute(x, 'dp', [(i, i ^ 1) for i in range(8)])]
  transfers between devices with their start and end apart: 20 -> 22, of which waited for: 16 -> 16; matrix products, arithmetic and copies ran while one was open for 4% -> 3% of each run, Pallas kernels for 0% -> 1%
where the time goes in v9:
time: 246 us; the launch traced here: 245 us
  starting transfers between devices  110 us (45%)
  waiting for transfers between devices  80.1 us (33%)
  blocking collectives  21.4 us (9%)
  Pallas kernels  13.2 us (5%)
  local copies, waits for them, and re-layouts  12.3 us (5%)
  matrix products  5.12 us (2%)
    ppermute x8, waiting for transfers between devices, shift(): lax.ppermute(x, 'dp', [(2 * h + c, 2 * ((h + k) % 4) + c) for h in range(...  39.2 us
    ppermute x8, starting transfers between devices, shift(): lax.ppermute(x, 'dp', [(2 * h + c, 2 * ((h + k) % 4) + c) for h in range(...  36.4 us
    ppermute x7, starting transfers between devices, step(): return lax.ppermute(v, 'expert', pairs)  26.7 us
    ppermute x3, starting transfers between devices, core_swap(): return lax.ppermute(x, 'dp', [(i, i ^ 1) for i in range(8)])  24 us
    all_to_all x4, starting transfers between devices, exchange(): lax.all_to_all(flat, 'expert', 0, 0, axis_index_groups=groups, tiled=True)  23.2 us
    ppermute x7, waiting for transfers between devices, step(): return lax.ppermute(v, 'expert', pairs)  22.4 us
    all_to_all x1, blocking collectives, exchange(): lax.all_to_all(flat, 'expert', 0, 0, axis_index_groups=groups, tiled=True)  21.4 us
    all_to_all x4, waiting for transfers between devices, exchange(): lax.all_to_all(flat, 'expert', 0, 0, axis_index_groups=groups, tiled=True)  15 us
  transfers between devices with their start and end apart: 22, of which 16 were waited for; matrix products, arithmetic and copies ran while one was open for 3% of the time, Pallas kernels for 1%

profile of v9, /device:TPU:1, one launch (start us, length us, event | category | flops | bytes accessed | tf_op | source)
XLA Modules:
  0.0 244.7 jit_solution(7682837798890561983)
XLA Ops:
  2.4 7.7 %all-to-all-start = ((bf16[8,16,1408]{2,1,0:T(8,128)(2,1)}), bf16[8,16,1408]{2,1,0:T(8,128)(2,1)S(1)}, u32[]{:S(2)}, u32[]{:S(2)}) async-start(bf16[8,16,1408]{2,1,0:T(8,128)(2,1)} %broadcast_in_dim.9), calls=%async_computation | async-start | bytes 720896 | tf_op jit(solution)/shard_map/all_to_all | solution.py:271
  13.1 1.2 shard_map.129
  14.3 6.1 %all-to-all-done = bf16[8,16,1408]{2,1,0:T(8,128)(2,1)S(1)} async-done(((bf16[8,16,1408]{2,1,0:T(8,128)(2,1)}), bf16[8,16,1408]{2,1,0:T(8,128)(2,1)S(1)}, u32[]{:S(2)}, u32[]{:S(2)}) %all-to-all-start) | async-done | bytes 360480 | tf_op jit(solution)/shard_map/all_to_all | solution.py:271
  20.4 3.7 %all-to-all-start.1 = ((bf16[8,32,1024]{2,1,0:T(8,128)(2,1)}), bf16[8,32,1024]{2,1,0:T(8,128)(2,1)S(1)}, u32[]{:S(2)}, u32[]{:S(2)}) async-start(bf16[8,32,1024]{2,1,0:T(8,128)(2,1)} %shard_map.129), calls=%async_computation.1 | async-start | bytes 1048576 | tf_op jit(solution)/shard_map/all_to_all | solution.py:271
  24.1 6.9 %collective-permute-start.2 = (bf16[128,1408]{1,0:T(8,128)(2,1)S(1)}, bf16[128,1408]{1,0:T(8,128)(2,1)S(1)}, u32[]{:S(2)}, u32[]{:S(2)}) collective-permute-start(bf16[128,1408]{1,0:T(8,128)(2,1)S(1)} %bitcast.27), channel_id=1, source_target_pairs={{0,48},{1,49},{2,50},{3,51},{4,52},{5,53},{6,54},{7,55},{8,56},{9,... | collective-permute-start | bytes 1081352 | tf_op jit(solution)/shard_map/ppermute | solution.py:282
  31.0 1.9 collective-permute-start.1
  32.9 4.0 %collective-permute-start = (bf16[128,1408]{1,0:T(8,128)(2,1)S(1)}, bf16[128,1408]{1,0:T(8,128)(2,1)}, u32[]{:S(2)}, u32[]{:S(2)}) collective-permute-start(bf16[128,1408]{1,0:T(8,128)(2,1)S(1)} %bitcast.29), channel_id=1, source_target_pairs={{0,1},{1,0},{2,3},{3,2},{4,5},{5,4},{6,7},{7,6},{8,9},{9,8},{10,11... | collective-permute-start | bytes 1081352 | tf_op jit(solution)/shard_map/ppermute | solution.py:282
  37.7 4.0 %collective-permute-done.1.s1 = bf16[128,1408]{1,0:T(8,128)(2,1)S(1)} collective-permute-done((bf16[128,1408]{1,0:T(8,128)(2,1)S(1)}, bf16[128,1408]{1,0:T(8,128)(2,1)S(1)}, u32[]{:S(2)}, u32[]{:S(2)}) %collective-permute-start.1) | collective-permute-done | bytes 360480 | tf_op jit(solution)/shard_map/ppermute | solution.py:282
  42.4 1.0 collective-permute-done.t0
  43.5 1.4 shard_map.130
  44.8 1.0 copy-done.4
  45.8 4.7 %all-to-all-start.2 = ((bf16[8,80,896]{2,1,0:T(8,128)(2,1)}), bf16[8,80,896]{2,1,0:T(8,128)(2,1)S(1)}, u32[]{:S(2)}, u32[]{:S(2)}) async-start(bf16[8,80,896]{2,1,0:T(8,128)(2,1)} %copy-done.4), calls=%async_computation.2 | async-start | bytes 2293760 | tf_op jit(solution)/shard_map/all_to_all | solution.py:271
  50.5 4.6 %collective-permute-start.5 = (bf16[128,1408]{1,0:T(8,128)(2,1)}, bf16[128,1408]{1,0:T(8,128)(2,1)}, u32[]{:S(2)}, u32[]{:S(2)}) collective-permute-start(bf16[128,1408]{1,0:T(8,128)(2,1)} %collective-permute-done.t0), channel_id=1, source_target_pairs={{0,48},{1,49},{2,50},{3,51},{4,52},{5,53},{6,54},{7,55},{8,56},{9,... | collective-permute-start | bytes 1081352 | tf_op jit(solution)/shard_map/ppermute | solution.py:282
  55.1 1.9 collective-permute-start.3
  57.0 2.2 collective-permute-start.4
  59.2 11.9 %collective-permute-done.5.t3 = bf16[128,1408]{1,0:T(8,128)(2,1)} collective-permute-done((bf16[128,1408]{1,0:T(8,128)(2,1)}, bf16[128,1408]{1,0:T(8,128)(2,1)}, u32[]{:S(2)}, u32[]{:S(2)}) %collective-permute-start.5) | collective-permute-done | bytes 360480 | tf_op jit(solution)/shard_map/ppermute | solution.py:282
  71.1 5.3 %collective-permute-start.6 = (bf16[128,1408]{1,0:T(8,128)(2,1)}, bf16[128,1408]{1,0:T(8,128)(2,1)}, u32[]{:S(2)}, u32[]{:S(2)}) collective-permute-start(bf16[128,1408]{1,0:T(8,128)(2,1)} %collective-permute-done.5.t3), channel_id=1, source_target_pairs={{0,48},{1,49},{2,50},{3,51},{4,52},{5,53},{6,54},{7,55},{8,56},{9,... | collective-permute-start | bytes 1081352 | tf_op jit(solution)/shard_map/ppermute | solution.py:282
  77.1 4.3 %collective-permute-done.4.s2 = bf16[128,1408]{1,0:T(8,128)(2,1)} collective-permute-done((bf16[128,1408]{1,0:T(8,128)(2,1)}, bf16[128,1408]{1,0:T(8,128)(2,1)}, u32[]{:S(2)}, u32[]{:S(2)}) %collective-permute-start.4) | collective-permute-done | bytes 360480 | tf_op jit(solution)/shard_map/ppermute | solution.py:282
  81.5 1.2 collective-permute-done.6.t2
  82.6 1.2 copy-done.2
  85.8 4.5 %shard_map.131 = (bf16[640,448]{1,0:T(8,128)(2,1)S(1)}, bf16[80,3072]{1,0:T(8,128)(2,1)S(1)}, bf16[240,3072]{1,0:T(8,128)(2,1)S(1)}, bf16[80,3072]{1,0:T(8,128)(...) custom-call(s32[5]{0:T(128)S(1)} %stack.27.who_ref.refs_0_, ...), custom_call_target="tpu_custom_call" | custom-call | tf_op jit(solution)/shard_map/pallas_call | solution.py:328
  90.3 4.6 %collective-permute-start.8 = (bf16[80,3072]{1,0:T(8,128)(2,1)S(1)}, bf16[80,3072]{1,0:T(8,128)(2,1)S(1)}, u32[]{:S(2)}, u32[]{:S(2)}) collective-permute-start(bf16[80,3072]{1,0:T(8,128)(2,1)S(1)} %get-tuple-element.32), channel_id=1, source_target_pairs={{0,64},{64,0},{128,192},{192,128},{256,320},{320,256},{384,448},{4... | collective-permute-start | bytes 1474568 | tf_op jit(solution)/shard_map/ppermute | solution.py:235
  94.9 1.9 collective-permute-start.7
  97.0 9.8 %collective-permute-start.11 = (bf16[40,3072]{1,0:T(8,128)(2,1)S(1)}, bf16[40,3072]{1,0:T(8,128)(2,1)S(1)}, u32[]{:S(2)}, u32[]{:S(2)}) collective-permute-start(bf16[40,3072]{1,0:T(8,128)(2,1)S(1)} %get-tuple-element.44), channel_id=1, source_target_pairs={{0,384},{64,448},{128,0},{192,64},{256,128},{320,192},{384,256},{4... | collective-permute-start | bytes 737288 | tf_op jit(solution)/shard_map/ppermute | solution.py:239
  106.7 1.9 collective-permute-start.9
  109.0 4.9 %collective-permute-done.11 = bf16[40,3072]{1,0:T(8,128)(2,1)S(1)} collective-permute-done((bf16[40,3072]{1,0:T(8,128)(2,1)S(1)}, bf16[40,3072]{1,0:T(8,128)(2,1)S(1)}, u32[]{:S(2)}, u32[]{:S(2)}) %collective-permute-start.11) | collective-permute-done | bytes 245792 | tf_op jit(solution)/shard_map/ppermute | solution.py:239
  114.0 3.8 %collective-permute-done.9 = bf16[40,3072]{1,0:T(8,128)(2,1)S(1)} collective-permute-done((bf16[40,3072]{1,0:T(8,128)(2,1)S(1)}, bf16[40,3072]{1,0:T(8,128)(2,1)S(1)}, u32[]{:S(2)}, u32[]{:S(2)}) %collective-permute-start.9) | collective-permute-done | bytes 245792 | tf_op jit(solution)/shard_map/ppermute | solution.py:239
  118.0 2.3 collective-permute-start.10
  120.3 5.1 %collective-permute-start.12 = (bf16[80,3072]{1,0:T(8,128)(2,1)S(1)}, bf16[80,3072]{1,0:T(8,128)(2,1)S(1)}, u32[]{:S(2)}, u32[]{:S(2)}) collective-permute-start(bf16[80,3072]{1,0:T(8,128)(2,1)S(1)} %pad_maximum_fusion.1), channel_id=1, source_target_pairs={{0,384},{64,448},{128,0},{192,64},{256,128},{320,192},{384,256},{4... | collective-permute-start | bytes 1474568 | tf_op jit(solution)/shard_map/ppermute | solution.py:239
  125.4 4.6 %collective-permute-done.10.left_ref = bf16[80,3072]{1,0:T(8,128)(2,1)S(1)} collective-permute-done((bf16[80,3072]{1,0:T(8,128)(2,1)S(1)}, bf16[80,3072]{1,0:T(8,128)(2,1)S(1)}, u32[]{:S(2)}, u32[]{:S(2)}) %collective-permute-start.10) | collective-permute-done | bytes 491552 | tf_op jit(solution)/shard_map/ppermute | solution.py:239
  130.0 1.2 collective-permute-done.12.right_ref
  131.6 7.8 %collective-permute-start.14 = (bf16[80,3072]{1,0:T(8,128)(2,1)S(1)}, bf16[80,3072]{1,0:T(8,128)(2,1)S(1)}, u32[]{:S(2)}, u32[]{:S(2)}) collective-permute-start(bf16[80,3072]{1,0:T(8,128)(2,1)S(1)} %shard_map.132), channel_id=1, source_target_pairs={{0,128},{64,192},{128,256},{192,320},{256,384},{320,448},{384,0},{... | collective-permute-start | bytes 1474568 | tf_op jit(solution)/shard_map/ppermute | solution.py:239
  139.4 1.9 collective-permute-start.13
  141.4 10.3 %collective-permute-done.14 = bf16[80,3072]{1,0:T(8,128)(2,1)S(1)} collective-permute-done((bf16[80,3072]{1,0:T(8,128)(2,1)S(1)}, bf16[80,3072]{1,0:T(8,128)(2,1)S(1)}, u32[]{:S(2)}, u32[]{:S(2)}) %collective-permute-start.14) | collective-permute-done | bytes 491552 | tf_op jit(solution)/shard_map/ppermute | solution.py:239
  151.8 1.9 collective-permute-start.15
  154.1 5.7 %collective-permute-start.16 = (bf16[40,3072]{1,0:T(8,128)(2,1)S(1)}, bf16[40,3072]{1,0:T(8,128)(2,1)S(1)}, u32[]{:S(2)}, u32[]{:S(2)}) collective-permute-start(bf16[40,3072]{1,0:T(8,128)(2,1)S(1)} %slice.62), channel_id=1, source_target_pairs={{0,384},{64,448},{128,0},{192,64},{256,128},{320,192},{384,256},{4... | collective-permute-start | bytes 737288 | tf_op jit(solution)/shard_map/ppermute | solution.py:239
  159.8 12.1 %collective-permute-done.15 = bf16[40,3072]{1,0:T(8,128)(2,1)S(1)} collective-permute-done((bf16[40,3072]{1,0:T(8,128)(2,1)S(1)}, bf16[40,3072]{1,0:T(8,128)(2,1)S(1)}, u32[]{:S(2)}, u32[]{:S(2)}) %collective-permute-start.15) | collective-permute-done | bytes 245792 | tf_op jit(solution)/shard_map/ppermute | solution.py:239
  171.9 1.8 collective-permute-done.16
  173.8 17.5 %collective-permute-start.17 = (bf16[320,3072]{1,0:T(8,128)(2,1)S(1)}, bf16[320,3072]{1,0:T(8,128)(2,1)S(1)}, u32[]{:S(2)}, u32[]{:S(2)}) collective-permute-start(bf16[320,3072]{1,0:T(8,128)(2,1)S(1)} %constant_dynamic-update-slice_fusion.refs_1_), channel_id=1, source_target_pairs={{0,64},{64,0},{128,192},{192,128},{256,320},{320,256},{384,448},{4... | collective-permute-start | bytes 5898248 | tf_op jit(solution)/shard_map/ppermute | solution.py:235
  191.3 3.6 %collective-permute-done.17.refs_2_ = bf16[320,3072]{1,0:T(8,128)(2,1)S(1)} collective-permute-done((bf16[320,3072]{1,0:T(8,128)(2,1)S(1)}, bf16[320,3072]{1,0:T(8,128)(2,1)S(1)}, u32[]{:S(2)}, u32[]{:S(2)}) %collective-permute-start.17) | collective-permute-done | bytes 1966112 | tf_op jit(solution)/shard_map/ppermute | solution.py:235
  194.9 3.2 %shard_map.133 = (bf16[8,80,896]{2,1,0:T(8,128)(2,1)S(1)}, bf16[640,2048]{1,0:T(8,128)(2,1)S(1)}) custom-call(s32[5]{0:T(128)S(1)} %stack.27.who_ref.refs_0_, bf16[320,3072]{1,0:T(8,128)(2,1)S(1)} %constant_dynamic-update-slice_fusion.refs_1_, bf16[320,3072]{1,0:T(8,128)(2,1)S(1)} %collective-permute-done.17.refs_2_, bf16[448,1024]{1,0:T(8,128)(2,1)S(1)} %bitcast.22, ...), custom_call_target="tpu_custom_call" | custom-call | tf_op jit(solution)/shard_map/pallas_call | solution.py:358
  198.1 1.5 copy-done.12
  199.6 21.4 %all_to_all.36.recv_ref = bf16[8,80,896]{2,1,0:T(8,128)(2,1)S(1)} all-to-all(bf16[8,80,896]{2,1,0:T(8,128)(2,1)S(1)} %get-tuple-element.34), channel_id=1, replica_groups={{0,1,16,17,32,33,48,49},{2,3,18,19,34,35,50,51},{4,5,20,21,36,37,52,53}..., dimensions={0} | all-to-all | bytes 2293760 | tf_op jit(solution)/shard_map/all_to_all | solution.py:271
  221.0 1.7 shard_map.134
  222.7 7.2 %all-to-all-start.4 = ((bf16[8,32,896]{2,1,0:T(8,128)(2,1)}), bf16[8,32,896]{2,1,0:T(8,128)(2,1)S(1)}, u32[]{:S(2)}, u32[]{:S(2)}) async-start(bf16[8,32,896]{2,1,0:T(8,128)(2,1)} %bitcast.12), calls=%async_computation.4 | async-start | bytes 917504 | tf_op jit(solution)/shard_map/all_to_all | solution.py:271
  229.9 3.3 %fusion.1 = bf16[1,448,1024]{2,1,0:T(8,128)(2,1)} fusion(bf16[640,448]{1,0:T(8,128)(2,1)S(1)} %copy-done.15, bf16[640,2048]{1,0:T(8,128)(2,1)} %copy-done.12), kind=kOutput, calls=%fused_computation.4 | convolution fusion | flops 587661312 | bytes 2801664 | tf_op jit(solution)/shard_map/dot_general | solution.py:22
  233.2 1.8 fusion
  235.0 8.9 %all-to-all-done.4.recv_ref = bf16[8,32,896]{2,1,0:T(8,128)(2,1)S(1)} async-done(((bf16[8,32,896]{2,1,0:T(8,128)(2,1)}), bf16[8,32,896]{2,1,0:T(8,128)(2,1)S(1)}, u32[]{:S(2)}, u32[]{:S(2)}) %all-to-all-start.4) | async-done | bytes 458784 | tf_op jit(solution)/shard_map/all_to_all | solution.py:271
  (59 shorter events, 10.7 us)
Async XLA Ops:
  0.6 42.8 %copy-start.9 = (f32[80,256]{1,0:T(8,128)S(1)}, f32[80,256]{1,0:T(8,128)}, u32[]{:S(2)}) copy-start(f32[80,256]{1,0:T(8,128)} %constant.53.clone.want_ref) | copy-start | bytes 245764
  2.4 18.0 %all-to-all-start = ((bf16[8,16,1408]{2,1,0:T(8,128)(2,1)}), bf16[8,16,1408]{2,1,0:T(8,128)(2,1)S(1)}, u32[]{:S(2)}, u32[]{:S(2)}) async-start(bf16[8,16,1408]{2,1,0:T(8,128)(2,1)} %broadcast_in_dim.9), calls=%async_computation | async-start | bytes 720896 | tf_op jit(solution)/shard_map/all_to_all | solution.py:271
  11.6 0.8 copy-start.10
  12.3 0.8 copy-start.11
  20.4 62.2 %copy-start = (bf16[1,448,1024]{2,1,0:T(8,128)(2,1)S(1)}, bf16[1,448,1024]{2,1,0:T(8,128)(2,1)}, u32[]{:S(2)}) copy-start(bf16[1,448,1024]{2,1,0:T(8,128)(2,1)} %param.15) | copy-start | bytes 2752516
  20.4 62.2 %copy-start.1 = (bf16[1,448,1024]{2,1,0:T(8,128)(2,1)S(1)}, bf16[1,448,1024]{2,1,0:T(8,128)(2,1)}, u32[]{:S(2)}) copy-start(bf16[1,448,1024]{2,1,0:T(8,128)(2,1)} %param.16) | copy-start | bytes 2752516
  20.4 23.0 %all-to-all-start.1 = ((bf16[8,32,1024]{2,1,0:T(8,128)(2,1)}), bf16[8,32,1024]{2,1,0:T(8,128)(2,1)S(1)}, u32[]{:S(2)}, u32[]{:S(2)}) async-start(bf16[8,32,1024]{2,1,0:T(8,128)(2,1)} %shard_map.129), calls=%async_computation.1 | async-start | bytes 1048576 | tf_op jit(solution)/shard_map/all_to_all | solution.py:271
  24.1 12.8 %collective-permute-start.2 = (bf16[128,1408]{1,0:T(8,128)(2,1)S(1)}, bf16[128,1408]{1,0:T(8,128)(2,1)S(1)}, u32[]{:S(2)}, u32[]{:S(2)}) collective-permute-start(bf16[128,1408]{1,0:T(8,128)(2,1)S(1)} %bitcast.27), channel_id=1, source_target_pairs={{0,48},{1,49},{2,50},{3,51},{4,52},{5,53},{6,54},{7,55},{8,56},{9,... | collective-permute-start | bytes 1081352 | tf_op jit(solution)/shard_map/ppermute | solution.py:282
  31.0 10.7 %collective-permute-start.1 = (bf16[128,1408]{1,0:T(8,128)(2,1)S(1)}, bf16[128,1408]{1,0:T(8,128)(2,1)S(1)}, u32[]{:S(2)}, u32[]{:S(2)}) collective-permute-start(bf16[128,1408]{1,0:T(8,128)(2,1)S(1)} %bitcast.28), channel_id=1, source_target_pairs={{0,16},{1,17},{2,18},{3,19},{4,20},{5,21},{6,22},{7,23},{8,24},{9,... | collective-permute-start | bytes 1081352 | tf_op jit(solution)/shard_map/ppermute | solution.py:282
  32.9 10.5 %collective-permute-start = (bf16[128,1408]{1,0:T(8,128)(2,1)S(1)}, bf16[128,1408]{1,0:T(8,128)(2,1)}, u32[]{:S(2)}, u32[]{:S(2)}) collective-permute-start(bf16[128,1408]{1,0:T(8,128)(2,1)S(1)} %bitcast.29), channel_id=1, source_target_pairs={{0,1},{1,0},{2,3},{3,2},{4,5},{5,4},{6,7},{7,6},{8,9},{9,8},{10,11... | collective-permute-start | bytes 1081352 | tf_op jit(solution)/shard_map/ppermute | solution.py:282
  36.9 0.7 copy-start.5
  41.7 0.7 copy-start.7
  44.8 1.0 copy-start.4
  45.8 36.8 %all-to-all-start.2 = ((bf16[8,80,896]{2,1,0:T(8,128)(2,1)}), bf16[8,80,896]{2,1,0:T(8,128)(2,1)S(1)}, u32[]{:S(2)}, u32[]{:S(2)}) async-start(bf16[8,80,896]{2,1,0:T(8,128)(2,1)} %copy-done.4), calls=%async_computation.2 | async-start | bytes 2293760 | tf_op jit(solution)/shard_map/all_to_all | solution.py:271
  50.5 20.5 %collective-permute-start.5 = (bf16[128,1408]{1,0:T(8,128)(2,1)}, bf16[128,1408]{1,0:T(8,128)(2,1)}, u32[]{:S(2)}, u32[]{:S(2)}) collective-permute-start(bf16[128,1408]{1,0:T(8,128)(2,1)} %collective-permute-done.t0), channel_id=1, source_target_pairs={{0,48},{1,49},{2,50},{3,51},{4,52},{5,53},{6,54},{7,55},{8,56},{9,... | collective-permute-start | bytes 1081352 | tf_op jit(solution)/shard_map/ppermute | solution.py:282
  55.1 26.4 %collective-permute-start.3 = (bf16[128,1408]{1,0:T(8,128)(2,1)}, bf16[128,1408]{1,0:T(8,128)(2,1)}, u32[]{:S(2)}, u32[]{:S(2)}) collective-permute-start(bf16[128,1408]{1,0:T(8,128)(2,1)} %collective-permute-done.t0), channel_id=1, source_target_pairs={{0,16},{1,17},{2,18},{3,19},{4,20},{5,21},{6,22},{7,23},{8,24},{9,... | collective-permute-start | bytes 1081352 | tf_op jit(solution)/shard_map/ppermute | solution.py:282
  57.0 24.4 %collective-permute-start.4 = (bf16[128,1408]{1,0:T(8,128)(2,1)}, bf16[128,1408]{1,0:T(8,128)(2,1)}, u32[]{:S(2)}, u32[]{:S(2)}) collective-permute-start(bf16[128,1408]{1,0:T(8,128)(2,1)} %copy-done.7), channel_id=1, source_target_pairs={{0,16},{1,17},{2,18},{3,19},{4,20},{5,21},{6,22},{7,23},{8,24},{9,... | collective-permute-start | bytes 1081352 | tf_op jit(solution)/shard_map/ppermute | solution.py:282
  71.1 11.6 %collective-permute-start.6 = (bf16[128,1408]{1,0:T(8,128)(2,1)}, bf16[128,1408]{1,0:T(8,128)(2,1)}, u32[]{:S(2)}, u32[]{:S(2)}) collective-permute-start(bf16[128,1408]{1,0:T(8,128)(2,1)} %collective-permute-done.5.t3), channel_id=1, source_target_pairs={{0,48},{1,49},{2,50},{3,51},{4,52},{5,53},{6,54},{7,55},{8,56},{9,... | collective-permute-start | bytes 1081352 | tf_op jit(solution)/shard_map/ppermute | solution.py:282
  82.6 1.2 copy-start.2
  83.8 1.0 copy-start.6
  84.8 1.0 copy-start.8
  90.3 18.7 %copy-start.14 = (bf16[640,448]{1,0:T(8,128)(2,1)}, bf16[640,448]{1,0:T(8,128)(2,1)S(1)}, u32[]{:S(2)}) copy-start(bf16[640,448]{1,0:T(8,128)(2,1)S(1)} %get-tuple-element.38) | copy-start | bytes 1720324
  90.3 6.5 %collective-permute-start.8 = (bf16[80,3072]{1,0:T(8,128)(2,1)S(1)}, bf16[80,3072]{1,0:T(8,128)(2,1)S(1)}, u32[]{:S(2)}, u32[]{:S(2)}) collective-permute-start(bf16[80,3072]{1,0:T(8,128)(2,1)S(1)} %get-tuple-element.32), channel_id=1, source_target_pairs={{0,64},{64,0},{128,192},{192,128},{256,320},{320,256},{384,448},{4... | collective-permute-start | bytes 1474568 | tf_op jit(solution)/shard_map/ppermute | solution.py:235
  94.9 13.8 %collective-permute-start.7 = (bf16[240,3072]{1,0:T(8,128)(2,1)S(1)}, bf16[240,3072]{1,0:T(8,128)(2,1)S(1)}, u32[]{:S(2)}, u32[]{:S(2)}) collective-permute-start(bf16[240,3072]{1,0:T(8,128)(2,1)S(1)} %get-tuple-element.30), channel_id=1, source_target_pairs={{0,64},{64,0},{128,192},{192,128},{256,320},{320,256},{384,448},{4... | collective-permute-start | bytes 4423688 | tf_op jit(solution)/shard_map/ppermute | solution.py:235
  97.0 17.0 %collective-permute-start.11 = (bf16[40,3072]{1,0:T(8,128)(2,1)S(1)}, bf16[40,3072]{1,0:T(8,128)(2,1)S(1)}, u32[]{:S(2)}, u32[]{:S(2)}) collective-permute-start(bf16[40,3072]{1,0:T(8,128)(2,1)S(1)} %get-tuple-element.44), channel_id=1, source_target_pairs={{0,384},{64,448},{128,0},{192,64},{256,128},{320,192},{384,256},{4... | collective-permute-start | bytes 737288 | tf_op jit(solution)/shard_map/ppermute | solution.py:239
  106.7 11.1 %collective-permute-start.9 = (bf16[40,3072]{1,0:T(8,128)(2,1)S(1)}, bf16[40,3072]{1,0:T(8,128)(2,1)S(1)}, u32[]{:S(2)}, u32[]{:S(2)}) collective-permute-start(bf16[40,3072]{1,0:T(8,128)(2,1)S(1)} %get-tuple-element.45), channel_id=1, source_target_pairs={{0,128},{64,192},{128,256},{192,320},{256,384},{320,448},{384,0},{... | collective-permute-start | bytes 737288 | tf_op jit(solution)/shard_map/ppermute | solution.py:239
  118.0 12.0 %collective-permute-start.10 = (bf16[80,3072]{1,0:T(8,128)(2,1)S(1)}, bf16[80,3072]{1,0:T(8,128)(2,1)S(1)}, u32[]{:S(2)}, u32[]{:S(2)}) collective-permute-start(bf16[80,3072]{1,0:T(8,128)(2,1)S(1)} %pad_maximum_fusion), channel_id=1, source_target_pairs={{0,128},{64,192},{128,256},{192,320},{256,384},{320,448},{384,0},{... | collective-permute-start | bytes 1474568 | tf_op jit(solution)/shard_map/ppermute | solution.py:239
  120.3 10.9 %collective-permute-start.12 = (bf16[80,3072]{1,0:T(8,128)(2,1)S(1)}, bf16[80,3072]{1,0:T(8,128)(2,1)S(1)}, u32[]{:S(2)}, u32[]{:S(2)}) collective-permute-start(bf16[80,3072]{1,0:T(8,128)(2,1)S(1)} %pad_maximum_fusion.1), channel_id=1, source_target_pairs={{0,384},{64,448},{128,0},{192,64},{256,128},{320,192},{384,256},{4... | collective-permute-start | bytes 1474568 | tf_op jit(solution)/shard_map/ppermute | solution.py:239
  131.6 20.1 %collective-permute-start.14 = (bf16[80,3072]{1,0:T(8,128)(2,1)S(1)}, bf16[80,3072]{1,0:T(8,128)(2,1)S(1)}, u32[]{:S(2)}, u32[]{:S(2)}) collective-permute-start(bf16[80,3072]{1,0:T(8,128)(2,1)S(1)} %shard_map.132), channel_id=1, source_target_pairs={{0,128},{64,192},{128,256},{192,320},{256,384},{320,448},{384,0},{... | collective-permute-start | bytes 1474568 | tf_op jit(solution)/shard_map/ppermute | solution.py:239
  139.4 14.6 %collective-permute-start.13 = (bf16[80,3072]{1,0:T(8,128)(2,1)S(1)}, bf16[80,3072]{1,0:T(8,128)(2,1)S(1)}, u32[]{:S(2)}, u32[]{:S(2)}) collective-permute-start(bf16[80,3072]{1,0:T(8,128)(2,1)S(1)} %shard_map.132), channel_id=1, source_target_pairs={{0,384},{64,448},{128,0},{192,64},{256,128},{320,192},{384,256},{4... | collective-permute-start | bytes 1474568 | tf_op jit(solution)/shard_map/ppermute | solution.py:239
  141.4 53.5 %copy-start.3 = (bf16[1,1024,448]{1,2,0:T(8,128)(2,1)S(1)}, bf16[1,1024,448]{1,2,0:T(8,128)(2,1)}, u32[]{:S(2)}) copy-start(bf16[1,1024,448]{1,2,0:T(8,128)(2,1)} %param.17) | copy-start | bytes 2752516
  151.8 20.2 %collective-permute-start.15 = (bf16[40,3072]{1,0:T(8,128)(2,1)S(1)}, bf16[40,3072]{1,0:T(8,128)(2,1)S(1)}, u32[]{:S(2)}, u32[]{:S(2)}) collective-permute-start(bf16[40,3072]{1,0:T(8,128)(2,1)S(1)} %slice.61), channel_id=1, source_target_pairs={{0,128},{64,192},{128,256},{192,320},{256,384},{320,448},{384,0},{... | collective-permute-start | bytes 737288 | tf_op jit(solution)/shard_map/ppermute | solution.py:239
  154.1 19.7 %collective-permute-start.16 = (bf16[40,3072]{1,0:T(8,128)(2,1)S(1)}, bf16[40,3072]{1,0:T(8,128)(2,1)S(1)}, u32[]{:S(2)}, u32[]{:S(2)}) collective-permute-start(bf16[40,3072]{1,0:T(8,128)(2,1)S(1)} %slice.62), channel_id=1, source_target_pairs={{0,384},{64,448},{128,0},{192,64},{256,128},{320,192},{384,256},{4... | collective-permute-start | bytes 737288 | tf_op jit(solution)/shard_map/ppermute | solution.py:239
  173.8 21.1 %collective-permute-start.17 = (bf16[320,3072]{1,0:T(8,128)(2,1)S(1)}, bf16[320,3072]{1,0:T(8,128)(2,1)S(1)}, u32[]{:S(2)}, u32[]{:S(2)}) collective-permute-start(bf16[320,3072]{1,0:T(8,128)(2,1)S(1)} %constant_dynamic-update-slice_fusion.refs_1_), channel_id=1, source_target_pairs={{0,64},{64,0},{128,192},{192,128},{256,320},{320,256},{384,448},{4... | collective-permute-start | bytes 5898248 | tf_op jit(solution)/shard_map/ppermute | solution.py:235
  198.1 1.5 copy-start.12
  199.6 30.3 %copy-start.15 = (bf16[640,448]{1,0:T(8,128)(2,1)S(1)}, bf16[640,448]{1,0:T(8,128)(2,1)}, u32[]{:S(2)}) copy-start(bf16[640,448]{1,0:T(8,128)(2,1)} %copy-done.14) | copy-start | bytes 1720324
  222.7 21.3 %all-to-all-start.4 = ((bf16[8,32,896]{2,1,0:T(8,128)(2,1)}), bf16[8,32,896]{2,1,0:T(8,128)(2,1)S(1)}, u32[]{:S(2)}, u32[]{:S(2)}) async-start(bf16[8,32,896]{2,1,0:T(8,128)(2,1)} %bitcast.12), calls=%async_computation.4 | async-start | bytes 917504 | tf_op jit(solution)/shard_map/all_to_all | solution.py:271
  229.9 3.3 %copy-start.13 = (bf16[640,2048]{1,0:T(8,128)(2,1)S(1)}, bf16[640,2048]{1,0:T(8,128)(2,1)}, u32[]{:S(2)}) copy-start(bf16[640,2048]{1,0:T(8,128)(2,1)} %copy-done.12) | copy-start | bytes 7864324

commit v10 on v9

--- a/solution.py
+++ b/solution.py
@@ -310,10 +310,10 @@
     before, after = step(saved, 1, 0), step(saved, -1, 0)
     first = exchange(first, along_y)
     first, other_z, before, after = lax.optimization_barrier((first, other_z, before, after))
+    half = saved.shape[0] // 2
+    two_before = jnp.concatenate([step(before[:half], 1, 0), step(after[half:], -1, 0)], axis=0)
     before_z, after_z = step(other_z, 1, 0), step(other_z, -1, 0)
-    blocks = (
-        saved, other_z, before, before_z, step(before, 1, 0), step(after_z, -1, 0), after, after_z,
-    )
+    blocks = saved, other_z, before, before_z, two_before, step(two_before, 0, 1), after, after_z
 
     out_rows, seen = ny * capacity, ny * tok
     row, col = np.arange(out_rows)[:, None], np.arange(seen)[None, :]

time: 246 us -> 252 us (1.024)
  local copies, waits for them, and re-layouts: 12.3 us -> 15.8 us
    ppermute x7 -> x8, starting transfers between devices: 26.7 us -> 29.6 us  [step(): return lax.ppermute(v, 'expert', pairs)]
    ppermute x7 -> x8, waiting for transfers between devices: 22.4 us -> 21.1 us  [step(): return lax.ppermute(v, 'expert', pairs)]
    unnamed x38 -> x43, local copies, waits for them, and re-layouts: 10.3 us -> 11.3 us
  transfers between devices with their start and end apart: 22 -> 23, of which waited for: 16 -> 16; matrix products, arithmetic and copies ran while one was open for 3% -> 4% of each run, Pallas kernels for 1% -> 0%
where the time goes in v10:
time: 252 us; the launch traced here: 250 us
  starting transfers between devices  111 us (44%)
  waiting for transfers between devices  80.6 us (32%)
  blocking collectives  21.9 us (9%)
  local copies, waits for them, and re-layouts  15.8 us (6%)
  Pallas kernels  13 us (5%)
  matrix products  5.11 us (2%)
    ppermute x8, waiting for transfers between devices, shift(): lax.ppermute(x, 'dp', [(2 * h + c, 2 * ((h + k) % 4) + c) for h in range(...  40.8 us
    ppermute x8, starting transfers between devices, shift(): lax.ppermute(x, 'dp', [(2 * h + c, 2 * ((h + k) % 4) + c) for h in range(...  35.9 us
    ppermute x8, starting transfers between devices, step(): return lax.ppermute(v, 'expert', pairs)  29.6 us
    all_to_all x4, starting transfers between devices, exchange(): lax.all_to_all(flat, 'expert', 0, 0, axis_index_groups=groups, tiled=True)  23.8 us
    all_to_all x1, blocking collectives, exchange(): lax.all_to_all(flat, 'expert', 0, 0, axis_index_groups=groups, tiled=True)  21.9 us
    ppermute x3, starting transfers between devices, core_swap(): return lax.ppermute(x, 'dp', [(i, i ^ 1) for i in range(8)])  21.6 us
    ppermute x8, waiting for transfers between devices, step(): return lax.ppermute(v, 'expert', pairs)  21.1 us
    all_to_all x4, waiting for transfers between devices, exchange(): lax.all_to_all(flat, 'expert', 0, 0, axis_index_groups=groups, tiled=True)  15.1 us
  transfers between devices with their start and end apart: 23, of which 16 were waited for; matrix products, arithmetic and copies ran while one was open for 4% of the time, Pallas kernels for 0%

profile of v10, /device:TPU:1, one launch (start us, length us, event | category | flops | bytes accessed | tf_op | source)
XLA Modules:
  0.0 249.8 jit_solution(3328038705588433280)
XLA Ops:
  2.4 7.7 %all-to-all-start = ((bf16[8,16,1408]{2,1,0:T(8,128)(2,1)}), bf16[8,16,1408]{2,1,0:T(8,128)(2,1)S(1)}, u32[]{:S(2)}, u32[]{:S(2)}) async-start(bf16[8,16,1408]{2,1,0:T(8,128)(2,1)} %broadcast_in_dim.9), calls=%async_computation | async-start | bytes 720896 | tf_op jit(solution)/shard_map/all_to_all | solution.py:271
  13.1 1.2 shard_map.129
  14.3 6.1 %all-to-all-done = bf16[8,16,1408]{2,1,0:T(8,128)(2,1)S(1)} async-done(((bf16[8,16,1408]{2,1,0:T(8,128)(2,1)}), bf16[8,16,1408]{2,1,0:T(8,128)(2,1)S(1)}, u32[]{:S(2)}, u32[]{:S(2)}) %all-to-all-start) | async-done | bytes 360480 | tf_op jit(solution)/shard_map/all_to_all | solution.py:271
  20.4 3.6 %all-to-all-start.1 = ((bf16[8,32,1024]{2,1,0:T(8,128)(2,1)}), bf16[8,32,1024]{2,1,0:T(8,128)(2,1)S(1)}, u32[]{:S(2)}, u32[]{:S(2)}) async-start(bf16[8,32,1024]{2,1,0:T(8,128)(2,1)} %shard_map.129), calls=%async_computation.1 | async-start | bytes 1048576 | tf_op jit(solution)/shard_map/all_to_all | solution.py:271
  24.0 6.9 %collective-permute-start.2 = (bf16[128,1408]{1,0:T(8,128)(2,1)S(1)}, bf16[128,1408]{1,0:T(8,128)(2,1)S(1)}, u32[]{:S(2)}, u32[]{:S(2)}) collective-permute-start(bf16[128,1408]{1,0:T(8,128)(2,1)S(1)} %bitcast.27), channel_id=1, source_target_pairs={{0,48},{1,49},{2,50},{3,51},{4,52},{5,53},{6,54},{7,55},{8,56},{9,... | collective-permute-start | bytes 1081352 | tf_op jit(solution)/shard_map/ppermute | solution.py:282
  30.9 1.9 collective-permute-start.1
  32.8 4.0 %collective-permute-start = (bf16[128,1408]{1,0:T(8,128)(2,1)S(1)}, bf16[128,1408]{1,0:T(8,128)(2,1)S(1)}, u32[]{:S(2)}, u32[]{:S(2)}) collective-permute-start(bf16[128,1408]{1,0:T(8,128)(2,1)S(1)} %bitcast.29), channel_id=1, source_target_pairs={{0,1},{1,0},{2,3},{3,2},{4,5},{5,4},{6,7},{7,6},{8,9},{9,8},{10,11... | collective-permute-start | bytes 1081352 | tf_op jit(solution)/shard_map/ppermute | solution.py:282
  36.8 4.7 %collective-permute-done.1.s1 = bf16[128,1408]{1,0:T(8,128)(2,1)S(1)} collective-permute-done((bf16[128,1408]{1,0:T(8,128)(2,1)S(1)}, bf16[128,1408]{1,0:T(8,128)(2,1)S(1)}, u32[]{:S(2)}, u32[]{:S(2)}) %collective-permute-start.1) | collective-permute-done | bytes 360480 | tf_op jit(solution)/shard_map/ppermute | solution.py:282
  41.6 1.6 collective-permute-done.t0
  44.0 1.4 shard_map.130
  46.4 4.7 %all-to-all-start.2 = ((bf16[8,80,896]{2,1,0:T(8,128)(2,1)}), bf16[8,80,896]{2,1,0:T(8,128)(2,1)S(1)}, u32[]{:S(2)}, u32[]{:S(2)}) async-start(bf16[8,80,896]{2,1,0:T(8,128)(2,1)} %copy-done.4), calls=%async_computation.2 | async-start | bytes 2293760 | tf_op jit(solution)/shard_map/all_to_all | solution.py:271
  52.0 3.4 %collective-permute-start.4 = (bf16[64,1408]{1,0:T(8,128)(2,1)S(1)}, bf16[64,1408]{1,0:T(8,128)(2,1)S(1)}, u32[]{:S(2)}, u32[]{:S(2)}) collective-permute-start(bf16[64,1408]{1,0:T(8,128)(2,1)S(1)} %slice.48), channel_id=1, source_target_pairs={{0,16},{1,17},{2,18},{3,19},{4,20},{5,21},{6,22},{7,23},{8,24},{9,... | collective-permute-start | bytes 540680 | tf_op jit(solution)/shard_map/ppermute | solution.py:282
  55.4 3.1 %collective-permute-start.7 = (bf16[128,1408]{1,0:T(8,128)(2,1)}, bf16[128,1408]{1,0:T(8,128)(2,1)}, u32[]{:S(2)}, u32[]{:S(2)}) collective-permute-start(bf16[128,1408]{1,0:T(8,128)(2,1)} %copy-done.9), channel_id=1, source_target_pairs={{0,48},{1,49},{2,50},{3,51},{4,52},{5,53},{6,54},{7,55},{8,56},{9,... | collective-permute-start | bytes 1081352 | tf_op jit(solution)/shard_map/ppermute | solution.py:282
  58.5 2.2 collective-permute-start.3
  61.6 4.3 %collective-permute-start.5 = (bf16[64,1408]{1,0:T(8,128)(2,1)S(1)}, bf16[64,1408]{1,0:T(8,128)(2,1)S(1)}, u32[]{:S(2)}, u32[]{:S(2)}) collective-permute-start(bf16[64,1408]{1,0:T(8,128)(2,1)S(1)} %slice.49), channel_id=1, source_target_pairs={{0,48},{1,49},{2,50},{3,51},{4,52},{5,53},{6,54},{7,55},{8,56},{9,... | collective-permute-start | bytes 540680 | tf_op jit(solution)/shard_map/ppermute | solution.py:282
  66.0 3.5 %collective-permute-done.4 = bf16[64,1408]{1,0:T(8,128)(2,1)S(1)} collective-permute-done((bf16[64,1408]{1,0:T(8,128)(2,1)S(1)}, bf16[64,1408]{1,0:T(8,128)(2,1)S(1)}, u32[]{:S(2)}, u32[]{:S(2)}) %collective-permute-start.4) | collective-permute-done | bytes 180256 | tf_op jit(solution)/shard_map/ppermute | solution.py:282
  70.2 5.4 %collective-permute-done.5 = bf16[64,1408]{1,0:T(8,128)(2,1)S(1)} collective-permute-done((bf16[64,1408]{1,0:T(8,128)(2,1)S(1)}, bf16[64,1408]{1,0:T(8,128)(2,1)S(1)}, u32[]{:S(2)}, u32[]{:S(2)}) %collective-permute-start.5) | collective-permute-done | bytes 180256 | tf_op jit(solution)/shard_map/ppermute | solution.py:282
  76.3 3.9 %collective-permute-start.6 = (bf16[128,1408]{1,0:T(8,128)(2,1)}, bf16[128,1408]{1,0:T(8,128)(2,1)}, u32[]{:S(2)}, u32[]{:S(2)}) collective-permute-start(bf16[128,1408]{1,0:T(8,128)(2,1)} %constant_dynamic-update-slice_fusion.s2), channel_id=1, source_target_pairs={{0,1},{1,0},{2,3},{3,2},{4,5},{5,4},{6,7},{7,6},{8,9},{9,8},{10,11... | collective-permute-start | bytes 1081352 | tf_op jit(solution)/shard_map/ppermute | solution.py:282
  80.9 5.8 %collective-permute-done.6.t2 = bf16[128,1408]{1,0:T(8,128)(2,1)} collective-permute-done((bf16[128,1408]{1,0:T(8,128)(2,1)}, bf16[128,1408]{1,0:T(8,128)(2,1)}, u32[]{:S(2)}, u32[]{:S(2)}) %collective-permute-start.6) | collective-permute-done | bytes 360480 | tf_op jit(solution)/shard_map/ppermute | solution.py:282
  86.7 1.2 copy-done.2
  90.9 4.4 %shard_map.131 = (bf16[640,448]{1,0:T(8,128)(2,1)S(1)}, bf16[80,3072]{1,0:T(8,128)(2,1)S(1)}, bf16[240,3072]{1,0:T(8,128)(2,1)S(1)}, bf16[80,3072]{1,0:T(8,128)(...) custom-call(s32[5]{0:T(128)S(1)} %stack.27.who_ref.refs_0_, ...), custom_call_target="tpu_custom_call" | custom-call | tf_op jit(solution)/shard_map/pallas_call | solution.py:328
  95.3 5.0 %collective-permute-start.9 = (bf16[80,3072]{1,0:T(8,128)(2,1)S(1)}, bf16[80,3072]{1,0:T(8,128)(2,1)S(1)}, u32[]{:S(2)}, u32[]{:S(2)}) collective-permute-start(bf16[80,3072]{1,0:T(8,128)(2,1)S(1)} %get-tuple-element.32), channel_id=1, source_target_pairs={{0,64},{64,0},{128,192},{192,128},{256,320},{320,256},{384,448},{4... | collective-permute-start | bytes 1474568 | tf_op jit(solution)/shard_map/ppermute | solution.py:235
  100.3 1.9 collective-permute-start.8
  102.4 9.8 %collective-permute-start.12 = (bf16[40,3072]{1,0:T(8,128)(2,1)S(1)}, bf16[40,3072]{1,0:T(8,128)(2,1)S(1)}, u32[]{:S(2)}, u32[]{:S(2)}) collective-permute-start(bf16[40,3072]{1,0:T(8,128)(2,1)S(1)} %get-tuple-element.44), channel_id=1, source_target_pairs={{0,384},{64,448},{128,0},{192,64},{256,128},{320,192},{384,256},{4... | collective-permute-start | bytes 737288 | tf_op jit(solution)/shard_map/ppermute | solution.py:239
  112.1 1.9 collective-permute-start.10
  114.4 4.9 %collective-permute-done.12 = bf16[40,3072]{1,0:T(8,128)(2,1)S(1)} collective-permute-done((bf16[40,3072]{1,0:T(8,128)(2,1)S(1)}, bf16[40,3072]{1,0:T(8,128)(2,1)S(1)}, u32[]{:S(2)}, u32[]{:S(2)}) %collective-permute-start.12) | collective-permute-done | bytes 245792 | tf_op jit(solution)/shard_map/ppermute | solution.py:239
  119.4 3.6 %collective-permute-done.10 = bf16[40,3072]{1,0:T(8,128)(2,1)S(1)} collective-permute-done((bf16[40,3072]{1,0:T(8,128)(2,1)S(1)}, bf16[40,3072]{1,0:T(8,128)(2,1)S(1)}, u32[]{:S(2)}, u32[]{:S(2)}) %collective-permute-start.10) | collective-permute-done | bytes 245792 | tf_op jit(solution)/shard_map/ppermute | solution.py:239
  123.1 1.9 collective-permute-start.11
  125.1 5.5 %collective-permute-start.13 = (bf16[80,3072]{1,0:T(8,128)(2,1)S(1)}, bf16[80,3072]{1,0:T(8,128)(2,1)S(1)}, u32[]{:S(2)}, u32[]{:S(2)}) collective-permute-start(bf16[80,3072]{1,0:T(8,128)(2,1)S(1)} %pad_maximum_fusion.1), channel_id=1, source_target_pairs={{0,384},{64,448},{128,0},{192,64},{256,128},{320,192},{384,256},{4... | collective-permute-start | bytes 1474568 | tf_op jit(solution)/shard_map/ppermute | solution.py:239
  130.6 4.3 %collective-permute-done.11.left_ref = bf16[80,3072]{1,0:T(8,128)(2,1)S(1)} collective-permute-done((bf16[80,3072]{1,0:T(8,128)(2,1)S(1)}, bf16[80,3072]{1,0:T(8,128)(2,1)S(1)}, u32[]{:S(2)}, u32[]{:S(2)}) %collective-permute-start.11) | collective-permute-done | bytes 491552 | tf_op jit(solution)/shard_map/ppermute | solution.py:239
  134.9 1.4 collective-permute-done.13.right_ref
  136.7 7.4 %collective-permute-start.15 = (bf16[80,3072]{1,0:T(8,128)(2,1)S(1)}, bf16[80,3072]{1,0:T(8,128)(2,1)S(1)}, u32[]{:S(2)}, u32[]{:S(2)}) collective-permute-start(bf16[80,3072]{1,0:T(8,128)(2,1)S(1)} %shard_map.132), channel_id=1, source_target_pairs={{0,128},{64,192},{128,256},{192,320},{256,384},{320,448},{384,0},{... | collective-permute-start | bytes 1474568 | tf_op jit(solution)/shard_map/ppermute | solution.py:239
  144.1 1.9 collective-permute-start.14
  146.1 11.7 %collective-permute-done.15 = bf16[80,3072]{1,0:T(8,128)(2,1)S(1)} collective-permute-done((bf16[80,3072]{1,0:T(8,128)(2,1)S(1)}, bf16[80,3072]{1,0:T(8,128)(2,1)S(1)}, u32[]{:S(2)}, u32[]{:S(2)}) %collective-permute-start.15) | collective-permute-done | bytes 491552 | tf_op jit(solution)/shard_map/ppermute | solution.py:239
  157.8 1.9 collective-permute-start.16
  159.9 5.7 %collective-permute-start.17 = (bf16[40,3072]{1,0:T(8,128)(2,1)S(1)}, bf16[40,3072]{1,0:T(8,128)(2,1)S(1)}, u32[]{:S(2)}, u32[]{:S(2)}) collective-permute-start(bf16[40,3072]{1,0:T(8,128)(2,1)S(1)} %slice.70), channel_id=1, source_target_pairs={{0,384},{64,448},{128,0},{192,64},{256,128},{320,192},{384,256},{4... | collective-permute-start | bytes 737288 | tf_op jit(solution)/shard_map/ppermute | solution.py:239
  165.7 12.0 %collective-permute-done.16 = bf16[40,3072]{1,0:T(8,128)(2,1)S(1)} collective-permute-done((bf16[40,3072]{1,0:T(8,128)(2,1)S(1)}, bf16[40,3072]{1,0:T(8,128)(2,1)S(1)}, u32[]{:S(2)}, u32[]{:S(2)}) %collective-permute-start.16) | collective-permute-done | bytes 245792 | tf_op jit(solution)/shard_map/ppermute | solution.py:239
  177.7 2.7 %collective-permute-done.17 = bf16[40,3072]{1,0:T(8,128)(2,1)S(1)} collective-permute-done((bf16[40,3072]{1,0:T(8,128)(2,1)S(1)}, bf16[40,3072]{1,0:T(8,128)(2,1)S(1)}, u32[]{:S(2)}, u32[]{:S(2)}) %collective-permute-start.17) | collective-permute-done | bytes 245792 | tf_op jit(solution)/shard_map/ppermute | solution.py:239
  180.4 14.7 %collective-permute-start.18 = (bf16[320,3072]{1,0:T(8,128)(2,1)S(1)}, bf16[320,3072]{1,0:T(8,128)(2,1)S(1)}, u32[]{:S(2)}, u32[]{:S(2)}) collective-permute-start(bf16[320,3072]{1,0:T(8,128)(2,1)S(1)} %constant_dynamic-update-slice_fusion.2.refs_1_), channel_id=1, source_target_pairs={{0,64},{64,0},{128,192},{192,128},{256,320},{320,256},{384,448},{4... | collective-permute-start | bytes 5898248 | tf_op jit(solution)/shard_map/ppermute | solution.py:235
  195.1 3.6 %collective-permute-done.18.refs_2_ = bf16[320,3072]{1,0:T(8,128)(2,1)S(1)} collective-permute-done((bf16[320,3072]{1,0:T(8,128)(2,1)S(1)}, bf16[320,3072]{1,0:T(8,128)(2,1)S(1)}, u32[]{:S(2)}, u32[]{:S(2)}) %collective-permute-start.18) | collective-permute-done | bytes 1966112 | tf_op jit(solution)/shard_map/ppermute | solution.py:235
  198.7 3.2 %shard_map.133 = (bf16[8,80,896]{2,1,0:T(8,128)(2,1)S(1)}, bf16[640,2048]{1,0:T(8,128)(2,1)S(1)}) custom-call(s32[5]{0:T(128)S(1)} %stack.27.who_ref.refs_0_, bf16[320,3072]{1,0:T(8,128)(2,1)S(1)} %constant_dynamic-update-slice_fusion.2.refs_1_, bf16[320,3072]{1,0:T(8,128)(2,1)S(1)} %collective-permute-done.18.refs_2_, bf16[448,1024]{1,0:T(8,128)(2,1)S(1)} %bitcast.22, ...), custom_call_target="tpu_custom_call" | custom-call | tf_op jit(solution)/shard_map/pallas_call | solution.py:358
  202.0 1.5 copy-done.14
  203.5 21.9 %all_to_all.36.recv_ref = bf16[8,80,896]{2,1,0:T(8,128)(2,1)S(1)} all-to-all(bf16[8,80,896]{2,1,0:T(8,128)(2,1)S(1)} %get-tuple-element.34), channel_id=1, replica_groups={{0,1,16,17,32,33,48,49},{2,3,18,19,34,35,50,51},{4,5,20,21,36,37,52,53}..., dimensions={0} | all-to-all | bytes 2293760 | tf_op jit(solution)/shard_map/all_to_all | solution.py:271
  225.3 1.7 shard_map.134
  227.0 7.9 %all-to-all-start.4 = ((bf16[8,32,896]{2,1,0:T(8,128)(2,1)}), bf16[8,32,896]{2,1,0:T(8,128)(2,1)S(1)}, u32[]{:S(2)}, u32[]{:S(2)}) async-start(bf16[8,32,896]{2,1,0:T(8,128)(2,1)} %bitcast.12), calls=%async_computation.4 | async-start | bytes 917504 | tf_op jit(solution)/shard_map/all_to_all | solution.py:271
  235.0 3.3 %fusion.1 = bf16[1,448,1024]{2,1,0:T(8,128)(2,1)} fusion(bf16[640,448]{1,0:T(8,128)(2,1)S(1)} %copy-done.17, bf16[640,2048]{1,0:T(8,128)(2,1)} %copy-done.14), kind=kOutput, calls=%fused_computation.4 | convolution fusion | flops 587661312 | bytes 2801664 | tf_op jit(solution)/shard_map/dot_general | solution.py:22
  238.3 1.8 fusion
  240.1 9.0 %all-to-all-done.4.recv_ref = bf16[8,32,896]{2,1,0:T(8,128)(2,1)S(1)} async-done(((bf16[8,32,896]{2,1,0:T(8,128)(2,1)}), bf16[8,32,896]{2,1,0:T(8,128)(2,1)S(1)}, u32[]{:S(2)}, u32[]{:S(2)}) %all-to-all-start.4) | async-done | bytes 458784 | tf_op jit(solution)/shard_map/all_to_all | solution.py:271
  (69 shorter events, 15.1 us)
Async XLA Ops:
  0.6 43.3 %copy-start.11 = (f32[80,256]{1,0:T(8,128)S(1)}, f32[80,256]{1,0:T(8,128)}, u32[]{:S(2)}) copy-start(f32[80,256]{1,0:T(8,128)} %constant.53.clone.want_ref) | copy-start | bytes 245764
  2.4 18.0 %all-to-all-start = ((bf16[8,16,1408]{2,1,0:T(8,128)(2,1)}), bf16[8,16,1408]{2,1,0:T(8,128)(2,1)S(1)}, u32[]{:S(2)}, u32[]{:S(2)}) async-start(bf16[8,16,1408]{2,1,0:T(8,128)(2,1)} %broadcast_in_dim.9), calls=%async_computation | async-start | bytes 720896 | tf_op jit(solution)/shard_map/all_to_all | solution.py:271
  11.6 0.8 copy-start.12
  12.3 0.8 copy-start.13
  20.4 23.5 %all-to-all-start.1 = ((bf16[8,32,1024]{2,1,0:T(8,128)(2,1)}), bf16[8,32,1024]{2,1,0:T(8,128)(2,1)S(1)}, u32[]{:S(2)}, u32[]{:S(2)}) async-start(bf16[8,32,1024]{2,1,0:T(8,128)(2,1)} %shard_map.129), calls=%async_computation.1 | async-start | bytes 1048576 | tf_op jit(solution)/shard_map/all_to_all | solution.py:271
  24.0 12.8 %collective-permute-start.2 = (bf16[128,1408]{1,0:T(8,128)(2,1)S(1)}, bf16[128,1408]{1,0:T(8,128)(2,1)S(1)}, u32[]{:S(2)}, u32[]{:S(2)}) collective-permute-start(bf16[128,1408]{1,0:T(8,128)(2,1)S(1)} %bitcast.27), channel_id=1, source_target_pairs={{0,48},{1,49},{2,50},{3,51},{4,52},{5,53},{6,54},{7,55},{8,56},{9,... | collective-permute-start | bytes 1081352 | tf_op jit(solution)/shard_map/ppermute | solution.py:282
  30.9 10.7 %collective-permute-start.1 = (bf16[128,1408]{1,0:T(8,128)(2,1)S(1)}, bf16[128,1408]{1,0:T(8,128)(2,1)S(1)}, u32[]{:S(2)}, u32[]{:S(2)}) collective-permute-start(bf16[128,1408]{1,0:T(8,128)(2,1)S(1)} %bitcast.28), channel_id=1, source_target_pairs={{0,16},{1,17},{2,18},{3,19},{4,20},{5,21},{6,22},{7,23},{8,24},{9,... | collective-permute-start | bytes 1081352 | tf_op jit(solution)/shard_map/ppermute | solution.py:282
  32.8 10.4 %collective-permute-start = (bf16[128,1408]{1,0:T(8,128)(2,1)S(1)}, bf16[128,1408]{1,0:T(8,128)(2,1)S(1)}, u32[]{:S(2)}, u32[]{:S(2)}) collective-permute-start(bf16[128,1408]{1,0:T(8,128)(2,1)S(1)} %bitcast.29), channel_id=1, source_target_pairs={{0,1},{1,0},{2,3},{3,2},{4,5},{5,4},{6,7},{7,6},{8,9},{9,8},{10,11... | collective-permute-start | bytes 1081352 | tf_op jit(solution)/shard_map/ppermute | solution.py:282
  36.8 6.4 %copy-start.5 = (bf16[128,1408]{1,0:T(8,128)(2,1)}, bf16[128,1408]{1,0:T(8,128)(2,1)S(1)}, u32[]{:S(2)}) copy-start(bf16[128,1408]{1,0:T(8,128)(2,1)S(1)} %collective-permute-done.2.s3) | copy-start | bytes 1081348
  41.6 1.6 copy-start.7
  43.2 0.7 copy-start.9
  45.3 1.0 copy-start.4
  46.4 40.3 %copy-start = (bf16[1,448,1024]{2,1,0:T(8,128)(2,1)S(1)}, bf16[1,448,1024]{2,1,0:T(8,128)(2,1)}, u32[]{:S(2)}) copy-start(bf16[1,448,1024]{2,1,0:T(8,128)(2,1)} %param.15) | copy-start | bytes 2752516
  46.4 40.3 %copy-start.1 = (bf16[1,448,1024]{2,1,0:T(8,128)(2,1)S(1)}, bf16[1,448,1024]{2,1,0:T(8,128)(2,1)}, u32[]{:S(2)}) copy-start(bf16[1,448,1024]{2,1,0:T(8,128)(2,1)} %param.16) | copy-start | bytes 2752516
  46.4 40.3 %all-to-all-start.2 = ((bf16[8,80,896]{2,1,0:T(8,128)(2,1)}), bf16[8,80,896]{2,1,0:T(8,128)(2,1)S(1)}, u32[]{:S(2)}, u32[]{:S(2)}) async-start(bf16[8,80,896]{2,1,0:T(8,128)(2,1)} %copy-done.4), calls=%async_computation.2 | async-start | bytes 2293760 | tf_op jit(solution)/shard_map/all_to_all | solution.py:271
  52.0 17.5 %collective-permute-start.4 = (bf16[64,1408]{1,0:T(8,128)(2,1)S(1)}, bf16[64,1408]{1,0:T(8,128)(2,1)S(1)}, u32[]{:S(2)}, u32[]{:S(2)}) collective-permute-start(bf16[64,1408]{1,0:T(8,128)(2,1)S(1)} %slice.48), channel_id=1, source_target_pairs={{0,16},{1,17},{2,18},{3,19},{4,20},{5,21},{6,22},{7,23},{8,24},{9,... | collective-permute-start | bytes 540680 | tf_op jit(solution)/shard_map/ppermute | solution.py:282
  55.4 25.5 %collective-permute-start.7 = (bf16[128,1408]{1,0:T(8,128)(2,1)}, bf16[128,1408]{1,0:T(8,128)(2,1)}, u32[]{:S(2)}, u32[]{:S(2)}) collective-permute-start(bf16[128,1408]{1,0:T(8,128)(2,1)} %copy-done.9), channel_id=1, source_target_pairs={{0,48},{1,49},{2,50},{3,51},{4,52},{5,53},{6,54},{7,55},{8,56},{9,... | collective-permute-start | bytes 1081352 | tf_op jit(solution)/shard_map/ppermute | solution.py:282
  58.5 22.4 %collective-permute-start.3 = (bf16[128,1408]{1,0:T(8,128)(2,1)}, bf16[128,1408]{1,0:T(8,128)(2,1)}, u32[]{:S(2)}, u32[]{:S(2)}) collective-permute-start(bf16[128,1408]{1,0:T(8,128)(2,1)} %copy-done.9), channel_id=1, source_target_pairs={{0,16},{1,17},{2,18},{3,19},{4,20},{5,21},{6,22},{7,23},{8,24},{9,... | collective-permute-start | bytes 1081352 | tf_op jit(solution)/shard_map/ppermute | solution.py:282
  61.6 14.0 %collective-permute-start.5 = (bf16[64,1408]{1,0:T(8,128)(2,1)S(1)}, bf16[64,1408]{1,0:T(8,128)(2,1)S(1)}, u32[]{:S(2)}, u32[]{:S(2)}) collective-permute-start(bf16[64,1408]{1,0:T(8,128)(2,1)S(1)} %slice.49), channel_id=1, source_target_pairs={{0,48},{1,49},{2,50},{3,51},{4,52},{5,53},{6,54},{7,55},{8,56},{9,... | collective-permute-start | bytes 540680 | tf_op jit(solution)/shard_map/ppermute | solution.py:282
  76.3 10.4 %collective-permute-start.6 = (bf16[128,1408]{1,0:T(8,128)(2,1)}, bf16[128,1408]{1,0:T(8,128)(2,1)}, u32[]{:S(2)}, u32[]{:S(2)}) collective-permute-start(bf16[128,1408]{1,0:T(8,128)(2,1)} %constant_dynamic-update-slice_fusion.s2), channel_id=1, source_target_pairs={{0,1},{1,0},{2,3},{3,2},{4,5},{5,4},{6,7},{7,6},{8,9},{9,8},{10,11... | collective-permute-start | bytes 1081352 | tf_op jit(solution)/shard_map/ppermute | solution.py:282
  86.7 1.2 copy-start.2
  87.9 1.0 copy-start.6
  88.9 1.0 copy-start.8
  89.9 1.0 copy-start.10
  95.2 19.1 %copy-start.16 = (bf16[640,448]{1,0:T(8,128)(2,1)}, bf16[640,448]{1,0:T(8,128)(2,1)S(1)}, u32[]{:S(2)}) copy-start(bf16[640,448]{1,0:T(8,128)(2,1)S(1)} %get-tuple-element.38) | copy-start | bytes 1720324
  95.3 6.9 %collective-permute-start.9 = (bf16[80,3072]{1,0:T(8,128)(2,1)S(1)}, bf16[80,3072]{1,0:T(8,128)(2,1)S(1)}, u32[]{:S(2)}, u32[]{:S(2)}) collective-permute-start(bf16[80,3072]{1,0:T(8,128)(2,1)S(1)} %get-tuple-element.32), channel_id=1, source_target_pairs={{0,64},{64,0},{128,192},{192,128},{256,320},{320,256},{384,448},{4... | collective-permute-start | bytes 1474568 | tf_op jit(solution)/shard_map/ppermute | solution.py:235
  100.3 13.8 %collective-permute-start.8 = (bf16[240,3072]{1,0:T(8,128)(2,1)S(1)}, bf16[240,3072]{1,0:T(8,128)(2,1)S(1)}, u32[]{:S(2)}, u32[]{:S(2)}) collective-permute-start(bf16[240,3072]{1,0:T(8,128)(2,1)S(1)} %get-tuple-element.30), channel_id=1, source_target_pairs={{0,64},{64,0},{128,192},{192,128},{256,320},{320,256},{384,448},{4... | collective-permute-start | bytes 4423688 | tf_op jit(solution)/shard_map/ppermute | solution.py:235
  102.4 17.0 %collective-permute-start.12 = (bf16[40,3072]{1,0:T(8,128)(2,1)S(1)}, bf16[40,3072]{1,0:T(8,128)(2,1)S(1)}, u32[]{:S(2)}, u32[]{:S(2)}) collective-permute-start(bf16[40,3072]{1,0:T(8,128)(2,1)S(1)} %get-tuple-element.44), channel_id=1, source_target_pairs={{0,384},{64,448},{128,0},{192,64},{256,128},{320,192},{384,256},{4... | collective-permute-start | bytes 737288 | tf_op jit(solution)/shard_map/ppermute | solution.py:239
  112.1 10.8 %collective-permute-start.10 = (bf16[40,3072]{1,0:T(8,128)(2,1)S(1)}, bf16[40,3072]{1,0:T(8,128)(2,1)S(1)}, u32[]{:S(2)}, u32[]{:S(2)}) collective-permute-start(bf16[40,3072]{1,0:T(8,128)(2,1)S(1)} %get-tuple-element.45), channel_id=1, source_target_pairs={{0,128},{64,192},{128,256},{192,320},{256,384},{320,448},{384,0},{... | collective-permute-start | bytes 737288 | tf_op jit(solution)/shard_map/ppermute | solution.py:239
  123.1 11.8 %collective-permute-start.11 = (bf16[80,3072]{1,0:T(8,128)(2,1)S(1)}, bf16[80,3072]{1,0:T(8,128)(2,1)S(1)}, u32[]{:S(2)}, u32[]{:S(2)}) collective-permute-start(bf16[80,3072]{1,0:T(8,128)(2,1)S(1)} %pad_maximum_fusion), channel_id=1, source_target_pairs={{0,128},{64,192},{128,256},{192,320},{256,384},{320,448},{384,0},{... | collective-permute-start | bytes 1474568 | tf_op jit(solution)/shard_map/ppermute | solution.py:239
  125.1 11.2 %collective-permute-start.13 = (bf16[80,3072]{1,0:T(8,128)(2,1)S(1)}, bf16[80,3072]{1,0:T(8,128)(2,1)S(1)}, u32[]{:S(2)}, u32[]{:S(2)}) collective-permute-start(bf16[80,3072]{1,0:T(8,128)(2,1)S(1)} %pad_maximum_fusion.1), channel_id=1, source_target_pairs={{0,384},{64,448},{128,0},{192,64},{256,128},{320,192},{384,256},{4... | collective-permute-start | bytes 1474568 | tf_op jit(solution)/shard_map/ppermute | solution.py:239
  136.7 21.0 %collective-permute-start.15 = (bf16[80,3072]{1,0:T(8,128)(2,1)S(1)}, bf16[80,3072]{1,0:T(8,128)(2,1)S(1)}, u32[]{:S(2)}, u32[]{:S(2)}) collective-permute-start(bf16[80,3072]{1,0:T(8,128)(2,1)S(1)} %shard_map.132), channel_id=1, source_target_pairs={{0,128},{64,192},{128,256},{192,320},{256,384},{320,448},{384,0},{... | collective-permute-start | bytes 1474568 | tf_op jit(solution)/shard_map/ppermute | solution.py:239
  144.1 15.8 %collective-permute-start.14 = (bf16[80,3072]{1,0:T(8,128)(2,1)S(1)}, bf16[80,3072]{1,0:T(8,128)(2,1)S(1)}, u32[]{:S(2)}, u32[]{:S(2)}) collective-permute-start(bf16[80,3072]{1,0:T(8,128)(2,1)S(1)} %shard_map.132), channel_id=1, source_target_pairs={{0,384},{64,448},{128,0},{192,64},{256,128},{320,192},{384,256},{4... | collective-permute-start | bytes 1474568 | tf_op jit(solution)/shard_map/ppermute | solution.py:239
  146.1 52.6 %copy-start.3 = (bf16[1,1024,448]{1,2,0:T(8,128)(2,1)S(1)}, bf16[1,1024,448]{1,2,0:T(8,128)(2,1)}, u32[]{:S(2)}) copy-start(bf16[1,1024,448]{1,2,0:T(8,128)(2,1)} %param.17) | copy-start | bytes 2752516
  157.8 19.8 %collective-permute-start.16 = (bf16[40,3072]{1,0:T(8,128)(2,1)S(1)}, bf16[40,3072]{1,0:T(8,128)(2,1)S(1)}, u32[]{:S(2)}, u32[]{:S(2)}) collective-permute-start(bf16[40,3072]{1,0:T(8,128)(2,1)S(1)} %slice.69), channel_id=1, source_target_pairs={{0,128},{64,192},{128,256},{192,320},{256,384},{320,448},{384,0},{... | collective-permute-start | bytes 737288 | tf_op jit(solution)/shard_map/ppermute | solution.py:239
  159.9 20.5 %collective-permute-start.17 = (bf16[40,3072]{1,0:T(8,128)(2,1)S(1)}, bf16[40,3072]{1,0:T(8,128)(2,1)S(1)}, u32[]{:S(2)}, u32[]{:S(2)}) collective-permute-start(bf16[40,3072]{1,0:T(8,128)(2,1)S(1)} %slice.70), channel_id=1, source_target_pairs={{0,384},{64,448},{128,0},{192,64},{256,128},{320,192},{384,256},{4... | collective-permute-start | bytes 737288 | tf_op jit(solution)/shard_map/ppermute | solution.py:239
  180.4 18.3 %collective-permute-start.18 = (bf16[320,3072]{1,0:T(8,128)(2,1)S(1)}, bf16[320,3072]{1,0:T(8,128)(2,1)S(1)}, u32[]{:S(2)}, u32[]{:S(2)}) collective-permute-start(bf16[320,3072]{1,0:T(8,128)(2,1)S(1)} %constant_dynamic-update-slice_fusion.2.refs_1_), channel_id=1, source_target_pairs={{0,64},{64,0},{128,192},{192,128},{256,320},{320,256},{384,448},{4... | collective-permute-start | bytes 5898248 | tf_op jit(solution)/shard_map/ppermute | solution.py:235
  202.0 1.5 copy-start.14
  203.5 31.5 %copy-start.17 = (bf16[640,448]{1,0:T(8,128)(2,1)S(1)}, bf16[640,448]{1,0:T(8,128)(2,1)}, u32[]{:S(2)}) copy-start(bf16[640,448]{1,0:T(8,128)(2,1)} %copy-done.16) | copy-start | bytes 1720324
  227.0 22.1 %all-to-all-start.4 = ((bf16[8,32,896]{2,1,0:T(8,128)(2,1)}), bf16[8,32,896]{2,1,0:T(8,128)(2,1)S(1)}, u32[]{:S(2)}, u32[]{:S(2)}) async-start(bf16[8,32,896]{2,1,0:T(8,128)(2,1)} %bitcast.12), calls=%async_computation.4 | async-start | bytes 917504 | tf_op jit(solution)/shard_map/all_to_all | solution.py:271
  235.0 3.3 %copy-start.15 = (bf16[640,2048]{1,0:T(8,128)(2,1)S(1)}, bf16[640,2048]{1,0:T(8,128)(2,1)}, u32[]{:S(2)}) copy-start(bf16[640,2048]{1,0:T(8,128)(2,1)} %copy-done.14) | copy-start | bytes 7864324

commit v11 on v9

--- a/solution.py
+++ b/solution.py
@@ -22,7 +22,7 @@
     return lax.dot_general(a, b, dims, preferred_element_type=F32)
 
 
-def call(kernel, outs, scratch=(), scalars=0, operands=0, megabytes=32):
+def call(kernel, outs, scratch=(), scalars=0, operands=0, megabytes=18, left_out=0):
     def of(shape, dtype=BF):
         return jax.ShapeDtypeStruct(shape, dtype)
 
@@ -32,7 +32,8 @@
         kernel,
         out_shape=[of(*s) if isinstance(s[0], tuple) else of(s) for s in outs],
         in_specs=specs,
-        out_specs=[pl.BlockSpec(memory_space=pltpu.VMEM)] * len(outs),
+        out_specs=[pl.BlockSpec(memory_space=pltpu.VMEM)] * (len(outs) - left_out)
+        + [pl.BlockSpec(memory_space=pltpu.HBM)] * left_out,
         scratch_shapes=list(scratch),
         compiler_params=pltpu.CompilerParams(vmem_limit_bytes=megabytes << 20),
     )
@@ -154,6 +155,20 @@
             store(2, j, dot(grads_ref[...], restored_ref[2, at, :], NT))
 
 
+def merge_kernel(at, low, own_ref, other_ref, arrived_ref, out_ref):
+    rows, width = out_ref.shape
+    mid = arrived_ref.shape[0]
+
+    @pl.loop(0, width // TILE)
+    def _(j):
+        lanes = pl.ds(pl.multiple_of(j * TILE, TILE), TILE)
+        value = own_ref[at : at + rows, lanes].astype(F32) + other_ref[at : at + rows, lanes].astype(F32)
+        more = arrived_ref[:, lanes].astype(F32)
+        none = jnp.zeros((rows - mid, TILE), F32)
+        value = value + jnp.concatenate([more, none] if low else [none, more], axis=0)
+        out_ref[:, lanes] = value.astype(BF)
+
+
 def activate_kernel(own_ref, other_ref, left_ref, right_ref, out_ref):
     ff = out_ref.shape[1] // 3
     rows = out_ref.shape[0]
@@ -177,36 +192,41 @@
             out_ref[:, at] = value.astype(BF)
 
 
-def back_kernel(*refs):
-    who_ref, parts = refs[0], refs[1:3]
-    gate_ref, up_ref, down_ref, restored_ref, out_ref, grads_ref, hidden_ref, y_ref, dx_ref = refs[3:]
+def back_kernel(
+    who_ref, mine_ref, other_ref, gate_ref, up_ref, down_ref, restored_ref,
+    out_ref, grads_ref, y_ref, dx_ref, sems,
+):
     feat, ff = gate_ref.shape
     chunk = out_ref.shape[1]
     target, h, c = who_ref[0], who_ref[1], who_ref[2]
-    for k, part in enumerate(parts):
+    copies = [
+        pltpu.make_async_copy(ref.at[:, ff : 3 * ff], grads_ref.at[k], sems.at[k])
+        for k, ref in enumerate((mine_ref, other_ref))
+    ]
+    for copy in copies:
+        copy.start()
+    for k, ref in enumerate((mine_ref, other_ref)):
         span = slice(4 * chunk * k, 4 * chunk * (k + 1))
-        hidden_ref[span, :] = part[:, 0:ff]
-        grads_ref[span, :] = part[:, ff : 3 * ff]
-
-    @pl.when(target == 0)
-    def _():
-        y_ref[...] = dot(hidden_ref[...], down_ref[...], NT).astype(BF)
-        dx_ref[...] = (
-            dot(grads_ref[:, 0:ff], gate_ref[...], NT) + dot(grads_ref[:, ff : 2 * ff], up_ref[...], NT)
-        ).astype(BF)
-
-    @pl.when(target == 1)
-    def _():
-        y_ref[...] = dot(hidden_ref[...], restored_ref[2]).astype(BF)
-        dx_ref[...] = (
-            dot(grads_ref[:, 0:ff], restored_ref[0]) + dot(grads_ref[:, ff : 2 * ff], restored_ref[1])
-        ).astype(BF)
+
+        @pl.when(target == 0)
+        def _():
+            y_ref[span, :] = dot(ref[:, 0:ff], down_ref[...], NT).astype(BF)
+            dx = dot(ref[:, ff : 2 * ff], gate_ref[...], NT)
+            dx_ref[span, :] = (dx + dot(ref[:, 2 * ff : 3 * ff], up_ref[...], NT)).astype(BF)
+
+        @pl.when(target == 1)
+        def _():
+            y_ref[span, :] = dot(ref[:, 0:ff], restored_ref[2]).astype(BF)
+            dx = dot(ref[:, ff : 2 * ff], restored_ref[0])
+            dx_ref[span, :] = (dx + dot(ref[:, 2 * ff : 3 * ff], restored_ref[1])).astype(BF)
 
     for p in range(8):
         g = chunk_at(h, c, p)
         span = slice(p * chunk, (p + 1) * chunk)
         out_ref[g, :, 0:feat] = y_ref[span, :]
         out_ref[g, :, feat : 2 * feat] = dx_ref[span, :]
+    for copy in copies:
+        copy.wait()
 
 
 def combine_kernel(recv_ref, meta_ref, want_ref, out_ref, pick_ref, share_ref):
@@ -341,11 +361,12 @@
     far = add(far, core_swap(far_out))
     rest_in = core_swap(rest_out)
     from_left, from_right = shift(far[:mid], 1), shift(far[mid:], -1)
-    sides = add(rest[chunk:], rest_in[chunk:])
-    right, left = sides[:chunk], sides[chunk:]
-    right = jnp.concatenate([add(right[:mid], from_left), right[mid:]], axis=0)
-    left = jnp.concatenate([left[:mid], add(left[mid:], from_right)], axis=0)
-    from_left, from_right = shift(right, 1), shift(left, -1)
+    def merged(at, low, arrived):
+        kernel = functools.partial(merge_kernel, at, low)
+        return call(kernel, [(chunk, wide)], operands=3)(rest, rest_in, arrived)[0]
+
+    from_left = shift(merged(chunk, True, from_left), 1)
+    from_right = shift(merged(2 * chunk, False, from_right), -1)
     (own,) = call(activate_kernel, [(chunk, wide)], operands=4)(
         rest, rest_in, from_left, from_right
     )
@@ -357,20 +378,23 @@
 
     out, grads = call(
         back_kernel,
-        [(8, chunk, 2 * feat), (8 * chunk, 2 * ff)],
+        [(8, chunk, 2 * feat), (2, 4 * chunk, 2 * ff)],
         scratch=[
-            pltpu.VMEM((8 * chunk, ff), BF),
             pltpu.VMEM((8 * chunk, feat), BF),
             pltpu.VMEM((8 * chunk, feat), BF),
+            pltpu.SemaphoreType.DMA((2,)),
         ],
         scalars=1,
         operands=6,
         megabytes=18,
+        left_out=1,
     )(who, mine, other, w_gate, w_up, w_down, restored)
+    grads = grads.reshape(8 * chunk, 2 * ff)
 
     out = exchange(out.reshape(nxz, out_rows, 2 * feat), along_xz)
     gate_grad = dot(rows, grads[:, :ff], TN).astype(BF)
     up_grad = dot(rows, grads[:, ff:], TN).astype(BF)
+    out, gate_grad = lax.optimization_barrier((out, gate_grad))
     (part,) = call(
         combine_kernel,
         [(seen, 2 * feat)],

time: 246 us -> 251 us (1.020)
  waiting for transfers between devices: 80.1 us -> 109 us
  blocking collectives: 21.4 us -> 0 us
  starting transfers between devices: 110 us -> 105 us
    all_to_all x1 -> x0, blocking collectives: 21.4 us -> none  [exchange(): lax.all_to_all(flat, 'expert', 0, 0, axis_index_groups=groups, tiled=True)]
    all_to_all x4 -> x5, waiting for transfers between devices: 15 us -> 30.7 us  [exchange(): lax.all_to_all(flat, 'expert', 0, 0, axis_index_groups=groups, tiled=True)]
    ppermute x3, starting transfers between devices: 24 us -> 9.82 us  [core_swap(): return lax.ppermute(x, 'dp', [(i, i ^ 1) for i in range(8)])]
    ppermute x8, waiting for transfers between devices: 39.2 us -> 52.7 us  [shift(): lax.ppermute(x, 'dp', [(2 * h + c, 2 * ((h + k) % 4) + c) for h in range(...]
    all_to_all x4 -> x5, starting transfers between devices: 23.2 us -> 31 us  [exchange(): lax.all_to_all(flat, 'expert', 0, 0, axis_index_groups=groups, tiled=True)]
    unnamed x38 -> x36, local copies, waits for them, and re-layouts: 10.3 us -> 10.3 us
  transfers between devices with their start and end apart: 22 -> 23, of which waited for: 16 -> 16; matrix products, arithmetic and copies ran while one was open for 3% -> 3% of each run, Pallas kernels for 1% -> 1%
where the time goes in v11:
time: 251 us; the launch traced here: 249 us
  waiting for transfers between devices  109 us (43%)
  starting transfers between devices  105 us (42%)
  Pallas kernels  14.8 us (6%)
  local copies, waits for them, and re-layouts  12.2 us (5%)
  matrix products  6.28 us (3%)
    ppermute x8, waiting for transfers between devices, shift(): lax.ppermute(x, 'dp', [(2 * h + c, 2 * ((h + k) % 4) + c) for h in range(...  52.7 us
    ppermute x8, starting transfers between devices, shift(): lax.ppermute(x, 'dp', [(2 * h + c, 2 * ((h + k) % 4) + c) for h in range(...  37.3 us
    all_to_all x5, starting transfers between devices, exchange(): lax.all_to_all(flat, 'expert', 0, 0, axis_index_groups=groups, tiled=True)  31 us
    all_to_all x5, waiting for transfers between devices, exchange(): lax.all_to_all(flat, 'expert', 0, 0, axis_index_groups=groups, tiled=True)  30.7 us
    ppermute x7, starting transfers between devices, step(): return lax.ppermute(v, 'expert', pairs)  26.7 us
    ppermute x7, waiting for transfers between devices, step(): return lax.ppermute(v, 'expert', pairs)  22.4 us
    unnamed x36, local copies, waits for them, and re-layouts  10.3 us
    ppermute x3, starting transfers between devices, core_swap(): return lax.ppermute(x, 'dp', [(i, i ^ 1) for i in range(8)])  9.82 us
  transfers between devices with their start and end apart: 23, of which 16 were waited for; matrix products, arithmetic and copies ran while one was open for 3% of the time, Pallas kernels for 1%

profile of v11, /device:TPU:1, one launch (start us, length us, event | category | flops | bytes accessed | tf_op | source)
XLA Modules:
  0.0 249.4 jit_solution(2937950754510041760)
XLA Ops:
  2.4 7.7 %all-to-all-start = ((bf16[8,16,1408]{2,1,0:T(8,128)(2,1)}), bf16[8,16,1408]{2,1,0:T(8,128)(2,1)S(1)}, u32[]{:S(2)}, u32[]{:S(2)}) async-start(bf16[8,16,1408]{2,1,0:T(8,128)(2,1)} %broadcast_in_dim.9), calls=%async_computation | async-start | bytes 720896 | tf_op jit(solution)/shard_map/all_to_all | solution.py:291
  13.1 1.2 shard_map.129
  14.3 6.1 %all-to-all-done = bf16[8,16,1408]{2,1,0:T(8,128)(2,1)S(1)} async-done(((bf16[8,16,1408]{2,1,0:T(8,128)(2,1)}), bf16[8,16,1408]{2,1,0:T(8,128)(2,1)S(1)}, u32[]{:S(2)}, u32[]{:S(2)}) %all-to-all-start) | async-done | bytes 360480 | tf_op jit(solution)/shard_map/all_to_all | solution.py:291
  20.4 3.7 %all-to-all-start.1 = ((bf16[8,32,1024]{2,1,0:T(8,128)(2,1)}), bf16[8,32,1024]{2,1,0:T(8,128)(2,1)S(1)}, u32[]{:S(2)}, u32[]{:S(2)}) async-start(bf16[8,32,1024]{2,1,0:T(8,128)(2,1)} %shard_map.129), calls=%async_computation.1 | async-start | bytes 1048576 | tf_op jit(solution)/shard_map/all_to_all | solution.py:291
  24.1 6.9 %collective-permute-start.2 = (bf16[128,1408]{1,0:T(8,128)(2,1)S(1)}, bf16[128,1408]{1,0:T(8,128)(2,1)S(1)}, u32[]{:S(2)}, u32[]{:S(2)}) collective-permute-start(bf16[128,1408]{1,0:T(8,128)(2,1)S(1)} %bitcast.27), channel_id=1, source_target_pairs={{0,48},{1,49},{2,50},{3,51},{4,52},{5,53},{6,54},{7,55},{8,56},{9,... | collective-permute-start | bytes 1081352 | tf_op jit(solution)/shard_map/ppermute | solution.py:302
  31.0 1.9 collective-permute-start.1
  32.9 4.0 %collective-permute-start = (bf16[128,1408]{1,0:T(8,128)(2,1)S(1)}, bf16[128,1408]{1,0:T(8,128)(2,1)}, u32[]{:S(2)}, u32[]{:S(2)}) collective-permute-start(bf16[128,1408]{1,0:T(8,128)(2,1)S(1)} %bitcast.29), channel_id=1, source_target_pairs={{0,1},{1,0},{2,3},{3,2},{4,5},{5,4},{6,7},{7,6},{8,9},{9,8},{10,11... | collective-permute-start | bytes 1081352 | tf_op jit(solution)/shard_map/ppermute | solution.py:302
  37.7 4.0 %collective-permute-done.1.s1 = bf16[128,1408]{1,0:T(8,128)(2,1)S(1)} collective-permute-done((bf16[128,1408]{1,0:T(8,128)(2,1)S(1)}, bf16[128,1408]{1,0:T(8,128)(2,1)S(1)}, u32[]{:S(2)}, u32[]{:S(2)}) %collective-permute-start.1) | collective-permute-done | bytes 360480 | tf_op jit(solution)/shard_map/ppermute | solution.py:302
  43.5 1.4 shard_map.130
  44.8 1.0 copy-done.4
  45.9 4.7 %all-to-all-start.2 = ((bf16[8,80,896]{2,1,0:T(8,128)(2,1)}), bf16[8,80,896]{2,1,0:T(8,128)(2,1)S(1)}, u32[]{:S(2)}, u32[]{:S(2)}) async-start(bf16[8,80,896]{2,1,0:T(8,128)(2,1)} %copy-done.4), calls=%async_computation.2 | async-start | bytes 2293760 | tf_op jit(solution)/shard_map/all_to_all | solution.py:291
  50.5 4.6 %collective-permute-start.5 = (bf16[128,1408]{1,0:T(8,128)(2,1)}, bf16[128,1408]{1,0:T(8,128)(2,1)}, u32[]{:S(2)}, u32[]{:S(2)}) collective-permute-start(bf16[128,1408]{1,0:T(8,128)(2,1)} %collective-permute-done.t0), channel_id=1, source_target_pairs={{0,48},{1,49},{2,50},{3,51},{4,52},{5,53},{6,54},{7,55},{8,56},{9,... | collective-permute-start | bytes 1081352 | tf_op jit(solution)/shard_map/ppermute | solution.py:302
  55.1 1.9 collective-permute-start.3
  57.0 2.2 collective-permute-start.4
  59.2 11.9 %collective-permute-done.5.t3 = bf16[128,1408]{1,0:T(8,128)(2,1)} collective-permute-done((bf16[128,1408]{1,0:T(8,128)(2,1)}, bf16[128,1408]{1,0:T(8,128)(2,1)}, u32[]{:S(2)}, u32[]{:S(2)}) %collective-permute-start.5) | collective-permute-done | bytes 360480 | tf_op jit(solution)/shard_map/ppermute | solution.py:302
  71.1 5.3 %collective-permute-start.6 = (bf16[128,1408]{1,0:T(8,128)(2,1)}, bf16[128,1408]{1,0:T(8,128)(2,1)}, u32[]{:S(2)}, u32[]{:S(2)}) collective-permute-start(bf16[128,1408]{1,0:T(8,128)(2,1)} %collective-permute-done.5.t3), channel_id=1, source_target_pairs={{0,48},{1,49},{2,50},{3,51},{4,52},{5,53},{6,54},{7,55},{8,56},{9,... | collective-permute-start | bytes 1081352 | tf_op jit(solution)/shard_map/ppermute | solution.py:302
  77.1 4.3 %collective-permute-done.4.s2 = bf16[128,1408]{1,0:T(8,128)(2,1)} collective-permute-done((bf16[128,1408]{1,0:T(8,128)(2,1)}, bf16[128,1408]{1,0:T(8,128)(2,1)}, u32[]{:S(2)}, u32[]{:S(2)}) %collective-permute-start.4) | collective-permute-done | bytes 360480 | tf_op jit(solution)/shard_map/ppermute | solution.py:302
  81.5 1.2 collective-permute-done.6.t2
  82.6 1.2 copy-done.2
  85.8 4.5 %shard_map.131 = (bf16[640,448]{1,0:T(8,128)(2,1)S(1)}, bf16[80,3072]{1,0:T(8,128)(2,1)S(1)}, bf16[240,3072]{1,0:T(8,128)(2,1)S(1)}, bf16[80,3072]{1,0:T(8,128)(...) custom-call(s32[5]{0:T(128)S(1)} %stack.27.who_ref, ...), custom_call_target="tpu_custom_call" | custom-call | tf_op jit(solution)/shard_map/pallas_call | solution.py:348
  90.3 4.6 %collective-permute-start.8 = (bf16[80,3072]{1,0:T(8,128)(2,1)S(1)}, bf16[80,3072]{1,0:T(8,128)(2,1)S(1)}, u32[]{:S(2)}, u32[]{:S(2)}) collective-permute-start(bf16[80,3072]{1,0:T(8,128)(2,1)S(1)} %get-tuple-element.34), channel_id=1, source_target_pairs={{0,64},{64,0},{128,192},{192,128},{256,320},{320,256},{384,448},{4... | collective-permute-start | bytes 1474568 | tf_op jit(solution)/shard_map/ppermute | solution.py:255
  94.9 1.9 collective-permute-start.7
  97.0 5.8 %collective-permute-start.9 = (bf16[40,3072]{1,0:T(8,128)(2,1)S(1)}, bf16[40,3072]{1,0:T(8,128)(2,1)S(1)}, u32[]{:S(2)}, u32[]{:S(2)}) collective-permute-start(bf16[40,3072]{1,0:T(8,128)(2,1)S(1)} %get-tuple-element.45), channel_id=1, source_target_pairs={{0,128},{64,192},{128,256},{192,320},{256,384},{320,448},{384,0},{... | collective-permute-start | bytes 737288 | tf_op jit(solution)/shard_map/ppermute | solution.py:259
  102.8 5.9 %collective-permute-start.11 = (bf16[40,3072]{1,0:T(8,128)(2,1)S(1)}, bf16[40,3072]{1,0:T(8,128)(2,1)S(1)}, u32[]{:S(2)}, u32[]{:S(2)}) collective-permute-start(bf16[40,3072]{1,0:T(8,128)(2,1)S(1)} %get-tuple-element.44), channel_id=1, source_target_pairs={{0,384},{64,448},{128,0},{192,64},{256,128},{320,192},{384,256},{4... | collective-permute-start | bytes 737288 | tf_op jit(solution)/shard_map/ppermute | solution.py:259
  108.7 4.8 %collective-permute-done.9.arrived_ref = bf16[40,3072]{1,0:T(8,128)(2,1)S(1)} collective-permute-done((bf16[40,3072]{1,0:T(8,128)(2,1)S(1)}, bf16[40,3072]{1,0:T(8,128)(2,1)S(1)}, u32[]{:S(2)}, u32[]{:S(2)}) %collective-permute-start.9) | collective-permute-done | bytes 245792 | tf_op jit(solution)/shard_map/ppermute | solution.py:259
  113.7 5.3 %collective-permute-start.10 = (bf16[80,3072]{1,0:T(8,128)(2,1)S(1)}, bf16[80,3072]{1,0:T(8,128)(2,1)S(1)}, u32[]{:S(2)}, u32[]{:S(2)}) collective-permute-start(bf16[80,3072]{1,0:T(8,128)(2,1)S(1)} %shard_map.132), channel_id=1, source_target_pairs={{0,128},{64,192},{128,256},{192,320},{256,384},{320,448},{384,0},{... | collective-permute-start | bytes 1474568 | tf_op jit(solution)/shard_map/ppermute | solution.py:259
  118.9 1.0 collective-permute-done.11.arrived_ref
  120.2 5.1 %collective-permute-start.12 = (bf16[80,3072]{1,0:T(8,128)(2,1)S(1)}, bf16[80,3072]{1,0:T(8,128)(2,1)S(1)}, u32[]{:S(2)}, u32[]{:S(2)}) collective-permute-start(bf16[80,3072]{1,0:T(8,128)(2,1)S(1)} %shard_map.133), channel_id=1, source_target_pairs={{0,384},{64,448},{128,0},{192,64},{256,128},{320,192},{384,256},{4... | collective-permute-start | bytes 1474568 | tf_op jit(solution)/shard_map/ppermute | solution.py:259
  125.3 13.1 %collective-permute-done.10.left_ref = bf16[80,3072]{1,0:T(8,128)(2,1)S(1)} collective-permute-done((bf16[80,3072]{1,0:T(8,128)(2,1)S(1)}, bf16[80,3072]{1,0:T(8,128)(2,1)S(1)}, u32[]{:S(2)}, u32[]{:S(2)}) %collective-permute-start.10) | collective-permute-done | bytes 491552 | tf_op jit(solution)/shard_map/ppermute | solution.py:259
  138.4 9.2 %collective-permute-done.12.right_ref = bf16[80,3072]{1,0:T(8,128)(2,1)S(1)} collective-permute-done((bf16[80,3072]{1,0:T(8,128)(2,1)S(1)}, bf16[80,3072]{1,0:T(8,128)(2,1)S(1)}, u32[]{:S(2)}, u32[]{:S(2)}) %collective-permute-start.12) | collective-permute-done | bytes 491552 | tf_op jit(solution)/shard_map/ppermute | solution.py:259
  148.0 5.0 %collective-permute-start.14 = (bf16[80,3072]{1,0:T(8,128)(2,1)S(1)}, bf16[80,3072]{1,0:T(8,128)(2,1)S(1)}, u32[]{:S(2)}, u32[]{:S(2)}) collective-permute-start(bf16[80,3072]{1,0:T(8,128)(2,1)S(1)} %shard_map.134), channel_id=1, source_target_pairs={{0,128},{64,192},{128,256},{192,320},{256,384},{320,448},{384,0},{... | collective-permute-start | bytes 1474568 | tf_op jit(solution)/shard_map/ppermute | solution.py:259
  152.9 2.4 collective-permute-start.13
  155.4 15.6 %collective-permute-done.14 = bf16[80,3072]{1,0:T(8,128)(2,1)S(1)} collective-permute-done((bf16[80,3072]{1,0:T(8,128)(2,1)S(1)}, bf16[80,3072]{1,0:T(8,128)(2,1)S(1)}, u32[]{:S(2)}, u32[]{:S(2)}) %collective-permute-start.14) | collective-permute-done | bytes 491552 | tf_op jit(solution)/shard_map/ppermute | solution.py:259
  171.1 4.0 %collective-permute-start.15 = (bf16[40,3072]{1,0:T(8,128)(2,1)S(1)}, bf16[40,3072]{1,0:T(8,128)(2,1)S(1)}, u32[]{:S(2)}, u32[]{:S(2)}) collective-permute-start(bf16[40,3072]{1,0:T(8,128)(2,1)S(1)} %slice.26), channel_id=1, source_target_pairs={{0,128},{64,192},{128,256},{192,320},{256,384},{320,448},{384,0},{... | collective-permute-start | bytes 737288 | tf_op jit(solution)/shard_map/ppermute | solution.py:259
  175.1 3.9 %collective-permute-start.16 = (bf16[40,3072]{1,0:T(8,128)(2,1)S(1)}, bf16[40,3072]{1,0:T(8,128)(2,1)S(1)}, u32[]{:S(2)}, u32[]{:S(2)}) collective-permute-start(bf16[40,3072]{1,0:T(8,128)(2,1)S(1)} %slice.27), channel_id=1, source_target_pairs={{0,384},{64,448},{128,0},{192,64},{256,128},{320,192},{384,256},{4... | collective-permute-start | bytes 737288 | tf_op jit(solution)/shard_map/ppermute | solution.py:259
  179.1 4.2 %collective-permute-done.15 = bf16[40,3072]{1,0:T(8,128)(2,1)S(1)} collective-permute-done((bf16[40,3072]{1,0:T(8,128)(2,1)S(1)}, bf16[40,3072]{1,0:T(8,128)(2,1)S(1)}, u32[]{:S(2)}, u32[]{:S(2)}) %collective-permute-start.15) | collective-permute-done | bytes 245792 | tf_op jit(solution)/shard_map/ppermute | solution.py:259
  183.4 4.9 %collective-permute-done.16 = bf16[40,3072]{1,0:T(8,128)(2,1)S(1)} collective-permute-done((bf16[40,3072]{1,0:T(8,128)(2,1)S(1)}, bf16[40,3072]{1,0:T(8,128)(2,1)S(1)}, u32[]{:S(2)}, u32[]{:S(2)}) %collective-permute-start.16) | collective-permute-done | bytes 245792 | tf_op jit(solution)/shard_map/ppermute | solution.py:259
  188.3 3.3 %collective-permute-start.17 = (bf16[320,3072]{1,0:T(8,128)(2,1)S(1)}, bf16[320,3072]{1,0:T(8,128)(2,1)S(1)}, u32[]{:S(2)}, u32[]{:S(2)}) collective-permute-start(bf16[320,3072]{1,0:T(8,128)(2,1)S(1)} %constant_dynamic-update-slice_fusion.mine_ref), channel_id=1, source_target_pairs={{0,64},{64,0},{128,192},{192,128},{256,320},{320,256},{384,448},{4... | collective-permute-start | bytes 5898248 | tf_op jit(solution)/shard_map/ppermute | solution.py:255
  191.6 3.6 %collective-permute-done.17.other_ref = bf16[320,3072]{1,0:T(8,128)(2,1)S(1)} collective-permute-done((bf16[320,3072]{1,0:T(8,128)(2,1)S(1)}, bf16[320,3072]{1,0:T(8,128)(2,1)S(1)}, u32[]{:S(2)}, u32[]{:S(2)}) %collective-permute-start.17) | collective-permute-done | bytes 1966112 | tf_op jit(solution)/shard_map/ppermute | solution.py:255
  195.2 4.4 %shard_map.135 = (bf16[8,80,896]{2,1,0:T(8,128)(2,1)}, bf16[2,320,2048]{2,1,0:T(8,128)(2,1)S(1)}) custom-call(s32[5]{0:T(128)S(1)} %stack.27.who_ref, bf16[320,3072]{1,0:T(8,128)(2,1)S(1)} %constant_dynamic-update-slice_fusion.mine_ref, bf16[320,3072]{1,0:T(8,128)(2,1)S(1)} %collective-permute-done.17.other_ref, bf16[448,1024]{1,0:T(8,128)(2,1)S(1)} %bitcast.22, ...), custom_call_target="tpu_custom_call" | custom-call | tf_op jit(solution)/shard_map/pallas_call | solution.py:379
  199.6 1.5 copy-done.12
  201.1 6.4 %all-to-all-start.3 = ((bf16[8,80,896]{2,1,0:T(8,128)(2,1)}), bf16[8,80,896]{2,1,0:T(8,128)(2,1)S(1)}, u32[]{:S(2)}, u32[]{:S(2)}) async-start(bf16[8,80,896]{2,1,0:T(8,128)(2,1)} %get-tuple-element.36), calls=%async_computation.3 | async-start | bytes 2293760 | tf_op jit(solution)/shard_map/all_to_all | solution.py:291
  207.5 3.1 %convolution_convert_fusion.1 = bf16[448,1024]{1,0:T(8,128)(2,1)} fusion(bf16[640,448]{1,0:T(8,128)(2,1)S(1)} %copy-done.14, bf16[640,2048]{1,0:T(8,128)(2,1)} %bitcast.31), kind=kOutput, calls=%fused_computation.1 | convolution fusion | flops 587661312 | bytes 2801664 | tf_op jit(solution)/shard_map/dot_general | solution.py:22
  210.7 13.1 %all-to-all-done.3.recv_ref = bf16[8,80,896]{2,1,0:T(8,128)(2,1)S(1)} async-done(((bf16[8,80,896]{2,1,0:T(8,128)(2,1)}), bf16[8,80,896]{2,1,0:T(8,128)(2,1)S(1)}, u32[]{:S(2)}, u32[]{:S(2)}) %all-to-all-start.3) | async-done | bytes 1146912 | tf_op jit(solution)/shard_map/all_to_all | solution.py:291
  223.8 1.7 shard_map.136
  225.4 8.6 %all-to-all-start.4 = ((bf16[8,32,896]{2,1,0:T(8,128)(2,1)}), bf16[8,32,896]{2,1,0:T(8,128)(2,1)S(1)}, u32[]{:S(2)}, u32[]{:S(2)}) async-start(bf16[8,32,896]{2,1,0:T(8,128)(2,1)} %bitcast.13), calls=%async_computation.4 | async-start | bytes 917504 | tf_op jit(solution)/shard_map/all_to_all | solution.py:291
  234.0 3.1 %fusion = bf16[1,448,1024]{2,1,0:T(8,128)(2,1)} fusion(bf16[640,448]{1,0:T(8,128)(2,1)S(1)} %copy-done.14, bf16[640,2048]{1,0:T(8,128)(2,1)} %bitcast.32), kind=kOutput, calls=%fused_computation.2 | convolution fusion | flops 587661312 | bytes 2801664 | tf_op jit(solution)/shard_map/dot_general | solution.py:22
  237.2 11.5 %all-to-all-done.4.recv_ref = bf16[8,32,896]{2,1,0:T(8,128)(2,1)S(1)} async-done(((bf16[8,32,896]{2,1,0:T(8,128)(2,1)}), bf16[8,32,896]{2,1,0:T(8,128)(2,1)S(1)}, u32[]{:S(2)}, u32[]{:S(2)}) %all-to-all-start.4) | async-done | bytes 458784 | tf_op jit(solution)/shard_map/all_to_all | solution.py:291
  (55 shorter events, 11.3 us)
Async XLA Ops:
  0.6 42.8 %copy-start.9 = (f32[80,256]{1,0:T(8,128)S(1)}, f32[80,256]{1,0:T(8,128)}, u32[]{:S(2)}) copy-start(f32[80,256]{1,0:T(8,128)} %constant.53.clone.want_ref) | copy-start | bytes 245764
  2.4 18.0 %all-to-all-start = ((bf16[8,16,1408]{2,1,0:T(8,128)(2,1)}), bf16[8,16,1408]{2,1,0:T(8,128)(2,1)S(1)}, u32[]{:S(2)}, u32[]{:S(2)}) async-start(bf16[8,16,1408]{2,1,0:T(8,128)(2,1)} %broadcast_in_dim.9), calls=%async_computation | async-start | bytes 720896 | tf_op jit(solution)/shard_map/all_to_all | solution.py:291
  11.6 0.8 copy-start.10
  12.3 0.8 copy-start.11
  20.4 62.2 %copy-start = (bf16[1,448,1024]{2,1,0:T(8,128)(2,1)S(1)}, bf16[1,448,1024]{2,1,0:T(8,128)(2,1)}, u32[]{:S(2)}) copy-start(bf16[1,448,1024]{2,1,0:T(8,128)(2,1)} %param.15) | copy-start | bytes 2752516
  20.4 62.2 %copy-start.1 = (bf16[1,448,1024]{2,1,0:T(8,128)(2,1)S(1)}, bf16[1,448,1024]{2,1,0:T(8,128)(2,1)}, u32[]{:S(2)}) copy-start(bf16[1,448,1024]{2,1,0:T(8,128)(2,1)} %param.16) | copy-start | bytes 2752516
  20.4 23.0 %all-to-all-start.1 = ((bf16[8,32,1024]{2,1,0:T(8,128)(2,1)}), bf16[8,32,1024]{2,1,0:T(8,128)(2,1)S(1)}, u32[]{:S(2)}, u32[]{:S(2)}) async-start(bf16[8,32,1024]{2,1,0:T(8,128)(2,1)} %shard_map.129), calls=%async_computation.1 | async-start | bytes 1048576 | tf_op jit(solution)/shard_map/all_to_all | solution.py:291
  24.1 12.8 %collective-permute-start.2 = (bf16[128,1408]{1,0:T(8,128)(2,1)S(1)}, bf16[128,1408]{1,0:T(8,128)(2,1)S(1)}, u32[]{:S(2)}, u32[]{:S(2)}) collective-permute-start(bf16[128,1408]{1,0:T(8,128)(2,1)S(1)} %bitcast.27), channel_id=1, source_target_pairs={{0,48},{1,49},{2,50},{3,51},{4,52},{5,53},{6,54},{7,55},{8,56},{9,... | collective-permute-start | bytes 1081352 | tf_op jit(solution)/shard_map/ppermute | solution.py:302
  31.0 10.7 %collective-permute-start.1 = (bf16[128,1408]{1,0:T(8,128)(2,1)S(1)}, bf16[128,1408]{1,0:T(8,128)(2,1)S(1)}, u32[]{:S(2)}, u32[]{:S(2)}) collective-permute-start(bf16[128,1408]{1,0:T(8,128)(2,1)S(1)} %bitcast.28), channel_id=1, source_target_pairs={{0,16},{1,17},{2,18},{3,19},{4,20},{5,21},{6,22},{7,23},{8,24},{9,... | collective-permute-start | bytes 1081352 | tf_op jit(solution)/shard_map/ppermute | solution.py:302
  32.9 10.5 %collective-permute-start = (bf16[128,1408]{1,0:T(8,128)(2,1)S(1)}, bf16[128,1408]{1,0:T(8,128)(2,1)}, u32[]{:S(2)}, u32[]{:S(2)}) collective-permute-start(bf16[128,1408]{1,0:T(8,128)(2,1)S(1)} %bitcast.29), channel_id=1, source_target_pairs={{0,1},{1,0},{2,3},{3,2},{4,5},{5,4},{6,7},{7,6},{8,9},{9,8},{10,11... | collective-permute-start | bytes 1081352 | tf_op jit(solution)/shard_map/ppermute | solution.py:302
  36.9 0.7 copy-start.5
  41.7 0.7 copy-start.7
  44.8 1.0 copy-start.4
  45.9 36.8 %all-to-all-start.2 = ((bf16[8,80,896]{2,1,0:T(8,128)(2,1)}), bf16[8,80,896]{2,1,0:T(8,128)(2,1)S(1)}, u32[]{:S(2)}, u32[]{:S(2)}) async-start(bf16[8,80,896]{2,1,0:T(8,128)(2,1)} %copy-done.4), calls=%async_computation.2 | async-start | bytes 2293760 | tf_op jit(solution)/shard_map/all_to_all | solution.py:291
  50.5 20.5 %collective-permute-start.5 = (bf16[128,1408]{1,0:T(8,128)(2,1)}, bf16[128,1408]{1,0:T(8,128)(2,1)}, u32[]{:S(2)}, u32[]{:S(2)}) collective-permute-start(bf16[128,1408]{1,0:T(8,128)(2,1)} %collective-permute-done.t0), channel_id=1, source_target_pairs={{0,48},{1,49},{2,50},{3,51},{4,52},{5,53},{6,54},{7,55},{8,56},{9,... | collective-permute-start | bytes 1081352 | tf_op jit(solution)/shard_map/ppermute | solution.py:302
  55.1 26.4 %collective-permute-start.3 = (bf16[128,1408]{1,0:T(8,128)(2,1)}, bf16[128,1408]{1,0:T(8,128)(2,1)}, u32[]{:S(2)}, u32[]{:S(2)}) collective-permute-start(bf16[128,1408]{1,0:T(8,128)(2,1)} %collective-permute-done.t0), channel_id=1, source_target_pairs={{0,16},{1,17},{2,18},{3,19},{4,20},{5,21},{6,22},{7,23},{8,24},{9,... | collective-permute-start | bytes 1081352 | tf_op jit(solution)/shard_map/ppermute | solution.py:302
  57.0 24.4 %collective-permute-start.4 = (bf16[128,1408]{1,0:T(8,128)(2,1)}, bf16[128,1408]{1,0:T(8,128)(2,1)}, u32[]{:S(2)}, u32[]{:S(2)}) collective-permute-start(bf16[128,1408]{1,0:T(8,128)(2,1)} %copy-done.7), channel_id=1, source_target_pairs={{0,16},{1,17},{2,18},{3,19},{4,20},{5,21},{6,22},{7,23},{8,24},{9,... | collective-permute-start | bytes 1081352 | tf_op jit(solution)/shard_map/ppermute | solution.py:302
  71.1 11.6 %collective-permute-start.6 = (bf16[128,1408]{1,0:T(8,128)(2,1)}, bf16[128,1408]{1,0:T(8,128)(2,1)}, u32[]{:S(2)}, u32[]{:S(2)}) collective-permute-start(bf16[128,1408]{1,0:T(8,128)(2,1)} %collective-permute-done.5.t3), channel_id=1, source_target_pairs={{0,48},{1,49},{2,50},{3,51},{4,52},{5,53},{6,54},{7,55},{8,56},{9,... | collective-permute-start | bytes 1081352 | tf_op jit(solution)/shard_map/ppermute | solution.py:302
  82.6 1.2 copy-start.2
  83.8 1.0 copy-start.6
  84.8 1.0 copy-start.8
  90.3 23.2 %copy-start.13 = (bf16[640,448]{1,0:T(8,128)(2,1)}, bf16[640,448]{1,0:T(8,128)(2,1)S(1)}, u32[]{:S(2)}) copy-start(bf16[640,448]{1,0:T(8,128)(2,1)S(1)} %get-tuple-element.37) | copy-start | bytes 1720324
  90.3 6.5 %collective-permute-start.8 = (bf16[80,3072]{1,0:T(8,128)(2,1)S(1)}, bf16[80,3072]{1,0:T(8,128)(2,1)S(1)}, u32[]{:S(2)}, u32[]{:S(2)}) collective-permute-start(bf16[80,3072]{1,0:T(8,128)(2,1)S(1)} %get-tuple-element.34), channel_id=1, source_target_pairs={{0,64},{64,0},{128,192},{192,128},{256,320},{320,256},{384,448},{4... | collective-permute-start | bytes 1474568 | tf_op jit(solution)/shard_map/ppermute | solution.py:255
  94.9 18.6 %collective-permute-start.7 = (bf16[240,3072]{1,0:T(8,128)(2,1)S(1)}, bf16[240,3072]{1,0:T(8,128)(2,1)S(1)}, u32[]{:S(2)}, u32[]{:S(2)}) collective-permute-start(bf16[240,3072]{1,0:T(8,128)(2,1)S(1)} %get-tuple-element.32), channel_id=1, source_target_pairs={{0,64},{64,0},{128,192},{192,128},{256,320},{320,256},{384,448},{4... | collective-permute-start | bytes 4423688 | tf_op jit(solution)/shard_map/ppermute | solution.py:255
  97.0 16.5 %collective-permute-start.9 = (bf16[40,3072]{1,0:T(8,128)(2,1)S(1)}, bf16[40,3072]{1,0:T(8,128)(2,1)S(1)}, u32[]{:S(2)}, u32[]{:S(2)}) collective-permute-start(bf16[40,3072]{1,0:T(8,128)(2,1)S(1)} %get-tuple-element.45), channel_id=1, source_target_pairs={{0,128},{64,192},{128,256},{192,320},{256,384},{320,448},{384,0},{... | collective-permute-start | bytes 737288 | tf_op jit(solution)/shard_map/ppermute | solution.py:259
  102.8 17.2 %collective-permute-start.11 = (bf16[40,3072]{1,0:T(8,128)(2,1)S(1)}, bf16[40,3072]{1,0:T(8,128)(2,1)S(1)}, u32[]{:S(2)}, u32[]{:S(2)}) collective-permute-start(bf16[40,3072]{1,0:T(8,128)(2,1)S(1)} %get-tuple-element.44), channel_id=1, source_target_pairs={{0,384},{64,448},{128,0},{192,64},{256,128},{320,192},{384,256},{4... | collective-permute-start | bytes 737288 | tf_op jit(solution)/shard_map/ppermute | solution.py:259
  113.7 24.7 %collective-permute-start.10 = (bf16[80,3072]{1,0:T(8,128)(2,1)S(1)}, bf16[80,3072]{1,0:T(8,128)(2,1)S(1)}, u32[]{:S(2)}, u32[]{:S(2)}) collective-permute-start(bf16[80,3072]{1,0:T(8,128)(2,1)S(1)} %shard_map.132), channel_id=1, source_target_pairs={{0,128},{64,192},{128,256},{192,320},{256,384},{320,448},{384,0},{... | collective-permute-start | bytes 1474568 | tf_op jit(solution)/shard_map/ppermute | solution.py:259
  120.2 27.3 %collective-permute-start.12 = (bf16[80,3072]{1,0:T(8,128)(2,1)S(1)}, bf16[80,3072]{1,0:T(8,128)(2,1)S(1)}, u32[]{:S(2)}, u32[]{:S(2)}) collective-permute-start(bf16[80,3072]{1,0:T(8,128)(2,1)S(1)} %shard_map.133), channel_id=1, source_target_pairs={{0,384},{64,448},{128,0},{192,64},{256,128},{320,192},{384,256},{4... | collective-permute-start | bytes 1474568 | tf_op jit(solution)/shard_map/ppermute | solution.py:259
  148.0 23.1 %collective-permute-start.14 = (bf16[80,3072]{1,0:T(8,128)(2,1)S(1)}, bf16[80,3072]{1,0:T(8,128)(2,1)S(1)}, u32[]{:S(2)}, u32[]{:S(2)}) collective-permute-start(bf16[80,3072]{1,0:T(8,128)(2,1)S(1)} %shard_map.134), channel_id=1, source_target_pairs={{0,128},{64,192},{128,256},{192,320},{256,384},{320,448},{384,0},{... | collective-permute-start | bytes 1474568 | tf_op jit(solution)/shard_map/ppermute | solution.py:259
  152.9 22.1 %collective-permute-start.13 = (bf16[80,3072]{1,0:T(8,128)(2,1)S(1)}, bf16[80,3072]{1,0:T(8,128)(2,1)S(1)}, u32[]{:S(2)}, u32[]{:S(2)}) collective-permute-start(bf16[80,3072]{1,0:T(8,128)(2,1)S(1)} %shard_map.134), channel_id=1, source_target_pairs={{0,384},{64,448},{128,0},{192,64},{256,128},{320,192},{384,256},{4... | collective-permute-start | bytes 1474568 | tf_op jit(solution)/shard_map/ppermute | solution.py:259
  155.4 39.7 %copy-start.3 = (bf16[1,1024,448]{1,2,0:T(8,128)(2,1)S(1)}, bf16[1,1024,448]{1,2,0:T(8,128)(2,1)}, u32[]{:S(2)}) copy-start(bf16[1,1024,448]{1,2,0:T(8,128)(2,1)} %param.17) | copy-start | bytes 2752516
  171.1 12.3 %collective-permute-start.15 = (bf16[40,3072]{1,0:T(8,128)(2,1)S(1)}, bf16[40,3072]{1,0:T(8,128)(2,1)S(1)}, u32[]{:S(2)}, u32[]{:S(2)}) collective-permute-start(bf16[40,3072]{1,0:T(8,128)(2,1)S(1)} %slice.26), channel_id=1, source_target_pairs={{0,128},{64,192},{128,256},{192,320},{256,384},{320,448},{384,0},{... | collective-permute-start | bytes 737288 | tf_op jit(solution)/shard_map/ppermute | solution.py:259
  175.1 13.1 %collective-permute-start.16 = (bf16[40,3072]{1,0:T(8,128)(2,1)S(1)}, bf16[40,3072]{1,0:T(8,128)(2,1)S(1)}, u32[]{:S(2)}, u32[]{:S(2)}) collective-permute-start(bf16[40,3072]{1,0:T(8,128)(2,1)S(1)} %slice.27), channel_id=1, source_target_pairs={{0,384},{64,448},{128,0},{192,64},{256,128},{320,192},{384,256},{4... | collective-permute-start | bytes 737288 | tf_op jit(solution)/shard_map/ppermute | solution.py:259
  188.3 6.9 %collective-permute-start.17 = (bf16[320,3072]{1,0:T(8,128)(2,1)S(1)}, bf16[320,3072]{1,0:T(8,128)(2,1)S(1)}, u32[]{:S(2)}, u32[]{:S(2)}) collective-permute-start(bf16[320,3072]{1,0:T(8,128)(2,1)S(1)} %constant_dynamic-update-slice_fusion.mine_ref), channel_id=1, source_target_pairs={{0,64},{64,0},{128,192},{192,128},{256,320},{320,256},{384,448},{4... | collective-permute-start | bytes 5898248 | tf_op jit(solution)/shard_map/ppermute | solution.py:255
  199.6 1.5 copy-start.12
  201.1 6.4 %copy-start.14 = (bf16[640,448]{1,0:T(8,128)(2,1)S(1)}, bf16[640,448]{1,0:T(8,128)(2,1)}, u32[]{:S(2)}) copy-start(bf16[640,448]{1,0:T(8,128)(2,1)} %copy-done.13) | copy-start | bytes 1720324
  201.1 22.7 %all-to-all-start.3 = ((bf16[8,80,896]{2,1,0:T(8,128)(2,1)}), bf16[8,80,896]{2,1,0:T(8,128)(2,1)S(1)}, u32[]{:S(2)}, u32[]{:S(2)}) async-start(bf16[8,80,896]{2,1,0:T(8,128)(2,1)} %get-tuple-element.36), calls=%async_computation.3 | async-start | bytes 2293760 | tf_op jit(solution)/shard_map/all_to_all | solution.py:291
  225.4 23.3 %all-to-all-start.4 = ((bf16[8,32,896]{2,1,0:T(8,128)(2,1)}), bf16[8,32,896]{2,1,0:T(8,128)(2,1)S(1)}, u32[]{:S(2)}, u32[]{:S(2)}) async-start(bf16[8,32,896]{2,1,0:T(8,128)(2,1)} %bitcast.13), calls=%async_computation.4 | async-start | bytes 917504 | tf_op jit(solution)/shard_map/all_to_all | solution.py:291

commit v12 on v9

--- a/solution.py
+++ b/solution.py
@@ -154,6 +154,20 @@
             store(2, j, dot(grads_ref[...], restored_ref[2, at, :], NT))
 
 
+def merge_kernel(at, low, own_ref, other_ref, arrived_ref, out_ref):
+    rows, width = out_ref.shape
+    mid = arrived_ref.shape[0]
+
+    @pl.loop(0, width // TILE)
+    def _(j):
+        lanes = pl.ds(pl.multiple_of(j * TILE, TILE), TILE)
+        value = own_ref[at : at + rows, lanes].astype(F32) + other_ref[at : at + rows, lanes].astype(F32)
+        more = arrived_ref[:, lanes].astype(F32)
+        none = jnp.zeros((rows - mid, TILE), F32)
+        value = value + jnp.concatenate([more, none] if low else [none, more], axis=0)
+        out_ref[:, lanes] = value.astype(BF)
+
+
 def activate_kernel(own_ref, other_ref, left_ref, right_ref, out_ref):
     ff = out_ref.shape[1] // 3
     rows = out_ref.shape[0]
@@ -341,11 +355,12 @@
     far = add(far, core_swap(far_out))
     rest_in = core_swap(rest_out)
     from_left, from_right = shift(far[:mid], 1), shift(far[mid:], -1)
-    sides = add(rest[chunk:], rest_in[chunk:])
-    right, left = sides[:chunk], sides[chunk:]
-    right = jnp.concatenate([add(right[:mid], from_left), right[mid:]], axis=0)
-    left = jnp.concatenate([left[:mid], add(left[mid:], from_right)], axis=0)
-    from_left, from_right = shift(right, 1), shift(left, -1)
+    def merged(at, low, arrived):
+        kernel = functools.partial(merge_kernel, at, low)
+        return call(kernel, [(chunk, wide)], operands=3)(rest, rest_in, arrived)[0]
+
+    from_left = shift(merged(chunk, True, from_left), 1)
+    from_right = shift(merged(2 * chunk, False, from_right), -1)
     (own,) = call(activate_kernel, [(chunk, wide)], operands=4)(
         rest, rest_in, from_left, from_right
     )

time: 246 us -> 249 us (1.012)
  waiting for transfers between devices: 80.1 us -> 93.8 us
  starting transfers between devices: 110 us -> 97.3 us
    ppermute x3, starting transfers between devices: 24 us -> 9.81 us  [core_swap(): return lax.ppermute(x, 'dp', [(i, i ^ 1) for i in range(8)])]
    ppermute x8, waiting for transfers between devices: 39.2 us -> 52.7 us  [shift(): lax.ppermute(x, 'dp', [(2 * h + c, 2 * ((h + k) % 4) + c) for h in range(...]
  transfers between devices with their start and end apart: 22 -> 22, of which waited for: 16 -> 15; matrix products, arithmetic and copies ran while one was open for 3% -> 3% of each run, Pallas kernels for 1% -> 1%
where the time goes in v12:
time: 249 us; the launch traced here: 246 us
  starting transfers between devices  97.3 us (39%)
  waiting for transfers between devices  93.8 us (38%)
  blocking collectives  22.4 us (9%)
  Pallas kernels  13.6 us (5%)
  local copies, waits for them, and re-layouts  12.2 us (5%)
  matrix products  5.11 us (2%)
    ppermute x8, waiting for transfers between devices, shift(): lax.ppermute(x, 'dp', [(2 * h + c, 2 * ((h + k) % 4) + c) for h in range(...  52.7 us
    ppermute x8, starting transfers between devices, shift(): lax.ppermute(x, 'dp', [(2 * h + c, 2 * ((h + k) % 4) + c) for h in range(...  37.4 us
    ppermute x7, starting transfers between devices, step(): return lax.ppermute(v, 'expert', pairs)  26.7 us
    all_to_all x4, starting transfers between devices, exchange(): lax.all_to_all(flat, 'expert', 0, 0, axis_index_groups=groups, tiled=True)  23.3 us
    all_to_all x1, blocking collectives, exchange(): lax.all_to_all(flat, 'expert', 0, 0, axis_index_groups=groups, tiled=True)  22.4 us
    ppermute x7, waiting for transfers between devices, step(): return lax.ppermute(v, 'expert', pairs)  22.4 us
    all_to_all x4, waiting for transfers between devices, exchange(): lax.all_to_all(flat, 'expert', 0, 0, axis_index_groups=groups, tiled=True)  15.1 us
    unnamed x38, local copies, waits for them, and re-layouts  10.3 us
  transfers between devices with their start and end apart: 22, of which 15 were waited for; matrix products, arithmetic and copies ran while one was open for 3% of the time, Pallas kernels for 1%

profile of v12, /device:TPU:1, one launch (start us, length us, event | category | flops | bytes accessed | tf_op | source)
XLA Modules:
  0.0 246.2 jit_solution(12534095544694425674)
XLA Ops:
  2.4 7.7 %all-to-all-start = ((bf16[8,16,1408]{2,1,0:T(8,128)(2,1)}), bf16[8,16,1408]{2,1,0:T(8,128)(2,1)S(1)}, u32[]{:S(2)}, u32[]{:S(2)}) async-start(bf16[8,16,1408]{2,1,0:T(8,128)(2,1)} %broadcast_in_dim.9), calls=%async_computation | async-start | bytes 720896 | tf_op jit(solution)/shard_map/all_to_all | solution.py:285
  13.1 1.2 shard_map.129
  14.3 6.1 %all-to-all-done = bf16[8,16,1408]{2,1,0:T(8,128)(2,1)S(1)} async-done(((bf16[8,16,1408]{2,1,0:T(8,128)(2,1)}), bf16[8,16,1408]{2,1,0:T(8,128)(2,1)S(1)}, u32[]{:S(2)}, u32[]{:S(2)}) %all-to-all-start) | async-done | bytes 360480 | tf_op jit(solution)/shard_map/all_to_all | solution.py:285
  20.4 3.7 %all-to-all-start.1 = ((bf16[8,32,1024]{2,1,0:T(8,128)(2,1)}), bf16[8,32,1024]{2,1,0:T(8,128)(2,1)S(1)}, u32[]{:S(2)}, u32[]{:S(2)}) async-start(bf16[8,32,1024]{2,1,0:T(8,128)(2,1)} %shard_map.129), calls=%async_computation.1 | async-start | bytes 1048576 | tf_op jit(solution)/shard_map/all_to_all | solution.py:285
  24.1 6.9 %collective-permute-start.2 = (bf16[128,1408]{1,0:T(8,128)(2,1)S(1)}, bf16[128,1408]{1,0:T(8,128)(2,1)S(1)}, u32[]{:S(2)}, u32[]{:S(2)}) collective-permute-start(bf16[128,1408]{1,0:T(8,128)(2,1)S(1)} %bitcast.27), channel_id=1, source_target_pairs={{0,48},{1,49},{2,50},{3,51},{4,52},{5,53},{6,54},{7,55},{8,56},{9,... | collective-permute-start | bytes 1081352 | tf_op jit(solution)/shard_map/ppermute | solution.py:296
  31.0 1.9 collective-permute-start.1
  32.9 4.0 %collective-permute-start = (bf16[128,1408]{1,0:T(8,128)(2,1)S(1)}, bf16[128,1408]{1,0:T(8,128)(2,1)}, u32[]{:S(2)}, u32[]{:S(2)}) collective-permute-start(bf16[128,1408]{1,0:T(8,128)(2,1)S(1)} %bitcast.29), channel_id=1, source_target_pairs={{0,1},{1,0},{2,3},{3,2},{4,5},{5,4},{6,7},{7,6},{8,9},{9,8},{10,11... | collective-permute-start | bytes 1081352 | tf_op jit(solution)/shard_map/ppermute | solution.py:296
  37.7 4.0 %collective-permute-done.1.s1 = bf16[128,1408]{1,0:T(8,128)(2,1)S(1)} collective-permute-done((bf16[128,1408]{1,0:T(8,128)(2,1)S(1)}, bf16[128,1408]{1,0:T(8,128)(2,1)S(1)}, u32[]{:S(2)}, u32[]{:S(2)}) %collective-permute-start.1) | collective-permute-done | bytes 360480 | tf_op jit(solution)/shard_map/ppermute | solution.py:296
  42.4 1.0 collective-permute-done.t0
  43.5 1.4 shard_map.130
  44.8 1.0 copy-done.4
  45.9 4.7 %all-to-all-start.2 = ((bf16[8,80,896]{2,1,0:T(8,128)(2,1)}), bf16[8,80,896]{2,1,0:T(8,128)(2,1)S(1)}, u32[]{:S(2)}, u32[]{:S(2)}) async-start(bf16[8,80,896]{2,1,0:T(8,128)(2,1)} %copy-done.4), calls=%async_computation.2 | async-start | bytes 2293760 | tf_op jit(solution)/shard_map/all_to_all | solution.py:285
  50.5 4.6 %collective-permute-start.5 = (bf16[128,1408]{1,0:T(8,128)(2,1)}, bf16[128,1408]{1,0:T(8,128)(2,1)}, u32[]{:S(2)}, u32[]{:S(2)}) collective-permute-start(bf16[128,1408]{1,0:T(8,128)(2,1)} %collective-permute-done.t0), channel_id=1, source_target_pairs={{0,48},{1,49},{2,50},{3,51},{4,52},{5,53},{6,54},{7,55},{8,56},{9,... | collective-permute-start | bytes 1081352 | tf_op jit(solution)/shard_map/ppermute | solution.py:296
  55.1 1.9 collective-permute-start.3
  57.0 2.2 collective-permute-start.4
  59.2 11.9 %collective-permute-done.5.t3 = bf16[128,1408]{1,0:T(8,128)(2,1)} collective-permute-done((bf16[128,1408]{1,0:T(8,128)(2,1)}, bf16[128,1408]{1,0:T(8,128)(2,1)}, u32[]{:S(2)}, u32[]{:S(2)}) %collective-permute-start.5) | collective-permute-done | bytes 360480 | tf_op jit(solution)/shard_map/ppermute | solution.py:296
  71.1 5.3 %collective-permute-start.6 = (bf16[128,1408]{1,0:T(8,128)(2,1)}, bf16[128,1408]{1,0:T(8,128)(2,1)}, u32[]{:S(2)}, u32[]{:S(2)}) collective-permute-start(bf16[128,1408]{1,0:T(8,128)(2,1)} %collective-permute-done.5.t3), channel_id=1, source_target_pairs={{0,48},{1,49},{2,50},{3,51},{4,52},{5,53},{6,54},{7,55},{8,56},{9,... | collective-permute-start | bytes 1081352 | tf_op jit(solution)/shard_map/ppermute | solution.py:296
  77.2 4.3 %collective-permute-done.4.s2 = bf16[128,1408]{1,0:T(8,128)(2,1)} collective-permute-done((bf16[128,1408]{1,0:T(8,128)(2,1)}, bf16[128,1408]{1,0:T(8,128)(2,1)}, u32[]{:S(2)}, u32[]{:S(2)}) %collective-permute-start.4) | collective-permute-done | bytes 360480 | tf_op jit(solution)/shard_map/ppermute | solution.py:296
  81.5 1.2 collective-permute-done.6.t2
  82.6 1.2 copy-done.2
  85.8 4.5 %shard_map.131 = (bf16[640,448]{1,0:T(8,128)(2,1)S(1)}, bf16[80,3072]{1,0:T(8,128)(2,1)S(1)}, bf16[240,3072]{1,0:T(8,128)(2,1)S(1)}, bf16[80,3072]{1,0:T(8,128)(...) custom-call(s32[5]{0:T(128)S(1)} %stack.27.who_ref.refs_0_, ...), custom_call_target="tpu_custom_call" | custom-call | tf_op jit(solution)/shard_map/pallas_call | solution.py:342
  90.3 4.6 %collective-permute-start.8 = (bf16[80,3072]{1,0:T(8,128)(2,1)S(1)}, bf16[80,3072]{1,0:T(8,128)(2,1)S(1)}, u32[]{:S(2)}, u32[]{:S(2)}) collective-permute-start(bf16[80,3072]{1,0:T(8,128)(2,1)S(1)} %get-tuple-element.32), channel_id=1, source_target_pairs={{0,64},{64,0},{128,192},{192,128},{256,320},{320,256},{384,448},{4... | collective-permute-start | bytes 1474568 | tf_op jit(solution)/shard_map/ppermute | solution.py:249
  94.9 1.9 collective-permute-start.7
  97.0 5.8 %collective-permute-start.9 = (bf16[40,3072]{1,0:T(8,128)(2,1)S(1)}, bf16[40,3072]{1,0:T(8,128)(2,1)S(1)}, u32[]{:S(2)}, u32[]{:S(2)}) collective-permute-start(bf16[40,3072]{1,0:T(8,128)(2,1)S(1)} %get-tuple-element.41), channel_id=1, source_target_pairs={{0,128},{64,192},{128,256},{192,320},{256,384},{320,448},{384,0},{... | collective-permute-start | bytes 737288 | tf_op jit(solution)/shard_map/ppermute | solution.py:253
  102.8 5.9 %collective-permute-start.11 = (bf16[40,3072]{1,0:T(8,128)(2,1)S(1)}, bf16[40,3072]{1,0:T(8,128)(2,1)S(1)}, u32[]{:S(2)}, u32[]{:S(2)}) collective-permute-start(bf16[40,3072]{1,0:T(8,128)(2,1)S(1)} %get-tuple-element.40), channel_id=1, source_target_pairs={{0,384},{64,448},{128,0},{192,64},{256,128},{320,192},{384,256},{4... | collective-permute-start | bytes 737288 | tf_op jit(solution)/shard_map/ppermute | solution.py:253
  108.7 4.8 %collective-permute-done.9.arrived_ref = bf16[40,3072]{1,0:T(8,128)(2,1)S(1)} collective-permute-done((bf16[40,3072]{1,0:T(8,128)(2,1)S(1)}, bf16[40,3072]{1,0:T(8,128)(2,1)S(1)}, u32[]{:S(2)}, u32[]{:S(2)}) %collective-permute-start.9) | collective-permute-done | bytes 245792 | tf_op jit(solution)/shard_map/ppermute | solution.py:253
  113.7 5.3 %collective-permute-start.10 = (bf16[80,3072]{1,0:T(8,128)(2,1)S(1)}, bf16[80,3072]{1,0:T(8,128)(2,1)S(1)}, u32[]{:S(2)}, u32[]{:S(2)}) collective-permute-start(bf16[80,3072]{1,0:T(8,128)(2,1)S(1)} %shard_map.132), channel_id=1, source_target_pairs={{0,128},{64,192},{128,256},{192,320},{256,384},{320,448},{384,0},{... | collective-permute-start | bytes 1474568 | tf_op jit(solution)/shard_map/ppermute | solution.py:253
  119.0 1.0 collective-permute-done.11.arrived_ref
  120.2 5.1 %collective-permute-start.12 = (bf16[80,3072]{1,0:T(8,128)(2,1)S(1)}, bf16[80,3072]{1,0:T(8,128)(2,1)S(1)}, u32[]{:S(2)}, u32[]{:S(2)}) collective-permute-start(bf16[80,3072]{1,0:T(8,128)(2,1)S(1)} %shard_map.133), channel_id=1, source_target_pairs={{0,384},{64,448},{128,0},{192,64},{256,128},{320,192},{384,256},{4... | collective-permute-start | bytes 1474568 | tf_op jit(solution)/shard_map/ppermute | solution.py:253
  125.3 13.1 %collective-permute-done.10.left_ref = bf16[80,3072]{1,0:T(8,128)(2,1)S(1)} collective-permute-done((bf16[80,3072]{1,0:T(8,128)(2,1)S(1)}, bf16[80,3072]{1,0:T(8,128)(2,1)S(1)}, u32[]{:S(2)}, u32[]{:S(2)}) %collective-permute-start.10) | collective-permute-done | bytes 491552 | tf_op jit(solution)/shard_map/ppermute | solution.py:253
  138.4 9.1 %collective-permute-done.12.right_ref = bf16[80,3072]{1,0:T(8,128)(2,1)S(1)} collective-permute-done((bf16[80,3072]{1,0:T(8,128)(2,1)S(1)}, bf16[80,3072]{1,0:T(8,128)(2,1)S(1)}, u32[]{:S(2)}, u32[]{:S(2)}) %collective-permute-start.12) | collective-permute-done | bytes 491552 | tf_op jit(solution)/shard_map/ppermute | solution.py:253
  148.0 5.0 %collective-permute-start.14 = (bf16[80,3072]{1,0:T(8,128)(2,1)S(1)}, bf16[80,3072]{1,0:T(8,128)(2,1)S(1)}, u32[]{:S(2)}, u32[]{:S(2)}) collective-permute-start(bf16[80,3072]{1,0:T(8,128)(2,1)S(1)} %shard_map.134), channel_id=1, source_target_pairs={{0,128},{64,192},{128,256},{192,320},{256,384},{320,448},{384,0},{... | collective-permute-start | bytes 1474568 | tf_op jit(solution)/shard_map/ppermute | solution.py:253
  152.9 2.4 collective-permute-start.13
  155.4 15.6 %collective-permute-done.14 = bf16[80,3072]{1,0:T(8,128)(2,1)S(1)} collective-permute-done((bf16[80,3072]{1,0:T(8,128)(2,1)S(1)}, bf16[80,3072]{1,0:T(8,128)(2,1)S(1)}, u32[]{:S(2)}, u32[]{:S(2)}) %collective-permute-start.14) | collective-permute-done | bytes 491552 | tf_op jit(solution)/shard_map/ppermute | solution.py:253
  171.1 4.0 %collective-permute-start.15 = (bf16[40,3072]{1,0:T(8,128)(2,1)S(1)}, bf16[40,3072]{1,0:T(8,128)(2,1)S(1)}, u32[]{:S(2)}, u32[]{:S(2)}) collective-permute-start(bf16[40,3072]{1,0:T(8,128)(2,1)S(1)} %slice.26), channel_id=1, source_target_pairs={{0,128},{64,192},{128,256},{192,320},{256,384},{320,448},{384,0},{... | collective-permute-start | bytes 737288 | tf_op jit(solution)/shard_map/ppermute | solution.py:253
  175.1 4.0 %collective-permute-start.16 = (bf16[40,3072]{1,0:T(8,128)(2,1)S(1)}, bf16[40,3072]{1,0:T(8,128)(2,1)S(1)}, u32[]{:S(2)}, u32[]{:S(2)}) collective-permute-start(bf16[40,3072]{1,0:T(8,128)(2,1)S(1)} %slice.27), channel_id=1, source_target_pairs={{0,384},{64,448},{128,0},{192,64},{256,128},{320,192},{384,256},{4... | collective-permute-start | bytes 737288 | tf_op jit(solution)/shard_map/ppermute | solution.py:253
  179.2 4.3 %collective-permute-done.15 = bf16[40,3072]{1,0:T(8,128)(2,1)S(1)} collective-permute-done((bf16[40,3072]{1,0:T(8,128)(2,1)S(1)}, bf16[40,3072]{1,0:T(8,128)(2,1)S(1)}, u32[]{:S(2)}, u32[]{:S(2)}) %collective-permute-start.15) | collective-permute-done | bytes 245792 | tf_op jit(solution)/shard_map/ppermute | solution.py:253
  183.5 4.8 %collective-permute-done.16 = bf16[40,3072]{1,0:T(8,128)(2,1)S(1)} collective-permute-done((bf16[40,3072]{1,0:T(8,128)(2,1)S(1)}, bf16[40,3072]{1,0:T(8,128)(2,1)S(1)}, u32[]{:S(2)}, u32[]{:S(2)}) %collective-permute-start.16) | collective-permute-done | bytes 245792 | tf_op jit(solution)/shard_map/ppermute | solution.py:253
  188.3 3.3 %collective-permute-start.17 = (bf16[320,3072]{1,0:T(8,128)(2,1)S(1)}, bf16[320,3072]{1,0:T(8,128)(2,1)S(1)}, u32[]{:S(2)}, u32[]{:S(2)}) collective-permute-start(bf16[320,3072]{1,0:T(8,128)(2,1)S(1)} %constant_dynamic-update-slice_fusion.refs_1_), channel_id=1, source_target_pairs={{0,64},{64,0},{128,192},{192,128},{256,320},{320,256},{384,448},{4... | collective-permute-start | bytes 5898248 | tf_op jit(solution)/shard_map/ppermute | solution.py:249
  191.6 3.6 %collective-permute-done.17.refs_2_ = bf16[320,3072]{1,0:T(8,128)(2,1)S(1)} collective-permute-done((bf16[320,3072]{1,0:T(8,128)(2,1)S(1)}, bf16[320,3072]{1,0:T(8,128)(2,1)S(1)}, u32[]{:S(2)}, u32[]{:S(2)}) %collective-permute-start.17) | collective-permute-done | bytes 1966112 | tf_op jit(solution)/shard_map/ppermute | solution.py:249
  195.2 3.2 %shard_map.135 = (bf16[8,80,896]{2,1,0:T(8,128)(2,1)S(1)}, bf16[640,2048]{1,0:T(8,128)(2,1)S(1)}) custom-call(s32[5]{0:T(128)S(1)} %stack.27.who_ref.refs_0_, bf16[320,3072]{1,0:T(8,128)(2,1)S(1)} %constant_dynamic-update-slice_fusion.refs_1_, bf16[320,3072]{1,0:T(8,128)(2,1)S(1)} %collective-permute-done.17.refs_2_, bf16[448,1024]{1,0:T(8,128)(2,1)S(1)} %bitcast.22, ...), custom_call_target="tpu_custom_call" | custom-call | tf_op jit(solution)/shard_map/pallas_call | solution.py:373
  198.4 1.5 copy-done.12
  199.9 22.4 %all_to_all.36.recv_ref = bf16[8,80,896]{2,1,0:T(8,128)(2,1)S(1)} all-to-all(bf16[8,80,896]{2,1,0:T(8,128)(2,1)S(1)} %get-tuple-element.34), channel_id=1, replica_groups={{0,1,16,17,32,33,48,49},{2,3,18,19,34,35,50,51},{4,5,20,21,36,37,52,53}..., dimensions={0} | all-to-all | bytes 2293760 | tf_op jit(solution)/shard_map/all_to_all | solution.py:285
  222.3 1.7 shard_map.136
  224.0 7.3 %all-to-all-start.4 = ((bf16[8,32,896]{2,1,0:T(8,128)(2,1)}), bf16[8,32,896]{2,1,0:T(8,128)(2,1)S(1)}, u32[]{:S(2)}, u32[]{:S(2)}) async-start(bf16[8,32,896]{2,1,0:T(8,128)(2,1)} %bitcast.12), calls=%async_computation.4 | async-start | bytes 917504 | tf_op jit(solution)/shard_map/all_to_all | solution.py:285
  231.3 3.3 %fusion.1 = bf16[1,448,1024]{2,1,0:T(8,128)(2,1)} fusion(bf16[640,448]{1,0:T(8,128)(2,1)S(1)} %copy-done.15, bf16[640,2048]{1,0:T(8,128)(2,1)} %copy-done.12), kind=kOutput, calls=%fused_computation.3 | convolution fusion | flops 587661312 | bytes 2801664 | tf_op jit(solution)/shard_map/dot_general | solution.py:22
  234.6 1.8 fusion
  236.4 9.0 %all-to-all-done.4.recv_ref = bf16[8,32,896]{2,1,0:T(8,128)(2,1)S(1)} async-done(((bf16[8,32,896]{2,1,0:T(8,128)(2,1)}), bf16[8,32,896]{2,1,0:T(8,128)(2,1)S(1)}, u32[]{:S(2)}, u32[]{:S(2)}) %all-to-all-start.4) | async-done | bytes 458784 | tf_op jit(solution)/shard_map/all_to_all | solution.py:285
  (56 shorter events, 10.3 us)
Async XLA Ops:
  0.6 42.8 %copy-start.9 = (f32[80,256]{1,0:T(8,128)S(1)}, f32[80,256]{1,0:T(8,128)}, u32[]{:S(2)}) copy-start(f32[80,256]{1,0:T(8,128)} %constant.53.clone.want_ref) | copy-start | bytes 245764
  2.4 18.0 %all-to-all-start = ((bf16[8,16,1408]{2,1,0:T(8,128)(2,1)}), bf16[8,16,1408]{2,1,0:T(8,128)(2,1)S(1)}, u32[]{:S(2)}, u32[]{:S(2)}) async-start(bf16[8,16,1408]{2,1,0:T(8,128)(2,1)} %broadcast_in_dim.9), calls=%async_computation | async-start | bytes 720896 | tf_op jit(solution)/shard_map/all_to_all | solution.py:285
  11.6 0.8 copy-start.10
  12.3 0.8 copy-start.11
  20.4 62.2 %copy-start = (bf16[1,448,1024]{2,1,0:T(8,128)(2,1)S(1)}, bf16[1,448,1024]{2,1,0:T(8,128)(2,1)}, u32[]{:S(2)}) copy-start(bf16[1,448,1024]{2,1,0:T(8,128)(2,1)} %param.15) | copy-start | bytes 2752516
  20.4 62.2 %copy-start.1 = (bf16[1,448,1024]{2,1,0:T(8,128)(2,1)S(1)}, bf16[1,448,1024]{2,1,0:T(8,128)(2,1)}, u32[]{:S(2)}) copy-start(bf16[1,448,1024]{2,1,0:T(8,128)(2,1)} %param.16) | copy-start | bytes 2752516
  20.4 23.0 %all-to-all-start.1 = ((bf16[8,32,1024]{2,1,0:T(8,128)(2,1)}), bf16[8,32,1024]{2,1,0:T(8,128)(2,1)S(1)}, u32[]{:S(2)}, u32[]{:S(2)}) async-start(bf16[8,32,1024]{2,1,0:T(8,128)(2,1)} %shard_map.129), calls=%async_computation.1 | async-start | bytes 1048576 | tf_op jit(solution)/shard_map/all_to_all | solution.py:285
  24.1 12.8 %collective-permute-start.2 = (bf16[128,1408]{1,0:T(8,128)(2,1)S(1)}, bf16[128,1408]{1,0:T(8,128)(2,1)S(1)}, u32[]{:S(2)}, u32[]{:S(2)}) collective-permute-start(bf16[128,1408]{1,0:T(8,128)(2,1)S(1)} %bitcast.27), channel_id=1, source_target_pairs={{0,48},{1,49},{2,50},{3,51},{4,52},{5,53},{6,54},{7,55},{8,56},{9,... | collective-permute-start | bytes 1081352 | tf_op jit(solution)/shard_map/ppermute | solution.py:296
  31.0 10.7 %collective-permute-start.1 = (bf16[128,1408]{1,0:T(8,128)(2,1)S(1)}, bf16[128,1408]{1,0:T(8,128)(2,1)S(1)}, u32[]{:S(2)}, u32[]{:S(2)}) collective-permute-start(bf16[128,1408]{1,0:T(8,128)(2,1)S(1)} %bitcast.28), channel_id=1, source_target_pairs={{0,16},{1,17},{2,18},{3,19},{4,20},{5,21},{6,22},{7,23},{8,24},{9,... | collective-permute-start | bytes 1081352 | tf_op jit(solution)/shard_map/ppermute | solution.py:296
  32.9 10.5 %collective-permute-start = (bf16[128,1408]{1,0:T(8,128)(2,1)S(1)}, bf16[128,1408]{1,0:T(8,128)(2,1)}, u32[]{:S(2)}, u32[]{:S(2)}) collective-permute-start(bf16[128,1408]{1,0:T(8,128)(2,1)S(1)} %bitcast.29), channel_id=1, source_target_pairs={{0,1},{1,0},{2,3},{3,2},{4,5},{5,4},{6,7},{7,6},{8,9},{9,8},{10,11... | collective-permute-start | bytes 1081352 | tf_op jit(solution)/shard_map/ppermute | solution.py:296
  36.9 0.7 copy-start.5
  41.7 0.7 copy-start.7
  44.8 1.0 copy-start.4
  45.9 36.8 %all-to-all-start.2 = ((bf16[8,80,896]{2,1,0:T(8,128)(2,1)}), bf16[8,80,896]{2,1,0:T(8,128)(2,1)S(1)}, u32[]{:S(2)}, u32[]{:S(2)}) async-start(bf16[8,80,896]{2,1,0:T(8,128)(2,1)} %copy-done.4), calls=%async_computation.2 | async-start | bytes 2293760 | tf_op jit(solution)/shard_map/all_to_all | solution.py:285
  50.5 20.5 %collective-permute-start.5 = (bf16[128,1408]{1,0:T(8,128)(2,1)}, bf16[128,1408]{1,0:T(8,128)(2,1)}, u32[]{:S(2)}, u32[]{:S(2)}) collective-permute-start(bf16[128,1408]{1,0:T(8,128)(2,1)} %collective-permute-done.t0), channel_id=1, source_target_pairs={{0,48},{1,49},{2,50},{3,51},{4,52},{5,53},{6,54},{7,55},{8,56},{9,... | collective-permute-start | bytes 1081352 | tf_op jit(solution)/shard_map/ppermute | solution.py:296
  55.1 26.4 %collective-permute-start.3 = (bf16[128,1408]{1,0:T(8,128)(2,1)}, bf16[128,1408]{1,0:T(8,128)(2,1)}, u32[]{:S(2)}, u32[]{:S(2)}) collective-permute-start(bf16[128,1408]{1,0:T(8,128)(2,1)} %collective-permute-done.t0), channel_id=1, source_target_pairs={{0,16},{1,17},{2,18},{3,19},{4,20},{5,21},{6,22},{7,23},{8,24},{9,... | collective-permute-start | bytes 1081352 | tf_op jit(solution)/shard_map/ppermute | solution.py:296
  57.0 24.4 %collective-permute-start.4 = (bf16[128,1408]{1,0:T(8,128)(2,1)}, bf16[128,1408]{1,0:T(8,128)(2,1)}, u32[]{:S(2)}, u32[]{:S(2)}) collective-permute-start(bf16[128,1408]{1,0:T(8,128)(2,1)} %copy-done.7), channel_id=1, source_target_pairs={{0,16},{1,17},{2,18},{3,19},{4,20},{5,21},{6,22},{7,23},{8,24},{9,... | collective-permute-start | bytes 1081352 | tf_op jit(solution)/shard_map/ppermute | solution.py:296
  71.1 11.6 %collective-permute-start.6 = (bf16[128,1408]{1,0:T(8,128)(2,1)}, bf16[128,1408]{1,0:T(8,128)(2,1)}, u32[]{:S(2)}, u32[]{:S(2)}) collective-permute-start(bf16[128,1408]{1,0:T(8,128)(2,1)} %collective-permute-done.5.t3), channel_id=1, source_target_pairs={{0,48},{1,49},{2,50},{3,51},{4,52},{5,53},{6,54},{7,55},{8,56},{9,... | collective-permute-start | bytes 1081352 | tf_op jit(solution)/shard_map/ppermute | solution.py:296
  82.6 1.2 copy-start.2
  83.8 1.0 copy-start.6
  84.8 1.0 copy-start.8
  90.3 23.2 %copy-start.14 = (bf16[640,448]{1,0:T(8,128)(2,1)}, bf16[640,448]{1,0:T(8,128)(2,1)S(1)}, u32[]{:S(2)}) copy-start(bf16[640,448]{1,0:T(8,128)(2,1)S(1)} %get-tuple-element.38) | copy-start | bytes 1720324
  90.3 6.5 %collective-permute-start.8 = (bf16[80,3072]{1,0:T(8,128)(2,1)S(1)}, bf16[80,3072]{1,0:T(8,128)(2,1)S(1)}, u32[]{:S(2)}, u32[]{:S(2)}) collective-permute-start(bf16[80,3072]{1,0:T(8,128)(2,1)S(1)} %get-tuple-element.32), channel_id=1, source_target_pairs={{0,64},{64,0},{128,192},{192,128},{256,320},{320,256},{384,448},{4... | collective-permute-start | bytes 1474568 | tf_op jit(solution)/shard_map/ppermute | solution.py:249
  94.9 18.6 %collective-permute-start.7 = (bf16[240,3072]{1,0:T(8,128)(2,1)S(1)}, bf16[240,3072]{1,0:T(8,128)(2,1)S(1)}, u32[]{:S(2)}, u32[]{:S(2)}) collective-permute-start(bf16[240,3072]{1,0:T(8,128)(2,1)S(1)} %get-tuple-element.30), channel_id=1, source_target_pairs={{0,64},{64,0},{128,192},{192,128},{256,320},{320,256},{384,448},{4... | collective-permute-start | bytes 4423688 | tf_op jit(solution)/shard_map/ppermute | solution.py:249
  97.0 16.4 %collective-permute-start.9 = (bf16[40,3072]{1,0:T(8,128)(2,1)S(1)}, bf16[40,3072]{1,0:T(8,128)(2,1)S(1)}, u32[]{:S(2)}, u32[]{:S(2)}) collective-permute-start(bf16[40,3072]{1,0:T(8,128)(2,1)S(1)} %get-tuple-element.41), channel_id=1, source_target_pairs={{0,128},{64,192},{128,256},{192,320},{256,384},{320,448},{384,0},{... | collective-permute-start | bytes 737288 | tf_op jit(solution)/shard_map/ppermute | solution.py:253
  102.8 17.2 %collective-permute-start.11 = (bf16[40,3072]{1,0:T(8,128)(2,1)S(1)}, bf16[40,3072]{1,0:T(8,128)(2,1)S(1)}, u32[]{:S(2)}, u32[]{:S(2)}) collective-permute-start(bf16[40,3072]{1,0:T(8,128)(2,1)S(1)} %get-tuple-element.40), channel_id=1, source_target_pairs={{0,384},{64,448},{128,0},{192,64},{256,128},{320,192},{384,256},{4... | collective-permute-start | bytes 737288 | tf_op jit(solution)/shard_map/ppermute | solution.py:253
  113.7 24.8 %collective-permute-start.10 = (bf16[80,3072]{1,0:T(8,128)(2,1)S(1)}, bf16[80,3072]{1,0:T(8,128)(2,1)S(1)}, u32[]{:S(2)}, u32[]{:S(2)}) collective-permute-start(bf16[80,3072]{1,0:T(8,128)(2,1)S(1)} %shard_map.132), channel_id=1, source_target_pairs={{0,128},{64,192},{128,256},{192,320},{256,384},{320,448},{384,0},{... | collective-permute-start | bytes 1474568 | tf_op jit(solution)/shard_map/ppermute | solution.py:253
  120.2 27.4 %collective-permute-start.12 = (bf16[80,3072]{1,0:T(8,128)(2,1)S(1)}, bf16[80,3072]{1,0:T(8,128)(2,1)S(1)}, u32[]{:S(2)}, u32[]{:S(2)}) collective-permute-start(bf16[80,3072]{1,0:T(8,128)(2,1)S(1)} %shard_map.133), channel_id=1, source_target_pairs={{0,384},{64,448},{128,0},{192,64},{256,128},{320,192},{384,256},{4... | collective-permute-start | bytes 1474568 | tf_op jit(solution)/shard_map/ppermute | solution.py:253
  148.0 23.1 %collective-permute-start.14 = (bf16[80,3072]{1,0:T(8,128)(2,1)S(1)}, bf16[80,3072]{1,0:T(8,128)(2,1)S(1)}, u32[]{:S(2)}, u32[]{:S(2)}) collective-permute-start(bf16[80,3072]{1,0:T(8,128)(2,1)S(1)} %shard_map.134), channel_id=1, source_target_pairs={{0,128},{64,192},{128,256},{192,320},{256,384},{320,448},{384,0},{... | collective-permute-start | bytes 1474568 | tf_op jit(solution)/shard_map/ppermute | solution.py:253
  152.9 22.1 %collective-permute-start.13 = (bf16[80,3072]{1,0:T(8,128)(2,1)S(1)}, bf16[80,3072]{1,0:T(8,128)(2,1)S(1)}, u32[]{:S(2)}, u32[]{:S(2)}) collective-permute-start(bf16[80,3072]{1,0:T(8,128)(2,1)S(1)} %shard_map.134), channel_id=1, source_target_pairs={{0,384},{64,448},{128,0},{192,64},{256,128},{320,192},{384,256},{4... | collective-permute-start | bytes 1474568 | tf_op jit(solution)/shard_map/ppermute | solution.py:253
  155.4 39.8 %copy-start.3 = (bf16[1,1024,448]{1,2,0:T(8,128)(2,1)S(1)}, bf16[1,1024,448]{1,2,0:T(8,128)(2,1)}, u32[]{:S(2)}) copy-start(bf16[1,1024,448]{1,2,0:T(8,128)(2,1)} %param.17) | copy-start | bytes 2752516
  171.1 12.4 %collective-permute-start.15 = (bf16[40,3072]{1,0:T(8,128)(2,1)S(1)}, bf16[40,3072]{1,0:T(8,128)(2,1)S(1)}, u32[]{:S(2)}, u32[]{:S(2)}) collective-permute-start(bf16[40,3072]{1,0:T(8,128)(2,1)S(1)} %slice.26), channel_id=1, source_target_pairs={{0,128},{64,192},{128,256},{192,320},{256,384},{320,448},{384,0},{... | collective-permute-start | bytes 737288 | tf_op jit(solution)/shard_map/ppermute | solution.py:253
  175.1 13.1 %collective-permute-start.16 = (bf16[40,3072]{1,0:T(8,128)(2,1)S(1)}, bf16[40,3072]{1,0:T(8,128)(2,1)S(1)}, u32[]{:S(2)}, u32[]{:S(2)}) collective-permute-start(bf16[40,3072]{1,0:T(8,128)(2,1)S(1)} %slice.27), channel_id=1, source_target_pairs={{0,384},{64,448},{128,0},{192,64},{256,128},{320,192},{384,256},{4... | collective-permute-start | bytes 737288 | tf_op jit(solution)/shard_map/ppermute | solution.py:253
  188.3 6.9 %collective-permute-start.17 = (bf16[320,3072]{1,0:T(8,128)(2,1)S(1)}, bf16[320,3072]{1,0:T(8,128)(2,1)S(1)}, u32[]{:S(2)}, u32[]{:S(2)}) collective-permute-start(bf16[320,3072]{1,0:T(8,128)(2,1)S(1)} %constant_dynamic-update-slice_fusion.refs_1_), channel_id=1, source_target_pairs={{0,64},{64,0},{128,192},{192,128},{256,320},{320,256},{384,448},{4... | collective-permute-start | bytes 5898248 | tf_op jit(solution)/shard_map/ppermute | solution.py:249
  198.4 1.5 copy-start.12
  199.9 31.4 %copy-start.15 = (bf16[640,448]{1,0:T(8,128)(2,1)S(1)}, bf16[640,448]{1,0:T(8,128)(2,1)}, u32[]{:S(2)}) copy-start(bf16[640,448]{1,0:T(8,128)(2,1)} %copy-done.14) | copy-start | bytes 1720324
  224.0 21.5 %all-to-all-start.4 = ((bf16[8,32,896]{2,1,0:T(8,128)(2,1)}), bf16[8,32,896]{2,1,0:T(8,128)(2,1)S(1)}, u32[]{:S(2)}, u32[]{:S(2)}) async-start(bf16[8,32,896]{2,1,0:T(8,128)(2,1)} %bitcast.12), calls=%async_computation.4 | async-start | bytes 917504 | tf_op jit(solution)/shard_map/all_to_all | solution.py:285
  231.3 3.3 %copy-start.13 = (bf16[640,2048]{1,0:T(8,128)(2,1)S(1)}, bf16[640,2048]{1,0:T(8,128)(2,1)}, u32[]{:S(2)}) copy-start(bf16[640,2048]{1,0:T(8,128)(2,1)} %copy-done.12) | copy-start | bytes 7864324

commit v13 on v9

--- a/solution.py
+++ b/solution.py
@@ -177,36 +177,35 @@
             out_ref[:, at] = value.astype(BF)
 
 
-def back_kernel(*refs):
-    who_ref, parts = refs[0], refs[1:3]
-    gate_ref, up_ref, down_ref, restored_ref, out_ref, grads_ref, hidden_ref, y_ref, dx_ref = refs[3:]
-    feat, ff = gate_ref.shape
+def back_kernel(who_ref, part_ref, gate_ref, up_ref, down_ref, restored_ref, y_ref, dx_ref):
+    ff = gate_ref.shape[1]
+
+    @pl.when(who_ref[0] == 0)
+    def _():
+        y_ref[...] = dot(part_ref[:, 0:ff], down_ref[...], NT).astype(BF)
+        dx = dot(part_ref[:, ff : 2 * ff], gate_ref[...], NT)
+        dx_ref[...] = (dx + dot(part_ref[:, 2 * ff : 3 * ff], up_ref[...], NT)).astype(BF)
+
+    @pl.when(who_ref[0] == 1)
+    def _():
+        y_ref[...] = dot(part_ref[:, 0:ff], restored_ref[2]).astype(BF)
+        dx = dot(part_ref[:, ff : 2 * ff], restored_ref[0])
+        dx_ref[...] = (dx + dot(part_ref[:, 2 * ff : 3 * ff], restored_ref[1])).astype(BF)
+
+
+def last_back_kernel(
+    who_ref, part_ref, gate_ref, up_ref, down_ref, restored_ref, own_y_ref, own_dx_ref,
+    out_ref, y_ref, dx_ref,
+):
+    feat = gate_ref.shape[0]
     chunk = out_ref.shape[1]
-    target, h, c = who_ref[0], who_ref[1], who_ref[2]
-    for k, part in enumerate(parts):
-        span = slice(4 * chunk * k, 4 * chunk * (k + 1))
-        hidden_ref[span, :] = part[:, 0:ff]
-        grads_ref[span, :] = part[:, ff : 3 * ff]
-
-    @pl.when(target == 0)
-    def _():
-        y_ref[...] = dot(hidden_ref[...], down_ref[...], NT).astype(BF)
-        dx_ref[...] = (
-            dot(grads_ref[:, 0:ff], gate_ref[...], NT) + dot(grads_ref[:, ff : 2 * ff], up_ref[...], NT)
-        ).astype(BF)
-
-    @pl.when(target == 1)
-    def _():
-        y_ref[...] = dot(hidden_ref[...], restored_ref[2]).astype(BF)
-        dx_ref[...] = (
-            dot(grads_ref[:, 0:ff], restored_ref[0]) + dot(grads_ref[:, ff : 2 * ff], restored_ref[1])
-        ).astype(BF)
-
+    back_kernel(who_ref, part_ref, gate_ref, up_ref, down_ref, restored_ref, y_ref, dx_ref)
     for p in range(8):
-        g = chunk_at(h, c, p)
-        span = slice(p * chunk, (p + 1) * chunk)
-        out_ref[g, :, 0:feat] = y_ref[span, :]
-        out_ref[g, :, feat : 2 * feat] = dx_ref[span, :]
+        g = chunk_at(who_ref[1], who_ref[2], p)
+        y, dx = (own_y_ref, own_dx_ref) if p < 4 else (y_ref, dx_ref)
+        span = slice(p % 4 * chunk, (p % 4 + 1) * chunk)
+        out_ref[g, :, 0:feat] = y[span, :]
+        out_ref[g, :, feat : 2 * feat] = dx[span, :]
 
 
 def combine_kernel(recv_ref, meta_ref, want_ref, out_ref, pick_ref, share_ref):
@@ -355,22 +354,23 @@
     mine = jnp.concatenate([own, right, left, *far], axis=0)
     other = core_swap(mine)
 
-    out, grads = call(
-        back_kernel,
-        [(8, chunk, 2 * feat), (8 * chunk, 2 * ff)],
-        scratch=[
-            pltpu.VMEM((8 * chunk, ff), BF),
-            pltpu.VMEM((8 * chunk, feat), BF),
-            pltpu.VMEM((8 * chunk, feat), BF),
-        ],
+    weights = w_gate, w_up, w_down, restored
+    half = (4 * chunk, feat)
+    own_back = call(back_kernel, [half, half], scalars=1, operands=5, megabytes=18)(who, mine, *weights)
+    (out,) = call(
+        last_back_kernel,
+        [(8, chunk, 2 * feat)],
+        scratch=[pltpu.VMEM(half, BF), pltpu.VMEM(half, BF)],
         scalars=1,
-        operands=6,
+        operands=7,
         megabytes=18,
-    )(who, mine, other, w_gate, w_up, w_down, restored)
+    )(who, other, *weights, *own_back)
 
     out = exchange(out.reshape(nxz, out_rows, 2 * feat), along_xz)
-    gate_grad = dot(rows, grads[:, :ff], TN).astype(BF)
-    up_grad = dot(rows, grads[:, ff:], TN).astype(BF)
+    halves = (rows[: 4 * chunk], mine), (rows[4 * chunk :], other)
+    gate_grad, up_grad = (
+        sum(dot(r, d[:, k : k + ff], TN) for r, d in halves).astype(BF) for k in (ff, 2 * ff)
+    )
     (part,) = call(
         combine_kernel,
         [(seen, 2 * feat)],

time: 246 us -> 247 us (level)
  waiting for transfers between devices: 80.1 us -> 75.8 us
  local copies, waits for them, and re-layouts: 12.3 us -> 15.7 us
  blocking collectives: 21.4 us -> 24.1 us
    unnamed x38 -> x52, local copies, waits for them, and re-layouts: 10.3 us -> 13.2 us
    all_to_all x1, blocking collectives: 21.4 us -> 24.1 us  [exchange(): lax.all_to_all(flat, 'expert', 0, 0, axis_index_groups=groups, tiled=True)]
    dot_general x2 -> x4, matrix products: 5.12 us -> 6.68 us  [dot(): return lax.dot_general(a, b, dims, preferred_element_type=F32)]
  transfers between devices with their start and end apart: 22 -> 22, of which waited for: 16 -> 16; matrix products, arithmetic and copies ran while one was open for 3% -> 4% of each run, Pallas kernels for 1% -> 1%
where the time goes in v13:
time: 247 us; the launch traced here: 245 us
  starting transfers between devices  108 us (44%)
  waiting for transfers between devices  75.8 us (31%)
  blocking collectives  24.1 us (10%)
  local copies, waits for them, and re-layouts  15.7 us (6%)
  Pallas kernels  13.1 us (5%)
  matrix products  6.68 us (3%)
    ppermute x8, waiting for transfers between devices, shift(): lax.ppermute(x, 'dp', [(2 * h + c, 2 * ((h + k) % 4) + c) for h in range(...  39.2 us
    ppermute x8, starting transfers between devices, shift(): lax.ppermute(x, 'dp', [(2 * h + c, 2 * ((h + k) % 4) + c) for h in range(...  36 us
    ppermute x7, starting transfers between devices, step(): return lax.ppermute(v, 'expert', pairs)  26.6 us
    all_to_all x1, blocking collectives, exchange(): lax.all_to_all(flat, 'expert', 0, 0, axis_index_groups=groups, tiled=True)  24.1 us
    ppermute x3, starting transfers between devices, core_swap(): return lax.ppermute(x, 'dp', [(i, i ^ 1) for i in range(8)])  23.9 us
    ppermute x7, waiting for transfers between devices, step(): return lax.ppermute(v, 'expert', pairs)  21.3 us
    all_to_all x4, starting transfers between devices, exchange(): lax.all_to_all(flat, 'expert', 0, 0, axis_index_groups=groups, tiled=True)  21 us
    all_to_all x4, waiting for transfers between devices, exchange(): lax.all_to_all(flat, 'expert', 0, 0, axis_index_groups=groups, tiled=True)  13.5 us
  transfers between devices with their start and end apart: 22, of which 16 were waited for; matrix products, arithmetic and copies ran while one was open for 4% of the time, Pallas kernels for 1%

profile of v13, /device:TPU:1, one launch (start us, length us, event | category | flops | bytes accessed | tf_op | source)
XLA Modules:
  0.0 245.2 jit_solution(10602889343578296459)
XLA Ops:
  2.4 7.7 %all-to-all-start = ((bf16[8,16,1408]{2,1,0:T(8,128)(2,1)}), bf16[8,16,1408]{2,1,0:T(8,128)(2,1)S(1)}, u32[]{:S(2)}, u32[]{:S(2)}) async-start(bf16[8,16,1408]{2,1,0:T(8,128)(2,1)} %broadcast_in_dim.9), calls=%async_computation | async-start | bytes 720896 | tf_op jit(solution)/shard_map/all_to_all | solution.py:270
  13.1 1.2 shard_map.129
  14.3 6.1 %all-to-all-done = bf16[8,16,1408]{2,1,0:T(8,128)(2,1)S(1)} async-done(((bf16[8,16,1408]{2,1,0:T(8,128)(2,1)}), bf16[8,16,1408]{2,1,0:T(8,128)(2,1)S(1)}, u32[]{:S(2)}, u32[]{:S(2)}) %all-to-all-start) | async-done | bytes 360480 | tf_op jit(solution)/shard_map/all_to_all | solution.py:270
  21.2 3.8 %all-to-all-start.1 = ((bf16[8,32,1024]{2,1,0:T(8,128)(2,1)}), bf16[8,32,1024]{2,1,0:T(8,128)(2,1)S(1)}, u32[]{:S(2)}, u32[]{:S(2)}) async-start(bf16[8,32,1024]{2,1,0:T(8,128)(2,1)} %shard_map.129), calls=%async_computation.1 | async-start | bytes 1048576 | tf_op jit(solution)/shard_map/all_to_all | solution.py:270
  25.0 6.9 %collective-permute-start.2 = (bf16[128,1408]{1,0:T(8,128)(2,1)}, bf16[128,1408]{1,0:T(8,128)(2,1)S(1)}, u32[]{:S(2)}, u32[]{:S(2)}) collective-permute-start(bf16[128,1408]{1,0:T(8,128)(2,1)} %bitcast.29), channel_id=1, source_target_pairs={{0,48},{1,49},{2,50},{3,51},{4,52},{5,53},{6,54},{7,55},{8,56},{9,... | collective-permute-start | bytes 1081352 | tf_op jit(solution)/shard_map/ppermute | solution.py:281
  31.9 1.9 collective-permute-start.1
  33.8 4.0 %collective-permute-start = (bf16[128,1408]{1,0:T(8,128)(2,1)}, bf16[128,1408]{1,0:T(8,128)(2,1)}, u32[]{:S(2)}, u32[]{:S(2)}) collective-permute-start(bf16[128,1408]{1,0:T(8,128)(2,1)} %bitcast.31), channel_id=1, source_target_pairs={{0,1},{1,0},{2,3},{3,2},{4,5},{5,4},{6,7},{7,6},{8,9},{9,8},{10,11... | collective-permute-start | bytes 1081352 | tf_op jit(solution)/shard_map/ppermute | solution.py:281
  38.6 4.2 %collective-permute-done.1.s1 = bf16[128,1408]{1,0:T(8,128)(2,1)S(1)} collective-permute-done((bf16[128,1408]{1,0:T(8,128)(2,1)}, bf16[128,1408]{1,0:T(8,128)(2,1)S(1)}, u32[]{:S(2)}, u32[]{:S(2)}) %collective-permute-start.1) | collective-permute-done | bytes 360480 | tf_op jit(solution)/shard_map/ppermute | solution.py:281
  43.5 1.0 collective-permute-done.t0
  44.5 1.4 shard_map.130
  45.9 1.0 copy-done.9
  47.6 4.6 %all-to-all-start.2 = ((bf16[8,80,896]{2,1,0:T(8,128)(2,1)}), bf16[8,80,896]{2,1,0:T(8,128)(2,1)}, u32[]{:S(2)}, u32[]{:S(2)}) async-start(bf16[8,80,896]{2,1,0:T(8,128)(2,1)} %copy-done.9), calls=%async_computation.2 | async-start | bytes 2293760 | tf_op jit(solution)/shard_map/all_to_all | solution.py:270
  52.1 4.6 %collective-permute-start.5 = (bf16[128,1408]{1,0:T(8,128)(2,1)}, bf16[128,1408]{1,0:T(8,128)(2,1)S(1)}, u32[]{:S(2)}, u32[]{:S(2)}) collective-permute-start(bf16[128,1408]{1,0:T(8,128)(2,1)} %collective-permute-done.t0), channel_id=1, source_target_pairs={{0,48},{1,49},{2,50},{3,51},{4,52},{5,53},{6,54},{7,55},{8,56},{9,... | collective-permute-start | bytes 1081352 | tf_op jit(solution)/shard_map/ppermute | solution.py:281
  56.7 1.9 collective-permute-start.3
  58.6 2.2 collective-permute-start.4
  60.8 11.9 %collective-permute-done.5.t3 = bf16[128,1408]{1,0:T(8,128)(2,1)S(1)} collective-permute-done((bf16[128,1408]{1,0:T(8,128)(2,1)}, bf16[128,1408]{1,0:T(8,128)(2,1)S(1)}, u32[]{:S(2)}, u32[]{:S(2)}) %collective-permute-start.5) | collective-permute-done | bytes 360480 | tf_op jit(solution)/shard_map/ppermute | solution.py:281
  72.6 5.2 %collective-permute-start.6 = (bf16[128,1408]{1,0:T(8,128)(2,1)S(1)}, bf16[128,1408]{1,0:T(8,128)(2,1)}, u32[]{:S(2)}, u32[]{:S(2)}) collective-permute-start(bf16[128,1408]{1,0:T(8,128)(2,1)S(1)} %collective-permute-done.5.t3), channel_id=1, source_target_pairs={{0,48},{1,49},{2,50},{3,51},{4,52},{5,53},{6,54},{7,55},{8,56},{9,... | collective-permute-start | bytes 1081352 | tf_op jit(solution)/shard_map/ppermute | solution.py:281
  79.9 3.1 %collective-permute-done.4.s2 = bf16[128,1408]{1,0:T(8,128)(2,1)} collective-permute-done((bf16[128,1408]{1,0:T(8,128)(2,1)S(1)}, bf16[128,1408]{1,0:T(8,128)(2,1)}, u32[]{:S(2)}, u32[]{:S(2)}) %collective-permute-start.4) | collective-permute-done | bytes 360480 | tf_op jit(solution)/shard_map/ppermute | solution.py:281
  83.0 1.1 collective-permute-done.6.t2
  88.7 4.7 %shard_map.131 = (bf16[640,448]{1,0:T(8,128)(2,1)S(1)}, bf16[80,3072]{1,0:T(8,128)(2,1)S(1)}, bf16[240,3072]{1,0:T(8,128)(2,1)S(1)}, bf16[80,3072]{1,0:T(8,128)(...) custom-call(s32[5]{0:T(128)S(1)} %copy-done.22, bf16[8,80,896]{2,1,0:T(8,128)(2,1)} %all-to-all-done.2.recv_ref, ...), custom_call_target="tpu_custom_call" | custom-call | tf_op jit(solution)/shard_map/pallas_call | solution.py:327
  93.4 4.5 %collective-permute-start.8 = (bf16[80,3072]{1,0:T(8,128)(2,1)S(1)}, bf16[80,3072]{1,0:T(8,128)(2,1)S(1)}, u32[]{:S(2)}, u32[]{:S(2)}) collective-permute-start(bf16[80,3072]{1,0:T(8,128)(2,1)S(1)} %get-tuple-element.32), channel_id=1, source_target_pairs={{0,64},{64,0},{128,192},{192,128},{256,320},{320,256},{384,448},{4... | collective-permute-start | bytes 1474568 | tf_op jit(solution)/shard_map/ppermute | solution.py:234
  97.9 1.9 collective-permute-start.7
  100.0 9.8 %collective-permute-start.11 = (bf16[40,3072]{1,0:T(8,128)(2,1)S(1)}, bf16[40,3072]{1,0:T(8,128)(2,1)S(1)}, u32[]{:S(2)}, u32[]{:S(2)}) collective-permute-start(bf16[40,3072]{1,0:T(8,128)(2,1)S(1)} %get-tuple-element.44), channel_id=1, source_target_pairs={{0,384},{64,448},{128,0},{192,64},{256,128},{320,192},{384,256},{4... | collective-permute-start | bytes 737288 | tf_op jit(solution)/shard_map/ppermute | solution.py:238
  109.8 1.9 collective-permute-start.9
  112.1 4.9 %collective-permute-done.11 = bf16[40,3072]{1,0:T(8,128)(2,1)S(1)} collective-permute-done((bf16[40,3072]{1,0:T(8,128)(2,1)S(1)}, bf16[40,3072]{1,0:T(8,128)(2,1)S(1)}, u32[]{:S(2)}, u32[]{:S(2)}) %collective-permute-start.11) | collective-permute-done | bytes 245792 | tf_op jit(solution)/shard_map/ppermute | solution.py:238
  117.0 3.9 %collective-permute-done.9 = bf16[40,3072]{1,0:T(8,128)(2,1)S(1)} collective-permute-done((bf16[40,3072]{1,0:T(8,128)(2,1)S(1)}, bf16[40,3072]{1,0:T(8,128)(2,1)S(1)}, u32[]{:S(2)}, u32[]{:S(2)}) %collective-permute-start.9) | collective-permute-done | bytes 245792 | tf_op jit(solution)/shard_map/ppermute | solution.py:238
  121.1 2.2 collective-permute-start.10
  123.3 5.2 %collective-permute-start.12 = (bf16[80,3072]{1,0:T(8,128)(2,1)S(1)}, bf16[80,3072]{1,0:T(8,128)(2,1)S(1)}, u32[]{:S(2)}, u32[]{:S(2)}) collective-permute-start(bf16[80,3072]{1,0:T(8,128)(2,1)S(1)} %pad_maximum_fusion.1), channel_id=1, source_target_pairs={{0,384},{64,448},{128,0},{192,64},{256,128},{320,192},{384,256},{4... | collective-permute-start | bytes 1474568 | tf_op jit(solution)/shard_map/ppermute | solution.py:238
  128.6 4.5 %collective-permute-done.10.left_ref = bf16[80,3072]{1,0:T(8,128)(2,1)S(1)} collective-permute-done((bf16[80,3072]{1,0:T(8,128)(2,1)S(1)}, bf16[80,3072]{1,0:T(8,128)(2,1)S(1)}, u32[]{:S(2)}, u32[]{:S(2)}) %collective-permute-start.10) | collective-permute-done | bytes 491552 | tf_op jit(solution)/shard_map/ppermute | solution.py:238
  133.1 1.3 collective-permute-done.12.right_ref
  134.8 7.5 %collective-permute-start.14 = (bf16[80,3072]{1,0:T(8,128)(2,1)S(1)}, bf16[80,3072]{1,0:T(8,128)(2,1)S(1)}, u32[]{:S(2)}, u32[]{:S(2)}) collective-permute-start(bf16[80,3072]{1,0:T(8,128)(2,1)S(1)} %shard_map.132), channel_id=1, source_target_pairs={{0,128},{64,192},{128,256},{192,320},{256,384},{320,448},{384,0},{... | collective-permute-start | bytes 1474568 | tf_op jit(solution)/shard_map/ppermute | solution.py:238
  142.3 1.9 collective-permute-start.13
  144.3 10.4 %collective-permute-done.14 = bf16[80,3072]{1,0:T(8,128)(2,1)S(1)} collective-permute-done((bf16[80,3072]{1,0:T(8,128)(2,1)S(1)}, bf16[80,3072]{1,0:T(8,128)(2,1)S(1)}, u32[]{:S(2)}, u32[]{:S(2)}) %collective-permute-start.14) | collective-permute-done | bytes 491552 | tf_op jit(solution)/shard_map/ppermute | solution.py:238
  154.7 1.9 collective-permute-start.15
  157.1 5.6 %collective-permute-start.16 = (bf16[40,3072]{1,0:T(8,128)(2,1)S(1)}, bf16[40,3072]{1,0:T(8,128)(2,1)S(1)}, u32[]{:S(2)}, u32[]{:S(2)}) collective-permute-start(bf16[40,3072]{1,0:T(8,128)(2,1)S(1)} %slice.78), channel_id=1, source_target_pairs={{0,384},{64,448},{128,0},{192,64},{256,128},{320,192},{384,256},{4... | collective-permute-start | bytes 737288 | tf_op jit(solution)/shard_map/ppermute | solution.py:238
  162.8 11.3 %collective-permute-done.15 = bf16[40,3072]{1,0:T(8,128)(2,1)S(1)} collective-permute-done((bf16[40,3072]{1,0:T(8,128)(2,1)S(1)}, bf16[40,3072]{1,0:T(8,128)(2,1)S(1)}, u32[]{:S(2)}, u32[]{:S(2)}) %collective-permute-start.15) | collective-permute-done | bytes 245792 | tf_op jit(solution)/shard_map/ppermute | solution.py:238
  174.1 2.4 collective-permute-done.16
  176.5 17.5 %collective-permute-start.17 = (bf16[320,3072]{1,0:T(8,128)(2,1)S(1)}, bf16[320,3072]{1,0:T(8,128)(2,1)S(1)}, u32[]{:S(2)}, u32[]{:S(2)}) collective-permute-start(bf16[320,3072]{1,0:T(8,128)(2,1)S(1)} %constant_dynamic-update-slice_fusion.part_ref), channel_id=1, source_target_pairs={{0,64},{64,0},{128,192},{192,128},{256,320},{320,256},{384,448},{4... | collective-permute-start | bytes 5898248 | tf_op jit(solution)/shard_map/ppermute | solution.py:234
  194.0 1.7 shard_map.133
  195.8 1.8 collective-permute-done.17.part_ref
  197.6 2.0 shard_map.134
  199.6 24.1 %all_to_all.36.recv_ref = bf16[8,80,896]{2,1,0:T(8,128)(2,1)S(1)} all-to-all(bf16[8,80,896]{2,1,0:T(8,128)(2,1)S(1)} %shard_map.134), channel_id=1, replica_groups={{0,1,16,17,32,33,48,49},{2,3,18,19,34,35,50,51},{4,5,20,21,36,37,52,53}..., dimensions={0} | all-to-all | bytes 2293760 | tf_op jit(solution)/shard_map/all_to_all | solution.py:270
  225.4 5.0 %all-to-all-start.4 = ((bf16[8,32,896]{2,1,0:T(8,128)(2,1)}), bf16[8,32,896]{2,1,0:T(8,128)(2,1)S(1)}, u32[]{:S(2)}, u32[]{:S(2)}) async-start(bf16[8,32,896]{2,1,0:T(8,128)(2,1)} %bitcast.28), calls=%async_computation.4 | async-start | bytes 917504 | tf_op jit(solution)/shard_map/all_to_all | solution.py:270
  230.4 1.7 fusion.2
  232.1 1.6 fusion.1
  233.7 1.7 fusion.5
  235.5 1.6 fusion
  237.1 7.4 %all-to-all-done.4.recv_ref = bf16[8,32,896]{2,1,0:T(8,128)(2,1)S(1)} async-done(((bf16[8,32,896]{2,1,0:T(8,128)(2,1)}), bf16[8,32,896]{2,1,0:T(8,128)(2,1)S(1)}, u32[]{:S(2)}, u32[]{:S(2)}) %all-to-all-start.4) | async-done | bytes 458784 | tf_op jit(solution)/shard_map/all_to_all | solution.py:270
  (76 shorter events, 17.8 us)
Async XLA Ops:
  0.6 43.9 %copy-start.17 = (f32[80,256]{1,0:T(8,128)S(1)}, f32[80,256]{1,0:T(8,128)}, u32[]{:S(2)}) copy-start(f32[80,256]{1,0:T(8,128)} %constant.53.clone.want_ref) | copy-start | bytes 245764
  2.4 18.0 %all-to-all-start = ((bf16[8,16,1408]{2,1,0:T(8,128)(2,1)}), bf16[8,16,1408]{2,1,0:T(8,128)(2,1)S(1)}, u32[]{:S(2)}, u32[]{:S(2)}) async-start(bf16[8,16,1408]{2,1,0:T(8,128)(2,1)} %broadcast_in_dim.9), calls=%async_computation | async-start | bytes 720896 | tf_op jit(solution)/shard_map/all_to_all | solution.py:270
  11.6 0.8 copy-start.20
  12.3 0.8 copy-start.21
  20.4 0.7 copy-start.7
  21.1 62.9 %copy-start = (bf16[1,448,1024]{2,1,0:T(8,128)(2,1)S(1)}, bf16[1,448,1024]{2,1,0:T(8,128)(2,1)}, u32[]{:S(2)}) copy-start(bf16[1,448,1024]{2,1,0:T(8,128)(2,1)} %param.15) | copy-start | bytes 2752516
  21.2 62.9 %copy-start.1 = (bf16[1,448,1024]{2,1,0:T(8,128)(2,1)S(1)}, bf16[1,448,1024]{2,1,0:T(8,128)(2,1)}, u32[]{:S(2)}) copy-start(bf16[1,448,1024]{2,1,0:T(8,128)(2,1)} %param.16) | copy-start | bytes 2752516
  21.2 62.9 %copy-start.2 = (bf16[1,1024,448]{1,2,0:T(8,128)(2,1)S(1)}, bf16[1,1024,448]{1,2,0:T(8,128)(2,1)}, u32[]{:S(2)}) copy-start(bf16[1,1024,448]{1,2,0:T(8,128)(2,1)} %param.17) | copy-start | bytes 2752516
  21.2 23.4 %all-to-all-start.1 = ((bf16[8,32,1024]{2,1,0:T(8,128)(2,1)}), bf16[8,32,1024]{2,1,0:T(8,128)(2,1)S(1)}, u32[]{:S(2)}, u32[]{:S(2)}) async-start(bf16[8,32,1024]{2,1,0:T(8,128)(2,1)} %shard_map.129), calls=%async_computation.1 | async-start | bytes 1048576 | tf_op jit(solution)/shard_map/all_to_all | solution.py:270
  25.0 12.9 %collective-permute-start.2 = (bf16[128,1408]{1,0:T(8,128)(2,1)}, bf16[128,1408]{1,0:T(8,128)(2,1)S(1)}, u32[]{:S(2)}, u32[]{:S(2)}) collective-permute-start(bf16[128,1408]{1,0:T(8,128)(2,1)} %bitcast.29), channel_id=1, source_target_pairs={{0,48},{1,49},{2,50},{3,51},{4,52},{5,53},{6,54},{7,55},{8,56},{9,... | collective-permute-start | bytes 1081352 | tf_op jit(solution)/shard_map/ppermute | solution.py:281
  31.9 10.9 %collective-permute-start.1 = (bf16[128,1408]{1,0:T(8,128)(2,1)}, bf16[128,1408]{1,0:T(8,128)(2,1)S(1)}, u32[]{:S(2)}, u32[]{:S(2)}) collective-permute-start(bf16[128,1408]{1,0:T(8,128)(2,1)} %bitcast.30), channel_id=1, source_target_pairs={{0,16},{1,17},{2,18},{3,19},{4,20},{5,21},{6,22},{7,23},{8,24},{9,... | collective-permute-start | bytes 1081352 | tf_op jit(solution)/shard_map/ppermute | solution.py:281
  33.8 10.7 %collective-permute-start = (bf16[128,1408]{1,0:T(8,128)(2,1)}, bf16[128,1408]{1,0:T(8,128)(2,1)}, u32[]{:S(2)}, u32[]{:S(2)}) collective-permute-start(bf16[128,1408]{1,0:T(8,128)(2,1)} %bitcast.31), channel_id=1, source_target_pairs={{0,1},{1,0},{2,3},{3,2},{4,5},{5,4},{6,7},{7,6},{8,9},{9,8},{10,11... | collective-permute-start | bytes 1081352 | tf_op jit(solution)/shard_map/ppermute | solution.py:281
  37.8 0.7 copy-start.10
  42.8 0.7 copy-start.12
  45.9 1.0 copy-start.9
  46.9 0.6 copy-start.18
  46.9 11.7 %copy-start.13 = (bf16[128,1408]{1,0:T(8,128)(2,1)S(1)}, bf16[128,1408]{1,0:T(8,128)(2,1)}, u32[]{:S(2)}) copy-start(bf16[128,1408]{1,0:T(8,128)(2,1)} %copy-done.12) | copy-start | bytes 1081348
  47.6 36.5 %all-to-all-start.2 = ((bf16[8,80,896]{2,1,0:T(8,128)(2,1)}), bf16[8,80,896]{2,1,0:T(8,128)(2,1)}, u32[]{:S(2)}, u32[]{:S(2)}) async-start(bf16[8,80,896]{2,1,0:T(8,128)(2,1)} %copy-done.9), calls=%async_computation.2 | async-start | bytes 2293760 | tf_op jit(solution)/shard_map/all_to_all | solution.py:270
  52.1 20.5 %collective-permute-start.5 = (bf16[128,1408]{1,0:T(8,128)(2,1)}, bf16[128,1408]{1,0:T(8,128)(2,1)S(1)}, u32[]{:S(2)}, u32[]{:S(2)}) collective-permute-start(bf16[128,1408]{1,0:T(8,128)(2,1)} %collective-permute-done.t0), channel_id=1, source_target_pairs={{0,48},{1,49},{2,50},{3,51},{4,52},{5,53},{6,54},{7,55},{8,56},{9,... | collective-permute-start | bytes 1081352 | tf_op jit(solution)/shard_map/ppermute | solution.py:281
  56.7 26.3 %collective-permute-start.3 = (bf16[128,1408]{1,0:T(8,128)(2,1)}, bf16[128,1408]{1,0:T(8,128)(2,1)}, u32[]{:S(2)}, u32[]{:S(2)}) collective-permute-start(bf16[128,1408]{1,0:T(8,128)(2,1)} %collective-permute-done.t0), channel_id=1, source_target_pairs={{0,16},{1,17},{2,18},{3,19},{4,20},{5,21},{6,22},{7,23},{8,24},{9,... | collective-permute-start | bytes 1081352 | tf_op jit(solution)/shard_map/ppermute | solution.py:281
  58.6 24.4 %collective-permute-start.4 = (bf16[128,1408]{1,0:T(8,128)(2,1)S(1)}, bf16[128,1408]{1,0:T(8,128)(2,1)}, u32[]{:S(2)}, u32[]{:S(2)}) collective-permute-start(bf16[128,1408]{1,0:T(8,128)(2,1)S(1)} %copy-done.13), channel_id=1, source_target_pairs={{0,16},{1,17},{2,18},{3,19},{4,20},{5,21},{6,22},{7,23},{8,24},{9,... | collective-permute-start | bytes 1081352 | tf_op jit(solution)/shard_map/ppermute | solution.py:281
  72.6 11.5 %collective-permute-start.6 = (bf16[128,1408]{1,0:T(8,128)(2,1)S(1)}, bf16[128,1408]{1,0:T(8,128)(2,1)}, u32[]{:S(2)}, u32[]{:S(2)}) collective-permute-start(bf16[128,1408]{1,0:T(8,128)(2,1)S(1)} %collective-permute-done.5.t3), channel_id=1, source_target_pairs={{0,48},{1,49},{2,50},{3,51},{4,52},{5,53},{6,54},{7,55},{8,56},{9,... | collective-permute-start | bytes 1081352 | tf_op jit(solution)/shard_map/ppermute | solution.py:281
  77.8 0.7 copy-start.15
  84.1 1.0 copy-start.8
  85.1 1.0 copy-start.11
  86.1 1.0 copy-start.14
  87.1 1.0 copy-start.16
  88.1 0.7 copy-start.22
  93.4 6.4 %collective-permute-start.8 = (bf16[80,3072]{1,0:T(8,128)(2,1)S(1)}, bf16[80,3072]{1,0:T(8,128)(2,1)S(1)}, u32[]{:S(2)}, u32[]{:S(2)}) collective-permute-start(bf16[80,3072]{1,0:T(8,128)(2,1)S(1)} %get-tuple-element.32), channel_id=1, source_target_pairs={{0,64},{64,0},{128,192},{192,128},{256,320},{320,256},{384,448},{4... | collective-permute-start | bytes 1474568 | tf_op jit(solution)/shard_map/ppermute | solution.py:234
  97.9 13.8 %collective-permute-start.7 = (bf16[240,3072]{1,0:T(8,128)(2,1)S(1)}, bf16[240,3072]{1,0:T(8,128)(2,1)S(1)}, u32[]{:S(2)}, u32[]{:S(2)}) collective-permute-start(bf16[240,3072]{1,0:T(8,128)(2,1)S(1)} %get-tuple-element.30), channel_id=1, source_target_pairs={{0,64},{64,0},{128,192},{192,128},{256,320},{320,256},{384,448},{4... | collective-permute-start | bytes 4423688 | tf_op jit(solution)/shard_map/ppermute | solution.py:234
  100.0 17.0 %collective-permute-start.11 = (bf16[40,3072]{1,0:T(8,128)(2,1)S(1)}, bf16[40,3072]{1,0:T(8,128)(2,1)S(1)}, u32[]{:S(2)}, u32[]{:S(2)}) collective-permute-start(bf16[40,3072]{1,0:T(8,128)(2,1)S(1)} %get-tuple-element.44), channel_id=1, source_target_pairs={{0,384},{64,448},{128,0},{192,64},{256,128},{320,192},{384,256},{4... | collective-permute-start | bytes 737288 | tf_op jit(solution)/shard_map/ppermute | solution.py:238
  109.8 11.1 %collective-permute-start.9 = (bf16[40,3072]{1,0:T(8,128)(2,1)S(1)}, bf16[40,3072]{1,0:T(8,128)(2,1)S(1)}, u32[]{:S(2)}, u32[]{:S(2)}) collective-permute-start(bf16[40,3072]{1,0:T(8,128)(2,1)S(1)} %get-tuple-element.45), channel_id=1, source_target_pairs={{0,128},{64,192},{128,256},{192,320},{256,384},{320,448},{384,0},{... | collective-permute-start | bytes 737288 | tf_op jit(solution)/shard_map/ppermute | solution.py:238
  121.1 12.0 %collective-permute-start.10 = (bf16[80,3072]{1,0:T(8,128)(2,1)S(1)}, bf16[80,3072]{1,0:T(8,128)(2,1)S(1)}, u32[]{:S(2)}, u32[]{:S(2)}) collective-permute-start(bf16[80,3072]{1,0:T(8,128)(2,1)S(1)} %pad_maximum_fusion), channel_id=1, source_target_pairs={{0,128},{64,192},{128,256},{192,320},{256,384},{320,448},{384,0},{... | collective-permute-start | bytes 1474568 | tf_op jit(solution)/shard_map/ppermute | solution.py:238
  123.3 11.0 %collective-permute-start.12 = (bf16[80,3072]{1,0:T(8,128)(2,1)S(1)}, bf16[80,3072]{1,0:T(8,128)(2,1)S(1)}, u32[]{:S(2)}, u32[]{:S(2)}) collective-permute-start(bf16[80,3072]{1,0:T(8,128)(2,1)S(1)} %pad_maximum_fusion.1), channel_id=1, source_target_pairs={{0,384},{64,448},{128,0},{192,64},{256,128},{320,192},{384,256},{4... | collective-permute-start | bytes 1474568 | tf_op jit(solution)/shard_map/ppermute | solution.py:238
  134.8 20.0 %collective-permute-start.14 = (bf16[80,3072]{1,0:T(8,128)(2,1)S(1)}, bf16[80,3072]{1,0:T(8,128)(2,1)S(1)}, u32[]{:S(2)}, u32[]{:S(2)}) collective-permute-start(bf16[80,3072]{1,0:T(8,128)(2,1)S(1)} %shard_map.132), channel_id=1, source_target_pairs={{0,128},{64,192},{128,256},{192,320},{256,384},{320,448},{384,0},{... | collective-permute-start | bytes 1474568 | tf_op jit(solution)/shard_map/ppermute | solution.py:238
  142.3 14.8 %collective-permute-start.13 = (bf16[80,3072]{1,0:T(8,128)(2,1)S(1)}, bf16[80,3072]{1,0:T(8,128)(2,1)S(1)}, u32[]{:S(2)}, u32[]{:S(2)}) collective-permute-start(bf16[80,3072]{1,0:T(8,128)(2,1)S(1)} %shard_map.132), channel_id=1, source_target_pairs={{0,384},{64,448},{128,0},{192,64},{256,128},{320,192},{384,256},{4... | collective-permute-start | bytes 1474568 | tf_op jit(solution)/shard_map/ppermute | solution.py:238
  154.7 19.4 %collective-permute-start.15 = (bf16[40,3072]{1,0:T(8,128)(2,1)S(1)}, bf16[40,3072]{1,0:T(8,128)(2,1)S(1)}, u32[]{:S(2)}, u32[]{:S(2)}) collective-permute-start(bf16[40,3072]{1,0:T(8,128)(2,1)S(1)} %slice.77), channel_id=1, source_target_pairs={{0,128},{64,192},{128,256},{192,320},{256,384},{320,448},{384,0},{... | collective-permute-start | bytes 737288 | tf_op jit(solution)/shard_map/ppermute | solution.py:238
  157.1 19.4 %collective-permute-start.16 = (bf16[40,3072]{1,0:T(8,128)(2,1)S(1)}, bf16[40,3072]{1,0:T(8,128)(2,1)S(1)}, u32[]{:S(2)}, u32[]{:S(2)}) collective-permute-start(bf16[40,3072]{1,0:T(8,128)(2,1)S(1)} %slice.78), channel_id=1, source_target_pairs={{0,384},{64,448},{128,0},{192,64},{256,128},{320,192},{384,256},{4... | collective-permute-start | bytes 737288 | tf_op jit(solution)/shard_map/ppermute | solution.py:238
  176.5 19.3 %copy-start.3 = (bf16[320,3072]{1,0:T(8,128)(2,1)}, bf16[320,3072]{1,0:T(8,128)(2,1)S(1)}, u32[]{:S(2)}) copy-start(bf16[320,3072]{1,0:T(8,128)(2,1)S(1)} %constant_dynamic-update-slice_fusion.part_ref) | copy-start | bytes 5898244
  176.5 21.1 %collective-permute-start.17 = (bf16[320,3072]{1,0:T(8,128)(2,1)S(1)}, bf16[320,3072]{1,0:T(8,128)(2,1)S(1)}, u32[]{:S(2)}, u32[]{:S(2)}) collective-permute-start(bf16[320,3072]{1,0:T(8,128)(2,1)S(1)} %constant_dynamic-update-slice_fusion.part_ref), channel_id=1, source_target_pairs={{0,64},{64,0},{128,192},{192,128},{256,320},{320,256},{384,448},{4... | collective-permute-start | bytes 5898248 | tf_op jit(solution)/shard_map/ppermute | solution.py:234
  197.6 2.0 copy-start.5
  199.6 24.1 %copy-start.19 = (f32[64,256]{1,0:T(8,128)S(1)}, f32[64,256]{1,0:T(8,128)}, u32[]{:S(2)}) copy-start(f32[64,256]{1,0:T(8,128)} %copy-done.18) | copy-start | bytes 196612
  224.6 0.8 copy-start.6
  225.4 6.7 %copy-start.4 = (bf16[320,3072]{1,0:T(8,128)(2,1)S(1)}, bf16[320,3072]{1,0:T(8,128)(2,1)}, u32[]{:S(2)}) copy-start(bf16[320,3072]{1,0:T(8,128)(2,1)} %copy-done.3) | copy-start | bytes 5898244
  225.4 19.0 %all-to-all-start.4 = ((bf16[8,32,896]{2,1,0:T(8,128)(2,1)}), bf16[8,32,896]{2,1,0:T(8,128)(2,1)S(1)}, u32[]{:S(2)}, u32[]{:S(2)}) async-start(bf16[8,32,896]{2,1,0:T(8,128)(2,1)} %bitcast.28), calls=%async_computation.4 | async-start | bytes 917504 | tf_op jit(solution)/shard_map/all_to_all | solution.py:270
